TPU v7x, 128 devices: a whole 4x4x4 slice. The times are simulated.
128 devices in a mesh: row: 8 (over y, core), col: 16 (over x, z).
Axes of the slice: x: 4, y: 4, z: 4, core: 2. Of those that a mesh axis runs over, the one named last changes fastest.
Arguments:
- object_planes: float32 [2, 4096, 8192], P(None, 'row', 'col'), may hold values from -6 to 6
- probe_planes: float32 [2, 2, 256, 256], replicated, may hold values from -3 to 3
- offsets: int32 [1024, 2], P(('row', 'col')), may hold values from 0 to 7936, as said below
- photon_counts: int32 [1024, 256, 256], P(('row', 'col')), may hold values from 0 to 8
- live_counts: int32 [8, 16], P('row', 'col'), may hold values from 1 to 8, as said below
Outputs:
- new_object: float32 [2, 4096, 8192], P(None, 'row', 'col')
- new_probe: float32 [2, 2, 256, 256], replicated
Inputs may be any that keep to these rules, and one draw needn't show every extreme that they name: `offsets`: each slot's patch lies inside the object and its top-left pixel lies in the tile of the device that holds the slot (tiles of 512 x 512 pixels, device (r, c) holding tile (r, c)). `live_counts`: some device has all 8 slots live in every draw.
All inputs are finite; a program needn't handle non-finite values.
Results may differ from a plain program's by a relative error of at most 0.0003.
Values sent between devices are 32-bit elements; how exact they have to be, the bound alone decides.
No kernel may reach another device: no remote copies, remote signals or barrier semaphores. Data moves between devices by JAX's collectives and lax.ppermute only.
A program may use at most 64 MiB of HBM per device.

v0:
```python
import math

import ml_dtypes
import numpy as np
import jax
import jax.numpy as jnp
from jax import lax
from jax.experimental import pallas as pl
from jax.experimental.pallas import tpu as pltpu
from jax.sharding import PartitionSpec as P

f32, bf16 = jnp.float32, jnp.bfloat16
W = 256
H = 128


def make_tables():
    b = np.arange(H)[:, None]
    q = np.arange(H)[None, :]
    right = []
    for p in (0, 1):
        ang = 2.0 * np.pi * (((2 * q + p) * b) % W) / W
        c, s = np.cos(ang) / 16.0, np.sin(ang) / 16.0
        right.append(np.block([[c, -s], [s, c]]))
    def split(t):
        hi = t.astype(np.float32).astype(ml_dtypes.bfloat16)
        lo = (t - hi.astype(np.float64)).astype(np.float32).astype(ml_dtypes.bfloat16)
        return hi, lo
    as_rhs = []
    as_lhs = []
    for t in (right[0], right[1], right[0].T, right[1].T):
        hi, lo = split(t)
        as_rhs.append(np.concatenate([hi, hi, lo], 0))
        as_lhs.append(np.concatenate([hi, hi, lo], 1))
    rhs = np.stack(as_rhs)
    lhs = np.stack(as_lhs)
    return rhs, lhs


def split(x):
    hi = x.astype(bf16)
    lo = (x - hi.astype(f32)).astype(bf16)
    return hi, lo


def rmul(x, t):
    hi, lo = split(x)
    return jnp.dot(jnp.concatenate([hi, lo, hi], 1), t, preferred_element_type=f32)


def lmul(t, x):
    hi, lo = split(x)
    return jnp.dot(t, jnp.concatenate([hi, lo, hi], 0), preferred_element_type=f32)


def cat1(a, b):
    return jnp.concatenate([a, b], 1)


def cat0(a, b):
    return jnp.concatenate([a, b], 0)


def main_kernel(offs, live, anchor, obj, right_top, right_bot, below, corner, probe, sq, rhs, lhs,
                o_part, o_rtop, o_rbot, o_corner, o_below, o_probe,
                cov, acc, patch, pacc, prv, sqv, rt, lt, far, term, sems):
    ins = [
        (obj, cov.at[:, 0:512, 0:512]),
        (right_top, cov.at[:, 0:256, 512:768]),
        (right_bot, cov.at[:, 256:512, 512:768]),
        (below, cov.at[:, 512:768, 0:512]),
        (corner, cov.at[:, 512:768, 512:768]),
        (probe, prv),
        (rhs, rt),
        (lhs, lt),
        (sq, sqv),
    ]
    copies = [pltpu.make_async_copy(s, d, sems.at[i]) for i, (s, d) in enumerate(ins)]
    for c in copies:
        c.start()
    acc[...] = jnp.zeros_like(acc)
    pacc[...] = jnp.zeros_like(pacc)
    for c in copies:
        c.wait()
    lane = lax.broadcasted_iota(jnp.int32, (W, H), 1)
    sub9 = lax.broadcasted_iota(jnp.int32, (33, 8, H), 1)
    sub = lax.broadcasted_iota(jnp.int32, (32, 8, H), 1)

    def slot(s, carry):
        top = offs[s, 0] - anchor[0]
        left = offs[s, 1] - anchor[1]
        la = pl.multiple_of(lax.div(left, 128) * 128, 128)
        ls = lax.rem(left, 128)
        back = lax.rem(128 - ls, 128)
        ta = pl.multiple_of(lax.div(top, 8) * 8, 8)
        rs = lax.rem(top, 8)
        rback = lax.rem(8 - rs, 8)
        for c in range(2):
            t = []
            for k in range(3):
                v = cov[c, pl.ds(ta, W + 8), pl.ds(la + 128 * k, H)]
                v = pltpu.roll(pltpu.roll(v, back, 1).reshape(33, 8, H), rback, 1)
                t.append(jnp.where(sub < 8 - rs, v[:32], v[1:]).reshape(W, H))
            for k in range(2):
                patch[c, :, 128 * k:128 * k + 128] = jnp.where(lane < 128 - ls, t[k], t[k + 1])
        for m in range(2):
            pr, pi = prv[0, m], prv[1, m]
            xr, xi = patch[0], patch[1]
            wr = pr * xr - pi * xi
            wi = pr * xi + pi * xr
            e = cat1(wr[:, :H] + wr[:, H:], wi[:, :H] + wi[:, H:])
            o = cat1(wr[:, :H] - wr[:, H:], wi[:, :H] - wi[:, H:])
            ye = rmul(e, rt[0])
            yo = rmul(o, rt[1])
            er, ei = cat1(ye[:, :H], yo[:, :H]), cat1(ye[:, H:], yo[:, H:])
            fe = cat0(er[:H] + er[H:], ei[:H] + ei[H:])
            fo = cat0(er[:H] - er[H:], ei[:H] - ei[H:])
            far[m, 0] = lmul(lt[2], fe)
            far[m, 1] = lmul(lt[3], fo)
        facs = []
        for p in range(2):
            mod = None
            for m in range(2):
                a = far[m, p]
                v = a[:H] * a[:H] + a[H:] * a[H:]
                mod = v if mod is None else mod + v
            facs.append(1.0 - sqv[s, H * p:H * p + H, :] * lax.rsqrt(jnp.maximum(mod, 0.1)))
        for m in range(2):
            be = lmul(lt[0], far[m, 0] * cat0(facs[0], facs[0]))
            bo = lmul(lt[1], far[m, 1] * cat0(facs[1], facs[1]))
            s_, d_ = be + bo, be - bo
            xr = cat0(s_[:H], d_[:H])
            xi = cat0(s_[H:], d_[H:])
            de = rmul(cat1(xr[:, :H], xi[:, :H]), rt[2])
            do = rmul(cat1(xr[:, H:], xi[:, H:]), rt[3])
            s_, d_ = de + do, de - do
            br = cat1(s_[:, :H], d_[:, :H])
            bi = cat1(s_[:, H:], d_[:, H:])
            pr, pi = prv[0, m], prv[1, m]
            xr, xi = patch[0], patch[1]
            tr, ti = pr * br + pi * bi, pr * bi - pi * br
            if m == 0:
                term[0], term[1] = tr, ti
            else:
                term[0] += tr
                term[1] += ti
            pacc[0, m] += xr * br + xi * bi
            pacc[1, m] += xr * bi - xi * br
        for c in range(2):
            r = [pltpu.roll(term[c, :, 128 * k:128 * k + 128], ls, 1) for k in range(2)]
            z = jnp.zeros_like(r[0])
            keep = lane >= ls
            parts = [jnp.where(keep, r[0], z), jnp.where(keep, r[1], r[0]), jnp.where(keep, z, r[1])]
            for k in range(3):
                v = pltpu.roll(parts[k].reshape(32, 8, H), rs, 1)
                z8 = jnp.zeros((1, 8, H), f32)
                v = jnp.where(sub9 >= rs, jnp.concatenate([v, z8], 0), jnp.concatenate([z8, v], 0))
                acc[c, pl.ds(ta, W + 8), pl.ds(la + 128 * k, H)] += v.reshape(W + 8, H)
        return carry

    lax.fori_loop(0, live[0], slot, 0)
    cov[:, 0:512, 0:512] = cov[:, 0:512, 0:512] - 0.5 * acc[:, 0:512, 0:512]
    outs = [
        (cov.at[:, 0:512, 0:512], o_part),
        (acc.at[:, 0:256, 512:768], o_rtop),
        (acc.at[:, 256:512, 512:768], o_rbot),
        (acc.at[:, 512:768, 512:768], o_corner),
        (acc.at[:, 512:768, 0:512], o_below),
        (pacc, o_probe),
    ]
    copies = [pltpu.make_async_copy(s, d, sems.at[i]) for i, (s, d) in enumerate(outs)]
    for c in copies:
        c.start()
    for c in copies:
        c.wait()


def main_call(offs, live, anchor, obj, right_top, right_bot, below, corner, probe, sq):
    rhs, lhs = (jnp.asarray(t) for t in make_tables())
    any_ = pl.BlockSpec(memory_space=pl.ANY)
    smem = pl.BlockSpec(memory_space=pltpu.SMEM)
    S = lambda *s: jax.ShapeDtypeStruct(s, f32)
    return pl.pallas_call(
        main_kernel,
        out_shape=(S(2, 512, 512), S(2, 256, 256), S(2, 256, 256), S(2, 256, 256), S(2, 256, 512), S(2, 2, 256, 256)),
        in_specs=[smem] * 3 + [any_] * 9,
        out_specs=[any_] * 6,
        scratch_shapes=[
            pltpu.VMEM((2, 768, 768), f32),
            pltpu.VMEM((2, 768, 768), f32),
            pltpu.VMEM((2, W, W), f32),
            pltpu.VMEM((2, 2, W, W), f32),
            pltpu.VMEM((2, 2, W, W), f32),
            pltpu.VMEM((8, W, W), f32),
            pltpu.VMEM((4, 768, W), bf16),
            pltpu.VMEM((4, W, 768), bf16),
            pltpu.VMEM((2, 2, W, W), f32),
            pltpu.VMEM((2, W, W), f32),
            pltpu.SemaphoreType.DMA((9,)),
        ],
        compiler_params=pltpu.CompilerParams(vmem_limit_bytes=40 * 2**20),
        name="slots",
    )(offs, live, anchor, obj, right_top, right_bot, below, corner, probe, sq, rhs, lhs)


def prep_kernel(counts, pm, pmt, out):
    i = counts[0].astype(f32).astype(bf16)
    a = jnp.dot(pm[...], i, preferred_element_type=f32).astype(bf16)
    out[0] = jnp.sqrt(jnp.dot(a, pmt[...], preferred_element_type=f32))


def prep_call(counts):
    order = np.concatenate([np.arange(0, W, 2), np.arange(1, W, 2)])
    pm = np.zeros((W, W), np.float32)
    pm[np.arange(W), order] = 1.0
    full = pl.BlockSpec((W, W), lambda s: (0, 0))
    blk = pl.BlockSpec((1, W, W), lambda s: (s, 0, 0))
    return pl.pallas_call(
        prep_kernel,
        grid=(8,),
        out_shape=jax.ShapeDtypeStruct((8, W, W), f32),
        in_specs=[blk, full, full],
        out_specs=blk,
        name="roots",
    )(counts, jnp.asarray(pm.astype(ml_dtypes.bfloat16)), jnp.asarray(pm.T.astype(ml_dtypes.bfloat16)))


def moved(value, axes, pairs):
    return lax.ppermute(value, axes, pairs)


def finish_kernel(part, above, top, bot, out):
    h = pl.program_id(1)

    @pl.when(h == 0)
    def _():
        out[0] = part[0] - 0.5 * above[0]
        out[0, :, :W] -= 0.5 * top[0]

    @pl.when(h == 1)
    def _():
        out[0, :, W:] = part[0, :, W:]
        out[0, :, :W] = part[0, :, :W] - 0.5 * bot[0]


def finish_call(part, above, top, bot):
    wide = pl.BlockSpec((1, W, 512), lambda c, h: (c, h, 0))
    return pl.pallas_call(
        finish_kernel,
        grid=(2, 2),
        out_shape=jax.ShapeDtypeStruct((2, 512, 512), f32),
        in_specs=[
            wide,
            pl.BlockSpec((1, W, 512), lambda c, h: (c, 0, 0)),
            pl.BlockSpec((1, W, W), lambda c, h: (c, 0, 0)),
            pl.BlockSpec((1, W, W), lambda c, h: (c, 0, 0)),
        ],
        out_specs=wide,
        name="finish",
    )(part, above, top, bot)


def swap_cores(value):
    return lax.ppermute(value, "core", [(0, 1), (1, 0)])


def summed_over_all(x):
    n = x.shape[0] // 2
    chips = lax.axis_size("y") * lax.axis_size("col")
    c = lax.axis_index("core")
    mine = lax.dynamic_slice_in_dim(x, c * n, n, 0)
    other = lax.dynamic_slice_in_dim(x, (1 - c) * n, n, 0)
    half = mine + swap_cores(other)
    rows = n // chips
    axes = ("y", "col")
    piece = lax.all_to_all(half.reshape(chips, rows, W), axes, 0, 0).sum(0)
    half = lax.all_to_all(jnp.broadcast_to(piece[None], (chips, rows, W)), axes, 0, 0).reshape(n, W)
    rest = swap_cores(half)
    return jnp.where(c == 0, jnp.concatenate([half, rest], 0), jnp.concatenate([rest, half], 0))


def shards(object_planes, probe_planes, offsets, photon_counts, live_counts):
    n_row = lax.axis_size("y") * lax.axis_size("core")
    n_col = lax.axis_size("col")
    rows = ("y", "core")
    row = lax.axis_index(rows)
    col = lax.axis_index("col")
    up = [(i, i - 1) for i in range(1, n_row)]
    down = [(i - 1, i) for i in range(1, n_row)]
    to_left = [(i, i - 1) for i in range(1, n_col)]
    to_right = [(i - 1, i) for i in range(1, n_col)]

    right_top = lax.ppermute(object_planes[:, :W, :W], "col", to_left)
    below = lax.ppermute(object_planes[:, :W, :], rows, up)
    right_bot = lax.ppermute(object_planes[:, W:, :W], "col", to_left)
    corner = lax.ppermute(right_top, rows, up)
    roots = prep_call(photon_counts)
    anchor = jnp.stack([row * 512, col * 512]).astype(jnp.int32)
    part, g_top, g_bot, g_corner, g_below, g_probe = main_call(
        offsets, live_counts.reshape(1), anchor, object_planes, right_top, right_bot, below, corner, probe_planes, roots
    )
    corner_in = lax.ppermute(g_corner, rows, down)
    bot_in = lax.ppermute(g_bot, "col", to_right)
    above_in = lax.ppermute(g_below, rows, down)
    top_in = lax.ppermute(g_top + corner_in, "col", to_right)
    total = summed_over_all(g_probe.reshape(1024, W)).reshape(probe_planes.shape)
    new_probe = probe_planes - total * (1.0 / math.sqrt(offsets.shape[0] * n_row * n_col))
    new_object = finish_call(part, above_in, top_in, bot_in)
    return new_object, new_probe


def solution(mesh):
    split = jax.sharding.Mesh(
        mesh.devices.reshape(mesh.shape["row"] // 2, 2, mesh.shape["col"]), ("y", "core", "col")
    )
    rows = ("y", "core")
    in_specs = (
        P(None, rows, "col"),
        P(),
        P(("y", "core", "col"), None),
        P(("y", "core", "col"), None, None),
        P(rows, "col"),
    )
    out_specs = (P(None, rows, "col"), P())
    return jax.shard_map(shards, mesh=split, in_specs=in_specs, out_specs=out_specs, check_vma=False)
```

profile of v0, /device:TPU:2, one launch (start us, length us, event | category | flops | bytes accessed | tf_op | source)
XLA Modules:
  0.0 143.4 jit_solution(7066059161541046475)
XLA Ops:
  0.7 2.2 %fusion.1 = (f32[2,256,256]{2,1,0:T(8,128)}, f32[2,256,256]{2,1,0:T(8,128)S(1)}) fusion(f32[2,512,512]{2,1,0:T(8,128)} %obj.1), kind=kLoop, calls=%fused_computation.5 | loop fusion | bytes 2097152 | tf_op jit(solution)/shard_map/slice | solution.py:295
  2.9 5.9 %collective-permute-start = (f32[2,256,256]{2,1,0:T(8,128)S(1)}, f32[2,256,256]{2,1,0:T(8,128)S(1)}, u32[]{:S(2)}, u32[]{:S(2)}) collective-permute-start(f32[2,256,256]{2,1,0:T(8,128)S(1)} %get-tuple-element.15), channel_id=1, source_target_pairs={{1,0},{2,1},{3,2},{4,3},{5,4},{6,5},{7,6},{8,7},{9,8},{10,9},{11,1... | collective-permute-start | bytes 1572872 | tf_op jit(solution)/shard_map/ppermute | solution.py:293
  8.8 1.0 slice.11
  9.9 1.3 collective-permute-start.2
  11.1 2.3 %collective-permute-start.1 = (f32[2,256,256]{2,1,0:T(8,128)}, f32[2,256,256]{2,1,0:T(8,128)}, u32[]{:S(2)}, u32[]{:S(2)}) collective-permute-start(f32[2,256,256]{2,1,0:T(8,128)} %get-tuple-element.14), channel_id=1, source_target_pairs={{1,0},{2,1},{3,2},{4,3},{5,4},{6,5},{7,6},{8,7},{9,8},{10,9},{11,1... | collective-permute-start | bytes 1572872 | tf_op jit(solution)/shard_map/ppermute | solution.py:295
  13.5 7.6 %collective-permute-done.right_top = f32[2,256,256]{2,1,0:T(8,128)S(1)} collective-permute-done((f32[2,256,256]{2,1,0:T(8,128)S(1)}, f32[2,256,256]{2,1,0:T(8,128)S(1)}, u32[]{:S(2)}, u32[]{:S(2)}) %collective-permute-start) | collective-permute-done | bytes 524320 | tf_op jit(solution)/shard_map/ppermute | solution.py:293
  21.1 1.3 collective-permute-start.3
  23.2 7.1 %roots.1.sq = f32[8,256,256]{2,1,0:T(8,128)} custom-call(s32[8,256,256]{2,1,0:T(8,128)} %counts.1, bf16[256,256]{1,0:T(8,128)(2,1)} %constant.37.clone.pm, bf16[256,256]{1,0:T(8,128)(2,1)} %constant.38.clone.pmt), custom_call_target="tpu_custom_call" | custom-call | tf_op jit(solution)/shard_map/roots/pallas_call | solution.py:218
  30.4 0.9 collective-permute-done.1.right_bot
  31.3 1.4 copy-done.3
  32.7 1.0 copy-done.6
  33.8 7.6 %slots.1 = (f32[2,512,512]{2,1,0:T(8,128)S(1)}, f32[2,256,256]{2,1,0:T(8,128)S(1)}, f32[2,256,256]{2,1,0:T(8,128)S(1)}, f32[2,256,256]{2,1,0:T(8,128)S(1)}, f32[...) custom-call(s32[8,2]{1,0:T(8,128)S(1)} %copy.11.offs, s32[1]{0:T(128)} %bitcast.8.live, s32[2]{0:T(128)S(1)} %pad_add_fusion.anchor, ...), custom_call_target="tpu_custom_call" | custom-call | tf_op jit(solution)/shard_map/slots/pallas_call | solution.py:183
  41.4 1.3 copy-done.1
  43.6 1.0 copy-done.4
  45.4 19.3 %collective-permute-start.8 = (f32[512,256]{1,0:T(8,128)}, f32[512,256]{1,0:T(8,128)}, u32[]{:S(2)}, u32[]{:S(2)}) collective-permute-start(f32[512,256]{1,0:T(8,128)} %constant_dynamic-slice_fusion), channel_id=1, source_target_pairs={{0,16},{16,0},{1,17},{17,1},{2,18},{18,2},{3,19},{19,3},{4,20},{20... | collective-permute-start | bytes 1572872 | tf_op jit(solution)/shard_map/ppermute | solution.py:264
  64.6 1.9 %collective-permute-done.8 = f32[512,256]{1,0:T(8,128)} collective-permute-done((f32[512,256]{1,0:T(8,128)}, f32[512,256]{1,0:T(8,128)}, u32[]{:S(2)}, u32[]{:S(2)}) %collective-permute-start.8) | collective-permute-done | bytes 524320 | tf_op jit(solution)/shard_map/ppermute | solution.py:264
  66.5 2.1 %add_bitcast_fusion = f32[64,8,256]{2,1,0:T(8,128)} fusion(f32[512,256]{1,0:T(8,128)} %collective-permute-done.8, f32[1024,256]{1,0:T(8,128)} %bitcast.10, s32[]{:T(128)S(6)} %select_n.17), kind=kLoop, calls=%fused_computation.2 | loop fusion | flops 131072 | bytes 1572868 | tf_op jit(solution)/shard_map/reshape | solution.py:276
  68.6 14.1 %all-to-all-start = ((f32[64,8,256]{2,1,0:T(8,128)}), f32[64,8,256]{2,1,0:T(8,128)}, u32[]{:S(2)}, u32[]{:S(2)}) async-start(f32[64,8,256]{2,1,0:T(8,128)} %add_bitcast_fusion), calls=%async_computation | async-start | bytes 1048576 | tf_op jit(solution)/shard_map/all_to_all | solution.py:276
  82.7 2.5 %collective-permute-start.5 = (f32[2,256,256]{2,1,0:T(8,128)}, f32[2,256,256]{2,1,0:T(8,128)}, u32[]{:S(2)}, u32[]{:S(2)}) collective-permute-start(f32[2,256,256]{2,1,0:T(8,128)} %copy-done.11), channel_id=1, source_target_pairs={{0,16},{16,32},{32,48},{48,64},{64,80},{80,96},{96,112},{1,17},{17... | collective-permute-start | bytes 1572872 | tf_op jit(solution)/shard_map/ppermute | solution.py:302
  85.2 3.9 %collective-permute-start.4 = (f32[2,256,512]{2,1,0:T(8,128)S(1)}, f32[2,256,512]{2,1,0:T(8,128)}, u32[]{:S(2)}, u32[]{:S(2)}) collective-permute-start(f32[2,256,512]{2,1,0:T(8,128)S(1)} %copy-done.8), channel_id=1, source_target_pairs={{0,16},{16,32},{32,48},{48,64},{64,80},{80,96},{96,112},{1,17},{17... | collective-permute-start | bytes 3145736 | tf_op jit(solution)/shard_map/ppermute | solution.py:304
  89.1 6.3 %all-to-all-done = f32[64,8,256]{2,1,0:T(8,128)} async-done(((f32[64,8,256]{2,1,0:T(8,128)}), f32[64,8,256]{2,1,0:T(8,128)}, u32[]{:S(2)}, u32[]{:S(2)}) %all-to-all-start) | async-done | bytes 524320 | tf_op jit(solution)/shard_map/all_to_all | solution.py:276
  95.5 1.1 reduce_sum.9
  97.4 6.3 %all-to-all-start.1 = ((f32[64,8,256]{2,1,0:T(8,128)}), f32[64,8,256]{2,1,0:T(8,128)}, u32[]{:S(2)}, u32[]{:S(2)}) async-start(f32[64,8,256]{2,1,0:T(8,128)} %broadcast_in_dim.2), calls=%async_computation.1 | async-start | bytes 1048576 | tf_op jit(solution)/shard_map/all_to_all | solution.py:277
  103.7 3.4 %collective-permute-start.7 = (f32[2,256,256]{2,1,0:T(8,128)S(1)}, f32[2,256,256]{2,1,0:T(8,128)}, u32[]{:S(2)}, u32[]{:S(2)}) collective-permute-start(f32[2,256,256]{2,1,0:T(8,128)S(1)} %copy-done.10), channel_id=1, source_target_pairs={{0,1},{1,2},{2,3},{3,4},{4,5},{5,6},{6,7},{7,8},{8,9},{9,10},{10,1... | collective-permute-start | bytes 1572872 | tf_op jit(solution)/shard_map/ppermute | solution.py:303
  107.1 1.9 %add.16 = f32[2,256,256]{2,1,0:T(8,128)} add(f32[2,256,256]{2,1,0:T(8,128)S(1)} %get-tuple-element.10, f32[2,256,256]{2,1,0:T(8,128)} %collective-permute-done.5) | non-fusion elementwise | flops 131072 | bytes 1572864 | tf_op jit(solution)/shard_map/add | solution.py:305
  109.0 3.4 %collective-permute-start.6 = (f32[2,256,256]{2,1,0:T(8,128)}, f32[2,256,256]{2,1,0:T(8,128)S(1)}, u32[]{:S(2)}, u32[]{:S(2)}) collective-permute-start(f32[2,256,256]{2,1,0:T(8,128)} %add.16), channel_id=1, source_target_pairs={{0,1},{1,2},{2,3},{3,4},{4,5},{5,6},{6,7},{7,8},{8,9},{9,10},{10,1... | collective-permute-start | bytes 1572872 | tf_op jit(solution)/shard_map/ppermute | solution.py:305
  112.4 3.6 %all-to-all-done.1 = f32[64,8,256]{2,1,0:T(8,128)} async-done(((f32[64,8,256]{2,1,0:T(8,128)}), f32[64,8,256]{2,1,0:T(8,128)}, u32[]{:S(2)}, u32[]{:S(2)}) %all-to-all-start.1) | async-done | bytes 524320 | tf_op jit(solution)/shard_map/all_to_all | solution.py:277
  116.7 9.7 %collective-permute-done.7.bot = f32[2,256,256]{2,1,0:T(8,128)} collective-permute-done((f32[2,256,256]{2,1,0:T(8,128)S(1)}, f32[2,256,256]{2,1,0:T(8,128)}, u32[]{:S(2)}, u32[]{:S(2)}) %collective-permute-start.7) | collective-permute-done | bytes 524320 | tf_op jit(solution)/shard_map/ppermute | solution.py:303
  126.4 9.0 %collective-permute-done.6.top = f32[2,256,256]{2,1,0:T(8,128)S(1)} collective-permute-done((f32[2,256,256]{2,1,0:T(8,128)}, f32[2,256,256]{2,1,0:T(8,128)S(1)}, u32[]{:S(2)}, u32[]{:S(2)}) %collective-permute-start.6) | collective-permute-done | bytes 524320 | tf_op jit(solution)/shard_map/ppermute | solution.py:305
  136.2 4.3 %finish.1 = f32[2,512,512]{2,1,0:T(8,128)} custom-call(f32[2,512,512]{2,1,0:T(8,128)} %copy-done.1, f32[2,256,512]{2,1,0:T(8,128)} %collective-permute-done.4.above, f32[2,256,256]{2,1,0:T(8,128)} %copy-done.13, f32[2,256,256]{2,1,0:T(8,128)} %collective-permute-done.7.bot), custom_call_target="tpu_custom_call" | custom-call | tf_op jit(solution)/shard_map/finish/pallas_call | solution.py:248
  140.5 1.7 %fusion = f32[1024,256]{1,0:T(8,128)S(1)} fusion(f32[512,256]{1,0:T(8,128)} %collective-permute-done.9, f32[512,256]{1,0:T(8,128)} %bitcast.5, pred[]{:T(512)S(6)} %eq.3), kind=kLoop, calls=%fused_computation.1 | loop fusion | flops 1048576 | bytes 2097153 | tf_op jit(solution)/shard_map/mul | solution.py:307
  142.3 1.1 sub.7
  (36 shorter events, 4.2 us)
Async XLA Ops:
  0.6 8.2 %copy-start.12 = (f32[2,512,512]{2,1,0:T(8,128)S(1)}, f32[2,512,512]{2,1,0:T(8,128)}, u32[]{:S(2)}) copy-start(f32[2,512,512]{2,1,0:T(8,128)} %obj.1) | copy-start | bytes 6291460
  0.6 21.8 %copy-start.14 = (s32[8,2]{0,1:T(2,128)S(1)}, s32[8,2]{0,1:T(2,128)}, u32[]{:S(2)}) copy-start(s32[8,2]{0,1:T(2,128)} %param.11) | copy-start | bytes 196
  2.9 18.2 %collective-permute-start = (f32[2,256,256]{2,1,0:T(8,128)S(1)}, f32[2,256,256]{2,1,0:T(8,128)S(1)}, u32[]{:S(2)}, u32[]{:S(2)}) collective-permute-start(f32[2,256,256]{2,1,0:T(8,128)S(1)} %get-tuple-element.15), channel_id=1, source_target_pairs={{1,0},{2,1},{3,2},{4,3},{5,4},{6,5},{7,6},{8,7},{9,8},{10,9},{11,1... | collective-permute-start | bytes 1572872 | tf_op jit(solution)/shard_map/ppermute | solution.py:293
  9.9 21.5 %collective-permute-start.2 = (f32[2,256,512]{2,1,0:T(8,128)}, f32[2,256,512]{2,1,0:T(8,128)}, u32[]{:S(2)}, u32[]{:S(2)}) collective-permute-start(f32[2,256,512]{2,1,0:T(8,128)} %slice.11), channel_id=1, source_target_pairs={{16,0},{32,16},{48,32},{64,48},{80,64},{96,80},{112,96},{17,1},{33... | collective-permute-start | bytes 3145736 | tf_op jit(solution)/shard_map/ppermute | solution.py:294
  11.1 20.2 %collective-permute-start.1 = (f32[2,256,256]{2,1,0:T(8,128)}, f32[2,256,256]{2,1,0:T(8,128)}, u32[]{:S(2)}, u32[]{:S(2)}) collective-permute-start(f32[2,256,256]{2,1,0:T(8,128)} %get-tuple-element.14), channel_id=1, source_target_pairs={{1,0},{2,1},{3,2},{4,3},{5,4},{6,5},{7,6},{8,7},{9,8},{10,9},{11,1... | collective-permute-start | bytes 1572872 | tf_op jit(solution)/shard_map/ppermute | solution.py:295
  21.1 9.2 %copy-start.5 = (f32[2,256,256]{2,1,0:T(8,128)}, f32[2,256,256]{2,1,0:T(8,128)S(1)}, u32[]{:S(2)}) copy-start(f32[2,256,256]{2,1,0:T(8,128)S(1)} %collective-permute-done.right_top) | copy-start | bytes 1572868
  21.1 10.2 %collective-permute-start.3 = (f32[2,256,256]{2,1,0:T(8,128)S(1)}, f32[2,256,256]{2,1,0:T(8,128)}, u32[]{:S(2)}, u32[]{:S(2)}) collective-permute-start(f32[2,256,256]{2,1,0:T(8,128)S(1)} %collective-permute-done.right_top), channel_id=1, source_target_pairs={{16,0},{32,16},{48,32},{64,48},{80,64},{96,80},{112,96},{17,1},{33... | collective-permute-start | bytes 1572872 | tf_op jit(solution)/shard_map/ppermute | solution.py:296
  23.2 8.2 %copy-start = (f32[2,2,256,256]{3,2,1,0:T(8,128)S(1)}, f32[2,2,256,256]{3,2,1,0:T(8,128)}, u32[]{:S(2)}) copy-start(f32[2,2,256,256]{3,2,1,0:T(8,128)} %probe.1) | copy-start | bytes 3145732
  23.2 8.1 %copy-start.2 = (bf16[4,768,256]{2,1,0:T(8,128)(2,1)S(1)}, bf16[4,768,256]{2,1,0:T(8,128)(2,1)}, u32[]{:S(2)}) copy-start(bf16[4,768,256]{2,1,0:T(8,128)(2,1)} %constant.39.clone.rhs) | copy-start | bytes 4718596
  31.3 1.4 copy-start.3
  32.7 1.0 copy-start.6
  41.4 1.3 copy-start.1
  42.8 0.8 copy-start.9
  43.5 1.0 copy-start.4
  43.6 1.8 %copy-start.7 = (f32[2,256,512]{2,1,0:T(8,128)}, f32[2,256,512]{2,1,0:T(8,128)S(1)}, u32[]{:S(2)}) copy-start(f32[2,256,512]{2,1,0:T(8,128)S(1)} %get-tuple-element.9) | copy-start | bytes 3145732
  43.6 1.8 %copy-start.11 = (f32[2,256,256]{2,1,0:T(8,128)}, f32[2,256,256]{2,1,0:T(8,128)S(1)}, u32[]{:S(2)}) copy-start(f32[2,256,256]{2,1,0:T(8,128)S(1)} %get-tuple-element.11) | copy-start | bytes 1572868
  45.4 21.2 %collective-permute-start.8 = (f32[512,256]{1,0:T(8,128)}, f32[512,256]{1,0:T(8,128)}, u32[]{:S(2)}, u32[]{:S(2)}) collective-permute-start(f32[512,256]{1,0:T(8,128)} %constant_dynamic-slice_fusion), channel_id=1, source_target_pairs={{0,16},{16,0},{1,17},{17,1},{2,18},{18,2},{3,19},{19,3},{4,20},{20... | collective-permute-start | bytes 1572872 | tf_op jit(solution)/shard_map/ppermute | solution.py:264
  64.6 20.6 %copy-start.8 = (f32[2,256,512]{2,1,0:T(8,128)S(1)}, f32[2,256,512]{2,1,0:T(8,128)}, u32[]{:S(2)}) copy-start(f32[2,256,512]{2,1,0:T(8,128)} %copy-done.7) | copy-start | bytes 3145732
  64.6 39.1 %copy-start.10 = (f32[2,256,256]{2,1,0:T(8,128)S(1)}, f32[2,256,256]{2,1,0:T(8,128)}, u32[]{:S(2)}) copy-start(f32[2,256,256]{2,1,0:T(8,128)} %copy-done.9) | copy-start | bytes 1572868
  68.6 26.9 %all-to-all-start = ((f32[64,8,256]{2,1,0:T(8,128)}), f32[64,8,256]{2,1,0:T(8,128)}, u32[]{:S(2)}, u32[]{:S(2)}) async-start(f32[64,8,256]{2,1,0:T(8,128)} %add_bitcast_fusion), calls=%async_computation | async-start | bytes 1048576 | tf_op jit(solution)/shard_map/all_to_all | solution.py:276
  82.7 24.4 %collective-permute-start.5 = (f32[2,256,256]{2,1,0:T(8,128)}, f32[2,256,256]{2,1,0:T(8,128)}, u32[]{:S(2)}, u32[]{:S(2)}) collective-permute-start(f32[2,256,256]{2,1,0:T(8,128)} %copy-done.11), channel_id=1, source_target_pairs={{0,16},{16,32},{32,48},{48,64},{64,80},{80,96},{96,112},{1,17},{17... | collective-permute-start | bytes 1572872 | tf_op jit(solution)/shard_map/ppermute | solution.py:302
  85.2 41.2 %collective-permute-start.4 = (f32[2,256,512]{2,1,0:T(8,128)S(1)}, f32[2,256,512]{2,1,0:T(8,128)}, u32[]{:S(2)}, u32[]{:S(2)}) collective-permute-start(f32[2,256,512]{2,1,0:T(8,128)S(1)} %copy-done.8), channel_id=1, source_target_pairs={{0,16},{16,32},{32,48},{48,64},{64,80},{80,96},{96,112},{1,17},{17... | collective-permute-start | bytes 3145736 | tf_op jit(solution)/shard_map/ppermute | solution.py:304
  97.4 18.6 %all-to-all-start.1 = ((f32[64,8,256]{2,1,0:T(8,128)}), f32[64,8,256]{2,1,0:T(8,128)}, u32[]{:S(2)}, u32[]{:S(2)}) async-start(f32[64,8,256]{2,1,0:T(8,128)} %broadcast_in_dim.2), calls=%async_computation.1 | async-start | bytes 1048576 | tf_op jit(solution)/shard_map/all_to_all | solution.py:277
  103.7 22.7 %collective-permute-start.7 = (f32[2,256,256]{2,1,0:T(8,128)S(1)}, f32[2,256,256]{2,1,0:T(8,128)}, u32[]{:S(2)}, u32[]{:S(2)}) collective-permute-start(f32[2,256,256]{2,1,0:T(8,128)S(1)} %copy-done.10), channel_id=1, source_target_pairs={{0,1},{1,2},{2,3},{3,4},{4,5},{5,6},{6,7},{7,8},{8,9},{9,10},{10,1... | collective-permute-start | bytes 1572872 | tf_op jit(solution)/shard_map/ppermute | solution.py:303
  109.0 26.4 %collective-permute-start.6 = (f32[2,256,256]{2,1,0:T(8,128)}, f32[2,256,256]{2,1,0:T(8,128)S(1)}, u32[]{:S(2)}, u32[]{:S(2)}) collective-permute-start(f32[2,256,256]{2,1,0:T(8,128)} %add.16), channel_id=1, source_target_pairs={{0,1},{1,2},{2,3},{3,4},{4,5},{5,6},{6,7},{7,8},{8,9},{9,10},{10,1... | collective-permute-start | bytes 1572872 | tf_op jit(solution)/shard_map/ppermute | solution.py:305
  116.0 24.5 %collective-permute-start.9 = (f32[512,256]{1,0:T(8,128)}, f32[512,256]{1,0:T(8,128)}, u32[]{:S(2)}, u32[]{:S(2)}) collective-permute-start(f32[512,256]{1,0:T(8,128)} %bitcast.5), channel_id=1, source_target_pairs={{0,16},{16,0},{1,17},{17,1},{2,18},{18,2},{3,19},{19,3},{4,20},{20... | collective-permute-start | bytes 1572872 | tf_op jit(solution)/shard_map/ppermute | solution.py:264
  135.4 0.8 copy-start.13
where the time goes:
time: 145 us; the launch traced here: 143 us
  starting transfers between devices  64.4 us (44%)
  waiting for transfers between devices  39.1 us (27%)
  Pallas kernels  19 us (13%)
  local copies, waits for them, and re-layouts  11.4 us (8%)
  other arithmetic  8.02 us (6%)
  between operations  1.48 us (1%)
    ppermute x2, starting transfers between devices, swap_cores(): return lax.ppermute(value, 'core', [(0, 1), (1, 0)])  20 us
    all_to_all x1, starting transfers between devices, summed_over_all(): piece = lax.all_to_all(half.reshape(chips, rows, W), axes, 0, 0).sum(0)  14.1 us
    ppermute x1, waiting for transfers between devices, shards(): bot_in = lax.ppermute(g_bot, 'col', to_right)  9.7 us
    ppermute x1, waiting for transfers between devices, shards(): top_in = lax.ppermute(g_top + corner_in, 'col', to_right)  8.99 us
    ppermute x1, waiting for transfers between devices, shards(): right_top = lax.ppermute(object_planes[:, :W, :W], 'col', to_left)  7.65 us
    pallas_call x1, Pallas kernels, main_call(): pl.pallas_call(main_kernel, out_shape=(S(2, 512, 512), S(2, 256, 256), S(...  7.63 us
    pallas_call x1, Pallas kernels, prep_call(): pl.pallas_call(prep_kernel, grid=(8,), out_shape=jax.ShapeDtypeStruct((8,...  7.11 us
    unnamed x31, local copies, waits for them, and re-layouts  6.45 us
  transfers between devices with their start and end apart: 12, of which 7 were waited for; matrix products, arithmetic and copies ran while one was open for 4% of the time, Pallas kernels for 8%

commit v1 on v0

--- a/solution.py
+++ b/solution.py
@@ -198,7 +198,7 @@
             pltpu.VMEM((2, W, W), f32),
             pltpu.SemaphoreType.DMA((9,)),
         ],
-        compiler_params=pltpu.CompilerParams(vmem_limit_bytes=40 * 2**20),
+        compiler_params=pltpu.CompilerParams(vmem_limit_bytes=62 * 2**20),
         name="slots",
     )(offs, live, anchor, obj, right_top, right_bot, below, corner, probe, sq, rhs, lhs)
 
@@ -229,21 +229,21 @@
     return lax.ppermute(value, axes, pairs)
 
 
-def finish_kernel(part, above, top, bot, out):
+def finish_kernel(part, above, left, out):
     h = pl.program_id(1)
+    out[0, :, :W] = part[0, :, :W] - 0.5 * left[0]
 
     @pl.when(h == 0)
     def _():
-        out[0] = part[0] - 0.5 * above[0]
-        out[0, :, :W] -= 0.5 * top[0]
+        out[0, :, :W] -= 0.5 * above[0, :, :W]
+        out[0, :, W:] = part[0, :, W:] - 0.5 * above[0, :, W:]
 
     @pl.when(h == 1)
     def _():
         out[0, :, W:] = part[0, :, W:]
-        out[0, :, :W] = part[0, :, :W] - 0.5 * bot[0]
-
-
-def finish_call(part, above, top, bot):
+
+
+def finish_call(part, above, left):
     wide = pl.BlockSpec((1, W, 512), lambda c, h: (c, h, 0))
     return pl.pallas_call(
         finish_kernel,
@@ -252,37 +252,37 @@
         in_specs=[
             wide,
             pl.BlockSpec((1, W, 512), lambda c, h: (c, 0, 0)),
-            pl.BlockSpec((1, W, W), lambda c, h: (c, 0, 0)),
-            pl.BlockSpec((1, W, W), lambda c, h: (c, 0, 0)),
+            pl.BlockSpec((1, W, W), lambda c, h: (c, h, 0)),
         ],
         out_specs=wide,
         name="finish",
-    )(part, above, top, bot)
+    )(part, above, left)
 
 
 def swap_cores(value):
     return lax.ppermute(value, "core", [(0, 1), (1, 0)])
 
 
-def summed_over_all(x):
+def core_half(x):
     n = x.shape[0] // 2
     chips = lax.axis_size("y") * lax.axis_size("col")
     c = lax.axis_index("core")
     mine = lax.dynamic_slice_in_dim(x, c * n, n, 0)
     other = lax.dynamic_slice_in_dim(x, (1 - c) * n, n, 0)
-    half = mine + swap_cores(other)
-    rows = n // chips
-    axes = ("y", "col")
-    piece = lax.all_to_all(half.reshape(chips, rows, W), axes, 0, 0).sum(0)
-    half = lax.all_to_all(jnp.broadcast_to(piece[None], (chips, rows, W)), axes, 0, 0).reshape(n, W)
+    return (mine + swap_cores(other)).reshape(chips, n // chips, W)
+
+
+def both_halves(half):
     rest = swap_cores(half)
-    return jnp.where(c == 0, jnp.concatenate([half, rest], 0), jnp.concatenate([rest, half], 0))
+    first = lax.axis_index("core") == 0
+    return jnp.where(first, jnp.concatenate([half, rest], 0), jnp.concatenate([rest, half], 0))
 
 
 def shards(object_planes, probe_planes, offsets, photon_counts, live_counts):
     n_row = lax.axis_size("y") * lax.axis_size("core")
     n_col = lax.axis_size("col")
     rows = ("y", "core")
+    axes = ("y", "col")
     row = lax.axis_index(rows)
     col = lax.axis_index("col")
     up = [(i, i - 1) for i in range(1, n_row)]
@@ -300,12 +300,20 @@
         offsets, live_counts.reshape(1), anchor, object_planes, right_top, right_bot, below, corner, probe_planes, roots
     )
     corner_in = lax.ppermute(g_corner, rows, down)
-    bot_in = lax.ppermute(g_bot, "col", to_right)
     above_in = lax.ppermute(g_below, rows, down)
-    top_in = lax.ppermute(g_top + corner_in, "col", to_right)
-    total = summed_over_all(g_probe.reshape(1024, W)).reshape(probe_planes.shape)
+    g_right = jnp.concatenate([g_top + corner_in, g_bot], 1)
+    left_in = lax.ppermute(g_right, "col", to_right)
+    pieces = core_half(g_probe.reshape(1024, W))
+
+    def exchange(step, pieces):
+        got = lax.all_to_all(pieces, axes, 0, 0)
+        return jnp.where(step == 0, jnp.broadcast_to(got.sum(0)[None], got.shape), got)
+
+    pieces = lax.fori_loop(0, 2, exchange, pieces)
+    pieces, left_in, above_in = lax.optimization_barrier((pieces, left_in, above_in))
+    total = both_halves(pieces.reshape(512, W)).reshape(probe_planes.shape)
     new_probe = probe_planes - total * (1.0 / math.sqrt(offsets.shape[0] * n_row * n_col))
-    new_object = finish_call(part, above_in, top_in, bot_in)
+    new_object = finish_call(part, above_in, left_in)
     return new_object, new_probe
 
 

time: 145 us -> 147 us (1.014)
  the two profiles are of different devices: /device:TPU:2 before, /device:TPU:1 now
where the time goes in v1:
time: 147 us; the launch traced here: 146 us
  waiting for transfers between devices  50.8 us (35%)
  starting transfers between devices  50.6 us (34%)
  Pallas kernels  31.4 us (21%)
  other arithmetic  6.98 us (5%)
  local copies, waits for them, and re-layouts  5.23 us (4%)
    all_to_all x2, waiting for transfers between devices, exchange(): got = lax.all_to_all(pieces, axes, 0, 0)  40.7 us
    pallas_call x1, Pallas kernels, main_call(): pl.pallas_call(main_kernel, out_shape=(S(2, 512, 512), S(2, 256, 256), S(...  20.2 us
    all_to_all x2, starting transfers between devices, exchange(): got = lax.all_to_all(pieces, axes, 0, 0)  19.5 us
    ppermute x1, starting transfers between devices, shards(): above_in = lax.ppermute(g_below, rows, down)  11.9 us
    ppermute x1, waiting for transfers between devices, shards(): right_top = lax.ppermute(object_planes[:, :W, :W], 'col', to_left)  10.1 us
    pallas_call x1, Pallas kernels, prep_call(): pl.pallas_call(prep_kernel, grid=(8,), out_shape=jax.ShapeDtypeStruct((8,...  6.97 us
    ppermute x1, starting transfers between devices, shards(): left_in = lax.ppermute(g_right, 'col', to_right)  4.57 us
    pallas_call x1, Pallas kernels, finish_call(): pl.pallas_call(finish_kernel, grid=(2, 2), out_shape=jax.ShapeDtypeStruct...  4.2 us
  transfers between devices with their start and end apart: 11, of which 3 were waited for; matrix products, arithmetic and copies ran while one was open for 5% of the time, Pallas kernels for 8%

profile of v1, /device:TPU:1, one launch (start us, length us, event | category | flops | bytes accessed | tf_op | source)
XLA Modules:
  0.0 146.4 jit_solution(12491131382546376097)
XLA Ops:
  0.7 1.4 fusion.1
  2.1 1.3 collective-permute-start
  3.4 0.1 slice.11
  3.5 3.3 %collective-permute-start.2 = (f32[2,256,512]{2,1,0:T(8,128)S(1)}, f32[2,256,512]{2,1,0:T(8,128)S(1)}, u32[]{:S(2)}, u32[]{:S(2)}) collective-permute-start(f32[2,256,512]{2,1,0:T(8,128)S(1)} %slice.11), channel_id=1, source_target_pairs={{16,0},{32,16},{48,32},{64,48},{80,64},{96,80},{112,96},{17,1},{33... | collective-permute-start | bytes 3145736 | tf_op jit(solution)/shard_map/ppermute | solution.py:294
  6.8 1.3 collective-permute-start.1
  8.1 10.1 %collective-permute-done.right_top = f32[2,256,256]{2,1,0:T(8,128)} collective-permute-done((f32[2,256,256]{2,1,0:T(8,128)S(1)}, f32[2,256,256]{2,1,0:T(8,128)}, u32[]{:S(2)}, u32[]{:S(2)}) %collective-permute-start) | collective-permute-done | bytes 524320 | tf_op jit(solution)/shard_map/ppermute | solution.py:293
  18.2 4.0 %collective-permute-start.3 = (f32[2,256,256]{2,1,0:T(8,128)}, f32[2,256,256]{2,1,0:T(8,128)}, u32[]{:S(2)}, u32[]{:S(2)}) collective-permute-start(f32[2,256,256]{2,1,0:T(8,128)} %collective-permute-done.right_top), channel_id=1, source_target_pairs={{16,0},{32,16},{48,32},{64,48},{80,64},{96,80},{112,96},{17,1},{33... | collective-permute-start | bytes 1572872 | tf_op jit(solution)/shard_map/ppermute | solution.py:296
  22.2 0.7 copy.11.offs
  23.6 7.0 %roots.1.sq = f32[8,256,256]{2,1,0:T(8,128)} custom-call(s32[8,256,256]{2,1,0:T(8,128)} %counts.1, bf16[256,256]{1,0:T(8,128)(2,1)} %constant.57.clone.pm, bf16[256,256]{1,0:T(8,128)(2,1)} %constant.58.clone.pmt), custom_call_target="tpu_custom_call" | custom-call | tf_op jit(solution)/shard_map/roots/pallas_call | solution.py:218
  30.5 0.6 pad_add_fusion.anchor
  31.2 1.0 copy-done.3
  32.1 20.2 %slots.1 = (f32[2,512,512]{2,1,0:T(8,128)}, f32[2,256,256]{2,1,0:T(8,128)}, f32[2,256,256]{2,1,0:T(8,128)}, f32[2,256,256]{2,1,0:T(8,128)}, f32[2,256,512]{2,1,0:T(8,128)}, /*index=5*/f32[2,2,256,256]{3,2,1,0:T(8,128)}) custom-call(s32[8,2]{1,0:T(8,128)} %copy.11.offs, s32[1]{0:T(128)} %bitcast.8.live, s32[2]{0:T(128)} %pad_add_fusion.anchor, ...), custom_call_target="tpu_custom_call" | custom-call | tf_op jit(solution)/shard_map/slots/pallas_call | solution.py:183
  52.3 3.2 %collective-permute-start.5 = (f32[2,256,256]{2,1,0:T(8,128)}, f32[2,256,256]{2,1,0:T(8,128)S(1)}, u32[]{:S(2)}, u32[]{:S(2)}) collective-permute-start(f32[2,256,256]{2,1,0:T(8,128)} %get-tuple-element.64), channel_id=1, source_target_pairs={{0,16},{16,32},{32,48},{48,64},{64,80},{80,96},{96,112},{1,17},{17... | collective-permute-start | bytes 1572872 | tf_op jit(solution)/shard_map/ppermute | solution.py:302
  55.5 1.9 %constant_dynamic-slice_fusion = f32[512,256]{1,0:T(8,128)} fusion(f32[1024,256]{1,0:T(8,128)} %bitcast.10, s32[]{:T(128)S(6)} %select_n.33), kind=kLoop, calls=%fused_computation.6 | loop fusion | bytes 1048580 | tf_op jit(solution)/shard_map/dynamic_slice | solution.py:271
  57.5 11.9 %collective-permute-start.7 = (f32[2,256,512]{2,1,0:T(8,128)}, f32[2,256,512]{2,1,0:T(8,128)}, u32[]{:S(2)}, u32[]{:S(2)}) collective-permute-start(f32[2,256,512]{2,1,0:T(8,128)} %get-tuple-element.66), channel_id=1, source_target_pairs={{0,16},{16,32},{32,48},{48,64},{64,80},{80,96},{96,112},{1,17},{17... | collective-permute-start | bytes 3145736 | tf_op jit(solution)/shard_map/ppermute | solution.py:303
  69.4 1.1 add.35
  70.5 0.1 pad_maximum_fusion
  70.6 4.6 %collective-permute-start.6 = (f32[2,512,256]{2,1,0:T(8,128)S(1)}, f32[2,512,256]{2,1,0:T(8,128)}, u32[]{:S(2)}, u32[]{:S(2)}) collective-permute-start(f32[2,512,256]{2,1,0:T(8,128)S(1)} %pad_maximum_fusion), channel_id=1, source_target_pairs={{0,1},{1,2},{2,3},{3,4},{4,5},{5,6},{6,7},{7,8},{8,9},{9,10},{10,1... | collective-permute-start | bytes 3145736 | tf_op jit(solution)/shard_map/ppermute | solution.py:305
  75.2 0.9 add_bitcast_fusion
  76.0 62.0 %while.13 = (s32[]{:T(128)}, f32[64,8,256]{2,1,0:T(8,128)}, s32[]{:T(128)}, f32[]{:T(128)}, s32[]{:T(128)}) while((s32[]{:T(128)}, f32[64,8,256]{2,1,0:T(8,128)}, s32[]{:T(128)}, f32[]{:T(128)}, s32[]{:T(128)}) %tuple.35), condition=%wide.region_2.3_spmd, body=%wide.region_0.2_spmd.sunk | while | flops 260099 | bytes 3162227 | solution.py:312
  76.0 14.2 %all-to-all-start = ((f32[64,8,256]{2,1,0:T(8,128)}), f32[64,8,256]{2,1,0:T(8,128)S(1)}, u32[]{:S(2)}, u32[]{:S(2)}) async-start(f32[64,8,256]{2,1,0:T(8,128)} %get-tuple-element.95), calls=%async_computation | async-start | bytes 1048576 | tf_op jit(solution)/shard_map/while/body/eval_jaxpr/all_to_all | solution.py:309
  90.3 27.9 %all-to-all-done = f32[64,8,256]{2,1,0:T(8,128)S(1)} async-done(((f32[64,8,256]{2,1,0:T(8,128)}), f32[64,8,256]{2,1,0:T(8,128)S(1)}, u32[]{:S(2)}, u32[]{:S(2)}) %all-to-all-start) | async-done | bytes 524320 | tf_op jit(solution)/shard_map/while/body/eval_jaxpr/all_to_all | solution.py:309
  118.2 0.1 reduce_sum.14
  118.3 0.8 broadcast_select_fusion.2
  119.1 5.3 %all-to-all-start = ((f32[64,8,256]{2,1,0:T(8,128)}), f32[64,8,256]{2,1,0:T(8,128)S(1)}, u32[]{:S(2)}, u32[]{:S(2)}) async-start(f32[64,8,256]{2,1,0:T(8,128)} %get-tuple-element.95), calls=%async_computation | async-start | bytes 1048576 | tf_op jit(solution)/shard_map/while/body/eval_jaxpr/all_to_all | solution.py:309
  124.4 12.7 %all-to-all-done = f32[64,8,256]{2,1,0:T(8,128)S(1)} async-done(((f32[64,8,256]{2,1,0:T(8,128)}), f32[64,8,256]{2,1,0:T(8,128)S(1)}, u32[]{:S(2)}, u32[]{:S(2)}) %all-to-all-start) | async-done | bytes 524320 | tf_op jit(solution)/shard_map/while/body/eval_jaxpr/all_to_all | solution.py:309
  137.2 0.8 broadcast_select_fusion.2
  138.0 1.5 %collective-permute-start.8 = (f32[512,256]{1,0:T(8,128)}, f32[512,256]{1,0:T(8,128)S(1)}, u32[]{:S(2)}, u32[]{:S(2)}) collective-permute-start(f32[512,256]{1,0:T(8,128)} %bitcast.5), channel_id=1, source_target_pairs={{0,16},{16,0},{1,17},{17,1},{2,18},{18,2},{3,19},{19,3},{4,20},{20... | collective-permute-start | bytes 1572872 | tf_op jit(solution)/shard_map/ppermute | solution.py:263
  139.6 4.2 %finish.1 = f32[2,512,512]{2,1,0:T(8,128)} custom-call(f32[2,512,512]{2,1,0:T(8,128)} %get-tuple-element.60.part, f32[2,256,512]{2,1,0:T(8,128)} %collective-permute-done.7.above, f32[2,512,256]{2,1,0:T(8,128)} %collective-permute-done.6.left), custom_call_target="tpu_custom_call" | custom-call | tf_op jit(solution)/shard_map/finish/pallas_call | solution.py:248
  143.8 1.4 fusion
  145.2 0.1 copy-done.1
  145.3 1.1 sub.7
  (20 shorter events, 0.1 us)
Async XLA Ops:
  0.6 2.8 %copy-start = (f32[2,512,512]{2,1,0:T(8,128)S(1)}, f32[2,512,512]{2,1,0:T(8,128)}, u32[]{:S(2)}) copy-start(f32[2,512,512]{2,1,0:T(8,128)} %obj.1) | copy-start | bytes 6291460
  0.6 21.6 %copy-start.5 = (s32[8,2]{0,1:T(2,128)S(1)}, s32[8,2]{0,1:T(2,128)}, u32[]{:S(2)}) copy-start(s32[8,2]{0,1:T(2,128)} %param.13) | copy-start | bytes 196
  2.1 16.1 %collective-permute-start = (f32[2,256,256]{2,1,0:T(8,128)S(1)}, f32[2,256,256]{2,1,0:T(8,128)}, u32[]{:S(2)}, u32[]{:S(2)}) collective-permute-start(f32[2,256,256]{2,1,0:T(8,128)S(1)} %get-tuple-element.75), channel_id=1, source_target_pairs={{1,0},{2,1},{3,2},{4,3},{5,4},{6,5},{7,6},{8,7},{9,8},{10,9},{11,1... | collective-permute-start | bytes 1572872 | tf_op jit(solution)/shard_map/ppermute | solution.py:293
  3.5 27.7 %collective-permute-start.2 = (f32[2,256,512]{2,1,0:T(8,128)S(1)}, f32[2,256,512]{2,1,0:T(8,128)S(1)}, u32[]{:S(2)}, u32[]{:S(2)}) collective-permute-start(f32[2,256,512]{2,1,0:T(8,128)S(1)} %slice.11), channel_id=1, source_target_pairs={{16,0},{32,16},{48,32},{64,48},{80,64},{96,80},{112,96},{17,1},{33... | collective-permute-start | bytes 3145736 | tf_op jit(solution)/shard_map/ppermute | solution.py:294
  6.8 24.3 %collective-permute-start.1 = (f32[2,256,256]{2,1,0:T(8,128)S(1)}, f32[2,256,256]{2,1,0:T(8,128)}, u32[]{:S(2)}, u32[]{:S(2)}) collective-permute-start(f32[2,256,256]{2,1,0:T(8,128)S(1)} %get-tuple-element.74), channel_id=1, source_target_pairs={{1,0},{2,1},{3,2},{4,3},{5,4},{6,5},{7,6},{8,7},{9,8},{10,9},{11,1... | collective-permute-start | bytes 1572872 | tf_op jit(solution)/shard_map/ppermute | solution.py:295
  18.2 13.0 %collective-permute-start.3 = (f32[2,256,256]{2,1,0:T(8,128)}, f32[2,256,256]{2,1,0:T(8,128)}, u32[]{:S(2)}, u32[]{:S(2)}) collective-permute-start(f32[2,256,256]{2,1,0:T(8,128)} %collective-permute-done.right_top), channel_id=1, source_target_pairs={{16,0},{32,16},{48,32},{64,48},{80,64},{96,80},{112,96},{17,1},{33... | collective-permute-start | bytes 1572872 | tf_op jit(solution)/shard_map/ppermute | solution.py:296
  31.2 1.0 copy-start.3
  52.3 17.1 %collective-permute-start.5 = (f32[2,256,256]{2,1,0:T(8,128)}, f32[2,256,256]{2,1,0:T(8,128)S(1)}, u32[]{:S(2)}, u32[]{:S(2)}) collective-permute-start(f32[2,256,256]{2,1,0:T(8,128)} %get-tuple-element.64), channel_id=1, source_target_pairs={{0,16},{16,32},{32,48},{48,64},{64,80},{80,96},{96,112},{1,17},{17... | collective-permute-start | bytes 1572872 | tf_op jit(solution)/shard_map/ppermute | solution.py:302
  55.5 15.0 %copy-start.4 = (f32[2,256,256]{2,1,0:T(8,128)S(1)}, f32[2,256,256]{2,1,0:T(8,128)}, u32[]{:S(2)}) copy-start(f32[2,256,256]{2,1,0:T(8,128)} %get-tuple-element.65) | copy-start | bytes 1572868
  57.5 17.7 %copy-start.2 = (f32[2,2,256,256]{3,2,1,0:T(8,128)S(1)}, f32[2,2,256,256]{3,2,1,0:T(8,128)}, u32[]{:S(2)}) copy-start(f32[2,2,256,256]{3,2,1,0:T(8,128)} %get-tuple-element.61) | copy-start | bytes 3145732
  57.5 17.7 %collective-permute-start.4 = (f32[512,256]{1,0:T(8,128)}, f32[512,256]{1,0:T(8,128)S(1)}, u32[]{:S(2)}, u32[]{:S(2)}) collective-permute-start(f32[512,256]{1,0:T(8,128)} %constant_dynamic-slice_fusion), channel_id=1, source_target_pairs={{0,16},{16,0},{1,17},{17,1},{2,18},{18,2},{3,19},{19,3},{4,20},{20... | collective-permute-start | bytes 1572872 | tf_op jit(solution)/shard_map/ppermute | solution.py:263
  57.5 80.6 %collective-permute-start.7 = (f32[2,256,512]{2,1,0:T(8,128)}, f32[2,256,512]{2,1,0:T(8,128)}, u32[]{:S(2)}, u32[]{:S(2)}) collective-permute-start(f32[2,256,512]{2,1,0:T(8,128)} %get-tuple-element.66), channel_id=1, source_target_pairs={{0,16},{16,32},{32,48},{48,64},{64,80},{80,96},{96,112},{1,17},{17... | collective-permute-start | bytes 3145736 | tf_op jit(solution)/shard_map/ppermute | solution.py:303
  70.6 67.4 %collective-permute-start.6 = (f32[2,512,256]{2,1,0:T(8,128)S(1)}, f32[2,512,256]{2,1,0:T(8,128)}, u32[]{:S(2)}, u32[]{:S(2)}) collective-permute-start(f32[2,512,256]{2,1,0:T(8,128)S(1)} %pad_maximum_fusion), channel_id=1, source_target_pairs={{0,1},{1,2},{2,3},{3,4},{4,5},{5,6},{6,7},{7,8},{8,9},{9,10},{10,1... | collective-permute-start | bytes 3145736 | tf_op jit(solution)/shard_map/ppermute | solution.py:305
  76.0 42.2 %all-to-all-start = ((f32[64,8,256]{2,1,0:T(8,128)}), f32[64,8,256]{2,1,0:T(8,128)S(1)}, u32[]{:S(2)}, u32[]{:S(2)}) async-start(f32[64,8,256]{2,1,0:T(8,128)} %get-tuple-element.95), calls=%async_computation | async-start | bytes 1048576 | tf_op jit(solution)/shard_map/while/body/eval_jaxpr/all_to_all | solution.py:309
  119.1 18.0 %all-to-all-start = ((f32[64,8,256]{2,1,0:T(8,128)}), f32[64,8,256]{2,1,0:T(8,128)S(1)}, u32[]{:S(2)}, u32[]{:S(2)}) async-start(f32[64,8,256]{2,1,0:T(8,128)} %get-tuple-element.95), calls=%async_computation | async-start | bytes 1048576 | tf_op jit(solution)/shard_map/while/body/eval_jaxpr/all_to_all | solution.py:309
  138.0 5.7 %collective-permute-start.8 = (f32[512,256]{1,0:T(8,128)}, f32[512,256]{1,0:T(8,128)S(1)}, u32[]{:S(2)}, u32[]{:S(2)}) collective-permute-start(f32[512,256]{1,0:T(8,128)} %bitcast.5), channel_id=1, source_target_pairs={{0,16},{16,0},{1,17},{17,1},{2,18},{18,2},{3,19},{19,3},{4,20},{20... | collective-permute-start | bytes 1572872 | tf_op jit(solution)/shard_map/ppermute | solution.py:263
  143.8 1.5 %copy-start.1 = (f32[2,2,256,256]{3,2,1,0:T(8,128)S(1)}, f32[2,2,256,256]{3,2,1,0:T(8,128)}, u32[]{:S(2)}) copy-start(f32[2,2,256,256]{3,2,1,0:T(8,128)} %probe.1) | copy-start | bytes 3145732

commit v2 on v1

--- a/solution.py
+++ b/solution.py
@@ -1,3 +1,4 @@
+import functools
 import math
 
 import ml_dtypes
@@ -62,7 +63,7 @@
 
 
 def main_kernel(offs, live, anchor, obj, right_top, right_bot, below, corner, probe, sq, rhs, lhs,
-                o_part, o_rtop, o_rbot, o_corner, o_below, o_probe,
+                o_part, o_rtop, o_rbot, o_corner, o_below, o_mine, o_other,
                 cov, acc, patch, pacc, prv, sqv, rt, lt, far, term, sems):
     ins = [
         (obj, cov.at[:, 0:512, 0:512]),
@@ -159,6 +160,12 @@
         return carry
 
     lax.fori_loop(0, live[0], slot, 0)
+    for n, (kc, kz, kx, ky) in enumerate(np.ndindex(2, 4, 4, 4)):
+        c = lax.rem(anchor[2] + kc, 2)
+        row = lax.rem(anchor[3] + kz, 4) * 128 + lax.rem(anchor[4] + kx, 4) * 32 + lax.rem(anchor[5] + ky, 4) * 8
+        r = pl.multiple_of(lax.rem(row, W), 8)
+        n8 = n % 64 * 8
+        prv[kc, n8 // W, n8 % W:n8 % W + 8, :] = pacc[c, lax.div(row, W), pl.ds(r, 8), :]
     cov[:, 0:512, 0:512] = cov[:, 0:512, 0:512] - 0.5 * acc[:, 0:512, 0:512]
     outs = [
         (cov.at[:, 0:512, 0:512], o_part),
@@ -166,7 +173,8 @@
         (acc.at[:, 256:512, 512:768], o_rbot),
         (acc.at[:, 512:768, 512:768], o_corner),
         (acc.at[:, 512:768, 0:512], o_below),
-        (pacc, o_probe),
+        (prv.at[0], o_mine),
+        (prv.at[1], o_other),
     ]
     copies = [pltpu.make_async_copy(s, d, sems.at[i]) for i, (s, d) in enumerate(outs)]
     for c in copies:
@@ -182,9 +190,9 @@
     S = lambda *s: jax.ShapeDtypeStruct(s, f32)
     return pl.pallas_call(
         main_kernel,
-        out_shape=(S(2, 512, 512), S(2, 256, 256), S(2, 256, 256), S(2, 256, 256), S(2, 256, 512), S(2, 2, 256, 256)),
+        out_shape=(S(2, 512, 512), S(2, 256, 256), S(2, 256, 256), S(2, 256, 256), S(2, 256, 512), S(2, 256, 256), S(2, 256, 256)),
         in_specs=[smem] * 3 + [any_] * 9,
-        out_specs=[any_] * 6,
+        out_specs=[any_] * 7,
         scratch_shapes=[
             pltpu.VMEM((2, 768, 768), f32),
             pltpu.VMEM((2, 768, 768), f32),
@@ -255,6 +263,7 @@
             pl.BlockSpec((1, W, W), lambda c, h: (c, h, 0)),
         ],
         out_specs=wide,
+        compiler_params=pltpu.CompilerParams(vmem_limit_bytes=8 * 2**20),
         name="finish",
     )(part, above, left)
 
@@ -263,71 +272,86 @@
     return lax.ppermute(value, "core", [(0, 1), (1, 0)])
 
 
-def core_half(x):
-    n = x.shape[0] // 2
-    chips = lax.axis_size("y") * lax.axis_size("col")
-    c = lax.axis_index("core")
-    mine = lax.dynamic_slice_in_dim(x, c * n, n, 0)
-    other = lax.dynamic_slice_in_dim(x, (1 - c) * n, n, 0)
-    return (mine + swap_cores(other)).reshape(chips, n // chips, W)
-
-
-def both_halves(half):
-    rest = swap_cores(half)
-    first = lax.axis_index("core") == 0
-    return jnp.where(first, jnp.concatenate([half, rest], 0), jnp.concatenate([rest, half], 0))
+def sum_along(pieces, axis):
+    got = [lax.ppermute(pieces[k], axis, [(i, (i + k) % 4) for i in range(4)]) for k in (2, 1, 3)]
+    return pieces[0] + got[0] + got[1] + got[2]
+
+
+def spread_along(value, axis):
+    return [value] + [lax.ppermute(value, axis, [(i, (i + k) % 4) for i in range(4)]) for k in (1, 2, 3)]
+
+
+def probe_kernel(step, place, probe, z0, z1, z2, z3, rest, out):
+    for n, (kc, kz, kx, ky) in enumerate(np.ndindex(2, 4, 4, 4)):
+        c = lax.rem(place[2] + kc, 2)
+        row = (
+            lax.rem(place[3] - kz + 4, 4) * 128
+            + lax.rem(place[4] - kx + 4, 4) * 32
+            + lax.rem(place[5] - ky + 4, 4) * 8
+        )
+        at = pl.multiple_of(c * 512 + row, 8)
+        total = (z0, z1, z2, z3)[kz][kx, ky] if kc == 0 else rest[kz, kx, ky]
+        out[pl.ds(at, 8), :] = probe[pl.ds(at, 8), :] - step * total
 
 
 def shards(object_planes, probe_planes, offsets, photon_counts, live_counts):
     n_row = lax.axis_size("y") * lax.axis_size("core")
-    n_col = lax.axis_size("col")
-    rows = ("y", "core")
-    axes = ("y", "col")
-    row = lax.axis_index(rows)
-    col = lax.axis_index("col")
+    n_col = lax.axis_size("x") * lax.axis_size("z")
+    rows, cols = ("y", "core"), ("x", "z")
     up = [(i, i - 1) for i in range(1, n_row)]
     down = [(i - 1, i) for i in range(1, n_row)]
     to_left = [(i, i - 1) for i in range(1, n_col)]
     to_right = [(i - 1, i) for i in range(1, n_col)]
 
-    right_top = lax.ppermute(object_planes[:, :W, :W], "col", to_left)
+    right_top = lax.ppermute(object_planes[:, :W, :W], cols, to_left)
     below = lax.ppermute(object_planes[:, :W, :], rows, up)
-    right_bot = lax.ppermute(object_planes[:, W:, :W], "col", to_left)
+    right_bot = lax.ppermute(object_planes[:, W:, :W], cols, to_left)
     corner = lax.ppermute(right_top, rows, up)
     roots = prep_call(photon_counts)
-    anchor = jnp.stack([row * 512, col * 512]).astype(jnp.int32)
-    part, g_top, g_bot, g_corner, g_below, g_probe = main_call(
-        offsets, live_counts.reshape(1), anchor, object_planes, right_top, right_bot, below, corner, probe_planes, roots
+    place = jnp.stack(
+        [lax.axis_index(rows) * 512, lax.axis_index(cols) * 512] + [lax.axis_index(a) for a in ("core", "z", "x", "y")]
+    ).astype(jnp.int32)
+    part, g_top, g_bot, g_corner, g_below, mine, other = main_call(
+        offsets, live_counts.reshape(1), place, object_planes, right_top, right_bot, below, corner, probe_planes, roots
     )
     corner_in = lax.ppermute(g_corner, rows, down)
     above_in = lax.ppermute(g_below, rows, down)
+    half = (mine + swap_cores(other)).reshape(4, 4, 4, 8, W)
+    piece = sum_along(half, "z")
     g_right = jnp.concatenate([g_top + corner_in, g_bot], 1)
-    left_in = lax.ppermute(g_right, "col", to_right)
-    pieces = core_half(g_probe.reshape(1024, W))
-
-    def exchange(step, pieces):
-        got = lax.all_to_all(pieces, axes, 0, 0)
-        return jnp.where(step == 0, jnp.broadcast_to(got.sum(0)[None], got.shape), got)
-
-    pieces = lax.fori_loop(0, 2, exchange, pieces)
-    pieces, left_in, above_in = lax.optimization_barrier((pieces, left_in, above_in))
-    total = both_halves(pieces.reshape(512, W)).reshape(probe_planes.shape)
-    new_probe = probe_planes - total * (1.0 / math.sqrt(offsets.shape[0] * n_row * n_col))
+    left_in = lax.ppermute(g_right, cols, to_right)
+    piece = sum_along(piece, "x")
+    piece = sum_along(piece, "y")
+    piece = jnp.stack(spread_along(piece, "y"))
+    piece = jnp.stack(spread_along(piece, "x"))
+    piece, left_in, above_in = lax.optimization_barrier((piece, left_in, above_in))
     new_object = finish_call(part, above_in, left_in)
-    return new_object, new_probe
+    quarters = spread_along(piece, "z")
+    rest = swap_cores(jnp.stack(quarters))
+    smem, vmem = pl.BlockSpec(memory_space=pltpu.SMEM), pl.BlockSpec(memory_space=pltpu.VMEM)
+    step = 1.0 / math.sqrt(offsets.shape[0] * n_row * n_col)
+    new_probe = pl.pallas_call(
+        functools.partial(probe_kernel, step),
+        out_shape=jax.ShapeDtypeStruct((1024, W), f32),
+        in_specs=[smem] + [vmem] * 6,
+        out_specs=vmem,
+        compiler_params=pltpu.CompilerParams(vmem_limit_bytes=8 * 2**20),
+        name="probe",
+    )(place, probe_planes.reshape(1024, W), *quarters, rest)
+    return new_object, new_probe.reshape(probe_planes.shape)
 
 
 def solution(mesh):
     split = jax.sharding.Mesh(
-        mesh.devices.reshape(mesh.shape["row"] // 2, 2, mesh.shape["col"]), ("y", "core", "col")
+        mesh.devices.reshape(mesh.shape["row"] // 2, 2, mesh.shape["col"] // 4, 4), ("y", "core", "x", "z")
     )
-    rows = ("y", "core")
+    rows, cols = ("y", "core"), ("x", "z")
     in_specs = (
-        P(None, rows, "col"),
+        P(None, rows, cols),
         P(),
-        P(("y", "core", "col"), None),
-        P(("y", "core", "col"), None, None),
-        P(rows, "col"),
+        P(rows + cols, None),
+        P(rows + cols, None, None),
+        P(rows, cols),
     )
-    out_specs = (P(None, rows, "col"), P())
+    out_specs = (P(None, rows, cols), P())
     return jax.shard_map(shards, mesh=split, in_specs=in_specs, out_specs=out_specs, check_vma=False)

time: 147 us -> 147 us (level)
  starting transfers between devices: 50.6 us -> 82.5 us
  waiting for transfers between devices: 50.8 us -> 29.3 us
  other arithmetic: 6.98 us -> 1.36 us
  Pallas kernels: 31.4 us -> 28.8 us
    ppermute x3 -> x21, starting transfers between devices: 7.15 us -> 48.3 us  [the longest x9 24.1 us: spread_along(): lax.ppermute(value, axis, [(i, (i + k) % 4) for i in range(4)])]
    all_to_all x2 -> x0, waiting for transfers between devices: 40.7 us -> none  [exchange(): got = lax.all_to_all(pieces, axes, 0, 0)]
    all_to_all x2 -> x0, starting transfers between devices: 19.5 us -> none  [exchange(): got = lax.all_to_all(pieces, axes, 0, 0)]
    ppermute x3 -> x21, waiting for transfers between devices: 10.1 us -> 29.3 us  [the longest x9 10.8 us: spread_along(): lax.ppermute(value, axis, [(i, (i + k) % 4) for i in range(4)])]
    ppermute x1, starting transfers between devices: 3.17 us -> 16.1 us  [shards(): corner_in = lax.ppermute(g_corner, rows, down)]
    ppermute x1, starting transfers between devices: 11.9 us -> 2.06 us  [shards(): above_in = lax.ppermute(g_below, rows, down)]
    ppermute x2, starting transfers between devices: 1.52 us -> 8.69 us  [swap_cores(): return lax.ppermute(value, 'core', [(0, 1), (1, 0)])]
    pallas_call x1, Pallas kernels: 20.2 us -> 17.9 us  [main_call(): pl.pallas_call(main_kernel, out_shape=(S(2, 512, 512), S(2, 256, 256), S(...]
  transfers between devices with their start and end apart: 11 -> 27, of which waited for: 3 -> 14; matrix products, arithmetic and copies ran while one was open for 5% -> 2% of each run, Pallas kernels for 8% -> 6%
where the time goes in v2:
time: 147 us
  starting transfers between devices  82.5 us (56%)
  waiting for transfers between devices  29.3 us (20%)
  Pallas kernels  28.8 us (20%)
  local copies, waits for them, and re-layouts  3.85 us (3%)
  between operations  1.57 us (1%)
    ppermute x9, starting transfers between devices, spread_along(): lax.ppermute(value, axis, [(i, (i + k) % 4) for i in range(4)])  24.1 us
    ppermute x9, starting transfers between devices, sum_along(): lax.ppermute(pieces[k], axis, [(i, (i + k) % 4) for i in range(4)])  18 us
    pallas_call x1, Pallas kernels, main_call(): pl.pallas_call(main_kernel, out_shape=(S(2, 512, 512), S(2, 256, 256), S(...  17.9 us
    ppermute x1, starting transfers between devices, shards(): corner_in = lax.ppermute(g_corner, rows, down)  16.1 us
    ppermute x9, waiting for transfers between devices, spread_along(): lax.ppermute(value, axis, [(i, (i + k) % 4) for i in range(4)])  10.8 us
    ppermute x1, waiting for transfers between devices, shards(): right_top = lax.ppermute(object_planes[:, :W, :W], cols, to_left)  10.1 us
    ppermute x2, starting transfers between devices, swap_cores(): return lax.ppermute(value, 'core', [(0, 1), (1, 0)])  8.69 us
    ppermute x9, waiting for transfers between devices, sum_along(): lax.ppermute(pieces[k], axis, [(i, (i + k) % 4) for i in range(4)])  8.39 us
  transfers between devices with their start and end apart: 27, of which 14 were waited for; matrix products, arithmetic and copies ran while one was open for 2% of the time, Pallas kernels for 6%

profile of v2, /device:TPU:1, one launch (start us, length us, event | category | flops | bytes accessed | tf_op | source)
XLA Modules:
  0.0 147.4 jit_solution(6756846452741438833)
XLA Ops:
  0.7 1.5 fusion.10
  2.1 1.3 collective-permute-start
  3.5 3.3 %collective-permute-start.2 = (f32[2,256,512]{2,1,0:T(8,128)S(1)}, f32[2,256,512]{2,1,0:T(8,128)S(1)}, u32[]{:S(2)}, u32[]{:S(2)}) collective-permute-start(f32[2,256,512]{2,1,0:T(8,128)S(1)} %slice.47), channel_id=1, source_target_pairs={{16,0},{32,16},{48,32},{64,48},{80,64},{96,80},{112,96},{17,1},{33... | collective-permute-start | bytes 3145736 | tf_op jit(solution)/shard_map/ppermute | solution.py:307
  6.8 1.3 collective-permute-start.1
  8.1 10.1 %collective-permute-done.right_top = f32[2,256,256]{2,1,0:T(8,128)} collective-permute-done((f32[2,256,256]{2,1,0:T(8,128)S(1)}, f32[2,256,256]{2,1,0:T(8,128)}, u32[]{:S(2)}, u32[]{:S(2)}) %collective-permute-start) | collective-permute-done | bytes 524320 | tf_op jit(solution)/shard_map/ppermute | solution.py:306
  18.2 4.0 %collective-permute-start.3 = (f32[2,256,256]{2,1,0:T(8,128)}, f32[2,256,256]{2,1,0:T(8,128)}, u32[]{:S(2)}, u32[]{:S(2)}) collective-permute-start(f32[2,256,256]{2,1,0:T(8,128)} %collective-permute-done.right_top), channel_id=1, source_target_pairs={{16,0},{32,16},{48,32},{64,48},{80,64},{96,80},{112,96},{17,1},{33... | collective-permute-start | bytes 1572872 | tf_op jit(solution)/shard_map/ppermute | solution.py:309
  23.6 6.9 %roots.1.sq = f32[8,256,256]{2,1,0:T(8,128)} custom-call(s32[8,256,256]{2,1,0:T(8,128)} %counts.1, bf16[256,256]{1,0:T(8,128)(2,1)} %constant.31.clone.pm, bf16[256,256]{1,0:T(8,128)(2,1)} %constant.32.clone.pmt), custom_call_target="tpu_custom_call" | custom-call | tf_op jit(solution)/shard_map/roots/pallas_call | solution.py:226
  32.1 17.9 %slots.1 = (f32[2,512,512]{2,1,0:T(8,128)}, f32[2,256,256]{2,1,0:T(8,128)}, f32[2,256,256]{2,1,0:T(8,128)}, f32[2,256,256]{2,1,0:T(8,128)}, f32[2,256,512]{2,1,0...) custom-call(s32[8,2]{1,0:T(8,128)} %copy.11.offs, s32[1]{0:T(128)} %bitcast.65.live, s32[6]{0:T(128)} %stack.72.anchor.place, ...), custom_call_target="tpu_custom_call" | custom-call | tf_op jit(solution)/shard_map/slots/pallas_call | solution.py:191
  50.1 16.1 %collective-permute-start.20 = (f32[2,256,256]{2,1,0:T(8,128)}, f32[2,256,256]{2,1,0:T(8,128)S(1)}, u32[]{:S(2)}, u32[]{:S(2)}) collective-permute-start(f32[2,256,256]{2,1,0:T(8,128)} %get-tuple-element.16), channel_id=1, source_target_pairs={{0,16},{16,32},{32,48},{48,64},{64,80},{80,96},{96,112},{1,17},{17... | collective-permute-start | bytes 1572872 | tf_op jit(solution)/shard_map/ppermute | solution.py:317
  66.3 2.1 %collective-permute-start.22 = (f32[2,256,512]{2,1,0:T(8,128)}, f32[2,256,512]{2,1,0:T(8,128)S(1)}, u32[]{:S(2)}, u32[]{:S(2)}) collective-permute-start(f32[2,256,512]{2,1,0:T(8,128)} %get-tuple-element.18), channel_id=1, source_target_pairs={{0,16},{16,32},{32,48},{48,64},{64,80},{80,96},{96,112},{1,17},{17... | collective-permute-start | bytes 3145736 | tf_op jit(solution)/shard_map/ppermute | solution.py:318
  68.3 1.1 add.41
  69.5 3.6 %collective-permute-start.5 = (f32[4,4,8,256]{3,2,1,0:T(8,128)S(1)}, f32[4,4,8,256]{3,2,1,0:T(8,128)S(1)}, u32[]{:S(2)}, u32[]{:S(2)}) collective-permute-start(f32[4,4,8,256]{3,2,1,0:T(8,128)S(1)} %get-tuple-element.24), channel_id=1, source_target_pairs={{0,2},{1,3},{2,0},{3,1},{4,6},{5,7},{6,4},{7,5},{8,10},{9,11},{10,... | collective-permute-start | bytes 393224 | tf_op jit(solution)/shard_map/ppermute | solution.py:276
  73.1 3.2 %collective-permute-start.7 = (f32[4,4,8,256]{3,2,1,0:T(8,128)S(1)}, f32[4,4,8,256]{3,2,1,0:T(8,128)S(1)}, u32[]{:S(2)}, u32[]{:S(2)}) collective-permute-start(f32[4,4,8,256]{3,2,1,0:T(8,128)S(1)} %get-tuple-element.25), channel_id=1, source_target_pairs={{0,3},{1,0},{2,1},{3,2},{4,7},{5,4},{6,5},{7,6},{8,11},{9,8},{10,9... | collective-permute-start | bytes 393224 | tf_op jit(solution)/shard_map/ppermute | solution.py:276
  76.9 3.6 %collective-permute-start.21 = (f32[2,512,256]{2,1,0:T(8,128)S(1)}, f32[2,512,256]{2,1,0:T(8,128)S(1)}, u32[]{:S(2)}, u32[]{:S(2)}) collective-permute-start(f32[2,512,256]{2,1,0:T(8,128)S(1)} %pad_maximum_fusion), channel_id=1, source_target_pairs={{0,1},{1,2},{2,3},{3,4},{4,5},{5,6},{6,7},{7,8},{8,9},{9,10},{10,1... | collective-permute-start | bytes 3145736 | tf_op jit(solution)/shard_map/ppermute | solution.py:322
  80.5 2.2 %collective-permute-done.7 = f32[4,4,8,256]{3,2,1,0:T(8,128)S(1)} collective-permute-done((f32[4,4,8,256]{3,2,1,0:T(8,128)S(1)}, f32[4,4,8,256]{3,2,1,0:T(8,128)S(1)}, u32[]{:S(2)}, u32[]{:S(2)}) %collective-permute-start.7) | collective-permute-done | bytes 131104 | tf_op jit(solution)/shard_map/ppermute | solution.py:276
  82.7 3.4 %collective-permute-start.8 = (f32[4,8,256]{2,1,0:T(8,128)S(1)}, f32[4,8,256]{2,1,0:T(8,128)S(1)}, u32[]{:S(2)}, u32[]{:S(2)}) collective-permute-start(f32[4,8,256]{2,1,0:T(8,128)S(1)} %get-tuple-element.27), channel_id=1, source_target_pairs={{0,8},{4,12},{8,0},{12,4},{1,9},{5,13},{9,1},{13,5},{2,10},{6,14},... | collective-permute-start | bytes 98312 | tf_op jit(solution)/shard_map/ppermute | solution.py:276
  86.2 1.5 collective-permute-start.9
  87.6 1.6 %collective-permute-done.10 = f32[4,8,256]{2,1,0:T(8,128)S(1)} collective-permute-done((f32[4,8,256]{2,1,0:T(8,128)S(1)}, f32[4,8,256]{2,1,0:T(8,128)S(1)}, u32[]{:S(2)}, u32[]{:S(2)}) %collective-permute-start.10) | collective-permute-done | bytes 32800 | tf_op jit(solution)/shard_map/ppermute | solution.py:276
  90.2 3.1 %collective-permute-start.11 = (f32[8,256]{1,0:T(8,128)S(1)}, f32[8,256]{1,0:T(8,128)S(1)}, u32[]{:S(2)}, u32[]{:S(2)}) collective-permute-start(f32[8,256]{1,0:T(8,128)S(1)} %get-tuple-element.32), channel_id=1, source_target_pairs={{0,64},{32,96},{64,0},{96,32},{1,65},{33,97},{65,1},{97,33},{2,66}... | collective-permute-start | bytes 24584 | tf_op jit(solution)/shard_map/ppermute | solution.py:276
  93.2 2.8 %collective-permute-start.13 = (f32[8,256]{1,0:T(8,128)S(1)}, f32[8,256]{1,0:T(8,128)S(1)}, u32[]{:S(2)}, u32[]{:S(2)}) collective-permute-start(f32[8,256]{1,0:T(8,128)S(1)} %get-tuple-element.33), channel_id=1, source_target_pairs={{0,96},{32,0},{64,32},{96,64},{1,97},{33,1},{65,33},{97,65},{2,98}... | collective-permute-start | bytes 24584 | tf_op jit(solution)/shard_map/ppermute | solution.py:276
  96.8 2.9 %collective-permute-done.12 = f32[8,256]{1,0:T(8,128)S(1)} collective-permute-done((f32[8,256]{1,0:T(8,128)S(1)}, f32[8,256]{1,0:T(8,128)S(1)}, u32[]{:S(2)}, u32[]{:S(2)}) %collective-permute-start.12) | collective-permute-done | bytes 8224 | tf_op jit(solution)/shard_map/ppermute | solution.py:276
  102.3 1.6 %collective-permute-done.15 = f32[8,256]{1,0:T(8,128)S(1)} collective-permute-done((f32[8,256]{1,0:T(8,128)S(1)}, f32[8,256]{1,0:T(8,128)S(1)}, u32[]{:S(2)}, u32[]{:S(2)}) %collective-permute-start.15) | collective-permute-done | bytes 8224 | tf_op jit(solution)/shard_map/ppermute | solution.py:281
  104.7 1.5 %collective-permute-start.18 = (f32[4,8,256]{2,1,0:T(8,128)S(1)}, f32[4,8,256]{2,1,0:T(8,128)S(1)}, u32[]{:S(2)}, u32[]{:S(2)}) collective-permute-start(f32[4,8,256]{2,1,0:T(8,128)S(1)} %get-tuple-element.31), channel_id=1, source_target_pairs={{0,8},{4,12},{8,0},{12,4},{1,9},{5,13},{9,1},{13,5},{2,10},{6,14},... | collective-permute-start | bytes 98312 | tf_op jit(solution)/shard_map/ppermute | solution.py:281
  106.2 2.7 %collective-permute-start.19 = (f32[4,8,256]{2,1,0:T(8,128)S(1)}, f32[4,8,256]{2,1,0:T(8,128)S(1)}, u32[]{:S(2)}, u32[]{:S(2)}) collective-permute-start(f32[4,8,256]{2,1,0:T(8,128)S(1)} %get-tuple-element.31), channel_id=1, source_target_pairs={{0,12},{4,0},{8,4},{12,8},{1,13},{5,1},{9,5},{13,9},{2,14},{6,2},{... | collective-permute-start | bytes 98312 | tf_op jit(solution)/shard_map/ppermute | solution.py:281
  108.9 1.2 collective-permute-done.17
  110.2 17.8 %collective-permute-start.25 = (f32[4,4,8,256]{3,2,1,0:T(8,128)S(1)}, f32[4,4,8,256]{3,2,1,0:T(8,128)S(1)}, u32[]{:S(2)}, u32[]{:S(2)}) collective-permute-start(f32[4,4,8,256]{3,2,1,0:T(8,128)S(1)} %pad_maximum_fusion.2.z0), channel_id=1, source_target_pairs={{0,3},{1,0},{2,1},{3,2},{4,7},{5,4},{6,5},{7,6},{8,11},{9,8},{10,9... | collective-permute-start | bytes 393224 | tf_op jit(solution)/shard_map/ppermute | solution.py:281
  128.7 2.6 %collective-permute-done.25.z3 = f32[4,4,8,256]{3,2,1,0:T(8,128)S(1)} collective-permute-done((f32[4,4,8,256]{3,2,1,0:T(8,128)S(1)}, f32[4,4,8,256]{3,2,1,0:T(8,128)S(1)}, u32[]{:S(2)}, u32[]{:S(2)}) %collective-permute-start.25) | collective-permute-done | bytes 131104 | tf_op jit(solution)/shard_map/ppermute | solution.py:281
  131.3 2.1 %collective-permute-done.24.z2 = f32[4,4,8,256]{3,2,1,0:T(8,128)S(1)} collective-permute-done((f32[4,4,8,256]{3,2,1,0:T(8,128)S(1)}, f32[4,4,8,256]{3,2,1,0:T(8,128)S(1)}, u32[]{:S(2)}, u32[]{:S(2)}) %collective-permute-start.24) | collective-permute-done | bytes 131104 | tf_op jit(solution)/shard_map/ppermute | solution.py:281
  133.4 1.3 collective-permute-done.23.z1
  134.8 8.6 %collective-permute-start.26 = (f32[4,4,4,8,256]{4,3,2,1,0:T(8,128)S(1)}, f32[4,4,4,8,256]{4,3,2,1,0:T(8,128)S(1)}, u32[]{:S(2)}, u32[]{:S(2)}) collective-permute-start(f32[4,4,4,8,256]{4,3,2,1,0:T(8,128)S(1)} %pad_maximum_fusion.1), channel_id=1, source_target_pairs={{0,16},{16,0},{1,17},{17,1},{2,18},{18,2},{3,19},{19,3},{4,20},{20... | collective-permute-start | bytes 1572872 | tf_op jit(solution)/shard_map/ppermute | solution.py:272
  143.4 2.0 %finish.1 = f32[2,512,512]{2,1,0:T(8,128)} custom-call(f32[2,512,512]{2,1,0:T(8,128)S(1)} %copy-done.1, f32[2,256,512]{2,1,0:T(8,128)S(1)} %collective-permute-done.22.above, f32[2,512,256]{2,1,0:T(8,128)S(1)} %collective-permute-done.21.left), custom_call_target="tpu_custom_call" | custom-call | tf_op jit(solution)/shard_map/finish/pallas_call | solution.py:256
  145.4 2.0 %probe.3 = f32[1024,256]{1,0:T(8,128)} custom-call(s32[6]{0:T(128)S(1)} %copy-done.2, f32[1024,256]{1,0:T(8,128)S(1)} %bitcast.66, f32[4,4,8,256]{3,2,1,0:T(8,128)S(1)} %pad_maximum_fusion.2.z0, f32[4,4,8,256]{3,2,1,0:T(8,128)S(1)} %collective-permute-done.23.z1, f32[4,4,8,256]{3,2,1,0:T(8,128)S(1)} %collective-permute-done.24.z2, ...), custom_call_target="tpu_custom_call" | custom-call | tf_op jit(solution)/shard_map/probe/pallas_call | solution.py:333
  (58 shorter events, 9.0 us)
Async XLA Ops:
  0.6 2.8 %copy-start.3 = (f32[2,512,512]{2,1,0:T(8,128)S(1)}, f32[2,512,512]{2,1,0:T(8,128)}, u32[]{:S(2)}) copy-start(f32[2,512,512]{2,1,0:T(8,128)} %obj.1) | copy-start | bytes 6291460
  0.6 22.2 %copy-start.7 = (s32[8,2]{0,1:T(2,128)S(1)}, s32[8,2]{0,1:T(2,128)}, u32[]{:S(2)}) copy-start(s32[8,2]{0,1:T(2,128)} %param.11) | copy-start | bytes 196
  2.1 16.1 %collective-permute-start = (f32[2,256,256]{2,1,0:T(8,128)S(1)}, f32[2,256,256]{2,1,0:T(8,128)}, u32[]{:S(2)}, u32[]{:S(2)}) collective-permute-start(f32[2,256,256]{2,1,0:T(8,128)S(1)} %get-tuple-element.23), channel_id=1, source_target_pairs={{1,0},{2,1},{3,2},{4,3},{5,4},{6,5},{7,6},{8,7},{9,8},{10,9},{11,1... | collective-permute-start | bytes 1572872 | tf_op jit(solution)/shard_map/ppermute | solution.py:306
  3.5 27.6 %collective-permute-start.2 = (f32[2,256,512]{2,1,0:T(8,128)S(1)}, f32[2,256,512]{2,1,0:T(8,128)S(1)}, u32[]{:S(2)}, u32[]{:S(2)}) collective-permute-start(f32[2,256,512]{2,1,0:T(8,128)S(1)} %slice.47), channel_id=1, source_target_pairs={{16,0},{32,16},{48,32},{64,48},{80,64},{96,80},{112,96},{17,1},{33... | collective-permute-start | bytes 3145736 | tf_op jit(solution)/shard_map/ppermute | solution.py:307
  6.8 24.3 %collective-permute-start.1 = (f32[2,256,256]{2,1,0:T(8,128)S(1)}, f32[2,256,256]{2,1,0:T(8,128)}, u32[]{:S(2)}, u32[]{:S(2)}) collective-permute-start(f32[2,256,256]{2,1,0:T(8,128)S(1)} %get-tuple-element.22), channel_id=1, source_target_pairs={{1,0},{2,1},{3,2},{4,3},{5,4},{6,5},{7,6},{8,7},{9,8},{10,9},{11,1... | collective-permute-start | bytes 1572872 | tf_op jit(solution)/shard_map/ppermute | solution.py:308
  18.2 12.9 %collective-permute-start.3 = (f32[2,256,256]{2,1,0:T(8,128)}, f32[2,256,256]{2,1,0:T(8,128)}, u32[]{:S(2)}, u32[]{:S(2)}) collective-permute-start(f32[2,256,256]{2,1,0:T(8,128)} %collective-permute-done.right_top), channel_id=1, source_target_pairs={{16,0},{32,16},{48,32},{64,48},{80,64},{96,80},{112,96},{17,1},{33... | collective-permute-start | bytes 1572872 | tf_op jit(solution)/shard_map/ppermute | solution.py:309
  50.0 26.7 %copy-start.5 = (f32[2,256,256]{2,1,0:T(8,128)S(1)}, f32[2,256,256]{2,1,0:T(8,128)}, u32[]{:S(2)}) copy-start(f32[2,256,256]{2,1,0:T(8,128)} %get-tuple-element.15) | copy-start | bytes 1572868
  50.0 26.8 %copy-start.6 = (f32[2,256,256]{2,1,0:T(8,128)S(1)}, f32[2,256,256]{2,1,0:T(8,128)}, u32[]{:S(2)}) copy-start(f32[2,256,256]{2,1,0:T(8,128)} %get-tuple-element.17) | copy-start | bytes 1572868
  50.0 18.3 %collective-permute-start.4 = (f32[2,256,256]{2,1,0:T(8,128)}, f32[2,256,256]{2,1,0:T(8,128)S(1)}, u32[]{:S(2)}, u32[]{:S(2)}) collective-permute-start(f32[2,256,256]{2,1,0:T(8,128)} %get-tuple-element.14), channel_id=1, source_target_pairs={{0,16},{16,0},{1,17},{17,1},{2,18},{18,2},{3,19},{19,3},{4,20},{20... | collective-permute-start | bytes 1572872 | tf_op jit(solution)/shard_map/ppermute | solution.py:272
  50.1 26.6 %collective-permute-start.20 = (f32[2,256,256]{2,1,0:T(8,128)}, f32[2,256,256]{2,1,0:T(8,128)S(1)}, u32[]{:S(2)}, u32[]{:S(2)}) collective-permute-start(f32[2,256,256]{2,1,0:T(8,128)} %get-tuple-element.16), channel_id=1, source_target_pairs={{0,16},{16,32},{32,48},{48,64},{64,80},{80,96},{96,112},{1,17},{17... | collective-permute-start | bytes 1572872 | tf_op jit(solution)/shard_map/ppermute | solution.py:317
  66.3 43.9 %collective-permute-start.22 = (f32[2,256,512]{2,1,0:T(8,128)}, f32[2,256,512]{2,1,0:T(8,128)S(1)}, u32[]{:S(2)}, u32[]{:S(2)}) collective-permute-start(f32[2,256,512]{2,1,0:T(8,128)} %get-tuple-element.18), channel_id=1, source_target_pairs={{0,16},{16,32},{32,48},{48,64},{64,80},{80,96},{96,112},{1,17},{17... | collective-permute-start | bytes 3145736 | tf_op jit(solution)/shard_map/ppermute | solution.py:318
  69.5 11.0 %collective-permute-start.5 = (f32[4,4,8,256]{3,2,1,0:T(8,128)S(1)}, f32[4,4,8,256]{3,2,1,0:T(8,128)S(1)}, u32[]{:S(2)}, u32[]{:S(2)}) collective-permute-start(f32[4,4,8,256]{3,2,1,0:T(8,128)S(1)} %get-tuple-element.24), channel_id=1, source_target_pairs={{0,2},{1,3},{2,0},{3,1},{4,6},{5,7},{6,4},{7,5},{8,10},{9,11},{10,... | collective-permute-start | bytes 393224 | tf_op jit(solution)/shard_map/ppermute | solution.py:276
  73.1 9.6 %collective-permute-start.7 = (f32[4,4,8,256]{3,2,1,0:T(8,128)S(1)}, f32[4,4,8,256]{3,2,1,0:T(8,128)S(1)}, u32[]{:S(2)}, u32[]{:S(2)}) collective-permute-start(f32[4,4,8,256]{3,2,1,0:T(8,128)S(1)} %get-tuple-element.25), channel_id=1, source_target_pairs={{0,3},{1,0},{2,1},{3,2},{4,7},{5,4},{6,5},{7,6},{8,11},{9,8},{10,9... | collective-permute-start | bytes 393224 | tf_op jit(solution)/shard_map/ppermute | solution.py:276
  76.2 6.4 %collective-permute-start.6 = (f32[4,4,8,256]{3,2,1,0:T(8,128)S(1)}, f32[4,4,8,256]{3,2,1,0:T(8,128)S(1)}, u32[]{:S(2)}, u32[]{:S(2)}) collective-permute-start(f32[4,4,8,256]{3,2,1,0:T(8,128)S(1)} %get-tuple-element.26), channel_id=1, source_target_pairs={{0,1},{1,2},{2,3},{3,0},{4,5},{5,6},{6,7},{7,4},{8,9},{9,10},{10,1... | collective-permute-start | bytes 393224 | tf_op jit(solution)/shard_map/ppermute | solution.py:276
  76.8 66.6 %copy-start.1 = (f32[2,512,512]{2,1,0:T(8,128)S(1)}, f32[2,512,512]{2,1,0:T(8,128)}, u32[]{:S(2)}) copy-start(f32[2,512,512]{2,1,0:T(8,128)} %get-tuple-element.12.part) | copy-start | bytes 6291460
  76.9 33.3 %collective-permute-start.21 = (f32[2,512,256]{2,1,0:T(8,128)S(1)}, f32[2,512,256]{2,1,0:T(8,128)S(1)}, u32[]{:S(2)}, u32[]{:S(2)}) collective-permute-start(f32[2,512,256]{2,1,0:T(8,128)S(1)} %pad_maximum_fusion), channel_id=1, source_target_pairs={{0,1},{1,2},{2,3},{3,4},{4,5},{5,6},{6,7},{7,8},{8,9},{9,10},{10,1... | collective-permute-start | bytes 3145736 | tf_op jit(solution)/shard_map/ppermute | solution.py:322
  82.7 4.9 %collective-permute-start.8 = (f32[4,8,256]{2,1,0:T(8,128)S(1)}, f32[4,8,256]{2,1,0:T(8,128)S(1)}, u32[]{:S(2)}, u32[]{:S(2)}) collective-permute-start(f32[4,8,256]{2,1,0:T(8,128)S(1)} %get-tuple-element.27), channel_id=1, source_target_pairs={{0,8},{4,12},{8,0},{12,4},{1,9},{5,13},{9,1},{13,5},{2,10},{6,14},... | collective-permute-start | bytes 98312 | tf_op jit(solution)/shard_map/ppermute | solution.py:276
  86.1 3.1 %collective-permute-start.10 = (f32[4,8,256]{2,1,0:T(8,128)S(1)}, f32[4,8,256]{2,1,0:T(8,128)S(1)}, u32[]{:S(2)}, u32[]{:S(2)}) collective-permute-start(f32[4,8,256]{2,1,0:T(8,128)S(1)} %get-tuple-element.28), channel_id=1, source_target_pairs={{0,12},{4,0},{8,4},{12,8},{1,13},{5,1},{9,5},{13,9},{2,14},{6,2},{... | collective-permute-start | bytes 98312 | tf_op jit(solution)/shard_map/ppermute | solution.py:276
  86.2 4.0 %collective-permute-start.9 = (f32[4,8,256]{2,1,0:T(8,128)S(1)}, f32[4,8,256]{2,1,0:T(8,128)S(1)}, u32[]{:S(2)}, u32[]{:S(2)}) collective-permute-start(f32[4,8,256]{2,1,0:T(8,128)S(1)} %get-tuple-element.29), channel_id=1, source_target_pairs={{0,4},{4,8},{8,12},{12,0},{1,5},{5,9},{9,13},{13,1},{2,6},{6,10},{... | collective-permute-start | bytes 98312 | tf_op jit(solution)/shard_map/ppermute | solution.py:276
  90.2 5.9 %collective-permute-start.11 = (f32[8,256]{1,0:T(8,128)S(1)}, f32[8,256]{1,0:T(8,128)S(1)}, u32[]{:S(2)}, u32[]{:S(2)}) collective-permute-start(f32[8,256]{1,0:T(8,128)S(1)} %get-tuple-element.32), channel_id=1, source_target_pairs={{0,64},{32,96},{64,0},{96,32},{1,65},{33,97},{65,1},{97,33},{2,66}... | collective-permute-start | bytes 24584 | tf_op jit(solution)/shard_map/ppermute | solution.py:276
  93.2 3.6 %collective-permute-start.13 = (f32[8,256]{1,0:T(8,128)S(1)}, f32[8,256]{1,0:T(8,128)S(1)}, u32[]{:S(2)}, u32[]{:S(2)}) collective-permute-start(f32[8,256]{1,0:T(8,128)S(1)} %get-tuple-element.33), channel_id=1, source_target_pairs={{0,96},{32,0},{64,32},{96,64},{1,97},{33,1},{65,33},{97,65},{2,98}... | collective-permute-start | bytes 24584 | tf_op jit(solution)/shard_map/ppermute | solution.py:276
  96.1 3.7 %collective-permute-start.12 = (f32[8,256]{1,0:T(8,128)S(1)}, f32[8,256]{1,0:T(8,128)S(1)}, u32[]{:S(2)}, u32[]{:S(2)}) collective-permute-start(f32[8,256]{1,0:T(8,128)S(1)} %get-tuple-element.34), channel_id=1, source_target_pairs={{0,32},{32,64},{64,96},{96,0},{1,33},{33,65},{65,97},{97,1},{2,34}... | collective-permute-start | bytes 24584 | tf_op jit(solution)/shard_map/ppermute | solution.py:276
  99.8 2.5 %collective-permute-start.16 = (f32[8,256]{1,0:T(8,128)S(1)}, f32[8,256]{1,0:T(8,128)S(1)}, u32[]{:S(2)}, u32[]{:S(2)}) collective-permute-start(f32[8,256]{1,0:T(8,128)S(1)} %fusion.8), channel_id=1, source_target_pairs={{0,96},{32,0},{64,32},{96,64},{1,97},{33,1},{65,33},{97,65},{2,98}... | collective-permute-start | bytes 24584 | tf_op jit(solution)/shard_map/ppermute | solution.py:281
  99.8 4.0 %collective-permute-start.15 = (f32[8,256]{1,0:T(8,128)S(1)}, f32[8,256]{1,0:T(8,128)S(1)}, u32[]{:S(2)}, u32[]{:S(2)}) collective-permute-start(f32[8,256]{1,0:T(8,128)S(1)} %fusion.8), channel_id=1, source_target_pairs={{0,64},{32,96},{64,0},{96,32},{1,65},{33,97},{65,1},{97,33},{2,66}... | collective-permute-start | bytes 24584 | tf_op jit(solution)/shard_map/ppermute | solution.py:281
  100.4 4.3 %collective-permute-start.14 = (f32[8,256]{1,0:T(8,128)S(1)}, f32[8,256]{1,0:T(8,128)S(1)}, u32[]{:S(2)}, u32[]{:S(2)}) collective-permute-start(f32[8,256]{1,0:T(8,128)S(1)} %fusion.8), channel_id=1, source_target_pairs={{0,32},{32,64},{64,96},{96,0},{1,33},{33,65},{65,97},{97,1},{2,34}... | collective-permute-start | bytes 24584 | tf_op jit(solution)/shard_map/ppermute | solution.py:281
  104.7 4.3 %collective-permute-start.18 = (f32[4,8,256]{2,1,0:T(8,128)S(1)}, f32[4,8,256]{2,1,0:T(8,128)S(1)}, u32[]{:S(2)}, u32[]{:S(2)}) collective-permute-start(f32[4,8,256]{2,1,0:T(8,128)S(1)} %get-tuple-element.31), channel_id=1, source_target_pairs={{0,8},{4,12},{8,0},{12,4},{1,9},{5,13},{9,1},{13,5},{2,10},{6,14},... | collective-permute-start | bytes 98312 | tf_op jit(solution)/shard_map/ppermute | solution.py:281
  106.2 4.0 %collective-permute-start.17 = (f32[4,8,256]{2,1,0:T(8,128)S(1)}, f32[4,8,256]{2,1,0:T(8,128)S(1)}, u32[]{:S(2)}, u32[]{:S(2)}) collective-permute-start(f32[4,8,256]{2,1,0:T(8,128)S(1)} %get-tuple-element.31), channel_id=1, source_target_pairs={{0,4},{4,8},{8,12},{12,0},{1,5},{5,9},{9,13},{13,1},{2,6},{6,10},{... | collective-permute-start | bytes 98312 | tf_op jit(solution)/shard_map/ppermute | solution.py:281
  106.2 4.0 %collective-permute-start.19 = (f32[4,8,256]{2,1,0:T(8,128)S(1)}, f32[4,8,256]{2,1,0:T(8,128)S(1)}, u32[]{:S(2)}, u32[]{:S(2)}) collective-permute-start(f32[4,8,256]{2,1,0:T(8,128)S(1)} %get-tuple-element.31), channel_id=1, source_target_pairs={{0,12},{4,0},{8,4},{12,8},{1,13},{5,1},{9,5},{13,9},{2,14},{6,2},{... | collective-permute-start | bytes 98312 | tf_op jit(solution)/shard_map/ppermute | solution.py:281
  110.2 21.1 %collective-permute-start.25 = (f32[4,4,8,256]{3,2,1,0:T(8,128)S(1)}, f32[4,4,8,256]{3,2,1,0:T(8,128)S(1)}, u32[]{:S(2)}, u32[]{:S(2)}) collective-permute-start(f32[4,4,8,256]{3,2,1,0:T(8,128)S(1)} %pad_maximum_fusion.2.z0), channel_id=1, source_target_pairs={{0,3},{1,0},{2,1},{3,2},{4,7},{5,4},{6,5},{7,6},{8,11},{9,8},{10,9... | collective-permute-start | bytes 393224 | tf_op jit(solution)/shard_map/ppermute | solution.py:281
  128.0 5.4 %collective-permute-start.24 = (f32[4,4,8,256]{3,2,1,0:T(8,128)S(1)}, f32[4,4,8,256]{3,2,1,0:T(8,128)S(1)}, u32[]{:S(2)}, u32[]{:S(2)}) collective-permute-start(f32[4,4,8,256]{3,2,1,0:T(8,128)S(1)} %pad_maximum_fusion.2.z0), channel_id=1, source_target_pairs={{0,2},{1,3},{2,0},{3,1},{4,6},{5,7},{6,4},{7,5},{8,10},{9,11},{10,... | collective-permute-start | bytes 393224 | tf_op jit(solution)/shard_map/ppermute | solution.py:281
  128.0 6.7 %collective-permute-start.23 = (f32[4,4,8,256]{3,2,1,0:T(8,128)S(1)}, f32[4,4,8,256]{3,2,1,0:T(8,128)S(1)}, u32[]{:S(2)}, u32[]{:S(2)}) collective-permute-start(f32[4,4,8,256]{3,2,1,0:T(8,128)S(1)} %pad_maximum_fusion.2.z0), channel_id=1, source_target_pairs={{0,1},{1,2},{2,3},{3,0},{4,5},{5,6},{6,7},{7,4},{8,9},{9,10},{10,1... | collective-permute-start | bytes 393224 | tf_op jit(solution)/shard_map/ppermute | solution.py:281
  134.8 10.6 %collective-permute-start.26 = (f32[4,4,4,8,256]{4,3,2,1,0:T(8,128)S(1)}, f32[4,4,4,8,256]{4,3,2,1,0:T(8,128)S(1)}, u32[]{:S(2)}, u32[]{:S(2)}) collective-permute-start(f32[4,4,4,8,256]{4,3,2,1,0:T(8,128)S(1)} %pad_maximum_fusion.1), channel_id=1, source_target_pairs={{0,16},{16,0},{1,17},{17,1},{2,18},{18,2},{3,19},{19,3},{4,20},{20... | collective-permute-start | bytes 1572872 | tf_op jit(solution)/shard_map/ppermute | solution.py:272
  (3 other events, 5.0 us)

commit v3 on v2

--- a/solution.py
+++ b/solution.py
@@ -160,12 +160,10 @@
         return carry
 
     lax.fori_loop(0, live[0], slot, 0)
-    for n, (kc, kz, kx, ky) in enumerate(np.ndindex(2, 4, 4, 4)):
-        c = lax.rem(anchor[2] + kc, 2)
-        row = lax.rem(anchor[3] + kz, 4) * 128 + lax.rem(anchor[4] + kx, 4) * 32 + lax.rem(anchor[5] + ky, 4) * 8
-        r = pl.multiple_of(lax.rem(row, W), 8)
-        n8 = n % 64 * 8
-        prv[kc, n8 // W, n8 % W:n8 % W + 8, :] = pacc[c, lax.div(row, W), pl.ds(r, 8), :]
+    for kc, kx in np.ndindex(2, 4):
+        c, x = lax.rem(anchor[2] + kc, 2), lax.rem(anchor[3] + kx, 4)
+        at = pl.multiple_of(lax.rem(x, 2) * H, H)
+        prv[kc, kx // 2, kx % 2 * H:kx % 2 * H + H, :] = pacc[c, lax.div(x, 2), pl.ds(at, H), :]
     cov[:, 0:512, 0:512] = cov[:, 0:512, 0:512] - 0.5 * acc[:, 0:512, 0:512]
     outs = [
         (cov.at[:, 0:512, 0:512], o_part),
@@ -237,21 +235,21 @@
     return lax.ppermute(value, axes, pairs)
 
 
-def finish_kernel(part, above, left, out):
+def finish_kernel(part, above, top, bot, out):
     h = pl.program_id(1)
-    out[0, :, :W] = part[0, :, :W] - 0.5 * left[0]
 
     @pl.when(h == 0)
     def _():
-        out[0, :, :W] -= 0.5 * above[0, :, :W]
-        out[0, :, W:] = part[0, :, W:] - 0.5 * above[0, :, W:]
+        out[0] = part[0] - 0.5 * above[0]
+        out[0, :, :W] -= 0.5 * top[0]
 
     @pl.when(h == 1)
     def _():
         out[0, :, W:] = part[0, :, W:]
-
-
-def finish_call(part, above, left):
+        out[0, :, :W] = part[0, :, :W] - 0.5 * bot[0]
+
+
+def finish_call(part, above, top, bot):
     wide = pl.BlockSpec((1, W, 512), lambda c, h: (c, h, 0))
     return pl.pallas_call(
         finish_kernel,
@@ -260,12 +258,13 @@
         in_specs=[
             wide,
             pl.BlockSpec((1, W, 512), lambda c, h: (c, 0, 0)),
-            pl.BlockSpec((1, W, W), lambda c, h: (c, h, 0)),
+            pl.BlockSpec((1, W, W), lambda c, h: (c, 0, 0)),
+            pl.BlockSpec((1, W, W), lambda c, h: (c, 0, 0)),
         ],
         out_specs=wide,
         compiler_params=pltpu.CompilerParams(vmem_limit_bytes=8 * 2**20),
         name="finish",
-    )(part, above, left)
+    )(part, above, top, bot)
 
 
 def swap_cores(value):
@@ -281,17 +280,17 @@
     return [value] + [lax.ppermute(value, axis, [(i, (i + k) % 4) for i in range(4)]) for k in (1, 2, 3)]
 
 
-def probe_kernel(step, place, probe, z0, z1, z2, z3, rest, out):
-    for n, (kc, kz, kx, ky) in enumerate(np.ndindex(2, 4, 4, 4)):
-        c = lax.rem(place[2] + kc, 2)
-        row = (
-            lax.rem(place[3] - kz + 4, 4) * 128
-            + lax.rem(place[4] - kx + 4, 4) * 32
-            + lax.rem(place[5] - ky + 4, 4) * 8
-        )
-        at = pl.multiple_of(c * 512 + row, 8)
-        total = (z0, z1, z2, z3)[kz][kx, ky] if kc == 0 else rest[kz, kx, ky]
-        out[pl.ds(at, 8), :] = probe[pl.ds(at, 8), :] - step * total
+def sum_everywhere(value, axis):
+    got = [lax.ppermute(value, axis, [(i, (i + k) % 4) for i in range(4)]) for k in (2, 1, 3)]
+    return (value + got[0]) + (got[1] + got[2])
+
+
+def probe_kernel(step, place, probe, x0, x1, x2, x3, rest, out):
+    for kc, kx in np.ndindex(2, 4):
+        row = lax.rem(place[2] + kc, 2) * 512 + lax.rem(place[3] - kx + 4, 4) * H
+        at = pl.multiple_of(row, H)
+        total = (x0, x1, x2, x3)[kx][...] if kc == 0 else rest[kx]
+        out[pl.ds(at, H), :] = probe[pl.ds(at, H), :] - step * total
 
 
 def shards(object_planes, probe_planes, offsets, photon_counts, live_counts):
@@ -309,24 +308,22 @@
     corner = lax.ppermute(right_top, rows, up)
     roots = prep_call(photon_counts)
     place = jnp.stack(
-        [lax.axis_index(rows) * 512, lax.axis_index(cols) * 512] + [lax.axis_index(a) for a in ("core", "z", "x", "y")]
+        [lax.axis_index(rows) * 512, lax.axis_index(cols) * 512] + [lax.axis_index(a) for a in ("core", "x")]
     ).astype(jnp.int32)
     part, g_top, g_bot, g_corner, g_below, mine, other = main_call(
         offsets, live_counts.reshape(1), place, object_planes, right_top, right_bot, below, corner, probe_planes, roots
     )
     corner_in = lax.ppermute(g_corner, rows, down)
+    bot_in = lax.ppermute(g_bot, cols, to_right)
     above_in = lax.ppermute(g_below, rows, down)
-    half = (mine + swap_cores(other)).reshape(4, 4, 4, 8, W)
-    piece = sum_along(half, "z")
-    g_right = jnp.concatenate([g_top + corner_in, g_bot], 1)
-    left_in = lax.ppermute(g_right, cols, to_right)
-    piece = sum_along(piece, "x")
-    piece = sum_along(piece, "y")
-    piece = jnp.stack(spread_along(piece, "y"))
-    piece = jnp.stack(spread_along(piece, "x"))
-    piece, left_in, above_in = lax.optimization_barrier((piece, left_in, above_in))
-    new_object = finish_call(part, above_in, left_in)
-    quarters = spread_along(piece, "z")
+    half = (mine + swap_cores(other)).reshape(4, H, W)
+    top_in = lax.ppermute(g_top + corner_in, cols, to_right)
+    piece = sum_along(half, "x")
+    piece = sum_everywhere(piece, "y")
+    piece, bot_in, top_in = lax.optimization_barrier((piece, bot_in, top_in))
+    piece = sum_everywhere(piece, "z")
+    new_object = finish_call(part, above_in, top_in, bot_in)
+    quarters = spread_along(piece, "x")
     rest = swap_cores(jnp.stack(quarters))
     smem, vmem = pl.BlockSpec(memory_space=pltpu.SMEM), pl.BlockSpec(memory_space=pltpu.VMEM)
     step = 1.0 / math.sqrt(offsets.shape[0] * n_row * n_col)

time: 147 us -> 131 us (0.89); the launches traced: 147 us -> 129 us
  starting transfers between devices: 82.5 us -> 50.6 us
  Pallas kernels: 28.8 us -> 43.3 us
    ppermute x1 -> x8, starting transfers between devices: 3.57 us -> 24.6 us  [the longest x6 18.2 us: sum_everywhere(): lax.ppermute(value, axis, [(i, (i + k) % 4) for i in range(4)])]
    ppermute x9 -> x3, starting transfers between devices: 24.1 us -> 5.63 us  [spread_along(): lax.ppermute(value, axis, [(i, (i + k) % 4) for i in range(4)])]
    pallas_call x1, Pallas kernels: 17.9 us -> 32.7 us  [main_call(): pl.pallas_call(main_kernel, out_shape=(S(2, 512, 512), S(2, 256, 256), S(...]
    ppermute x9 -> x3, starting transfers between devices: 18 us -> 3.59 us  [sum_along(): lax.ppermute(pieces[k], axis, [(i, (i + k) % 4) for i in range(4)])]
    ppermute x1, starting transfers between devices: 16.1 us -> 2.05 us  [shards(): corner_in = lax.ppermute(g_corner, rows, down)]
    ppermute x1 -> x8, waiting for transfers between devices: 0.01 us -> 12.6 us  [the longest x6 9.16 us: sum_everywhere(): lax.ppermute(value, axis, [(i, (i + k) % 4) for i in range(4)])]
    ppermute x9 -> x3, waiting for transfers between devices: 8.39 us -> 0.01 us  [sum_along(): lax.ppermute(pieces[k], axis, [(i, (i + k) % 4) for i in range(4)])]
    ppermute x2, starting transfers between devices: 8.69 us -> 2.94 us  [swap_cores(): return lax.ppermute(value, 'core', [(0, 1), (1, 0)])]
  transfers between devices with their start and end apart: 27 -> 22, of which waited for: 14 -> 9; matrix products, arithmetic and copies ran while one was open for 2% -> 2% of each run, Pallas kernels for 6% -> 7%
where the time goes in v3:
time: 131 us; the launch traced here: 129 us
  starting transfers between devices  50.6 us (39%)
  Pallas kernels  43.3 us (33%)
  waiting for transfers between devices  28.7 us (22%)
  local copies, waits for them, and re-layouts  3.21 us (2%)
  other arithmetic  1.97 us (2%)
  between operations  1.56 us (1%)
    pallas_call x1, Pallas kernels, main_call(): pl.pallas_call(main_kernel, out_shape=(S(2, 512, 512), S(2, 256, 256), S(...  32.7 us
    ppermute x6, starting transfers between devices, sum_everywhere(): lax.ppermute(value, axis, [(i, (i + k) % 4) for i in range(4)])  18.2 us
    ppermute x1, waiting for transfers between devices, shards(): right_top = lax.ppermute(object_planes[:, :W, :W], cols, to_left)  10.1 us
    ppermute x6, waiting for transfers between devices, sum_everywhere(): lax.ppermute(value, axis, [(i, (i + k) % 4) for i in range(4)])  9.16 us
    pallas_call x1, Pallas kernels, prep_call(): pl.pallas_call(prep_kernel, grid=(8,), out_shape=jax.ShapeDtypeStruct((8,...  6.95 us
    ppermute x3, waiting for transfers between devices, spread_along(): lax.ppermute(value, axis, [(i, (i + k) % 4) for i in range(4)])  5.66 us
    ppermute x3, starting transfers between devices, spread_along(): lax.ppermute(value, axis, [(i, (i + k) % 4) for i in range(4)])  5.63 us
    ppermute x1, starting transfers between devices, shards(): top_in = lax.ppermute(g_top + corner_in, cols, to_right)  5.05 us
  transfers between devices with their start and end apart: 22, of which 9 were waited for; matrix products, arithmetic and copies ran while one was open for 2% of the time, Pallas kernels for 7%

profile of v3, /device:TPU:1, one launch (start us, length us, event | category | flops | bytes accessed | tf_op | source)
XLA Modules:
  0.0 129.4 jit_solution(16668214711636052160)
XLA Ops:
  0.7 1.4 %fusion.3 = (f32[2,256,256]{2,1,0:T(8,128)S(1)}, f32[2,256,256]{2,1,0:T(8,128)S(1)}) fusion(f32[2,512,512]{2,1,0:T(8,128)} %obj.1), kind=kLoop, calls=%fused_computation.11 | loop fusion | bytes 2097152 | tf_op jit(solution)/shard_map/slice | solution.py:307
  2.1 1.3 collective-permute-start
  3.5 3.3 %collective-permute-start.2 = (f32[2,256,512]{2,1,0:T(8,128)S(1)}, f32[2,256,512]{2,1,0:T(8,128)S(1)}, u32[]{:S(2)}, u32[]{:S(2)}) collective-permute-start(f32[2,256,512]{2,1,0:T(8,128)S(1)} %slice.23), channel_id=1, source_target_pairs={{16,0},{32,16},{48,32},{64,48},{80,64},{96,80},{112,96},{17,1},{33... | collective-permute-start | bytes 3145736 | tf_op jit(solution)/shard_map/ppermute | solution.py:306
  6.8 1.3 collective-permute-start.1
  8.1 10.1 %collective-permute-done.right_top = f32[2,256,256]{2,1,0:T(8,128)} collective-permute-done((f32[2,256,256]{2,1,0:T(8,128)S(1)}, f32[2,256,256]{2,1,0:T(8,128)}, u32[]{:S(2)}, u32[]{:S(2)}) %collective-permute-start) | collective-permute-done | bytes 524320 | tf_op jit(solution)/shard_map/ppermute | solution.py:305
  18.2 4.0 %collective-permute-start.3 = (f32[2,256,256]{2,1,0:T(8,128)}, f32[2,256,256]{2,1,0:T(8,128)}, u32[]{:S(2)}, u32[]{:S(2)}) collective-permute-start(f32[2,256,256]{2,1,0:T(8,128)} %collective-permute-done.right_top), channel_id=1, source_target_pairs={{16,0},{32,16},{48,32},{64,48},{80,64},{96,80},{112,96},{17,1},{33... | collective-permute-start | bytes 1572872 | tf_op jit(solution)/shard_map/ppermute | solution.py:308
  22.9 0.7 copy.11.offs
  23.5 6.9 %roots.1.sq = f32[8,256,256]{2,1,0:T(8,128)} custom-call(s32[8,256,256]{2,1,0:T(8,128)} %counts.1, bf16[256,256]{1,0:T(8,128)(2,1)} %constant.31.clone.pm, bf16[256,256]{1,0:T(8,128)(2,1)} %constant.32.clone.pmt), custom_call_target="tpu_custom_call" | custom-call | tf_op jit(solution)/shard_map/roots/pallas_call | solution.py:224
  31.2 1.0 copy-done.4
  32.1 32.7 %slots.1 = (f32[2,512,512]{2,1,0:T(8,128)}, f32[2,256,256]{2,1,0:T(8,128)}, f32[2,256,256]{2,1,0:T(8,128)}, f32[2,256,256]{2,1,0:T(8,128)}, f32[2,256,512]{2,1,0...) custom-call(s32[8,2]{1,0:T(8,128)} %copy.11.offs, s32[1]{0:T(128)} %bitcast.26.live, ...), custom_call_target="tpu_custom_call" | custom-call | tf_op jit(solution)/shard_map/slots/pallas_call | solution.py:189
  65.0 2.1 %collective-permute-start.13 = (f32[2,256,256]{2,1,0:T(8,128)}, f32[2,256,256]{2,1,0:T(8,128)S(1)}, u32[]{:S(2)}, u32[]{:S(2)}) collective-permute-start(f32[2,256,256]{2,1,0:T(8,128)} %get-tuple-element.18), channel_id=1, source_target_pairs={{0,16},{16,32},{32,48},{48,64},{64,80},{80,96},{96,112},{1,17},{17... | collective-permute-start | bytes 1572872 | tf_op jit(solution)/shard_map/ppermute | solution.py:316
  67.1 1.1 add.41
  68.4 3.5 %collective-permute-start.8 = (f32[128,256]{1,0:T(8,128)S(1)}, f32[128,256]{1,0:T(8,128)S(1)}, u32[]{:S(2)}, u32[]{:S(2)}) collective-permute-start(f32[128,256]{1,0:T(8,128)S(1)} %get-tuple-element.25), channel_id=1, source_target_pairs={{0,12},{4,0},{8,4},{12,8},{1,13},{5,1},{9,5},{13,9},{2,14},{6,2},{... | collective-permute-start | bytes 393224 | tf_op jit(solution)/shard_map/ppermute | solution.py:275
  71.9 1.3 %collective-permute-start.12 = (f32[2,256,256]{2,1,0:T(8,128)S(1)}, f32[2,256,256]{2,1,0:T(8,128)S(1)}, u32[]{:S(2)}, u32[]{:S(2)}) collective-permute-start(f32[2,256,256]{2,1,0:T(8,128)S(1)} %copy-done.8), channel_id=1, source_target_pairs={{0,1},{1,2},{2,3},{3,4},{4,5},{5,6},{6,7},{7,8},{8,9},{9,10},{10,1... | collective-permute-start | bytes 1572872 | tf_op jit(solution)/shard_map/ppermute | solution.py:317
  73.6 5.0 %collective-permute-start.14 = (f32[2,256,256]{2,1,0:T(8,128)S(1)}, f32[2,256,256]{2,1,0:T(8,128)S(1)}, u32[]{:S(2)}, u32[]{:S(2)}) collective-permute-start(f32[2,256,256]{2,1,0:T(8,128)S(1)} %add.48), channel_id=1, source_target_pairs={{0,1},{1,2},{2,3},{3,4},{4,5},{5,6},{6,7},{7,8},{8,9},{9,10},{10,1... | collective-permute-start | bytes 1572872 | tf_op jit(solution)/shard_map/ppermute | solution.py:320
  78.7 4.2 %collective-permute-start.11 = (f32[128,256]{1,0:T(8,128)S(1)}, f32[128,256]{1,0:T(8,128)S(1)}, u32[]{:S(2)}, u32[]{:S(2)}) collective-permute-start(f32[128,256]{1,0:T(8,128)S(1)} %fusion.2), channel_id=1, source_target_pairs={{0,96},{32,0},{64,32},{96,64},{1,97},{33,1},{65,33},{97,65},{2,98}... | collective-permute-start | bytes 393224 | tf_op jit(solution)/shard_map/ppermute | solution.py:284
  83.0 2.8 %collective-permute-start.9 = (f32[128,256]{1,0:T(8,128)S(1)}, f32[128,256]{1,0:T(8,128)S(1)}, u32[]{:S(2)}, u32[]{:S(2)}) collective-permute-start(f32[128,256]{1,0:T(8,128)S(1)} %fusion.2), channel_id=1, source_target_pairs={{0,64},{32,96},{64,0},{96,32},{1,65},{33,97},{65,1},{97,33},{2,66}... | collective-permute-start | bytes 393224 | tf_op jit(solution)/shard_map/ppermute | solution.py:284
  86.1 1.8 %collective-permute-done.10 = f32[128,256]{1,0:T(8,128)S(1)} collective-permute-done((f32[128,256]{1,0:T(8,128)S(1)}, f32[128,256]{1,0:T(8,128)S(1)}, u32[]{:S(2)}, u32[]{:S(2)}) %collective-permute-start.10) | collective-permute-done | bytes 131104 | tf_op jit(solution)/shard_map/ppermute | solution.py:284
  87.9 3.5 %collective-permute-done.9 = f32[128,256]{1,0:T(8,128)S(1)} collective-permute-done((f32[128,256]{1,0:T(8,128)S(1)}, f32[128,256]{1,0:T(8,128)S(1)}, u32[]{:S(2)}, u32[]{:S(2)}) %collective-permute-start.9) | collective-permute-done | bytes 131104 | tf_op jit(solution)/shard_map/ppermute | solution.py:284
  91.5 3.5 %collective-permute-done.14.top = f32[2,256,256]{2,1,0:T(8,128)S(1)} collective-permute-done((f32[2,256,256]{2,1,0:T(8,128)S(1)}, f32[2,256,256]{2,1,0:T(8,128)S(1)}, u32[]{:S(2)}, u32[]{:S(2)}) %collective-permute-start.14) | collective-permute-done | bytes 524320 | tf_op jit(solution)/shard_map/ppermute | solution.py:320
  94.9 9.8 %collective-permute-start.17 = (f32[128,256]{1,0:T(8,128)S(1)}, f32[128,256]{1,0:T(8,128)S(1)}, u32[]{:S(2)}, u32[]{:S(2)}) collective-permute-start(f32[128,256]{1,0:T(8,128)S(1)} %add_add_fusion.1), channel_id=1, source_target_pairs={{0,3},{1,0},{2,1},{3,2},{4,7},{5,4},{6,5},{7,6},{8,11},{9,8},{10,9... | collective-permute-start | bytes 393224 | tf_op jit(solution)/shard_map/ppermute | solution.py:284
  104.8 1.2 collective-permute-start.15
  105.9 1.9 %collective-permute-start.4 = (f32[2,256,512]{2,1,0:T(8,128)S(1)}, f32[2,256,512]{2,1,0:T(8,128)S(1)}, u32[]{:S(2)}, u32[]{:S(2)}) collective-permute-start(f32[2,256,512]{2,1,0:T(8,128)S(1)} %copy-done.7), channel_id=1, source_target_pairs={{0,16},{16,32},{32,48},{48,64},{64,80},{80,96},{96,112},{1,17},{17... | collective-permute-start | bytes 3145736 | tf_op jit(solution)/shard_map/ppermute | solution.py:318
  107.9 3.6 %collective-permute-done.16 = f32[128,256]{1,0:T(8,128)S(1)} collective-permute-done((f32[128,256]{1,0:T(8,128)S(1)}, f32[128,256]{1,0:T(8,128)S(1)}, u32[]{:S(2)}, u32[]{:S(2)}) %collective-permute-start.16) | collective-permute-done | bytes 131104 | tf_op jit(solution)/shard_map/ppermute | solution.py:284
  111.5 1.3 %collective-permute-start.20 = (f32[128,256]{1,0:T(8,128)S(1)}, f32[128,256]{1,0:T(8,128)S(1)}, u32[]{:S(2)}, u32[]{:S(2)}) collective-permute-start(f32[128,256]{1,0:T(8,128)S(1)} %add_add_fusion.x0), channel_id=1, source_target_pairs={{0,12},{4,0},{8,4},{12,8},{1,13},{5,1},{9,5},{13,9},{2,14},{6,2},{... | collective-permute-start | bytes 393224 | tf_op jit(solution)/shard_map/ppermute | solution.py:280
  112.8 3.6 %collective-permute-start.19 = (f32[128,256]{1,0:T(8,128)S(1)}, f32[128,256]{1,0:T(8,128)S(1)}, u32[]{:S(2)}, u32[]{:S(2)}) collective-permute-start(f32[128,256]{1,0:T(8,128)S(1)} %add_add_fusion.x0), channel_id=1, source_target_pairs={{0,8},{4,12},{8,0},{12,4},{1,9},{5,13},{9,1},{13,5},{2,10},{6,14},... | collective-permute-start | bytes 393224 | tf_op jit(solution)/shard_map/ppermute | solution.py:280
  116.4 0.8 collective-permute-start.18
  117.2 1.6 %collective-permute-done.19.x2 = f32[128,256]{1,0:T(8,128)S(1)} collective-permute-done((f32[128,256]{1,0:T(8,128)S(1)}, f32[128,256]{1,0:T(8,128)S(1)}, u32[]{:S(2)}, u32[]{:S(2)}) %collective-permute-start.19) | collective-permute-done | bytes 131104 | tf_op jit(solution)/shard_map/ppermute | solution.py:280
  118.8 4.1 %collective-permute-done.18.x1 = f32[128,256]{1,0:T(8,128)S(1)} collective-permute-done((f32[128,256]{1,0:T(8,128)S(1)}, f32[128,256]{1,0:T(8,128)S(1)}, u32[]{:S(2)}, u32[]{:S(2)}) %collective-permute-start.18) | collective-permute-done | bytes 131104 | tf_op jit(solution)/shard_map/ppermute | solution.py:280
  122.9 2.9 %collective-permute-start.21 = (f32[4,128,256]{2,1,0:T(8,128)S(1)}, f32[4,128,256]{2,1,0:T(8,128)S(1)}, u32[]{:S(2)}, u32[]{:S(2)}) collective-permute-start(f32[4,128,256]{2,1,0:T(8,128)S(1)} %pad_maximum_fusion), channel_id=1, source_target_pairs={{0,16},{16,0},{1,17},{17,1},{2,18},{18,2},{3,19},{19,3},{4,20},{20... | collective-permute-start | bytes 1572872 | tf_op jit(solution)/shard_map/ppermute | solution.py:271
  125.7 2.0 %finish.1 = f32[2,512,512]{2,1,0:T(8,128)} custom-call(f32[2,512,512]{2,1,0:T(8,128)S(1)} %copy-done.1, f32[2,256,512]{2,1,0:T(8,128)S(1)} %collective-permute-done.4.above, f32[2,256,256]{2,1,0:T(8,128)S(1)} %collective-permute-done.14.top, f32[2,256,256]{2,1,0:T(8,128)S(1)} %collective-permute-done.12.bot), custom_call_target="tpu_custom_call" | custom-call | tf_op jit(solution)/shard_map/finish/pallas_call | solution.py:254
  127.8 1.6 %probe.3 = f32[1024,256]{1,0:T(8,128)} custom-call(s32[4]{0:T(128)S(1)} %copy-done.2, f32[1024,256]{1,0:T(8,128)S(1)} %bitcast.27, f32[128,256]{1,0:T(8,128)S(1)} %add_add_fusion.x0, f32[128,256]{1,0:T(8,128)S(1)} %collective-permute-done.18.x1, f32[128,256]{1,0:T(8,128)S(1)} %collective-permute-done.19.x2, f32[128,256]{1,0:T(8,128)S(1)} %collective-permute-done.20.x3, ...), custom_call_target="tpu_custom_call" | custom-call | tf_op jit(solution)/shard_map/probe/pallas_call | solution.py:330
  (45 shorter events, 1.9 us)
Async XLA Ops:
  0.6 2.8 %copy-start.3 = (f32[2,512,512]{2,1,0:T(8,128)S(1)}, f32[2,512,512]{2,1,0:T(8,128)}, u32[]{:S(2)}) copy-start(f32[2,512,512]{2,1,0:T(8,128)} %obj.1) | copy-start | bytes 6291460
  0.6 22.2 %copy-start.6 = (s32[8,2]{0,1:T(2,128)S(1)}, s32[8,2]{0,1:T(2,128)}, u32[]{:S(2)}) copy-start(s32[8,2]{0,1:T(2,128)} %param.11) | copy-start | bytes 196
  2.1 16.1 %collective-permute-start = (f32[2,256,256]{2,1,0:T(8,128)S(1)}, f32[2,256,256]{2,1,0:T(8,128)}, u32[]{:S(2)}, u32[]{:S(2)}) collective-permute-start(f32[2,256,256]{2,1,0:T(8,128)S(1)} %get-tuple-element.23), channel_id=1, source_target_pairs={{1,0},{2,1},{3,2},{4,3},{5,4},{6,5},{7,6},{8,7},{9,8},{10,9},{11,1... | collective-permute-start | bytes 1572872 | tf_op jit(solution)/shard_map/ppermute | solution.py:305
  3.5 27.7 %collective-permute-start.2 = (f32[2,256,512]{2,1,0:T(8,128)S(1)}, f32[2,256,512]{2,1,0:T(8,128)S(1)}, u32[]{:S(2)}, u32[]{:S(2)}) collective-permute-start(f32[2,256,512]{2,1,0:T(8,128)S(1)} %slice.23), channel_id=1, source_target_pairs={{16,0},{32,16},{48,32},{64,48},{80,64},{96,80},{112,96},{17,1},{33... | collective-permute-start | bytes 3145736 | tf_op jit(solution)/shard_map/ppermute | solution.py:306
  6.8 24.3 %collective-permute-start.1 = (f32[2,256,256]{2,1,0:T(8,128)S(1)}, f32[2,256,256]{2,1,0:T(8,128)}, u32[]{:S(2)}, u32[]{:S(2)}) collective-permute-start(f32[2,256,256]{2,1,0:T(8,128)S(1)} %get-tuple-element.22), channel_id=1, source_target_pairs={{1,0},{2,1},{3,2},{4,3},{5,4},{6,5},{7,6},{8,7},{9,8},{10,9},{11,1... | collective-permute-start | bytes 1572872 | tf_op jit(solution)/shard_map/ppermute | solution.py:307
  18.2 12.9 %collective-permute-start.3 = (f32[2,256,256]{2,1,0:T(8,128)}, f32[2,256,256]{2,1,0:T(8,128)}, u32[]{:S(2)}, u32[]{:S(2)}) collective-permute-start(f32[2,256,256]{2,1,0:T(8,128)} %collective-permute-done.right_top), channel_id=1, source_target_pairs={{16,0},{32,16},{48,32},{64,48},{80,64},{96,80},{112,96},{17,1},{33... | collective-permute-start | bytes 1572872 | tf_op jit(solution)/shard_map/ppermute | solution.py:308
  31.2 1.0 copy-start.4
  64.9 7.0 %copy-start.8 = (f32[2,256,256]{2,1,0:T(8,128)S(1)}, f32[2,256,256]{2,1,0:T(8,128)}, u32[]{:S(2)}) copy-start(f32[2,256,256]{2,1,0:T(8,128)} %get-tuple-element.16) | copy-start | bytes 1572868
  64.9 8.6 %copy-start.5 = (f32[2,256,256]{2,1,0:T(8,128)S(1)}, f32[2,256,256]{2,1,0:T(8,128)}, u32[]{:S(2)}) copy-start(f32[2,256,256]{2,1,0:T(8,128)} %get-tuple-element.17) | copy-start | bytes 1572868
  64.9 2.2 %collective-permute-start.5 = (f32[2,256,256]{2,1,0:T(8,128)}, f32[2,256,256]{2,1,0:T(8,128)S(1)}, u32[]{:S(2)}, u32[]{:S(2)}) collective-permute-start(f32[2,256,256]{2,1,0:T(8,128)} %get-tuple-element.15), channel_id=1, source_target_pairs={{0,16},{16,0},{1,17},{17,1},{2,18},{18,2},{3,19},{19,3},{4,20},{20... | collective-permute-start | bytes 1572872 | tf_op jit(solution)/shard_map/ppermute | solution.py:271
  65.0 8.5 %collective-permute-start.13 = (f32[2,256,256]{2,1,0:T(8,128)}, f32[2,256,256]{2,1,0:T(8,128)S(1)}, u32[]{:S(2)}, u32[]{:S(2)}) collective-permute-start(f32[2,256,256]{2,1,0:T(8,128)} %get-tuple-element.18), channel_id=1, source_target_pairs={{0,16},{16,32},{32,48},{48,64},{64,80},{80,96},{96,112},{1,17},{17... | collective-permute-start | bytes 1572872 | tf_op jit(solution)/shard_map/ppermute | solution.py:316
  68.2 37.7 %copy-start.7 = (f32[2,256,512]{2,1,0:T(8,128)S(1)}, f32[2,256,512]{2,1,0:T(8,128)}, u32[]{:S(2)}) copy-start(f32[2,256,512]{2,1,0:T(8,128)} %get-tuple-element.13) | copy-start | bytes 3145732
  68.3 10.3 %collective-permute-start.6 = (f32[128,256]{1,0:T(8,128)S(1)}, f32[128,256]{1,0:T(8,128)S(1)}, u32[]{:S(2)}, u32[]{:S(2)}) collective-permute-start(f32[128,256]{1,0:T(8,128)S(1)} %get-tuple-element.24), channel_id=1, source_target_pairs={{0,8},{4,12},{8,0},{12,4},{1,9},{5,13},{9,1},{13,5},{2,10},{6,14},... | collective-permute-start | bytes 393224 | tf_op jit(solution)/shard_map/ppermute | solution.py:275
  68.4 10.3 %collective-permute-start.8 = (f32[128,256]{1,0:T(8,128)S(1)}, f32[128,256]{1,0:T(8,128)S(1)}, u32[]{:S(2)}, u32[]{:S(2)}) collective-permute-start(f32[128,256]{1,0:T(8,128)S(1)} %get-tuple-element.25), channel_id=1, source_target_pairs={{0,12},{4,0},{8,4},{12,8},{1,13},{5,1},{9,5},{13,9},{2,14},{6,2},{... | collective-permute-start | bytes 393224 | tf_op jit(solution)/shard_map/ppermute | solution.py:275
  71.9 6.8 %collective-permute-start.7 = (f32[128,256]{1,0:T(8,128)S(1)}, f32[128,256]{1,0:T(8,128)S(1)}, u32[]{:S(2)}, u32[]{:S(2)}) collective-permute-start(f32[128,256]{1,0:T(8,128)S(1)} %get-tuple-element.26), channel_id=1, source_target_pairs={{0,4},{4,8},{8,12},{12,0},{1,5},{5,9},{9,13},{13,1},{2,6},{6,10},{... | collective-permute-start | bytes 393224 | tf_op jit(solution)/shard_map/ppermute | solution.py:275
  71.9 19.6 %collective-permute-start.12 = (f32[2,256,256]{2,1,0:T(8,128)S(1)}, f32[2,256,256]{2,1,0:T(8,128)S(1)}, u32[]{:S(2)}, u32[]{:S(2)}) collective-permute-start(f32[2,256,256]{2,1,0:T(8,128)S(1)} %copy-done.8), channel_id=1, source_target_pairs={{0,1},{1,2},{2,3},{3,4},{4,5},{5,6},{6,7},{7,8},{8,9},{9,10},{10,1... | collective-permute-start | bytes 1572872 | tf_op jit(solution)/shard_map/ppermute | solution.py:317
  73.5 52.2 %copy-start.1 = (f32[2,512,512]{2,1,0:T(8,128)S(1)}, f32[2,512,512]{2,1,0:T(8,128)}, u32[]{:S(2)}) copy-start(f32[2,512,512]{2,1,0:T(8,128)} %get-tuple-element.12.part) | copy-start | bytes 6291460
  73.6 21.4 %collective-permute-start.14 = (f32[2,256,256]{2,1,0:T(8,128)S(1)}, f32[2,256,256]{2,1,0:T(8,128)S(1)}, u32[]{:S(2)}, u32[]{:S(2)}) collective-permute-start(f32[2,256,256]{2,1,0:T(8,128)S(1)} %add.48), channel_id=1, source_target_pairs={{0,1},{1,2},{2,3},{3,4},{4,5},{5,6},{6,7},{7,8},{8,9},{9,10},{10,1... | collective-permute-start | bytes 1572872 | tf_op jit(solution)/shard_map/ppermute | solution.py:320
  78.7 7.4 %collective-permute-start.11 = (f32[128,256]{1,0:T(8,128)S(1)}, f32[128,256]{1,0:T(8,128)S(1)}, u32[]{:S(2)}, u32[]{:S(2)}) collective-permute-start(f32[128,256]{1,0:T(8,128)S(1)} %fusion.2), channel_id=1, source_target_pairs={{0,96},{32,0},{64,32},{96,64},{1,97},{33,1},{65,33},{97,65},{2,98}... | collective-permute-start | bytes 393224 | tf_op jit(solution)/shard_map/ppermute | solution.py:284
  82.9 5.0 %collective-permute-start.10 = (f32[128,256]{1,0:T(8,128)S(1)}, f32[128,256]{1,0:T(8,128)S(1)}, u32[]{:S(2)}, u32[]{:S(2)}) collective-permute-start(f32[128,256]{1,0:T(8,128)S(1)} %fusion.2), channel_id=1, source_target_pairs={{0,32},{32,64},{64,96},{96,0},{1,33},{33,65},{65,97},{97,1},{2,34}... | collective-permute-start | bytes 393224 | tf_op jit(solution)/shard_map/ppermute | solution.py:284
  83.0 8.4 %collective-permute-start.9 = (f32[128,256]{1,0:T(8,128)S(1)}, f32[128,256]{1,0:T(8,128)S(1)}, u32[]{:S(2)}, u32[]{:S(2)}) collective-permute-start(f32[128,256]{1,0:T(8,128)S(1)} %fusion.2), channel_id=1, source_target_pairs={{0,64},{32,96},{64,0},{96,32},{1,65},{33,97},{65,1},{97,33},{2,66}... | collective-permute-start | bytes 393224 | tf_op jit(solution)/shard_map/ppermute | solution.py:284
  94.9 12.9 %collective-permute-start.17 = (f32[128,256]{1,0:T(8,128)S(1)}, f32[128,256]{1,0:T(8,128)S(1)}, u32[]{:S(2)}, u32[]{:S(2)}) collective-permute-start(f32[128,256]{1,0:T(8,128)S(1)} %add_add_fusion.1), channel_id=1, source_target_pairs={{0,3},{1,0},{2,1},{3,2},{4,7},{5,4},{6,5},{7,6},{8,11},{9,8},{10,9... | collective-permute-start | bytes 393224 | tf_op jit(solution)/shard_map/ppermute | solution.py:284
  104.8 6.7 %collective-permute-start.16 = (f32[128,256]{1,0:T(8,128)S(1)}, f32[128,256]{1,0:T(8,128)S(1)}, u32[]{:S(2)}, u32[]{:S(2)}) collective-permute-start(f32[128,256]{1,0:T(8,128)S(1)} %add_add_fusion.1), channel_id=1, source_target_pairs={{0,1},{1,2},{2,3},{3,0},{4,5},{5,6},{6,7},{7,4},{8,9},{9,10},{10,1... | collective-permute-start | bytes 393224 | tf_op jit(solution)/shard_map/ppermute | solution.py:284
  104.8 6.7 %collective-permute-start.15 = (f32[128,256]{1,0:T(8,128)S(1)}, f32[128,256]{1,0:T(8,128)S(1)}, u32[]{:S(2)}, u32[]{:S(2)}) collective-permute-start(f32[128,256]{1,0:T(8,128)S(1)} %add_add_fusion.1), channel_id=1, source_target_pairs={{0,2},{1,3},{2,0},{3,1},{4,6},{5,7},{6,4},{7,5},{8,10},{9,11},{10,... | collective-permute-start | bytes 393224 | tf_op jit(solution)/shard_map/ppermute | solution.py:284
  105.9 19.8 %collective-permute-start.4 = (f32[2,256,512]{2,1,0:T(8,128)S(1)}, f32[2,256,512]{2,1,0:T(8,128)S(1)}, u32[]{:S(2)}, u32[]{:S(2)}) collective-permute-start(f32[2,256,512]{2,1,0:T(8,128)S(1)} %copy-done.7), channel_id=1, source_target_pairs={{0,16},{16,32},{32,48},{48,64},{64,80},{80,96},{96,112},{1,17},{17... | collective-permute-start | bytes 3145736 | tf_op jit(solution)/shard_map/ppermute | solution.py:318
  111.5 5.6 %collective-permute-start.20 = (f32[128,256]{1,0:T(8,128)S(1)}, f32[128,256]{1,0:T(8,128)S(1)}, u32[]{:S(2)}, u32[]{:S(2)}) collective-permute-start(f32[128,256]{1,0:T(8,128)S(1)} %add_add_fusion.x0), channel_id=1, source_target_pairs={{0,12},{4,0},{8,4},{12,8},{1,13},{5,1},{9,5},{13,9},{2,14},{6,2},{... | collective-permute-start | bytes 393224 | tf_op jit(solution)/shard_map/ppermute | solution.py:280
  112.8 5.9 %collective-permute-start.19 = (f32[128,256]{1,0:T(8,128)S(1)}, f32[128,256]{1,0:T(8,128)S(1)}, u32[]{:S(2)}, u32[]{:S(2)}) collective-permute-start(f32[128,256]{1,0:T(8,128)S(1)} %add_add_fusion.x0), channel_id=1, source_target_pairs={{0,8},{4,12},{8,0},{12,4},{1,9},{5,13},{9,1},{13,5},{2,10},{6,14},... | collective-permute-start | bytes 393224 | tf_op jit(solution)/shard_map/ppermute | solution.py:280
  116.4 6.4 %collective-permute-start.18 = (f32[128,256]{1,0:T(8,128)S(1)}, f32[128,256]{1,0:T(8,128)S(1)}, u32[]{:S(2)}, u32[]{:S(2)}) collective-permute-start(f32[128,256]{1,0:T(8,128)S(1)} %add_add_fusion.x0), channel_id=1, source_target_pairs={{0,4},{4,8},{8,12},{12,0},{1,5},{5,9},{9,13},{13,1},{2,6},{6,10},{... | collective-permute-start | bytes 393224 | tf_op jit(solution)/shard_map/ppermute | solution.py:280
  122.9 4.9 %collective-permute-start.21 = (f32[4,128,256]{2,1,0:T(8,128)S(1)}, f32[4,128,256]{2,1,0:T(8,128)S(1)}, u32[]{:S(2)}, u32[]{:S(2)}) collective-permute-start(f32[4,128,256]{2,1,0:T(8,128)S(1)} %pad_maximum_fusion), channel_id=1, source_target_pairs={{0,16},{16,0},{1,17},{17,1},{2,18},{18,2},{3,19},{19,3},{4,20},{20... | collective-permute-start | bytes 1572872 | tf_op jit(solution)/shard_map/ppermute | solution.py:271
  125.7 2.0 %copy-start = (f32[2,2,256,256]{3,2,1,0:T(8,128)S(1)}, f32[2,2,256,256]{3,2,1,0:T(8,128)}, u32[]{:S(2)}) copy-start(f32[2,2,256,256]{3,2,1,0:T(8,128)} %probe.2) | copy-start | bytes 3145732
  125.7 2.0 %copy-start.2 = (s32[4]{0:T(128)S(1)}, s32[4]{0:T(128)}, u32[]{:S(2)}) copy-start(s32[4]{0:T(128)} %pad_add_fusion.anchor.place) | copy-start | bytes 52

commit v4 on v3

--- a/solution.py
+++ b/solution.py
@@ -13,6 +13,9 @@
 f32, bf16 = jnp.float32, jnp.bfloat16
 W = 256
 H = 128
+HC = 128
+NB = 2
+LAG = 0
 
 
 def make_tables():
@@ -23,19 +26,12 @@
         ang = 2.0 * np.pi * (((2 * q + p) * b) % W) / W
         c, s = np.cos(ang) / 16.0, np.sin(ang) / 16.0
         right.append(np.block([[c, -s], [s, c]]))
-    def split(t):
+    out = []
+    for t in (right[0], right[1], right[0].T, right[1].T):
         hi = t.astype(np.float32).astype(ml_dtypes.bfloat16)
         lo = (t - hi.astype(np.float64)).astype(np.float32).astype(ml_dtypes.bfloat16)
-        return hi, lo
-    as_rhs = []
-    as_lhs = []
-    for t in (right[0], right[1], right[0].T, right[1].T):
-        hi, lo = split(t)
-        as_rhs.append(np.concatenate([hi, hi, lo], 0))
-        as_lhs.append(np.concatenate([hi, hi, lo], 1))
-    rhs = np.stack(as_rhs)
-    lhs = np.stack(as_lhs)
-    return rhs, lhs
+        out.append(np.stack([hi, lo]))
+    return np.stack(out)
 
 
 def split(x):
@@ -44,14 +40,17 @@
     return hi, lo
 
 
+def rmul2(hi, lo, t):
+    return jnp.dot(jnp.concatenate([hi, lo, hi], 1), jnp.concatenate([t[0], t[0], t[1]], 0), preferred_element_type=f32)
+
+
 def rmul(x, t):
     hi, lo = split(x)
-    return jnp.dot(jnp.concatenate([hi, lo, hi], 1), t, preferred_element_type=f32)
-
-
-def lmul(t, x):
-    hi, lo = split(x)
-    return jnp.dot(t, jnp.concatenate([hi, lo, hi], 0), preferred_element_type=f32)
+    return rmul2(hi, lo, t)
+
+
+def lmul2(t, hi, lo):
+    return jnp.dot(jnp.concatenate([t[0], t[0], t[1]], 1), jnp.concatenate([hi, lo, hi], 0), preferred_element_type=f32)
 
 
 def cat1(a, b):
@@ -62,9 +61,9 @@
     return jnp.concatenate([a, b], 0)
 
 
-def main_kernel(offs, live, anchor, obj, right_top, right_bot, below, corner, probe, sq, rhs, lhs,
+def main_kernel(offs, live, anchor, obj, right_top, right_bot, below, corner, probe, sq, tables,
                 o_part, o_rtop, o_rbot, o_corner, o_below, o_mine, o_other,
-                cov, acc, patch, pacc, prv, sqv, rt, lt, far, term, sems):
+                cov, acc, patch, pacc, prv, sqv, tb, gs, hs, ds, term, sems, sqsems):
     ins = [
         (obj, cov.at[:, 0:512, 0:512]),
         (right_top, cov.at[:, 0:256, 512:768]),
@@ -72,13 +71,14 @@
         (below, cov.at[:, 512:768, 0:512]),
         (corner, cov.at[:, 512:768, 512:768]),
         (probe, prv),
-        (rhs, rt),
-        (lhs, lt),
-        (sq, sqv),
+        (tables, tb),
     ]
     copies = [pltpu.make_async_copy(s, d, sems.at[i]) for i, (s, d) in enumerate(ins)]
+    roots = lambda s: pltpu.make_async_copy(sq.at[s], sqv.at[s], sqsems.at[s])
     for c in copies:
         c.start()
+    for s in range(8):
+        roots(s).start()
     acc[...] = jnp.zeros_like(acc)
     pacc[...] = jnp.zeros_like(pacc)
     for c in copies:
@@ -87,14 +87,16 @@
     sub9 = lax.broadcasted_iota(jnp.int32, (33, 8, H), 1)
     sub = lax.broadcasted_iota(jnp.int32, (32, 8, H), 1)
 
-    def slot(s, carry):
+    def place_of(s):
         top = offs[s, 0] - anchor[0]
         left = offs[s, 1] - anchor[1]
         la = pl.multiple_of(lax.div(left, 128) * 128, 128)
-        ls = lax.rem(left, 128)
+        ta = pl.multiple_of(lax.div(top, 8) * 8, 8)
+        return ta, lax.rem(top, 8), la, lax.rem(left, 128)
+
+    def fetch(s, b):
+        ta, rs, la, ls = place_of(s)
         back = lax.rem(128 - ls, 128)
-        ta = pl.multiple_of(lax.div(top, 8) * 8, 8)
-        rs = lax.rem(top, 8)
         rback = lax.rem(8 - rs, 8)
         for c in range(2):
             t = []
@@ -103,52 +105,12 @@
                 v = pltpu.roll(pltpu.roll(v, back, 1).reshape(33, 8, H), rback, 1)
                 t.append(jnp.where(sub < 8 - rs, v[:32], v[1:]).reshape(W, H))
             for k in range(2):
-                patch[c, :, 128 * k:128 * k + 128] = jnp.where(lane < 128 - ls, t[k], t[k + 1])
-        for m in range(2):
-            pr, pi = prv[0, m], prv[1, m]
-            xr, xi = patch[0], patch[1]
-            wr = pr * xr - pi * xi
-            wi = pr * xi + pi * xr
-            e = cat1(wr[:, :H] + wr[:, H:], wi[:, :H] + wi[:, H:])
-            o = cat1(wr[:, :H] - wr[:, H:], wi[:, :H] - wi[:, H:])
-            ye = rmul(e, rt[0])
-            yo = rmul(o, rt[1])
-            er, ei = cat1(ye[:, :H], yo[:, :H]), cat1(ye[:, H:], yo[:, H:])
-            fe = cat0(er[:H] + er[H:], ei[:H] + ei[H:])
-            fo = cat0(er[:H] - er[H:], ei[:H] - ei[H:])
-            far[m, 0] = lmul(lt[2], fe)
-            far[m, 1] = lmul(lt[3], fo)
-        facs = []
-        for p in range(2):
-            mod = None
-            for m in range(2):
-                a = far[m, p]
-                v = a[:H] * a[:H] + a[H:] * a[H:]
-                mod = v if mod is None else mod + v
-            facs.append(1.0 - sqv[s, H * p:H * p + H, :] * lax.rsqrt(jnp.maximum(mod, 0.1)))
-        for m in range(2):
-            be = lmul(lt[0], far[m, 0] * cat0(facs[0], facs[0]))
-            bo = lmul(lt[1], far[m, 1] * cat0(facs[1], facs[1]))
-            s_, d_ = be + bo, be - bo
-            xr = cat0(s_[:H], d_[:H])
-            xi = cat0(s_[H:], d_[H:])
-            de = rmul(cat1(xr[:, :H], xi[:, :H]), rt[2])
-            do = rmul(cat1(xr[:, H:], xi[:, H:]), rt[3])
-            s_, d_ = de + do, de - do
-            br = cat1(s_[:, :H], d_[:, :H])
-            bi = cat1(s_[:, H:], d_[:, H:])
-            pr, pi = prv[0, m], prv[1, m]
-            xr, xi = patch[0], patch[1]
-            tr, ti = pr * br + pi * bi, pr * bi - pi * br
-            if m == 0:
-                term[0], term[1] = tr, ti
-            else:
-                term[0] += tr
-                term[1] += ti
-            pacc[0, m] += xr * br + xi * bi
-            pacc[1, m] += xr * bi - xi * br
+                patch[b, c, :, 128 * k:128 * k + 128] = jnp.where(lane < 128 - ls, t[k], t[k + 1])
+
+    def deposit(s, b):
+        ta, rs, la, ls = place_of(s)
         for c in range(2):
-            r = [pltpu.roll(term[c, :, 128 * k:128 * k + 128], ls, 1) for k in range(2)]
+            r = [pltpu.roll(term[b, c, :, 128 * k:128 * k + 128], ls, 1) for k in range(2)]
             z = jnp.zeros_like(r[0])
             keep = lane >= ls
             parts = [jnp.where(keep, r[0], z), jnp.where(keep, r[1], r[0]), jnp.where(keep, z, r[1])]
@@ -157,56 +119,177 @@
                 z8 = jnp.zeros((1, 8, H), f32)
                 v = jnp.where(sub9 >= rs, jnp.concatenate([v, z8], 0), jnp.concatenate([z8, v], 0))
                 acc[c, pl.ds(ta, W + 8), pl.ds(la + 128 * k, H)] += v.reshape(W + 8, H)
+
+    def units(s, b, used):
+        for m in range(2):
+            for j in range(0, H, HC):
+                def waves(m=m, j=j):
+                    at = [slice(j, j + HC), slice(H + j, H + j + HC)]
+                    get = lambda ref, *i: cat0(ref[(*i, at[0])], ref[(*i, at[1])])
+                    pr, pi = get(prv, 0, m), get(prv, 1, m)
+                    xr, xi = get(patch, b, 0), get(patch, b, 1)
+                    wr = pr * xr - pi * xi
+                    wi = pr * xi + pi * xr
+                    e = cat1(wr[:, :H] + wr[:, H:], wi[:, :H] + wi[:, H:])
+                    o = cat1(wr[:, :H] - wr[:, H:], wi[:, :H] - wi[:, H:])
+                    return rmul(e, tb[0]), rmul(o, tb[1])
+
+                def rows(ys, m=m, j=j):
+                    for p in range(2):
+                        lanes = slice(H * p, H * p + H)
+                        y = ys[p]
+                        for q in range(2):
+                            f = y[:HC] + y[HC:] if q == 0 else y[:HC] - y[HC:]
+                            hi, lo = split(f)
+                            for part in range(2):
+                                r = H * part + j
+                                gs[b, m, q, r:r + HC, lanes] = hi[:, H * part:H * part + H]
+                                gs[b, m, q, W + r:W + r + HC, lanes] = lo[:, H * part:H * part + H]
+
+                yield waves, rows
+        for q in range(2):
+            for j in range(0, H, HC):
+                def fars(q=q, j=j):
+                    t = tb[2 + q]
+                    return [lmul2(t, gs[b, m, q, :W], gs[b, m, q, W:]) for m in range(2)]
+
+                def factors(fars, q=q, j=j):
+                    mod = sum(a[:HC] * a[:HC] + a[HC:] * a[HC:] for a in fars)
+                    root = sqv[s, H * q + j:H * q + j + HC, :]
+                    fac = used - (used * root) * lax.rsqrt(jnp.maximum(mod, 0.1))
+                    for m in range(2):
+                        for part in range(2):
+                            hi, lo = split(fars[m][HC * part:HC * part + HC] * fac)
+                            r = H * part + j
+                            hs[b, m, q, r:r + HC] = hi
+                            hs[b, m, q, W + r:W + r + HC] = lo
+
+                yield fars, factors
+        for m in range(2):
+            for j in range(0, H, HC):
+                def backs(m=m, j=j):
+                    out = []
+                    for q in range(2):
+                        t = tb[q]
+                        out.append(lmul2(t, hs[b, m, q, :W], hs[b, m, q, W:]))
+                    return out
+
+                def columns(v, m=m, j=j):
+                    for top in range(2):
+                        x = v[0] + v[1] if top == 0 else v[0] - v[1]
+                        for p in range(2):
+                            hi, lo = split(cat1(x[:HC, H * p:H * p + H], x[HC:, H * p:H * p + H]))
+                            r = H * top + j
+                            ds[b, m, p, r:r + HC, :W] = hi
+                            ds[b, m, p, r:r + HC, W:] = lo
+
+                yield backs, columns
+        for m in range(2):
+            for j in (0, H):
+                at = slice(j, j + H)
+
+                def last(m=m, at=at):
+                    return [rmul2(ds[b, m, p, at, :W], ds[b, m, p, at, W:], tb[2 + p]) for p in range(2)]
+
+                def terms(d, m=m, at=at):
+                    for h in range(2):
+                        x = d[0] + d[1] if h == 0 else d[0] - d[1]
+                        br, bi = x[:, :H], x[:, H:]
+                        lanes = slice(H * h, H * h + H)
+                        pr, pi = prv[0, m, at, lanes], prv[1, m, at, lanes]
+                        xr, xi = patch[b, 0, at, lanes], patch[b, 1, at, lanes]
+                        tr, ti = pr * br + pi * bi, pr * bi - pi * br
+                        if m == 0:
+                            term[b, 0, at, lanes], term[b, 1, at, lanes] = tr, ti
+                        else:
+                            term[b, 0, at, lanes] += tr
+                            term[b, 1, at, lanes] += ti
+                        pacc[0, m, at, lanes] += xr * br + xi * bi
+                        pacc[1, m, at, lanes] += xr * bi - xi * br
+
+                yield last, terms
+
+    def pair(i, carry):
+        slots = [i * NB + b for b in range(NB)]
+        used = [jnp.where(s < live[0], 1.0, 0.0) for s in slots]
+        for b in range(NB):
+            roots(slots[b]).wait()
+            fetch(slots[b], b)
+        streams = [list(units(slots[b], b, used[b])) for b in range(NB)]
+        todo = []
+        for group in zip(*streams):
+            for product, then in group:
+                todo.append((then, product()))
+                if len(todo) > LAG:
+                    then, value = todo.pop(0)
+                    then(value)
+        for then, value in todo:
+            then(value)
+        for b in range(NB):
+            deposit(slots[b], b)
         return carry
 
-    lax.fori_loop(0, live[0], slot, 0)
+    pairs = lax.div(live[0] + NB - 1, NB)
+    lax.fori_loop(0, pairs, pair, 0)
+
+    def skip(s, carry):
+        roots(s).wait()
+        return carry
+
+    lax.fori_loop(pairs * NB, 8, skip, 0)
+    outs = [
+        (acc.at[:, 512:768, 512:768], o_corner),
+        (acc.at[:, 256:512, 512:768], o_rbot),
+        (acc.at[:, 0:256, 512:768], o_rtop),
+        (acc.at[:, 512:768, 0:512], o_below),
+        (prv.at[1], o_other),
+        (prv.at[0], o_mine),
+        (cov.at[0, 0:512, 0:512], o_part.at[0]),
+        (cov.at[1, 0:512, 0:512], o_part.at[1]),
+    ]
+    copies = [pltpu.make_async_copy(s, d, sems.at[i]) for i, (s, d) in enumerate(outs)]
+    for c in copies[:4]:
+        c.start()
     for kc, kx in np.ndindex(2, 4):
         c, x = lax.rem(anchor[2] + kc, 2), lax.rem(anchor[3] + kx, 4)
         at = pl.multiple_of(lax.rem(x, 2) * H, H)
         prv[kc, kx // 2, kx % 2 * H:kx % 2 * H + H, :] = pacc[c, lax.div(x, 2), pl.ds(at, H), :]
-    cov[:, 0:512, 0:512] = cov[:, 0:512, 0:512] - 0.5 * acc[:, 0:512, 0:512]
-    outs = [
-        (cov.at[:, 0:512, 0:512], o_part),
-        (acc.at[:, 0:256, 512:768], o_rtop),
-        (acc.at[:, 256:512, 512:768], o_rbot),
-        (acc.at[:, 512:768, 512:768], o_corner),
-        (acc.at[:, 512:768, 0:512], o_below),
-        (prv.at[0], o_mine),
-        (prv.at[1], o_other),
-    ]
-    copies = [pltpu.make_async_copy(s, d, sems.at[i]) for i, (s, d) in enumerate(outs)]
-    for c in copies:
+    for c in copies[4:6]:
         c.start()
+    for c in range(2):
+        cov[c, 0:512, 0:512] = cov[c, 0:512, 0:512] - 0.5 * acc[c, 0:512, 0:512]
+        copies[6 + c].start()
     for c in copies:
         c.wait()
 
 
 def main_call(offs, live, anchor, obj, right_top, right_bot, below, corner, probe, sq):
-    rhs, lhs = (jnp.asarray(t) for t in make_tables())
     any_ = pl.BlockSpec(memory_space=pl.ANY)
     smem = pl.BlockSpec(memory_space=pltpu.SMEM)
     S = lambda *s: jax.ShapeDtypeStruct(s, f32)
     return pl.pallas_call(
         main_kernel,
         out_shape=(S(2, 512, 512), S(2, 256, 256), S(2, 256, 256), S(2, 256, 256), S(2, 256, 512), S(2, 256, 256), S(2, 256, 256)),
-        in_specs=[smem] * 3 + [any_] * 9,
+        in_specs=[smem] * 3 + [any_] * 8,
         out_specs=[any_] * 7,
         scratch_shapes=[
             pltpu.VMEM((2, 768, 768), f32),
             pltpu.VMEM((2, 768, 768), f32),
-            pltpu.VMEM((2, W, W), f32),
+            pltpu.VMEM((NB, 2, W, W), f32),
             pltpu.VMEM((2, 2, W, W), f32),
             pltpu.VMEM((2, 2, W, W), f32),
             pltpu.VMEM((8, W, W), f32),
-            pltpu.VMEM((4, 768, W), bf16),
-            pltpu.VMEM((4, W, 768), bf16),
-            pltpu.VMEM((2, 2, W, W), f32),
-            pltpu.VMEM((2, W, W), f32),
+            pltpu.VMEM((4, 2, W, W), bf16),
+            pltpu.VMEM((NB, 2, 2, 2 * W, W), bf16),
+            pltpu.VMEM((NB, 2, 2, 2 * W, W), bf16),
+            pltpu.VMEM((NB, 2, 2, W, 2 * W), bf16),
+            pltpu.VMEM((NB, 2, W, W), f32),
             pltpu.SemaphoreType.DMA((9,)),
+            pltpu.SemaphoreType.DMA((8,)),
         ],
         compiler_params=pltpu.CompilerParams(vmem_limit_bytes=62 * 2**20),
         name="slots",
-    )(offs, live, anchor, obj, right_top, right_bot, below, corner, probe, sq, rhs, lhs)
+    )(offs, live, anchor, obj, right_top, right_bot, below, corner, probe, sq, jnp.asarray(make_tables()))
 
 
 def prep_kernel(counts, pm, pmt, out):
@@ -305,8 +388,9 @@
     right_top = lax.ppermute(object_planes[:, :W, :W], cols, to_left)
     below = lax.ppermute(object_planes[:, :W, :], rows, up)
     right_bot = lax.ppermute(object_planes[:, W:, :W], cols, to_left)
+    roots = prep_call(photon_counts)
+    right_top, roots = lax.optimization_barrier((right_top, roots))
     corner = lax.ppermute(right_top, rows, up)
-    roots = prep_call(photon_counts)
     place = jnp.stack(
         [lax.axis_index(rows) * 512, lax.axis_index(cols) * 512] + [lax.axis_index(a) for a in ("core", "x")]
     ).astype(jnp.int32)
@@ -319,8 +403,9 @@
     half = (mine + swap_cores(other)).reshape(4, H, W)
     top_in = lax.ppermute(g_top + corner_in, cols, to_right)
     piece = sum_along(half, "x")
+    piece, bot_in = lax.optimization_barrier((piece, bot_in))
     piece = sum_everywhere(piece, "y")
-    piece, bot_in, top_in = lax.optimization_barrier((piece, bot_in, top_in))
+    piece, top_in = lax.optimization_barrier((piece, top_in))
     piece = sum_everywhere(piece, "z")
     new_object = finish_call(part, above_in, top_in, bot_in)
     quarters = spread_along(piece, "x")

time: 131 us -> 123 us (0.939); the launches traced: 129 us -> 123 us
  Pallas kernels: 43.3 us -> 32.1 us
  starting transfers between devices: 50.6 us -> 60.6 us
  waiting for transfers between devices: 28.7 us -> 23.5 us
    pallas_call x1, Pallas kernels: 32.7 us -> 21.5 us  [main_call(): pl.pallas_call(main_kernel, out_shape=(S(2, 512, 512), S(2, 256, 256), S(...]
    ppermute x1, starting transfers between devices: 1.31 us -> 9.55 us  [shards(): bot_in = lax.ppermute(g_bot, cols, to_right)]
    ppermute x1, waiting for transfers between devices: 10.1 us -> 3.21 us  [shards(): right_top = lax.ppermute(object_planes[:, :W, :W], cols, to_left)]
    ppermute x1, waiting for transfers between devices: 0.01 us -> 5.35 us  [shards(): right_bot = lax.ppermute(object_planes[:, W:, :W], cols, to_left)]
    ppermute x1, waiting for transfers between devices: 3.47 us -> 0.01 us  [shards(): top_in = lax.ppermute(g_top + corner_in, cols, to_right)]
    ppermute x1, starting transfers between devices: 5.05 us -> 2.07 us  [shards(): top_in = lax.ppermute(g_top + corner_in, cols, to_right)]
    ppermute x3, waiting for transfers between devices: 0.01 us -> 2.82 us  [sum_along(): lax.ppermute(pieces[k], axis, [(i, (i + k) % 4) for i in range(4)])]
    ppermute x6, waiting for transfers between devices: 9.16 us -> 6.5 us  [sum_everywhere(): lax.ppermute(value, axis, [(i, (i + k) % 4) for i in range(4)])]
  transfers between devices with their start and end apart: 22 -> 22, of which waited for: 9 -> 10; matrix products, arithmetic and copies ran while one was open for 2% -> 2% of each run, Pallas kernels for 7% -> 7%
where the time goes in v4:
time: 123 us
  starting transfers between devices  60.6 us (49%)
  Pallas kernels  32.1 us (26%)
  waiting for transfers between devices  23.5 us (19%)
  local copies, waits for them, and re-layouts  3.31 us (3%)
  other arithmetic  1.97 us (2%)
  between operations  1.52 us (1%)
    pallas_call x1, Pallas kernels, main_call(): pl.pallas_call(main_kernel, out_shape=(S(2, 512, 512), S(2, 256, 256), S(...  21.5 us
    ppermute x6, starting transfers between devices, sum_everywhere(): lax.ppermute(value, axis, [(i, (i + k) % 4) for i in range(4)])  15.9 us
    ppermute x1, starting transfers between devices, shards(): bot_in = lax.ppermute(g_bot, cols, to_right)  9.55 us
    ppermute x3, starting transfers between devices, spread_along(): lax.ppermute(value, axis, [(i, (i + k) % 4) for i in range(4)])  7.37 us
    pallas_call x1, Pallas kernels, prep_call(): pl.pallas_call(prep_kernel, grid=(8,), out_shape=jax.ShapeDtypeStruct((8,...  6.96 us
    ppermute x6, waiting for transfers between devices, sum_everywhere(): lax.ppermute(value, axis, [(i, (i + k) % 4) for i in range(4)])  6.5 us
    ppermute x1, waiting for transfers between devices, shards(): right_bot = lax.ppermute(object_planes[:, W:, :W], cols, to_left)  5.35 us
    ppermute x3, starting transfers between devices, sum_along(): lax.ppermute(pieces[k], axis, [(i, (i + k) % 4) for i in range(4)])  4.96 us
  transfers between devices with their start and end apart: 22, of which 10 were waited for; matrix products, arithmetic and copies ran while one was open for 2% of the time, Pallas kernels for 7%

profile of v4, /device:TPU:1, one launch (start us, length us, event | category | flops | bytes accessed | tf_op | source)
XLA Modules:
  0.0 123.0 jit_solution(6483196722019240770)
XLA Ops:
  0.6 2.4 %fusion.3 = (f32[2,256,256]{2,1,0:T(8,128)}, f32[2,256,256]{2,1,0:T(8,128)}) fusion(f32[2,512,512]{2,1,0:T(8,128)} %obj.1), kind=kLoop, calls=%fused_computation.11 | loop fusion | bytes 2097152 | tf_op jit(solution)/shard_map/slice | solution.py:390
  3.1 1.3 %collective-permute-start = (f32[2,256,256]{2,1,0:T(8,128)}, f32[2,256,256]{2,1,0:T(8,128)S(1)}, u32[]{:S(2)}, u32[]{:S(2)}) collective-permute-start(f32[2,256,256]{2,1,0:T(8,128)} %get-tuple-element.29), channel_id=1, source_target_pairs={{1,0},{2,1},{3,2},{4,3},{5,4},{6,5},{7,6},{8,7},{9,8},{10,9},{11,1... | collective-permute-start | bytes 1572872 | tf_op jit(solution)/shard_map/ppermute | solution.py:388
  4.4 3.3 %collective-permute-start.2 = (f32[2,256,512]{2,1,0:T(8,128)S(1)}, f32[2,256,512]{2,1,0:T(8,128)S(1)}, u32[]{:S(2)}, u32[]{:S(2)}) collective-permute-start(f32[2,256,512]{2,1,0:T(8,128)S(1)} %slice.23), channel_id=1, source_target_pairs={{16,0},{32,16},{48,32},{64,48},{80,64},{96,80},{112,96},{17,1},{33... | collective-permute-start | bytes 3145736 | tf_op jit(solution)/shard_map/ppermute | solution.py:389
  7.8 1.3 %collective-permute-start.1 = (f32[2,256,256]{2,1,0:T(8,128)}, f32[2,256,256]{2,1,0:T(8,128)}, u32[]{:S(2)}, u32[]{:S(2)}) collective-permute-start(f32[2,256,256]{2,1,0:T(8,128)} %get-tuple-element.28), channel_id=1, source_target_pairs={{1,0},{2,1},{3,2},{4,3},{5,4},{6,5},{7,6},{8,7},{9,8},{10,9},{11,1... | collective-permute-start | bytes 1572872 | tf_op jit(solution)/shard_map/ppermute | solution.py:390
  9.1 7.0 %roots.1.sq = f32[8,256,256]{2,1,0:T(8,128)} custom-call(s32[8,256,256]{2,1,0:T(8,128)} %counts.1, bf16[256,256]{1,0:T(8,128)(2,1)} %constant.29.clone.pm, bf16[256,256]{1,0:T(8,128)(2,1)} %constant.30.clone.pmt), custom_call_target="tpu_custom_call" | custom-call | tf_op jit(solution)/shard_map/roots/pallas_call | solution.py:307
  16.0 3.2 %collective-permute-done.right_top = f32[2,256,256]{2,1,0:T(8,128)S(1)} collective-permute-done((f32[2,256,256]{2,1,0:T(8,128)}, f32[2,256,256]{2,1,0:T(8,128)S(1)}, u32[]{:S(2)}, u32[]{:S(2)}) %collective-permute-start) | collective-permute-done | bytes 524320 | tf_op jit(solution)/shard_map/ppermute | solution.py:388
  19.3 4.0 %collective-permute-start.3 = (f32[2,256,256]{2,1,0:T(8,128)S(1)}, f32[2,256,256]{2,1,0:T(8,128)}, u32[]{:S(2)}, u32[]{:S(2)}) collective-permute-start(f32[2,256,256]{2,1,0:T(8,128)S(1)} %collective-permute-done.right_top), channel_id=1, source_target_pairs={{16,0},{32,16},{48,32},{64,48},{80,64},{96,80},{112,96},{17,1},{33... | collective-permute-start | bytes 1572872 | tf_op jit(solution)/shard_map/ppermute | solution.py:393
  25.3 5.3 %collective-permute-done.1.right_bot = f32[2,256,256]{2,1,0:T(8,128)} collective-permute-done((f32[2,256,256]{2,1,0:T(8,128)}, f32[2,256,256]{2,1,0:T(8,128)}, u32[]{:S(2)}, u32[]{:S(2)}) %collective-permute-start.1) | collective-permute-done | bytes 524320 | tf_op jit(solution)/shard_map/ppermute | solution.py:390
  30.6 0.9 collective-permute-done.3.corner
  31.6 21.5 %slots.1 = (f32[2,512,512]{2,1,0:T(8,128)}, f32[2,256,256]{2,1,0:T(8,128)}, f32[2,256,256]{2,1,0:T(8,128)}, f32[2,256,256]{2,1,0:T(8,128)}, f32[2,256,512]{2,1,0...) custom-call(s32[8,2]{1,0:T(8,128)} %copy.10.offs, s32[1]{0:T(128)} %bitcast.26.live, ...), custom_call_target="tpu_custom_call" | custom-call | tf_op jit(solution)/shard_map/slots/pallas_call | solution.py:270
  53.1 2.1 %collective-permute-start.13 = (f32[2,256,256]{2,1,0:T(8,128)}, f32[2,256,256]{2,1,0:T(8,128)S(1)}, u32[]{:S(2)}, u32[]{:S(2)}) collective-permute-start(f32[2,256,256]{2,1,0:T(8,128)} %get-tuple-element.24), channel_id=1, source_target_pairs={{0,16},{16,32},{32,48},{48,64},{64,80},{80,96},{96,112},{1,17},{17... | collective-permute-start | bytes 1572872 | tf_op jit(solution)/shard_map/ppermute | solution.py:400
  55.2 9.5 %collective-permute-start.9 = (f32[2,256,256]{2,1,0:T(8,128)}, f32[2,256,256]{2,1,0:T(8,128)S(1)}, u32[]{:S(2)}, u32[]{:S(2)}) collective-permute-start(f32[2,256,256]{2,1,0:T(8,128)} %get-tuple-element.21), channel_id=1, source_target_pairs={{0,1},{1,2},{2,3},{3,4},{4,5},{5,6},{6,7},{7,8},{8,9},{9,10},{10,1... | collective-permute-start | bytes 1572872 | tf_op jit(solution)/shard_map/ppermute | solution.py:401
  64.8 1.1 add.41
  65.9 3.5 %collective-permute-start.6 = (f32[128,256]{1,0:T(8,128)S(1)}, f32[128,256]{1,0:T(8,128)S(1)}, u32[]{:S(2)}, u32[]{:S(2)}) collective-permute-start(f32[128,256]{1,0:T(8,128)S(1)} %get-tuple-element.30), channel_id=1, source_target_pairs={{0,8},{4,12},{8,0},{12,4},{1,9},{5,13},{9,1},{13,5},{2,10},{6,14},... | collective-permute-start | bytes 393224 | tf_op jit(solution)/shard_map/ppermute | solution.py:358
  69.4 1.5 %collective-permute-start.7 = (f32[128,256]{1,0:T(8,128)S(1)}, f32[128,256]{1,0:T(8,128)S(1)}, u32[]{:S(2)}, u32[]{:S(2)}) collective-permute-start(f32[128,256]{1,0:T(8,128)S(1)} %get-tuple-element.32), channel_id=1, source_target_pairs={{0,4},{4,8},{8,12},{12,0},{1,5},{5,9},{9,13},{13,1},{2,6},{6,10},{... | collective-permute-start | bytes 393224 | tf_op jit(solution)/shard_map/ppermute | solution.py:358
  71.0 2.1 %collective-permute-start.14 = (f32[2,256,256]{2,1,0:T(8,128)S(1)}, f32[2,256,256]{2,1,0:T(8,128)S(1)}, u32[]{:S(2)}, u32[]{:S(2)}) collective-permute-start(f32[2,256,256]{2,1,0:T(8,128)S(1)} %add.48), channel_id=1, source_target_pairs={{0,1},{1,2},{2,3},{3,4},{4,5},{5,6},{6,7},{7,8},{8,9},{9,10},{10,1... | collective-permute-start | bytes 1572872 | tf_op jit(solution)/shard_map/ppermute | solution.py:404
  73.1 1.8 %collective-permute-done.8 = f32[128,256]{1,0:T(8,128)S(1)} collective-permute-done((f32[128,256]{1,0:T(8,128)S(1)}, f32[128,256]{1,0:T(8,128)S(1)}, u32[]{:S(2)}, u32[]{:S(2)}) %collective-permute-start.8) | collective-permute-done | bytes 131104 | tf_op jit(solution)/shard_map/ppermute | solution.py:358
  74.9 1.0 collective-permute-done.7
  77.5 4.0 %collective-permute-start.10 = (f32[128,256]{1,0:T(8,128)S(1)}, f32[128,256]{1,0:T(8,128)S(1)}, u32[]{:S(2)}, u32[]{:S(2)}) collective-permute-start(f32[128,256]{1,0:T(8,128)S(1)} %fusion.2), channel_id=1, source_target_pairs={{0,64},{32,96},{64,0},{96,32},{1,65},{33,97},{65,1},{97,33},{2,66}... | collective-permute-start | bytes 393224 | tf_op jit(solution)/shard_map/ppermute | solution.py:367
  81.5 1.2 collective-permute-done.11
  82.6 4.3 %collective-permute-done.10 = f32[128,256]{1,0:T(8,128)S(1)} collective-permute-done((f32[128,256]{1,0:T(8,128)S(1)}, f32[128,256]{1,0:T(8,128)S(1)}, u32[]{:S(2)}, u32[]{:S(2)}) %collective-permute-start.10) | collective-permute-done | bytes 131104 | tf_op jit(solution)/shard_map/ppermute | solution.py:367
  87.0 9.1 %collective-permute-start.17 = (f32[128,256]{1,0:T(8,128)S(1)}, f32[128,256]{1,0:T(8,128)S(1)}, u32[]{:S(2)}, u32[]{:S(2)}) collective-permute-start(f32[128,256]{1,0:T(8,128)S(1)} %add_add_fusion.1), channel_id=1, source_target_pairs={{0,3},{1,0},{2,1},{3,2},{4,7},{5,4},{6,5},{7,6},{8,11},{9,8},{10,9... | collective-permute-start | bytes 393224 | tf_op jit(solution)/shard_map/ppermute | solution.py:367
  96.1 1.3 %collective-permute-start.15 = (f32[128,256]{1,0:T(8,128)S(1)}, f32[128,256]{1,0:T(8,128)S(1)}, u32[]{:S(2)}, u32[]{:S(2)}) collective-permute-start(f32[128,256]{1,0:T(8,128)S(1)} %add_add_fusion.1), channel_id=1, source_target_pairs={{0,2},{1,3},{2,0},{3,1},{4,6},{5,7},{6,4},{7,5},{8,10},{9,11},{10,... | collective-permute-start | bytes 393224 | tf_op jit(solution)/shard_map/ppermute | solution.py:367
  97.4 4.2 %collective-permute-start.4 = (f32[2,256,512]{2,1,0:T(8,128)S(1)}, f32[2,256,512]{2,1,0:T(8,128)S(1)}, u32[]{:S(2)}, u32[]{:S(2)}) collective-permute-start(f32[2,256,512]{2,1,0:T(8,128)S(1)} %copy-done.8), channel_id=1, source_target_pairs={{0,16},{16,32},{32,48},{48,64},{64,80},{80,96},{96,112},{1,17},{17... | collective-permute-start | bytes 3145736 | tf_op jit(solution)/shard_map/ppermute | solution.py:402
  101.6 1.0 collective-permute-done.16
  102.6 5.4 %collective-permute-start.20 = (f32[128,256]{1,0:T(8,128)S(1)}, f32[128,256]{1,0:T(8,128)S(1)}, u32[]{:S(2)}, u32[]{:S(2)}) collective-permute-start(f32[128,256]{1,0:T(8,128)S(1)} %add_add_fusion.x0), channel_id=1, source_target_pairs={{0,12},{4,0},{8,4},{12,8},{1,13},{5,1},{9,5},{13,9},{2,14},{6,2},{... | collective-permute-start | bytes 393224 | tf_op jit(solution)/shard_map/ppermute | solution.py:363
  108.0 1.2 %collective-permute-start.19 = (f32[128,256]{1,0:T(8,128)S(1)}, f32[128,256]{1,0:T(8,128)S(1)}, u32[]{:S(2)}, u32[]{:S(2)}) collective-permute-start(f32[128,256]{1,0:T(8,128)S(1)} %add_add_fusion.x0), channel_id=1, source_target_pairs={{0,8},{4,12},{8,0},{12,4},{1,9},{5,13},{9,1},{13,5},{2,10},{6,14},... | collective-permute-start | bytes 393224 | tf_op jit(solution)/shard_map/ppermute | solution.py:363
  110.0 3.4 %collective-permute-done.19.x2 = f32[128,256]{1,0:T(8,128)S(1)} collective-permute-done((f32[128,256]{1,0:T(8,128)S(1)}, f32[128,256]{1,0:T(8,128)S(1)}, u32[]{:S(2)}, u32[]{:S(2)}) %collective-permute-start.19) | collective-permute-done | bytes 131104 | tf_op jit(solution)/shard_map/ppermute | solution.py:363
  113.4 1.4 %collective-permute-done.18.x1 = f32[128,256]{1,0:T(8,128)S(1)} collective-permute-done((f32[128,256]{1,0:T(8,128)S(1)}, f32[128,256]{1,0:T(8,128)S(1)}, u32[]{:S(2)}, u32[]{:S(2)}) %collective-permute-start.18) | collective-permute-done | bytes 131104 | tf_op jit(solution)/shard_map/ppermute | solution.py:363
  114.7 4.6 %collective-permute-start.21 = (f32[4,128,256]{2,1,0:T(8,128)S(1)}, f32[4,128,256]{2,1,0:T(8,128)S(1)}, u32[]{:S(2)}, u32[]{:S(2)}) collective-permute-start(f32[4,128,256]{2,1,0:T(8,128)S(1)} %pad_maximum_fusion), channel_id=1, source_target_pairs={{0,16},{16,0},{1,17},{17,1},{2,18},{18,2},{3,19},{19,3},{4,20},{20... | collective-permute-start | bytes 1572872 | tf_op jit(solution)/shard_map/ppermute | solution.py:354
  119.3 2.0 %finish.1 = f32[2,512,512]{2,1,0:T(8,128)} custom-call(f32[2,512,512]{2,1,0:T(8,128)S(1)} %copy-done.1, f32[2,256,512]{2,1,0:T(8,128)S(1)} %collective-permute-done.4.above, f32[2,256,256]{2,1,0:T(8,128)S(1)} %collective-permute-done.14.top, f32[2,256,256]{2,1,0:T(8,128)S(1)} %collective-permute-done.9.bot), custom_call_target="tpu_custom_call" | custom-call | tf_op jit(solution)/shard_map/finish/pallas_call | solution.py:337
  121.3 1.7 %probe.3 = f32[1024,256]{1,0:T(8,128)} custom-call(s32[4]{0:T(128)S(1)} %copy-done.2, f32[1024,256]{1,0:T(8,128)S(1)} %bitcast.27, f32[128,256]{1,0:T(8,128)S(1)} %add_add_fusion.x0, f32[128,256]{1,0:T(8,128)S(1)} %collective-permute-done.18.x1, f32[128,256]{1,0:T(8,128)S(1)} %collective-permute-done.19.x2, f32[128,256]{1,0:T(8,128)S(1)} %collective-permute-done.20.x3, ...), custom_call_target="tpu_custom_call" | custom-call | tf_op jit(solution)/shard_map/probe/pallas_call | solution.py:415
  (45 shorter events, 4.2 us)
Async XLA Ops:
  0.6 3.7 %copy-start.3 = (f32[2,512,512]{2,1,0:T(8,128)S(1)}, f32[2,512,512]{2,1,0:T(8,128)}, u32[]{:S(2)}) copy-start(f32[2,512,512]{2,1,0:T(8,128)} %obj.1) | copy-start | bytes 6291460
  3.1 16.2 %collective-permute-start = (f32[2,256,256]{2,1,0:T(8,128)}, f32[2,256,256]{2,1,0:T(8,128)S(1)}, u32[]{:S(2)}, u32[]{:S(2)}) collective-permute-start(f32[2,256,256]{2,1,0:T(8,128)} %get-tuple-element.29), channel_id=1, source_target_pairs={{1,0},{2,1},{3,2},{4,3},{5,4},{6,5},{7,6},{8,7},{9,8},{10,9},{11,1... | collective-permute-start | bytes 1572872 | tf_op jit(solution)/shard_map/ppermute | solution.py:388
  4.4 26.2 %collective-permute-start.2 = (f32[2,256,512]{2,1,0:T(8,128)S(1)}, f32[2,256,512]{2,1,0:T(8,128)S(1)}, u32[]{:S(2)}, u32[]{:S(2)}) collective-permute-start(f32[2,256,512]{2,1,0:T(8,128)S(1)} %slice.23), channel_id=1, source_target_pairs={{16,0},{32,16},{48,32},{64,48},{80,64},{96,80},{112,96},{17,1},{33... | collective-permute-start | bytes 3145736 | tf_op jit(solution)/shard_map/ppermute | solution.py:389
  7.8 16.1 %copy-start.7 = (s32[8,2]{0,1:T(2,128)S(1)}, s32[8,2]{0,1:T(2,128)}, u32[]{:S(2)}) copy-start(s32[8,2]{0,1:T(2,128)} %param.10) | copy-start | bytes 196
  7.8 22.8 %collective-permute-start.1 = (f32[2,256,256]{2,1,0:T(8,128)}, f32[2,256,256]{2,1,0:T(8,128)}, u32[]{:S(2)}, u32[]{:S(2)}) collective-permute-start(f32[2,256,256]{2,1,0:T(8,128)} %get-tuple-element.28), channel_id=1, source_target_pairs={{1,0},{2,1},{3,2},{4,3},{5,4},{6,5},{7,6},{8,7},{9,8},{10,9},{11,1... | collective-permute-start | bytes 1572872 | tf_op jit(solution)/shard_map/ppermute | solution.py:390
  19.3 12.2 %copy-start.5 = (f32[2,256,256]{2,1,0:T(8,128)}, f32[2,256,256]{2,1,0:T(8,128)S(1)}, u32[]{:S(2)}) copy-start(f32[2,256,256]{2,1,0:T(8,128)S(1)} %collective-permute-done.right_top) | copy-start | bytes 1572868
  19.3 12.2 %collective-permute-start.3 = (f32[2,256,256]{2,1,0:T(8,128)S(1)}, f32[2,256,256]{2,1,0:T(8,128)}, u32[]{:S(2)}, u32[]{:S(2)}) collective-permute-start(f32[2,256,256]{2,1,0:T(8,128)S(1)} %collective-permute-done.right_top), channel_id=1, source_target_pairs={{16,0},{32,16},{48,32},{64,48},{80,64},{96,80},{112,96},{17,1},{33... | collective-permute-start | bytes 1572872 | tf_op jit(solution)/shard_map/ppermute | solution.py:393
  30.6 1.0 copy-start.4
  53.0 17.9 %copy-start.6 = (f32[2,256,256]{2,1,0:T(8,128)S(1)}, f32[2,256,256]{2,1,0:T(8,128)}, u32[]{:S(2)}) copy-start(f32[2,256,256]{2,1,0:T(8,128)} %get-tuple-element.23) | copy-start | bytes 1572868
  53.1 11.7 %collective-permute-start.5 = (f32[2,256,256]{2,1,0:T(8,128)}, f32[2,256,256]{2,1,0:T(8,128)S(1)}, u32[]{:S(2)}, u32[]{:S(2)}) collective-permute-start(f32[2,256,256]{2,1,0:T(8,128)} %get-tuple-element.20), channel_id=1, source_target_pairs={{0,16},{16,0},{1,17},{17,1},{2,18},{18,2},{3,19},{19,3},{4,20},{20... | collective-permute-start | bytes 1572872 | tf_op jit(solution)/shard_map/ppermute | solution.py:354
  53.1 17.7 %collective-permute-start.13 = (f32[2,256,256]{2,1,0:T(8,128)}, f32[2,256,256]{2,1,0:T(8,128)S(1)}, u32[]{:S(2)}, u32[]{:S(2)}) collective-permute-start(f32[2,256,256]{2,1,0:T(8,128)} %get-tuple-element.24), channel_id=1, source_target_pairs={{0,16},{16,32},{32,48},{48,64},{64,80},{80,96},{96,112},{1,17},{17... | collective-permute-start | bytes 1572872 | tf_op jit(solution)/shard_map/ppermute | solution.py:400
  55.2 20.7 %collective-permute-start.9 = (f32[2,256,256]{2,1,0:T(8,128)}, f32[2,256,256]{2,1,0:T(8,128)S(1)}, u32[]{:S(2)}, u32[]{:S(2)}) collective-permute-start(f32[2,256,256]{2,1,0:T(8,128)} %get-tuple-element.21), channel_id=1, source_target_pairs={{0,1},{1,2},{2,3},{3,4},{4,5},{5,6},{6,7},{7,8},{8,9},{9,10},{10,1... | collective-permute-start | bytes 1572872 | tf_op jit(solution)/shard_map/ppermute | solution.py:401
  65.9 31.5 %copy-start.8 = (f32[2,256,512]{2,1,0:T(8,128)S(1)}, f32[2,256,512]{2,1,0:T(8,128)}, u32[]{:S(2)}) copy-start(f32[2,256,512]{2,1,0:T(8,128)} %get-tuple-element.18) | copy-start | bytes 3145732
  65.9 7.1 %collective-permute-start.6 = (f32[128,256]{1,0:T(8,128)S(1)}, f32[128,256]{1,0:T(8,128)S(1)}, u32[]{:S(2)}, u32[]{:S(2)}) collective-permute-start(f32[128,256]{1,0:T(8,128)S(1)} %get-tuple-element.30), channel_id=1, source_target_pairs={{0,8},{4,12},{8,0},{12,4},{1,9},{5,13},{9,1},{13,5},{2,10},{6,14},... | collective-permute-start | bytes 393224 | tf_op jit(solution)/shard_map/ppermute | solution.py:358
  69.4 5.5 %collective-permute-start.8 = (f32[128,256]{1,0:T(8,128)S(1)}, f32[128,256]{1,0:T(8,128)S(1)}, u32[]{:S(2)}, u32[]{:S(2)}) collective-permute-start(f32[128,256]{1,0:T(8,128)S(1)} %get-tuple-element.31), channel_id=1, source_target_pairs={{0,12},{4,0},{8,4},{12,8},{1,13},{5,1},{9,5},{13,9},{2,14},{6,2},{... | collective-permute-start | bytes 393224 | tf_op jit(solution)/shard_map/ppermute | solution.py:358
  69.4 6.5 %collective-permute-start.7 = (f32[128,256]{1,0:T(8,128)S(1)}, f32[128,256]{1,0:T(8,128)S(1)}, u32[]{:S(2)}, u32[]{:S(2)}) collective-permute-start(f32[128,256]{1,0:T(8,128)S(1)} %get-tuple-element.32), channel_id=1, source_target_pairs={{0,4},{4,8},{8,12},{12,0},{1,5},{5,9},{9,13},{13,1},{2,6},{6,10},{... | collective-permute-start | bytes 393224 | tf_op jit(solution)/shard_map/ppermute | solution.py:358
  70.9 48.4 %copy-start.1 = (f32[2,512,512]{2,1,0:T(8,128)S(1)}, f32[2,512,512]{2,1,0:T(8,128)}, u32[]{:S(2)}) copy-start(f32[2,512,512]{2,1,0:T(8,128)} %get-tuple-element.17.part) | copy-start | bytes 6291460
  71.0 16.0 %collective-permute-start.14 = (f32[2,256,256]{2,1,0:T(8,128)S(1)}, f32[2,256,256]{2,1,0:T(8,128)S(1)}, u32[]{:S(2)}, u32[]{:S(2)}) collective-permute-start(f32[2,256,256]{2,1,0:T(8,128)S(1)} %add.48), channel_id=1, source_target_pairs={{0,1},{1,2},{2,3},{3,4},{4,5},{5,6},{6,7},{7,8},{8,9},{9,10},{10,1... | collective-permute-start | bytes 1572872 | tf_op jit(solution)/shard_map/ppermute | solution.py:404
  75.9 5.5 %collective-permute-start.12 = (f32[128,256]{1,0:T(8,128)S(1)}, f32[128,256]{1,0:T(8,128)S(1)}, u32[]{:S(2)}, u32[]{:S(2)}) collective-permute-start(f32[128,256]{1,0:T(8,128)S(1)} %fusion.2), channel_id=1, source_target_pairs={{0,96},{32,0},{64,32},{96,64},{1,97},{33,1},{65,33},{97,65},{2,98}... | collective-permute-start | bytes 393224 | tf_op jit(solution)/shard_map/ppermute | solution.py:367
  76.6 6.0 %collective-permute-start.11 = (f32[128,256]{1,0:T(8,128)S(1)}, f32[128,256]{1,0:T(8,128)S(1)}, u32[]{:S(2)}, u32[]{:S(2)}) collective-permute-start(f32[128,256]{1,0:T(8,128)S(1)} %fusion.2), channel_id=1, source_target_pairs={{0,32},{32,64},{64,96},{96,0},{1,33},{33,65},{65,97},{97,1},{2,34}... | collective-permute-start | bytes 393224 | tf_op jit(solution)/shard_map/ppermute | solution.py:367
  77.5 9.5 %collective-permute-start.10 = (f32[128,256]{1,0:T(8,128)S(1)}, f32[128,256]{1,0:T(8,128)S(1)}, u32[]{:S(2)}, u32[]{:S(2)}) collective-permute-start(f32[128,256]{1,0:T(8,128)S(1)} %fusion.2), channel_id=1, source_target_pairs={{0,64},{32,96},{64,0},{96,32},{1,65},{33,97},{65,1},{97,33},{2,66}... | collective-permute-start | bytes 393224 | tf_op jit(solution)/shard_map/ppermute | solution.py:367
  87.0 14.6 %collective-permute-start.17 = (f32[128,256]{1,0:T(8,128)S(1)}, f32[128,256]{1,0:T(8,128)S(1)}, u32[]{:S(2)}, u32[]{:S(2)}) collective-permute-start(f32[128,256]{1,0:T(8,128)S(1)} %add_add_fusion.1), channel_id=1, source_target_pairs={{0,3},{1,0},{2,1},{3,2},{4,7},{5,4},{6,5},{7,6},{8,11},{9,8},{10,9... | collective-permute-start | bytes 393224 | tf_op jit(solution)/shard_map/ppermute | solution.py:367
  96.1 6.4 %collective-permute-start.16 = (f32[128,256]{1,0:T(8,128)S(1)}, f32[128,256]{1,0:T(8,128)S(1)}, u32[]{:S(2)}, u32[]{:S(2)}) collective-permute-start(f32[128,256]{1,0:T(8,128)S(1)} %add_add_fusion.1), channel_id=1, source_target_pairs={{0,1},{1,2},{2,3},{3,0},{4,5},{5,6},{6,7},{7,4},{8,9},{9,10},{10,1... | collective-permute-start | bytes 393224 | tf_op jit(solution)/shard_map/ppermute | solution.py:367
  96.1 6.4 %collective-permute-start.15 = (f32[128,256]{1,0:T(8,128)S(1)}, f32[128,256]{1,0:T(8,128)S(1)}, u32[]{:S(2)}, u32[]{:S(2)}) collective-permute-start(f32[128,256]{1,0:T(8,128)S(1)} %add_add_fusion.1), channel_id=1, source_target_pairs={{0,2},{1,3},{2,0},{3,1},{4,6},{5,7},{6,4},{7,5},{8,10},{9,11},{10,... | collective-permute-start | bytes 393224 | tf_op jit(solution)/shard_map/ppermute | solution.py:367
  97.4 21.9 %collective-permute-start.4 = (f32[2,256,512]{2,1,0:T(8,128)S(1)}, f32[2,256,512]{2,1,0:T(8,128)S(1)}, u32[]{:S(2)}, u32[]{:S(2)}) collective-permute-start(f32[2,256,512]{2,1,0:T(8,128)S(1)} %copy-done.8), channel_id=1, source_target_pairs={{0,16},{16,32},{32,48},{48,64},{64,80},{80,96},{96,112},{1,17},{17... | collective-permute-start | bytes 3145736 | tf_op jit(solution)/shard_map/ppermute | solution.py:402
  102.6 7.4 %collective-permute-start.20 = (f32[128,256]{1,0:T(8,128)S(1)}, f32[128,256]{1,0:T(8,128)S(1)}, u32[]{:S(2)}, u32[]{:S(2)}) collective-permute-start(f32[128,256]{1,0:T(8,128)S(1)} %add_add_fusion.x0), channel_id=1, source_target_pairs={{0,12},{4,0},{8,4},{12,8},{1,13},{5,1},{9,5},{13,9},{2,14},{6,2},{... | collective-permute-start | bytes 393224 | tf_op jit(solution)/shard_map/ppermute | solution.py:363
  108.0 5.4 %collective-permute-start.19 = (f32[128,256]{1,0:T(8,128)S(1)}, f32[128,256]{1,0:T(8,128)S(1)}, u32[]{:S(2)}, u32[]{:S(2)}) collective-permute-start(f32[128,256]{1,0:T(8,128)S(1)} %add_add_fusion.x0), channel_id=1, source_target_pairs={{0,8},{4,12},{8,0},{12,4},{1,9},{5,13},{9,1},{13,5},{2,10},{6,14},... | collective-permute-start | bytes 393224 | tf_op jit(solution)/shard_map/ppermute | solution.py:363
  109.2 5.5 %collective-permute-start.18 = (f32[128,256]{1,0:T(8,128)S(1)}, f32[128,256]{1,0:T(8,128)S(1)}, u32[]{:S(2)}, u32[]{:S(2)}) collective-permute-start(f32[128,256]{1,0:T(8,128)S(1)} %add_add_fusion.x0), channel_id=1, source_target_pairs={{0,4},{4,8},{8,12},{12,0},{1,5},{5,9},{9,13},{13,1},{2,6},{6,10},{... | collective-permute-start | bytes 393224 | tf_op jit(solution)/shard_map/ppermute | solution.py:363
  114.7 6.6 %collective-permute-start.21 = (f32[4,128,256]{2,1,0:T(8,128)S(1)}, f32[4,128,256]{2,1,0:T(8,128)S(1)}, u32[]{:S(2)}, u32[]{:S(2)}) collective-permute-start(f32[4,128,256]{2,1,0:T(8,128)S(1)} %pad_maximum_fusion), channel_id=1, source_target_pairs={{0,16},{16,0},{1,17},{17,1},{2,18},{18,2},{3,19},{19,3},{4,20},{20... | collective-permute-start | bytes 1572872 | tf_op jit(solution)/shard_map/ppermute | solution.py:354
  119.3 2.0 %copy-start = (f32[2,2,256,256]{3,2,1,0:T(8,128)S(1)}, f32[2,2,256,256]{3,2,1,0:T(8,128)}, u32[]{:S(2)}) copy-start(f32[2,2,256,256]{3,2,1,0:T(8,128)} %probe.2) | copy-start | bytes 3145732
  119.3 2.0 %copy-start.2 = (s32[4]{0:T(128)S(1)}, s32[4]{0:T(128)}, u32[]{:S(2)}) copy-start(s32[4]{0:T(128)} %pad_add_fusion.anchor.place) | copy-start | bytes 52

commit v5 on v4

--- a/solution.py
+++ b/solution.py
@@ -250,10 +250,8 @@
     copies = [pltpu.make_async_copy(s, d, sems.at[i]) for i, (s, d) in enumerate(outs)]
     for c in copies[:4]:
         c.start()
-    for kc, kx in np.ndindex(2, 4):
-        c, x = lax.rem(anchor[2] + kc, 2), lax.rem(anchor[3] + kx, 4)
-        at = pl.multiple_of(lax.rem(x, 2) * H, H)
-        prv[kc, kx // 2, kx % 2 * H:kx % 2 * H + H, :] = pacc[c, lax.div(x, 2), pl.ds(at, H), :]
+    for kc in range(2):
+        prv[kc] = pacc[lax.rem(anchor[2] + kc, 2)]
     for c in copies[4:6]:
         c.start()
     for c in range(2):
@@ -354,26 +352,15 @@
     return lax.ppermute(value, "core", [(0, 1), (1, 0)])
 
 
-def sum_along(pieces, axis):
-    got = [lax.ppermute(pieces[k], axis, [(i, (i + k) % 4) for i in range(4)]) for k in (2, 1, 3)]
-    return pieces[0] + got[0] + got[1] + got[2]
-
-
-def spread_along(value, axis):
-    return [value] + [lax.ppermute(value, axis, [(i, (i + k) % 4) for i in range(4)]) for k in (1, 2, 3)]
-
-
 def sum_everywhere(value, axis):
     got = [lax.ppermute(value, axis, [(i, (i + k) % 4) for i in range(4)]) for k in (2, 1, 3)]
     return (value + got[0]) + (got[1] + got[2])
 
 
-def probe_kernel(step, place, probe, x0, x1, x2, x3, rest, out):
-    for kc, kx in np.ndindex(2, 4):
-        row = lax.rem(place[2] + kc, 2) * 512 + lax.rem(place[3] - kx + 4, 4) * H
-        at = pl.multiple_of(row, H)
-        total = (x0, x1, x2, x3)[kx][...] if kc == 0 else rest[kx]
-        out[pl.ds(at, H), :] = probe[pl.ds(at, H), :] - step * total
+def probe_kernel(step, place, probe, mine, rest, out):
+    for kc in range(2):
+        at = pl.multiple_of(lax.rem(place[2] + kc, 2) * 512, 512)
+        out[pl.ds(at, 512), :] = probe[pl.ds(at, 512), :] - step * (mine, rest)[kc][...]
 
 
 def shards(object_planes, probe_planes, offsets, photon_counts, live_counts):
@@ -392,7 +379,7 @@
     right_top, roots = lax.optimization_barrier((right_top, roots))
     corner = lax.ppermute(right_top, rows, up)
     place = jnp.stack(
-        [lax.axis_index(rows) * 512, lax.axis_index(cols) * 512] + [lax.axis_index(a) for a in ("core", "x")]
+        [lax.axis_index(rows) * 512, lax.axis_index(cols) * 512] + [lax.axis_index(a) for a in ("core",)]
     ).astype(jnp.int32)
     part, g_top, g_bot, g_corner, g_below, mine, other = main_call(
         offsets, live_counts.reshape(1), place, object_planes, right_top, right_bot, below, corner, probe_planes, roots
@@ -400,26 +387,26 @@
     corner_in = lax.ppermute(g_corner, rows, down)
     bot_in = lax.ppermute(g_bot, cols, to_right)
     above_in = lax.ppermute(g_below, rows, down)
-    half = (mine + swap_cores(other)).reshape(4, H, W)
+    half = (mine + swap_cores(other)).reshape(16, 32, W)
     top_in = lax.ppermute(g_top + corner_in, cols, to_right)
-    piece = sum_along(half, "x")
+    plane = ("y", "x")
+    piece = lax.all_to_all(half, plane, 0, 0).sum(0)
     piece, bot_in = lax.optimization_barrier((piece, bot_in))
-    piece = sum_everywhere(piece, "y")
-    piece, top_in = lax.optimization_barrier((piece, top_in))
     piece = sum_everywhere(piece, "z")
+    piece, top_in, above_in = lax.optimization_barrier((piece, top_in, above_in))
     new_object = finish_call(part, above_in, top_in, bot_in)
-    quarters = spread_along(piece, "x")
-    rest = swap_cores(jnp.stack(quarters))
+    half = lax.all_to_all(jnp.broadcast_to(piece[None], half.shape), plane, 0, 0).reshape(512, W)
+    rest = swap_cores(half)
     smem, vmem = pl.BlockSpec(memory_space=pltpu.SMEM), pl.BlockSpec(memory_space=pltpu.VMEM)
     step = 1.0 / math.sqrt(offsets.shape[0] * n_row * n_col)
     new_probe = pl.pallas_call(
         functools.partial(probe_kernel, step),
         out_shape=jax.ShapeDtypeStruct((1024, W), f32),
-        in_specs=[smem] + [vmem] * 6,
+        in_specs=[smem] + [vmem] * 3,
         out_specs=vmem,
         compiler_params=pltpu.CompilerParams(vmem_limit_bytes=8 * 2**20),
         name="probe",
-    )(place, probe_planes.reshape(1024, W), *quarters, rest)
+    )(place, probe_planes.reshape(1024, W), half, rest)
     return new_object, new_probe.reshape(probe_planes.shape)
 
 

time: 123 us -> 128 us (1.041)
  starting transfers between devices: 60.6 us -> 39.6 us
  blocking collectives: 0 us -> 20.9 us
  Pallas kernels: 32.1 us -> 38.7 us
  waiting for transfers between devices: 23.5 us -> 17.7 us
  other arithmetic: 1.97 us -> 5.85 us
    all_to_all x0 -> x1, blocking collectives: none -> 20.9 us  [shards(): lax.all_to_all(jnp.broadcast_to(piece[None], half.shape), plane, 0, 0)]
    ppermute x6 -> x0, starting transfers between devices: 12.3 us -> none  [the longest x3 7.37 us: spread_along(): lax.ppermute(value, axis, [(i, (i + k) % 4) for i in range(4)])]
    ppermute x6 -> x3, starting transfers between devices: 15.9 us -> 6.75 us  [sum_everywhere(): lax.ppermute(value, axis, [(i, (i + k) % 4) for i in range(4)])]
    ppermute x6 -> x0, waiting for transfers between devices: 7.54 us -> none  [the longest x3 4.72 us: spread_along(): lax.ppermute(value, axis, [(i, (i + k) % 4) for i in range(4)])]
    all_to_all x0 -> x1, starting transfers between devices: none -> 7.05 us  [shards(): piece = lax.all_to_all(half, plane, 0, 0).sum(0)]
    pallas_call x1, Pallas kernels: 21.5 us -> 26.4 us  [main_call(): pl.pallas_call(main_kernel, out_shape=(S(2, 512, 512), S(2, 256, 256), S(...]
    ppermute x1, starting transfers between devices: 9.55 us -> 4.75 us  [shards(): bot_in = lax.ppermute(g_bot, cols, to_right)]
    all_to_all x0 -> x1, waiting for transfers between devices: none -> 4.48 us  [shards(): piece = lax.all_to_all(half, plane, 0, 0).sum(0)]
  transfers between devices with their start and end apart: 22 -> 14, of which waited for: 10 -> 6; matrix products, arithmetic and copies ran while one was open for 2% -> 5% of each run, Pallas kernels for 7% -> 8%
where the time goes in v5:
time: 128 us; the launch traced here: 127 us
  starting transfers between devices  39.6 us (31%)
  Pallas kernels  38.7 us (30%)
  blocking collectives  20.9 us (16%)
  waiting for transfers between devices  17.7 us (14%)
  other arithmetic  5.85 us (5%)
  local copies, waits for them, and re-layouts  3.33 us (3%)
  between operations  1.47 us (1%)
    pallas_call x1, Pallas kernels, main_call(): pl.pallas_call(main_kernel, out_shape=(S(2, 512, 512), S(2, 256, 256), S(...  26.4 us
    all_to_all x1, blocking collectives, shards(): lax.all_to_all(jnp.broadcast_to(piece[None], half.shape), plane, 0, 0)  20.9 us
    all_to_all x1, starting transfers between devices, shards(): piece = lax.all_to_all(half, plane, 0, 0).sum(0)  7.05 us
    pallas_call x1, Pallas kernels, prep_call(): pl.pallas_call(prep_kernel, grid=(8,), out_shape=jax.ShapeDtypeStruct((8,...  6.97 us
    ppermute x3, starting transfers between devices, sum_everywhere(): lax.ppermute(value, axis, [(i, (i + k) % 4) for i in range(4)])  6.75 us
    ppermute x1, waiting for transfers between devices, shards(): right_bot = lax.ppermute(object_planes[:, W:, :W], cols, to_left)  5.35 us
    ppermute x1, starting transfers between devices, shards(): bot_in = lax.ppermute(g_bot, cols, to_right)  4.75 us
    all_to_all x1, waiting for transfers between devices, shards(): piece = lax.all_to_all(half, plane, 0, 0).sum(0)  4.48 us
  transfers between devices with their start and end apart: 14, of which 6 were waited for; matrix products, arithmetic and copies ran while one was open for 5% of the time, Pallas kernels for 8%

profile of v5, /device:TPU:1, one launch (start us, length us, event | category | flops | bytes accessed | tf_op | source)
XLA Modules:
  0.0 127.5 jit_solution(6966295309684241856)
XLA Ops:
  0.6 2.4 %fusion = (f32[2,256,256]{2,1,0:T(8,128)}, f32[2,256,256]{2,1,0:T(8,128)}) fusion(f32[2,512,512]{2,1,0:T(8,128)} %obj.1), kind=kLoop, calls=%fused_computation.2 | loop fusion | bytes 2097152 | tf_op jit(solution)/shard_map/slice | solution.py:377
  3.1 1.3 %collective-permute-start = (f32[2,256,256]{2,1,0:T(8,128)}, f32[2,256,256]{2,1,0:T(8,128)S(1)}, u32[]{:S(2)}, u32[]{:S(2)}) collective-permute-start(f32[2,256,256]{2,1,0:T(8,128)} %get-tuple-element.31), channel_id=1, source_target_pairs={{1,0},{2,1},{3,2},{4,3},{5,4},{6,5},{7,6},{8,7},{9,8},{10,9},{11,1... | collective-permute-start | bytes 1572872 | tf_op jit(solution)/shard_map/ppermute | solution.py:375
  4.4 0.1 slice.11
  4.5 3.3 %collective-permute-start.2 = (f32[2,256,512]{2,1,0:T(8,128)S(1)}, f32[2,256,512]{2,1,0:T(8,128)S(1)}, u32[]{:S(2)}, u32[]{:S(2)}) collective-permute-start(f32[2,256,512]{2,1,0:T(8,128)S(1)} %slice.11), channel_id=1, source_target_pairs={{16,0},{32,16},{48,32},{64,48},{80,64},{96,80},{112,96},{17,1},{33... | collective-permute-start | bytes 3145736 | tf_op jit(solution)/shard_map/ppermute | solution.py:376
  7.8 1.3 %collective-permute-start.1 = (f32[2,256,256]{2,1,0:T(8,128)}, f32[2,256,256]{2,1,0:T(8,128)}, u32[]{:S(2)}, u32[]{:S(2)}) collective-permute-start(f32[2,256,256]{2,1,0:T(8,128)} %get-tuple-element.30), channel_id=1, source_target_pairs={{1,0},{2,1},{3,2},{4,3},{5,4},{6,5},{7,6},{8,7},{9,8},{10,9},{11,1... | collective-permute-start | bytes 1572872 | tf_op jit(solution)/shard_map/ppermute | solution.py:377
  9.1 7.0 %roots.1.sq = f32[8,256,256]{2,1,0:T(8,128)} custom-call(s32[8,256,256]{2,1,0:T(8,128)} %counts.1, bf16[256,256]{1,0:T(8,128)(2,1)} %constant.31.clone.pm, bf16[256,256]{1,0:T(8,128)(2,1)} %constant.32.clone.pmt), custom_call_target="tpu_custom_call" | custom-call | tf_op jit(solution)/shard_map/roots/pallas_call | solution.py:305
  16.1 3.2 %collective-permute-done.right_top = f32[2,256,256]{2,1,0:T(8,128)S(1)} collective-permute-done((f32[2,256,256]{2,1,0:T(8,128)}, f32[2,256,256]{2,1,0:T(8,128)S(1)}, u32[]{:S(2)}, u32[]{:S(2)}) %collective-permute-start) | collective-permute-done | bytes 524320 | tf_op jit(solution)/shard_map/ppermute | solution.py:375
  19.3 4.0 %collective-permute-start.3 = (f32[2,256,256]{2,1,0:T(8,128)S(1)}, f32[2,256,256]{2,1,0:T(8,128)}, u32[]{:S(2)}, u32[]{:S(2)}) collective-permute-start(f32[2,256,256]{2,1,0:T(8,128)S(1)} %collective-permute-done.right_top), channel_id=1, source_target_pairs={{16,0},{32,16},{48,32},{64,48},{80,64},{96,80},{112,96},{17,1},{33... | collective-permute-start | bytes 1572872 | tf_op jit(solution)/shard_map/ppermute | solution.py:380
  23.9 0.7 copy.10.offs
  24.6 0.7 pad_add_fusion.anchor.place
  25.3 5.4 %collective-permute-done.1.right_bot = f32[2,256,256]{2,1,0:T(8,128)} collective-permute-done((f32[2,256,256]{2,1,0:T(8,128)}, f32[2,256,256]{2,1,0:T(8,128)}, u32[]{:S(2)}, u32[]{:S(2)}) %collective-permute-start.1) | collective-permute-done | bytes 524320 | tf_op jit(solution)/shard_map/ppermute | solution.py:377
  30.6 0.9 collective-permute-done.3.corner
  31.5 0.1 copy-done.4
  31.6 26.4 %slots.1 = (f32[2,512,512]{2,1,0:T(8,128)}, f32[2,256,256]{2,1,0:T(8,128)}, f32[2,256,256]{2,1,0:T(8,128)}, f32[2,256,256]{2,1,0:T(8,128)}, f32[2,256,512]{2,1,0...) custom-call(s32[8,2]{1,0:T(8,128)} %copy.10.offs, s32[1]{0:T(128)} %bitcast.8.live, ...), custom_call_target="tpu_custom_call" | custom-call | tf_op jit(solution)/shard_map/slots/pallas_call | solution.py:268
  58.0 1.3 %collective-permute-start.4 = (f32[2,256,256]{2,1,0:T(8,128)}, f32[2,256,256]{2,1,0:T(8,128)S(1)}, u32[]{:S(2)}, u32[]{:S(2)}) collective-permute-start(f32[2,256,256]{2,1,0:T(8,128)} %get-tuple-element.20), channel_id=1, source_target_pairs={{0,16},{16,0},{1,17},{17,1},{2,18},{18,2},{3,19},{19,3},{4,20},{20... | collective-permute-start | bytes 1572872 | tf_op jit(solution)/shard_map/ppermute | solution.py:352
  59.3 1.9 %collective-permute-start.9 = (f32[2,256,256]{2,1,0:T(8,128)}, f32[2,256,256]{2,1,0:T(8,128)}, u32[]{:S(2)}, u32[]{:S(2)}) collective-permute-start(f32[2,256,256]{2,1,0:T(8,128)} %get-tuple-element.24), channel_id=1, source_target_pairs={{0,16},{16,32},{32,48},{48,64},{64,80},{80,96},{96,112},{1,17},{17... | collective-permute-start | bytes 1572872 | tf_op jit(solution)/shard_map/ppermute | solution.py:387
  61.2 1.9 %collective-permute-start.11 = (f32[2,256,512]{2,1,0:T(8,128)}, f32[2,256,512]{2,1,0:T(8,128)S(1)}, u32[]{:S(2)}, u32[]{:S(2)}) collective-permute-start(f32[2,256,512]{2,1,0:T(8,128)} %get-tuple-element.25), channel_id=1, source_target_pairs={{0,16},{16,32},{32,48},{48,64},{64,80},{80,96},{96,112},{1,17},{17... | collective-permute-start | bytes 3145736 | tf_op jit(solution)/shard_map/ppermute | solution.py:389
  63.1 4.7 %collective-permute-start.5 = (f32[2,256,256]{2,1,0:T(8,128)}, f32[2,256,256]{2,1,0:T(8,128)}, u32[]{:S(2)}, u32[]{:S(2)}) collective-permute-start(f32[2,256,256]{2,1,0:T(8,128)} %get-tuple-element.21), channel_id=1, source_target_pairs={{0,1},{1,2},{2,3},{3,4},{4,5},{5,6},{6,7},{7,8},{8,9},{9,10},{10,1... | collective-permute-start | bytes 1572872 | tf_op jit(solution)/shard_map/ppermute | solution.py:388
  67.9 1.9 %add.23 = f32[2,256,256]{2,1,0:T(8,128)} add(f32[2,256,256]{2,1,0:T(8,128)} %get-tuple-element.19, f32[2,256,256]{2,1,0:T(8,128)S(1)} %collective-permute-done.4) | non-fusion elementwise | flops 131072 | bytes 1572864 | tf_op jit(solution)/shard_map/add | solution.py:390
  69.8 7.1 %all-to-all-start = ((f32[16,32,256]{2,1,0:T(8,128)}), f32[16,32,256]{2,1,0:T(8,128)}, u32[]{:S(2)}, u32[]{:S(2)}) async-start(f32[16,32,256]{2,1,0:T(8,128)} %bitcast.4), calls=%async_computation | async-start | bytes 1048576 | tf_op jit(solution)/shard_map/all_to_all | solution.py:393
  76.8 2.2 %add.27 = f32[2,256,256]{2,1,0:T(8,128)} add(f32[2,256,256]{2,1,0:T(8,128)} %get-tuple-element.23, f32[2,256,256]{2,1,0:T(8,128)} %collective-permute-done.9) | non-fusion elementwise | flops 131072 | bytes 1572864 | tf_op jit(solution)/shard_map/add | solution.py:391
  79.0 4.1 %collective-permute-start.10 = (f32[2,256,256]{2,1,0:T(8,128)}, f32[2,256,256]{2,1,0:T(8,128)}, u32[]{:S(2)}, u32[]{:S(2)}) collective-permute-start(f32[2,256,256]{2,1,0:T(8,128)} %add.27), channel_id=1, source_target_pairs={{0,1},{1,2},{2,3},{3,4},{4,5},{5,6},{6,7},{7,8},{8,9},{9,10},{10,1... | collective-permute-start | bytes 1572872 | tf_op jit(solution)/shard_map/ppermute | solution.py:391
  83.2 4.5 %all-to-all-done = f32[16,32,256]{2,1,0:T(8,128)} async-done(((f32[16,32,256]{2,1,0:T(8,128)}), f32[16,32,256]{2,1,0:T(8,128)}, u32[]{:S(2)}, u32[]{:S(2)}) %all-to-all-start) | async-done | bytes 524320 | tf_op jit(solution)/shard_map/all_to_all | solution.py:393
  87.7 1.1 reduce_sum.9
  88.8 4.6 %collective-permute-start.8 = (f32[32,256]{1,0:T(8,128)S(1)}, f32[32,256]{1,0:T(8,128)S(1)}, u32[]{:S(2)}, u32[]{:S(2)}) collective-permute-start(f32[32,256]{1,0:T(8,128)S(1)} %reduce_sum.9), channel_id=1, source_target_pairs={{0,3},{1,0},{2,1},{3,2},{4,7},{5,4},{6,5},{7,6},{8,11},{9,8},{10,9... | collective-permute-start | bytes 98312 | tf_op jit(solution)/shard_map/ppermute | solution.py:356
  93.4 2.1 %collective-permute-start.6 = (f32[32,256]{1,0:T(8,128)S(1)}, f32[32,256]{1,0:T(8,128)S(1)}, u32[]{:S(2)}, u32[]{:S(2)}) collective-permute-start(f32[32,256]{1,0:T(8,128)S(1)} %reduce_sum.9), channel_id=1, source_target_pairs={{0,2},{1,3},{2,0},{3,1},{4,6},{5,7},{6,4},{7,5},{8,10},{9,11},{10,... | collective-permute-start | bytes 98312 | tf_op jit(solution)/shard_map/ppermute | solution.py:356
  95.5 1.8 %collective-permute-done.7 = f32[32,256]{1,0:T(8,128)S(1)} collective-permute-done((f32[32,256]{1,0:T(8,128)S(1)}, f32[32,256]{1,0:T(8,128)S(1)}, u32[]{:S(2)}, u32[]{:S(2)}) %collective-permute-start.7) | collective-permute-done | bytes 32800 | tf_op jit(solution)/shard_map/ppermute | solution.py:356
  97.4 1.9 %collective-permute-done.6 = f32[32,256]{1,0:T(8,128)S(1)} collective-permute-done((f32[32,256]{1,0:T(8,128)S(1)}, f32[32,256]{1,0:T(8,128)S(1)}, u32[]{:S(2)}, u32[]{:S(2)}) %collective-permute-start.6) | collective-permute-done | bytes 32800 | tf_op jit(solution)/shard_map/ppermute | solution.py:356
  99.3 20.9 %all_to_all.10 = f32[16,32,256]{2,1,0:T(8,128)S(1)} all-to-all(f32[16,32,256]{2,1,0:T(8,128)S(1)} %broadcast_in_dim.2), channel_id=1, replica_groups=mesh['y'=4,'core'=2,'x'=4,'z'=4] {'y','x'}, dimensions={0} | all-to-all | bytes 1048576 | tf_op jit(solution)/shard_map/all_to_all | solution.py:398
  120.2 1.9 %collective-permute-start.12 = (f32[512,256]{1,0:T(8,128)S(1)}, f32[512,256]{1,0:T(8,128)S(1)}, u32[]{:S(2)}, u32[]{:S(2)}) collective-permute-start(f32[512,256]{1,0:T(8,128)S(1)} %bitcast.10), channel_id=1, source_target_pairs={{0,16},{16,0},{1,17},{17,1},{2,18},{18,2},{3,19},{19,3},{4,20},{20... | collective-permute-start | bytes 1572872 | tf_op jit(solution)/shard_map/ppermute | solution.py:352
  122.1 3.7 %finish.1 = f32[2,512,512]{2,1,0:T(8,128)} custom-call(f32[2,512,512]{2,1,0:T(8,128)S(1)} %copy-done.1, f32[2,256,512]{2,1,0:T(8,128)S(1)} %collective-permute-done.11.above, f32[2,256,256]{2,1,0:T(8,128)} %collective-permute-done.10.top, f32[2,256,256]{2,1,0:T(8,128)} %collective-permute-done.5.bot), custom_call_target="tpu_custom_call" | custom-call | tf_op jit(solution)/shard_map/finish/pallas_call | solution.py:335
  125.8 1.6 %probe.3 = f32[1024,256]{1,0:T(8,128)} custom-call(s32[3]{0:T(128)S(1)} %copy-done.2, f32[1024,256]{1,0:T(8,128)S(1)} %bitcast.9, f32[512,256]{1,0:T(8,128)S(1)} %bitcast.11, f32[512,256]{1,0:T(8,128)S(1)} %collective-permute-done.12.rest), custom_call_target="tpu_custom_call" | custom-call | tf_op jit(solution)/shard_map/probe/pallas_call | solution.py:402
  (24 shorter events, 0.1 us)
Async XLA Ops:
  0.6 3.7 %copy-start.3 = (f32[2,512,512]{2,1,0:T(8,128)S(1)}, f32[2,512,512]{2,1,0:T(8,128)}, u32[]{:S(2)}) copy-start(f32[2,512,512]{2,1,0:T(8,128)} %obj.1) | copy-start | bytes 6291460
  3.1 16.2 %collective-permute-start = (f32[2,256,256]{2,1,0:T(8,128)}, f32[2,256,256]{2,1,0:T(8,128)S(1)}, u32[]{:S(2)}, u32[]{:S(2)}) collective-permute-start(f32[2,256,256]{2,1,0:T(8,128)} %get-tuple-element.31), channel_id=1, source_target_pairs={{1,0},{2,1},{3,2},{4,3},{5,4},{6,5},{7,6},{8,7},{9,8},{10,9},{11,1... | collective-permute-start | bytes 1572872 | tf_op jit(solution)/shard_map/ppermute | solution.py:375
  4.5 26.2 %collective-permute-start.2 = (f32[2,256,512]{2,1,0:T(8,128)S(1)}, f32[2,256,512]{2,1,0:T(8,128)S(1)}, u32[]{:S(2)}, u32[]{:S(2)}) collective-permute-start(f32[2,256,512]{2,1,0:T(8,128)S(1)} %slice.11), channel_id=1, source_target_pairs={{16,0},{32,16},{48,32},{64,48},{80,64},{96,80},{112,96},{17,1},{33... | collective-permute-start | bytes 3145736 | tf_op jit(solution)/shard_map/ppermute | solution.py:376
  7.8 16.1 %copy-start.6 = (s32[8,2]{0,1:T(2,128)S(1)}, s32[8,2]{0,1:T(2,128)}, u32[]{:S(2)}) copy-start(s32[8,2]{0,1:T(2,128)} %param.10) | copy-start | bytes 196
  7.8 22.8 %collective-permute-start.1 = (f32[2,256,256]{2,1,0:T(8,128)}, f32[2,256,256]{2,1,0:T(8,128)}, u32[]{:S(2)}, u32[]{:S(2)}) collective-permute-start(f32[2,256,256]{2,1,0:T(8,128)} %get-tuple-element.30), channel_id=1, source_target_pairs={{1,0},{2,1},{3,2},{4,3},{5,4},{6,5},{7,6},{8,7},{9,8},{10,9},{11,1... | collective-permute-start | bytes 1572872 | tf_op jit(solution)/shard_map/ppermute | solution.py:377
  19.3 12.2 %copy-start.5 = (f32[2,256,256]{2,1,0:T(8,128)}, f32[2,256,256]{2,1,0:T(8,128)S(1)}, u32[]{:S(2)}) copy-start(f32[2,256,256]{2,1,0:T(8,128)S(1)} %collective-permute-done.right_top) | copy-start | bytes 1572868
  19.3 12.2 %collective-permute-start.3 = (f32[2,256,256]{2,1,0:T(8,128)S(1)}, f32[2,256,256]{2,1,0:T(8,128)}, u32[]{:S(2)}, u32[]{:S(2)}) collective-permute-start(f32[2,256,256]{2,1,0:T(8,128)S(1)} %collective-permute-done.right_top), channel_id=1, source_target_pairs={{16,0},{32,16},{48,32},{64,48},{80,64},{96,80},{112,96},{17,1},{33... | collective-permute-start | bytes 1572872 | tf_op jit(solution)/shard_map/ppermute | solution.py:380
  30.6 1.0 copy-start.4
  58.0 9.9 %collective-permute-start.4 = (f32[2,256,256]{2,1,0:T(8,128)}, f32[2,256,256]{2,1,0:T(8,128)S(1)}, u32[]{:S(2)}, u32[]{:S(2)}) collective-permute-start(f32[2,256,256]{2,1,0:T(8,128)} %get-tuple-element.20), channel_id=1, source_target_pairs={{0,16},{16,0},{1,17},{17,1},{2,18},{18,2},{3,19},{19,3},{4,20},{20... | collective-permute-start | bytes 1572872 | tf_op jit(solution)/shard_map/ppermute | solution.py:352
  59.3 17.6 %collective-permute-start.9 = (f32[2,256,256]{2,1,0:T(8,128)}, f32[2,256,256]{2,1,0:T(8,128)}, u32[]{:S(2)}, u32[]{:S(2)}) collective-permute-start(f32[2,256,256]{2,1,0:T(8,128)} %get-tuple-element.24), channel_id=1, source_target_pairs={{0,16},{16,32},{32,48},{48,64},{64,80},{80,96},{96,112},{1,17},{17... | collective-permute-start | bytes 1572872 | tf_op jit(solution)/shard_map/ppermute | solution.py:387
  61.2 38.1 %collective-permute-start.11 = (f32[2,256,512]{2,1,0:T(8,128)}, f32[2,256,512]{2,1,0:T(8,128)S(1)}, u32[]{:S(2)}, u32[]{:S(2)}) collective-permute-start(f32[2,256,512]{2,1,0:T(8,128)} %get-tuple-element.25), channel_id=1, source_target_pairs={{0,16},{16,32},{32,48},{48,64},{64,80},{80,96},{96,112},{1,17},{17... | collective-permute-start | bytes 3145736 | tf_op jit(solution)/shard_map/ppermute | solution.py:389
  63.1 25.6 %collective-permute-start.5 = (f32[2,256,256]{2,1,0:T(8,128)}, f32[2,256,256]{2,1,0:T(8,128)}, u32[]{:S(2)}, u32[]{:S(2)}) collective-permute-start(f32[2,256,256]{2,1,0:T(8,128)} %get-tuple-element.21), channel_id=1, source_target_pairs={{0,1},{1,2},{2,3},{3,4},{4,5},{5,6},{6,7},{7,8},{8,9},{9,10},{10,1... | collective-permute-start | bytes 1572872 | tf_op jit(solution)/shard_map/ppermute | solution.py:388
  69.8 17.9 %all-to-all-start = ((f32[16,32,256]{2,1,0:T(8,128)}), f32[16,32,256]{2,1,0:T(8,128)}, u32[]{:S(2)}, u32[]{:S(2)}) async-start(f32[16,32,256]{2,1,0:T(8,128)} %bitcast.4), calls=%async_computation | async-start | bytes 1048576 | tf_op jit(solution)/shard_map/all_to_all | solution.py:393
  76.8 45.3 %copy-start.1 = (f32[2,512,512]{2,1,0:T(8,128)S(1)}, f32[2,512,512]{2,1,0:T(8,128)}, u32[]{:S(2)}) copy-start(f32[2,512,512]{2,1,0:T(8,128)} %get-tuple-element.18.part) | copy-start | bytes 6291460
  79.0 20.2 %collective-permute-start.10 = (f32[2,256,256]{2,1,0:T(8,128)}, f32[2,256,256]{2,1,0:T(8,128)}, u32[]{:S(2)}, u32[]{:S(2)}) collective-permute-start(f32[2,256,256]{2,1,0:T(8,128)} %add.27), channel_id=1, source_target_pairs={{0,1},{1,2},{2,3},{3,4},{4,5},{5,6},{6,7},{7,8},{8,9},{9,10},{10,1... | collective-permute-start | bytes 1572872 | tf_op jit(solution)/shard_map/ppermute | solution.py:391
  88.8 6.7 %collective-permute-start.8 = (f32[32,256]{1,0:T(8,128)S(1)}, f32[32,256]{1,0:T(8,128)S(1)}, u32[]{:S(2)}, u32[]{:S(2)}) collective-permute-start(f32[32,256]{1,0:T(8,128)S(1)} %reduce_sum.9), channel_id=1, source_target_pairs={{0,3},{1,0},{2,1},{3,2},{4,7},{5,4},{6,5},{7,6},{8,11},{9,8},{10,9... | collective-permute-start | bytes 98312 | tf_op jit(solution)/shard_map/ppermute | solution.py:356
  93.4 4.0 %collective-permute-start.7 = (f32[32,256]{1,0:T(8,128)S(1)}, f32[32,256]{1,0:T(8,128)S(1)}, u32[]{:S(2)}, u32[]{:S(2)}) collective-permute-start(f32[32,256]{1,0:T(8,128)S(1)} %reduce_sum.9), channel_id=1, source_target_pairs={{0,1},{1,2},{2,3},{3,0},{4,5},{5,6},{6,7},{7,4},{8,9},{9,10},{10,1... | collective-permute-start | bytes 98312 | tf_op jit(solution)/shard_map/ppermute | solution.py:356
  93.4 5.8 %collective-permute-start.6 = (f32[32,256]{1,0:T(8,128)S(1)}, f32[32,256]{1,0:T(8,128)S(1)}, u32[]{:S(2)}, u32[]{:S(2)}) collective-permute-start(f32[32,256]{1,0:T(8,128)S(1)} %reduce_sum.9), channel_id=1, source_target_pairs={{0,2},{1,3},{2,0},{3,1},{4,6},{5,7},{6,4},{7,5},{8,10},{9,11},{10,... | collective-permute-start | bytes 98312 | tf_op jit(solution)/shard_map/ppermute | solution.py:356
  120.2 5.7 %collective-permute-start.12 = (f32[512,256]{1,0:T(8,128)S(1)}, f32[512,256]{1,0:T(8,128)S(1)}, u32[]{:S(2)}, u32[]{:S(2)}) collective-permute-start(f32[512,256]{1,0:T(8,128)S(1)} %bitcast.10), channel_id=1, source_target_pairs={{0,16},{16,0},{1,17},{17,1},{2,18},{18,2},{3,19},{19,3},{4,20},{20... | collective-permute-start | bytes 1572872 | tf_op jit(solution)/shard_map/ppermute | solution.py:352
  122.1 3.7 %copy-start = (f32[2,2,256,256]{3,2,1,0:T(8,128)S(1)}, f32[2,2,256,256]{3,2,1,0:T(8,128)}, u32[]{:S(2)}) copy-start(f32[2,2,256,256]{3,2,1,0:T(8,128)} %probe.2) | copy-start | bytes 3145732
  122.1 3.7 %copy-start.2 = (s32[3]{0:T(128)S(1)}, s32[3]{0:T(128)}, u32[]{:S(2)}) copy-start(s32[3]{0:T(128)} %pad_add_fusion.anchor.place) | copy-start | bytes 40

commit v6 on v5

--- a/solution.py
+++ b/solution.py
@@ -62,7 +62,7 @@
 
 
 def main_kernel(offs, live, anchor, obj, right_top, right_bot, below, corner, probe, sq, tables,
-                o_part, o_rtop, o_rbot, o_corner, o_below, o_mine, o_other,
+                o_part, o_rtop, o_rbot, o_below, o_mine, o_other,
                 cov, acc, patch, pacc, prv, sqv, tb, gs, hs, ds, term, sems, sqsems):
     ins = [
         (obj, cov.at[:, 0:512, 0:512]),
@@ -238,25 +238,24 @@
 
     lax.fori_loop(pairs * NB, 8, skip, 0)
     outs = [
-        (acc.at[:, 512:768, 512:768], o_corner),
         (acc.at[:, 256:512, 512:768], o_rbot),
         (acc.at[:, 0:256, 512:768], o_rtop),
-        (acc.at[:, 512:768, 0:512], o_below),
+        (acc.at[:, 512:768, :], o_below),
         (prv.at[1], o_other),
         (prv.at[0], o_mine),
         (cov.at[0, 0:512, 0:512], o_part.at[0]),
         (cov.at[1, 0:512, 0:512], o_part.at[1]),
     ]
     copies = [pltpu.make_async_copy(s, d, sems.at[i]) for i, (s, d) in enumerate(outs)]
-    for c in copies[:4]:
+    for c in copies[:3]:
         c.start()
     for kc in range(2):
         prv[kc] = pacc[lax.rem(anchor[2] + kc, 2)]
-    for c in copies[4:6]:
+    for c in copies[3:5]:
         c.start()
     for c in range(2):
         cov[c, 0:512, 0:512] = cov[c, 0:512, 0:512] - 0.5 * acc[c, 0:512, 0:512]
-        copies[6 + c].start()
+        copies[5 + c].start()
     for c in copies:
         c.wait()
 
@@ -267,9 +266,9 @@
     S = lambda *s: jax.ShapeDtypeStruct(s, f32)
     return pl.pallas_call(
         main_kernel,
-        out_shape=(S(2, 512, 512), S(2, 256, 256), S(2, 256, 256), S(2, 256, 256), S(2, 256, 512), S(2, 256, 256), S(2, 256, 256)),
+        out_shape=(S(2, 512, 512), S(2, 256, 256), S(2, 256, 256), S(2, 256, 768), S(2, 256, 256), S(2, 256, 256)),
         in_specs=[smem] * 3 + [any_] * 8,
-        out_specs=[any_] * 7,
+        out_specs=[any_] * 6,
         scratch_shapes=[
             pltpu.VMEM((2, 768, 768), f32),
             pltpu.VMEM((2, 768, 768), f32),
@@ -372,23 +371,24 @@
     to_left = [(i, i - 1) for i in range(1, n_col)]
     to_right = [(i - 1, i) for i in range(1, n_col)]
 
-    right_top = lax.ppermute(object_planes[:, :W, :W], cols, to_left)
-    below = lax.ppermute(object_planes[:, :W, :], rows, up)
-    right_bot = lax.ppermute(object_planes[:, W:, :W], cols, to_left)
+    edge = object_planes[:, :W, :W]
+    edge, whole = lax.optimization_barrier((edge, object_planes))
+    right_top = lax.ppermute(edge, cols, to_left)
+    below = lax.ppermute(whole[:, :W, :], rows, up)
+    right_bot = lax.ppermute(whole[:, W:, :W], cols, to_left)
     roots = prep_call(photon_counts)
     right_top, roots = lax.optimization_barrier((right_top, roots))
     corner = lax.ppermute(right_top, rows, up)
     place = jnp.stack(
         [lax.axis_index(rows) * 512, lax.axis_index(cols) * 512] + [lax.axis_index(a) for a in ("core",)]
     ).astype(jnp.int32)
-    part, g_top, g_bot, g_corner, g_below, mine, other = main_call(
+    part, g_top, g_bot, g_below, mine, other = main_call(
         offsets, live_counts.reshape(1), place, object_planes, right_top, right_bot, below, corner, probe_planes, roots
     )
-    corner_in = lax.ppermute(g_corner, rows, down)
     bot_in = lax.ppermute(g_bot, cols, to_right)
     above_in = lax.ppermute(g_below, rows, down)
     half = (mine + swap_cores(other)).reshape(16, 32, W)
-    top_in = lax.ppermute(g_top + corner_in, cols, to_right)
+    top_in = lax.ppermute(g_top + above_in[:, :, 512:], cols, to_right)
     plane = ("y", "x")
     piece = lax.all_to_all(half, plane, 0, 0).sum(0)
     piece, bot_in = lax.optimization_barrier((piece, bot_in))
@@ -396,6 +396,7 @@
     piece, top_in, above_in = lax.optimization_barrier((piece, top_in, above_in))
     new_object = finish_call(part, above_in, top_in, bot_in)
     half = lax.all_to_all(jnp.broadcast_to(piece[None], half.shape), plane, 0, 0).reshape(512, W)
+    half, new_object = lax.optimization_barrier((half, new_object))
     rest = swap_cores(half)
     smem, vmem = pl.BlockSpec(memory_space=pltpu.SMEM), pl.BlockSpec(memory_space=pltpu.VMEM)
     step = 1.0 / math.sqrt(offsets.shape[0] * n_row * n_col)

time: 128 us -> 130 us (1.016)
  starting transfers between devices: 39.6 us -> 68.9 us
  blocking collectives: 20.9 us -> 0 us
  Pallas kernels: 38.7 us -> 27.2 us
  local copies, waits for them, and re-layouts: 3.33 us -> 10.5 us
  other arithmetic: 5.85 us -> 3.46 us
    all_to_all x1 -> x0, blocking collectives: 20.9 us -> none  [shards(): lax.all_to_all(jnp.broadcast_to(piece[None], half.shape), plane, 0, 0)]
    all_to_all x0 -> x1, starting transfers between devices: none -> 14.1 us  [shards(): lax.all_to_all(jnp.broadcast_to(piece[None], half.shape), plane, 0, 0)]
    pallas_call x1, Pallas kernels: 26.4 us -> 16.6 us  [main_call(): pl.pallas_call(main_kernel, out_shape=(S(2, 512, 512), S(2, 256, 256), S(...]
    ppermute x1, starting transfers between devices: 1.92 us -> 9.36 us  [shards(): above_in = lax.ppermute(g_below, rows, down)]
    ppermute x5 -> x4, starting transfers between devices: 11.9 us -> 17.7 us  [the longest x1 11.7 us: shards(): top_in = lax.ppermute(g_top + above_in[:, :, 512:], cols, to_right)]
    all_to_all x0 -> x1, waiting for transfers between devices: none -> 4.88 us  [shards(): lax.all_to_all(jnp.broadcast_to(piece[None], half.shape), plane, 0, 0)]
    all_to_all x1, waiting for transfers between devices: 4.48 us -> 0.01 us  [shards(): piece = lax.all_to_all(half, plane, 0, 0).sum(0)]
    ppermute x1, starting transfers between devices: 4.75 us -> 8.43 us  [shards(): bot_in = lax.ppermute(g_bot, cols, to_right)]
  transfers between devices with their start and end apart: 14 -> 14, of which waited for: 6 -> 6; matrix products, arithmetic and copies ran while one was open for 5% -> 6% of each run, Pallas kernels for 8% -> 7%
where the time goes in v6:
time: 130 us; the launch traced here: 129 us
  starting transfers between devices  68.9 us (53%)
  Pallas kernels  27.2 us (21%)
  waiting for transfers between devices  17.9 us (14%)
  local copies, waits for them, and re-layouts  10.5 us (8%)
  other arithmetic  3.46 us (3%)
  between operations  1.51 us (1%)
    pallas_call x1, Pallas kernels, main_call(): pl.pallas_call(main_kernel, out_shape=(S(2, 512, 512), S(2, 256, 256), S(...  16.6 us
    all_to_all x1, starting transfers between devices, shards(): lax.all_to_all(jnp.broadcast_to(piece[None], half.shape), plane, 0, 0)  14.1 us
    ppermute x1, starting transfers between devices, shards(): top_in = lax.ppermute(g_top + above_in[:, :, 512:], cols, to_right)  11.7 us
    ppermute x1, starting transfers between devices, shards(): above_in = lax.ppermute(g_below, rows, down)  9.36 us
    all_to_all x1, starting transfers between devices, shards(): piece = lax.all_to_all(half, plane, 0, 0).sum(0)  8.85 us
    ppermute x1, starting transfers between devices, shards(): bot_in = lax.ppermute(g_bot, cols, to_right)  8.43 us
    pallas_call x1, Pallas kernels, prep_call(): pl.pallas_call(prep_kernel, grid=(8,), out_shape=jax.ShapeDtypeStruct((8,...  6.97 us
    ppermute x1, waiting for transfers between devices, shards(): right_bot = lax.ppermute(whole[:, W:, :W], cols, to_left)  5.35 us
  transfers between devices with their start and end apart: 14, of which 6 were waited for; matrix products, arithmetic and copies ran while one was open for 6% of the time, Pallas kernels for 7%

profile of v6, /device:TPU:1, one launch (start us, length us, event | category | flops | bytes accessed | tf_op | source)
XLA Modules:
  0.0 129.5 jit_solution(1634587127513371533)
XLA Ops:
  0.6 1.9 %slice.12 = f32[2,256,256]{2,1,0:T(8,128)} slice(f32[2,512,512]{2,1,0:T(8,128)} %obj.1), slice={[0:2], [0:256], [0:256]} | slice | bytes 1048576 | tf_op jit(solution)/shard_map/slice | solution.py:374
  2.5 1.3 collective-permute-start
  3.8 1.3 %slice.14 = f32[2,256,512]{2,1,0:T(8,128)S(1)} slice(f32[2,512,512]{2,1,0:T(8,128)} %obj.1), slice={[0:2], [0:256], [0:512]} | slice | bytes 2097152 | tf_op jit(solution)/shard_map/slice | solution.py:377
  5.1 3.3 %collective-permute-start.2 = (f32[2,256,512]{2,1,0:T(8,128)S(1)}, f32[2,256,512]{2,1,0:T(8,128)S(1)}, u32[]{:S(2)}, u32[]{:S(2)}) collective-permute-start(f32[2,256,512]{2,1,0:T(8,128)S(1)} %slice.14), channel_id=1, source_target_pairs={{16,0},{32,16},{48,32},{64,48},{80,64},{96,80},{112,96},{17,1},{33... | collective-permute-start | bytes 3145736 | tf_op jit(solution)/shard_map/ppermute | solution.py:377
  8.4 1.9 %slice.13 = f32[2,256,256]{2,1,0:T(8,128)} slice(f32[2,512,512]{2,1,0:T(8,128)} %obj.1), slice={[0:2], [256:512], [0:256]} | slice | bytes 1048576 | tf_op jit(solution)/shard_map/slice | solution.py:378
  10.3 1.4 %collective-permute-start.1 = (f32[2,256,256]{2,1,0:T(8,128)}, f32[2,256,256]{2,1,0:T(8,128)}, u32[]{:S(2)}, u32[]{:S(2)}) collective-permute-start(f32[2,256,256]{2,1,0:T(8,128)} %slice.13), channel_id=1, source_target_pairs={{1,0},{2,1},{3,2},{4,3},{5,4},{6,5},{7,6},{8,7},{9,8},{10,9},{11,1... | collective-permute-start | bytes 1572872 | tf_op jit(solution)/shard_map/ppermute | solution.py:378
  11.8 7.0 %roots.1.sq = f32[8,256,256]{2,1,0:T(8,128)} custom-call(s32[8,256,256]{2,1,0:T(8,128)} %counts.1, bf16[256,256]{1,0:T(8,128)(2,1)} %constant.31.clone.pm, bf16[256,256]{1,0:T(8,128)(2,1)} %constant.32.clone.pmt), custom_call_target="tpu_custom_call" | custom-call | tf_op jit(solution)/shard_map/roots/pallas_call | solution.py:304
  18.7 4.0 %collective-permute-start.3 = (f32[2,256,256]{2,1,0:T(8,128)S(1)}, f32[2,256,256]{2,1,0:T(8,128)}, u32[]{:S(2)}, u32[]{:S(2)}) collective-permute-start(f32[2,256,256]{2,1,0:T(8,128)S(1)} %collective-permute-done.right_top), channel_id=1, source_target_pairs={{16,0},{32,16},{48,32},{64,48},{80,64},{96,80},{112,96},{17,1},{33... | collective-permute-start | bytes 1572872 | tf_op jit(solution)/shard_map/ppermute | solution.py:381
  23.4 0.7 copy.10.offs
  24.7 5.3 %collective-permute-done.1.right_bot = f32[2,256,256]{2,1,0:T(8,128)} collective-permute-done((f32[2,256,256]{2,1,0:T(8,128)}, f32[2,256,256]{2,1,0:T(8,128)}, u32[]{:S(2)}, u32[]{:S(2)}) %collective-permute-start.1) | collective-permute-done | bytes 524320 | tf_op jit(solution)/shard_map/ppermute | solution.py:378
  30.1 0.9 collective-permute-done.3.corner
  31.0 16.6 %slots.1 = (f32[2,512,512]{2,1,0:T(8,128)}, f32[2,256,256]{2,1,0:T(8,128)}, f32[2,256,256]{2,1,0:T(8,128)}, f32[2,256,768]{2,1,0:T(8,128)}, f32[2,256,256]{2,1,0:T(8,128)}, /*index=5*/f32[2,256,256]{2,1,0:T(8,128)}) custom-call(s32[8,2]{1,0:T(8,128)} %copy.10.offs, s32[1]{0:T(128)} %bitcast.8.live, s32[3]{0:T(128)} %pad_add_fusion.anchor.place, ...), custom_call_target="tpu_custom_call" | custom-call | tf_op jit(solution)/shard_map/slots/pallas_call | solution.py:267
  47.7 9.4 %collective-permute-start.9 = (f32[2,256,768]{2,1,0:T(8,128)}, f32[2,256,768]{2,1,0:T(8,128)S(1)}, u32[]{:S(2)}, u32[]{:S(2)}) collective-permute-start(f32[2,256,768]{2,1,0:T(8,128)} %get-tuple-element.28), channel_id=1, source_target_pairs={{0,16},{16,32},{32,48},{48,64},{64,80},{80,96},{96,112},{1,17},{17... | collective-permute-start | bytes 4718600 | tf_op jit(solution)/shard_map/ppermute | solution.py:389
  57.1 8.4 %collective-permute-start.5 = (f32[2,256,256]{2,1,0:T(8,128)}, f32[2,256,256]{2,1,0:T(8,128)S(1)}, u32[]{:S(2)}, u32[]{:S(2)}) collective-permute-start(f32[2,256,256]{2,1,0:T(8,128)} %get-tuple-element.25), channel_id=1, source_target_pairs={{0,1},{1,2},{2,3},{3,4},{4,5},{5,6},{6,7},{7,8},{8,9},{9,10},{10,1... | collective-permute-start | bytes 1572872 | tf_op jit(solution)/shard_map/ppermute | solution.py:388
  65.6 1.9 %add.23 = f32[2,256,256]{2,1,0:T(8,128)} add(f32[2,256,256]{2,1,0:T(8,128)} %get-tuple-element.23, f32[2,256,256]{2,1,0:T(8,128)S(1)} %collective-permute-done.4) | non-fusion elementwise | flops 131072 | bytes 1572864 | tf_op jit(solution)/shard_map/add | solution.py:390
  67.5 8.8 %all-to-all-start = ((f32[16,32,256]{2,1,0:T(8,128)}), f32[16,32,256]{2,1,0:T(8,128)S(1)}, u32[]{:S(2)}, u32[]{:S(2)}) async-start(f32[16,32,256]{2,1,0:T(8,128)} %bitcast.4), calls=%async_computation | async-start | bytes 1048576 | tf_op jit(solution)/shard_map/all_to_all | solution.py:393
  76.3 0.9 slice_add_fusion
  77.2 11.7 %collective-permute-start.10 = (f32[2,256,256]{2,1,0:T(8,128)}, f32[2,256,256]{2,1,0:T(8,128)S(1)}, u32[]{:S(2)}, u32[]{:S(2)}) collective-permute-start(f32[2,256,256]{2,1,0:T(8,128)} %slice_add_fusion), channel_id=1, source_target_pairs={{0,1},{1,2},{2,3},{3,4},{4,5},{5,6},{6,7},{7,8},{8,9},{9,10},{10,1... | collective-permute-start | bytes 1572872 | tf_op jit(solution)/shard_map/ppermute | solution.py:391
  89.0 3.3 %collective-permute-start.8 = (f32[32,256]{1,0:T(8,128)S(1)}, f32[32,256]{1,0:T(8,128)S(1)}, u32[]{:S(2)}, u32[]{:S(2)}) collective-permute-start(f32[32,256]{1,0:T(8,128)S(1)} %reduce_sum.9), channel_id=1, source_target_pairs={{0,3},{1,0},{2,1},{3,2},{4,7},{5,4},{6,5},{7,6},{8,11},{9,8},{10,9... | collective-permute-start | bytes 98312 | tf_op jit(solution)/shard_map/ppermute | solution.py:355
  92.3 1.3 collective-permute-start.6
  93.5 3.2 %collective-permute-done.7 = f32[32,256]{1,0:T(8,128)S(1)} collective-permute-done((f32[32,256]{1,0:T(8,128)S(1)}, f32[32,256]{1,0:T(8,128)S(1)}, u32[]{:S(2)}, u32[]{:S(2)}) %collective-permute-start.7) | collective-permute-done | bytes 32800 | tf_op jit(solution)/shard_map/ppermute | solution.py:355
  96.8 2.0 %collective-permute-done.6 = f32[32,256]{1,0:T(8,128)S(1)} collective-permute-done((f32[32,256]{1,0:T(8,128)S(1)}, f32[32,256]{1,0:T(8,128)S(1)}, u32[]{:S(2)}, u32[]{:S(2)}) %collective-permute-start.6) | collective-permute-done | bytes 32800 | tf_op jit(solution)/shard_map/ppermute | solution.py:355
  98.8 0.9 broadcast_in_dim.2
  99.7 14.1 %all-to-all-start.1 = ((f32[16,32,256]{2,1,0:T(8,128)}), f32[16,32,256]{2,1,0:T(8,128)S(1)}, u32[]{:S(2)}, u32[]{:S(2)}) async-start(f32[16,32,256]{2,1,0:T(8,128)} %broadcast_in_dim.2), calls=%async_computation.1 | async-start | bytes 1048576 | tf_op jit(solution)/shard_map/all_to_all | solution.py:398
  113.9 1.6 %copy-done.1 = f32[2,512,512]{2,1,0:T(8,128)S(1)} copy-done((f32[2,512,512]{2,1,0:T(8,128)S(1)}, f32[2,512,512]{2,1,0:T(8,128)}, u32[]{:S(2)}) %copy-start.1) | copy-done | bytes 2097176
  115.4 1.0 copy-done.3
  116.5 1.0 copy-done.5
  117.5 2.0 %finish.1 = f32[2,512,512]{2,1,0:T(8,128)} custom-call(f32[2,512,512]{2,1,0:T(8,128)S(1)} %copy-done.1, f32[2,256,768]{2,1,0:T(8,128)S(1)} %collective-permute-done.9.above, f32[2,256,256]{2,1,0:T(8,128)S(1)} %copy-done.5, f32[2,256,256]{2,1,0:T(8,128)S(1)} %copy-done.3), custom_call_target="tpu_custom_call" | custom-call | tf_op jit(solution)/shard_map/finish/pallas_call | solution.py:334
  119.6 4.9 %all-to-all-done.1 = f32[16,32,256]{2,1,0:T(8,128)S(1)} async-done(((f32[16,32,256]{2,1,0:T(8,128)}), f32[16,32,256]{2,1,0:T(8,128)S(1)}, u32[]{:S(2)}, u32[]{:S(2)}) %all-to-all-start.1) | async-done | bytes 524320 | tf_op jit(solution)/shard_map/all_to_all | solution.py:398
  124.5 1.9 %collective-permute-start.11 = (f32[512,256]{1,0:T(8,128)S(1)}, f32[512,256]{1,0:T(8,128)S(1)}, u32[]{:S(2)}, u32[]{:S(2)}) collective-permute-start(f32[512,256]{1,0:T(8,128)S(1)} %bitcast.10), channel_id=1, source_target_pairs={{0,16},{16,0},{1,17},{17,1},{2,18},{18,2},{3,19},{19,3},{4,20},{20... | collective-permute-start | bytes 1572872 | tf_op jit(solution)/shard_map/ppermute | solution.py:351
  126.3 1.5 %collective-permute-done.11.rest = f32[512,256]{1,0:T(8,128)S(1)} collective-permute-done((f32[512,256]{1,0:T(8,128)S(1)}, f32[512,256]{1,0:T(8,128)S(1)}, u32[]{:S(2)}, u32[]{:S(2)}) %collective-permute-start.11) | collective-permute-done | bytes 524320 | tf_op jit(solution)/shard_map/ppermute | solution.py:351
  127.9 1.6 %probe.3 = f32[1024,256]{1,0:T(8,128)} custom-call(s32[3]{0:T(128)S(1)} %copy-done.6, f32[1024,256]{1,0:T(8,128)S(1)} %bitcast.9, f32[512,256]{1,0:T(8,128)S(1)} %bitcast.11, f32[512,256]{1,0:T(8,128)S(1)} %collective-permute-done.11.rest), custom_call_target="tpu_custom_call" | custom-call | tf_op jit(solution)/shard_map/probe/pallas_call | solution.py:403
  (32 shorter events, 0.9 us)
Async XLA Ops:
  2.5 16.2 %collective-permute-start = (f32[2,256,256]{2,1,0:T(8,128)}, f32[2,256,256]{2,1,0:T(8,128)S(1)}, u32[]{:S(2)}, u32[]{:S(2)}) collective-permute-start(f32[2,256,256]{2,1,0:T(8,128)} %slice.12), channel_id=1, source_target_pairs={{1,0},{2,1},{3,2},{4,3},{5,4},{6,5},{7,6},{8,7},{9,8},{10,9},{11,1... | collective-permute-start | bytes 1572872 | tf_op jit(solution)/shard_map/ppermute | solution.py:376
  5.1 25.0 %collective-permute-start.2 = (f32[2,256,512]{2,1,0:T(8,128)S(1)}, f32[2,256,512]{2,1,0:T(8,128)S(1)}, u32[]{:S(2)}, u32[]{:S(2)}) collective-permute-start(f32[2,256,512]{2,1,0:T(8,128)S(1)} %slice.14), channel_id=1, source_target_pairs={{16,0},{32,16},{48,32},{64,48},{80,64},{96,80},{112,96},{17,1},{33... | collective-permute-start | bytes 3145736 | tf_op jit(solution)/shard_map/ppermute | solution.py:377
  10.3 13.0 %copy-start.10 = (s32[8,2]{0,1:T(2,128)S(1)}, s32[8,2]{0,1:T(2,128)}, u32[]{:S(2)}) copy-start(s32[8,2]{0,1:T(2,128)} %param.10) | copy-start | bytes 196
  10.3 19.7 %collective-permute-start.1 = (f32[2,256,256]{2,1,0:T(8,128)}, f32[2,256,256]{2,1,0:T(8,128)}, u32[]{:S(2)}, u32[]{:S(2)}) collective-permute-start(f32[2,256,256]{2,1,0:T(8,128)} %slice.13), channel_id=1, source_target_pairs={{1,0},{2,1},{3,2},{4,3},{5,4},{6,5},{7,6},{8,7},{9,8},{10,9},{11,1... | collective-permute-start | bytes 1572872 | tf_op jit(solution)/shard_map/ppermute | solution.py:378
  18.7 12.2 %copy-start.8 = (f32[2,256,256]{2,1,0:T(8,128)}, f32[2,256,256]{2,1,0:T(8,128)S(1)}, u32[]{:S(2)}) copy-start(f32[2,256,256]{2,1,0:T(8,128)S(1)} %collective-permute-done.right_top) | copy-start | bytes 1572868
  18.7 12.2 %collective-permute-start.3 = (f32[2,256,256]{2,1,0:T(8,128)S(1)}, f32[2,256,256]{2,1,0:T(8,128)}, u32[]{:S(2)}, u32[]{:S(2)}) collective-permute-start(f32[2,256,256]{2,1,0:T(8,128)S(1)} %collective-permute-done.right_top), channel_id=1, source_target_pairs={{16,0},{32,16},{48,32},{64,48},{80,64},{96,80},{112,96},{17,1},{33... | collective-permute-start | bytes 1572872 | tf_op jit(solution)/shard_map/ppermute | solution.py:381
  30.1 1.0 copy-start.7
  47.6 28.7 %copy-start.9 = (f32[2,256,256]{2,1,0:T(8,128)S(1)}, f32[2,256,256]{2,1,0:T(8,128)}, u32[]{:S(2)}) copy-start(f32[2,256,256]{2,1,0:T(8,128)} %get-tuple-element.27) | copy-start | bytes 1572868
  47.7 28.7 %collective-permute-start.9 = (f32[2,256,768]{2,1,0:T(8,128)}, f32[2,256,768]{2,1,0:T(8,128)S(1)}, u32[]{:S(2)}, u32[]{:S(2)}) collective-permute-start(f32[2,256,768]{2,1,0:T(8,128)} %get-tuple-element.28), channel_id=1, source_target_pairs={{0,16},{16,32},{32,48},{48,64},{64,80},{80,96},{96,112},{1,17},{17... | collective-permute-start | bytes 4718600 | tf_op jit(solution)/shard_map/ppermute | solution.py:389
  57.0 8.5 %collective-permute-start.4 = (f32[2,256,256]{2,1,0:T(8,128)}, f32[2,256,256]{2,1,0:T(8,128)S(1)}, u32[]{:S(2)}, u32[]{:S(2)}) collective-permute-start(f32[2,256,256]{2,1,0:T(8,128)} %get-tuple-element.24), channel_id=1, source_target_pairs={{0,16},{16,0},{1,17},{17,1},{2,18},{18,2},{3,19},{19,3},{4,20},{20... | collective-permute-start | bytes 1572872 | tf_op jit(solution)/shard_map/ppermute | solution.py:351
  57.1 31.8 %collective-permute-start.5 = (f32[2,256,256]{2,1,0:T(8,128)}, f32[2,256,256]{2,1,0:T(8,128)S(1)}, u32[]{:S(2)}, u32[]{:S(2)}) collective-permute-start(f32[2,256,256]{2,1,0:T(8,128)} %get-tuple-element.25), channel_id=1, source_target_pairs={{0,1},{1,2},{2,3},{3,4},{4,5},{5,6},{6,7},{7,8},{8,9},{9,10},{10,1... | collective-permute-start | bytes 1572872 | tf_op jit(solution)/shard_map/ppermute | solution.py:388
  67.5 21.4 %all-to-all-start = ((f32[16,32,256]{2,1,0:T(8,128)}), f32[16,32,256]{2,1,0:T(8,128)S(1)}, u32[]{:S(2)}, u32[]{:S(2)}) async-start(f32[16,32,256]{2,1,0:T(8,128)} %bitcast.4), calls=%async_computation | async-start | bytes 1048576 | tf_op jit(solution)/shard_map/all_to_all | solution.py:393
  77.2 21.6 %collective-permute-start.10 = (f32[2,256,256]{2,1,0:T(8,128)}, f32[2,256,256]{2,1,0:T(8,128)S(1)}, u32[]{:S(2)}, u32[]{:S(2)}) collective-permute-start(f32[2,256,256]{2,1,0:T(8,128)} %slice_add_fusion), channel_id=1, source_target_pairs={{0,1},{1,2},{2,3},{3,4},{4,5},{5,6},{6,7},{7,8},{8,9},{9,10},{10,1... | collective-permute-start | bytes 1572872 | tf_op jit(solution)/shard_map/ppermute | solution.py:391
  88.9 24.9 %copy-start.2 = (f32[2,256,256]{2,1,0:T(8,128)}, f32[2,256,256]{2,1,0:T(8,128)S(1)}, u32[]{:S(2)}) copy-start(f32[2,256,256]{2,1,0:T(8,128)S(1)} %collective-permute-done.5.bot) | copy-start | bytes 1572868
  89.0 4.6 %collective-permute-start.8 = (f32[32,256]{1,0:T(8,128)S(1)}, f32[32,256]{1,0:T(8,128)S(1)}, u32[]{:S(2)}, u32[]{:S(2)}) collective-permute-start(f32[32,256]{1,0:T(8,128)S(1)} %reduce_sum.9), channel_id=1, source_target_pairs={{0,3},{1,0},{2,1},{3,2},{4,7},{5,4},{6,5},{7,6},{8,11},{9,8},{10,9... | collective-permute-start | bytes 98312 | tf_op jit(solution)/shard_map/ppermute | solution.py:355
  92.3 4.5 %collective-permute-start.7 = (f32[32,256]{1,0:T(8,128)S(1)}, f32[32,256]{1,0:T(8,128)S(1)}, u32[]{:S(2)}, u32[]{:S(2)}) collective-permute-start(f32[32,256]{1,0:T(8,128)S(1)} %reduce_sum.9), channel_id=1, source_target_pairs={{0,1},{1,2},{2,3},{3,0},{4,5},{5,6},{6,7},{7,4},{8,9},{9,10},{10,1... | collective-permute-start | bytes 98312 | tf_op jit(solution)/shard_map/ppermute | solution.py:355
  92.3 6.5 %collective-permute-start.6 = (f32[32,256]{1,0:T(8,128)S(1)}, f32[32,256]{1,0:T(8,128)S(1)}, u32[]{:S(2)}, u32[]{:S(2)}) collective-permute-start(f32[32,256]{1,0:T(8,128)S(1)} %reduce_sum.9), channel_id=1, source_target_pairs={{0,2},{1,3},{2,0},{3,1},{4,6},{5,7},{6,4},{7,5},{8,10},{9,11},{10,... | collective-permute-start | bytes 98312 | tf_op jit(solution)/shard_map/ppermute | solution.py:355
  98.8 15.0 %copy-start.4 = (f32[2,256,256]{2,1,0:T(8,128)}, f32[2,256,256]{2,1,0:T(8,128)S(1)}, u32[]{:S(2)}) copy-start(f32[2,256,256]{2,1,0:T(8,128)S(1)} %collective-permute-done.10.top) | copy-start | bytes 1572868
  99.7 24.7 %all-to-all-start.1 = ((f32[16,32,256]{2,1,0:T(8,128)}), f32[16,32,256]{2,1,0:T(8,128)S(1)}, u32[]{:S(2)}, u32[]{:S(2)}) async-start(f32[16,32,256]{2,1,0:T(8,128)} %broadcast_in_dim.2), calls=%async_computation.1 | async-start | bytes 1048576 | tf_op jit(solution)/shard_map/all_to_all | solution.py:398
  113.9 1.6 %copy-start.1 = (f32[2,512,512]{2,1,0:T(8,128)S(1)}, f32[2,512,512]{2,1,0:T(8,128)}, u32[]{:S(2)}) copy-start(f32[2,512,512]{2,1,0:T(8,128)} %get-tuple-element.30.part) | copy-start | bytes 6291460
  115.4 1.0 copy-start.3
  116.5 1.0 copy-start.5
  117.5 10.3 %copy-start = (f32[2,2,256,256]{3,2,1,0:T(8,128)S(1)}, f32[2,2,256,256]{3,2,1,0:T(8,128)}, u32[]{:S(2)}) copy-start(f32[2,2,256,256]{3,2,1,0:T(8,128)} %probe.2) | copy-start | bytes 3145732
  117.5 10.3 %copy-start.6 = (s32[3]{0:T(128)S(1)}, s32[3]{0:T(128)}, u32[]{:S(2)}) copy-start(s32[3]{0:T(128)} %pad_add_fusion.anchor.place) | copy-start | bytes 40
  124.5 3.4 %collective-permute-start.11 = (f32[512,256]{1,0:T(8,128)S(1)}, f32[512,256]{1,0:T(8,128)S(1)}, u32[]{:S(2)}, u32[]{:S(2)}) collective-permute-start(f32[512,256]{1,0:T(8,128)S(1)} %bitcast.10), channel_id=1, source_target_pairs={{0,16},{16,0},{1,17},{17,1},{2,18},{18,2},{3,19},{19,3},{4,20},{20... | collective-permute-start | bytes 1572872 | tf_op jit(solution)/shard_map/ppermute | solution.py:351

commit v7 on v5

--- a/solution.py
+++ b/solution.py
@@ -317,32 +317,31 @@
 
 
 def finish_kernel(part, above, top, bot, out):
-    h = pl.program_id(1)
-
-    @pl.when(h == 0)
+    q = pl.program_id(1)
+
+    @pl.when(q == 0)
     def _():
-        out[0] = part[0] - 0.5 * above[0]
-        out[0, :, :W] -= 0.5 * top[0]
-
-    @pl.when(h == 1)
+        out[...] = part[...] - 0.5 * (above[...] + top[...])
+
+    @pl.when(q == 1)
     def _():
-        out[0, :, W:] = part[0, :, W:]
-        out[0, :, :W] = part[0, :, :W] - 0.5 * bot[0]
+        out[...] = part[...] - 0.5 * above[...]
+
+    @pl.when(q == 2)
+    def _():
+        out[...] = part[...] - 0.5 * bot[...]
 
 
 def finish_call(part, above, top, bot):
-    wide = pl.BlockSpec((1, W, 512), lambda c, h: (c, h, 0))
+    quarter = pl.BlockSpec((1, W, W), lambda c, q: (c, q // 2, q % 2))
+    plane = pl.BlockSpec((1, W, W), lambda c, q: (c, 0, 0))
     return pl.pallas_call(
         finish_kernel,
-        grid=(2, 2),
+        grid=(2, 3),
         out_shape=jax.ShapeDtypeStruct((2, 512, 512), f32),
-        in_specs=[
-            wide,
-            pl.BlockSpec((1, W, 512), lambda c, h: (c, 0, 0)),
-            pl.BlockSpec((1, W, W), lambda c, h: (c, 0, 0)),
-            pl.BlockSpec((1, W, W), lambda c, h: (c, 0, 0)),
-        ],
-        out_specs=wide,
+        in_specs=[quarter, pl.BlockSpec((1, W, W), lambda c, q: (c, 0, q % 2)), plane, plane],
+        out_specs=quarter,
+        input_output_aliases={0: 0},
         compiler_params=pltpu.CompilerParams(vmem_limit_bytes=8 * 2**20),
         name="finish",
     )(part, above, top, bot)
@@ -393,7 +392,7 @@
     piece = lax.all_to_all(half, plane, 0, 0).sum(0)
     piece, bot_in = lax.optimization_barrier((piece, bot_in))
     piece = sum_everywhere(piece, "z")
-    piece, top_in, above_in = lax.optimization_barrier((piece, top_in, above_in))
+    piece, top_in = lax.optimization_barrier((piece, top_in))
     new_object = finish_call(part, above_in, top_in, bot_in)
     half = lax.all_to_all(jnp.broadcast_to(piece[None], half.shape), plane, 0, 0).reshape(512, W)
     rest = swap_cores(half)

time: 128 us -> 126 us (0.984)
  starting transfers between devices: 39.6 us -> 36.4 us
  other arithmetic: 5.85 us -> 2.67 us
  waiting for transfers between devices: 17.7 us -> 20.4 us
    all_to_all x1, waiting for transfers between devices: 4.48 us -> 9.73 us  [shards(): piece = lax.all_to_all(half, plane, 0, 0).sum(0)]
    ppermute x3, waiting for transfers between devices: 3.71 us -> 1.25 us  [sum_everywhere(): lax.ppermute(value, axis, [(i, (i + k) % 4) for i in range(4)])]
    ppermute x3, starting transfers between devices: 6.75 us -> 4.5 us  [sum_everywhere(): lax.ppermute(value, axis, [(i, (i + k) % 4) for i in range(4)])]
    ppermute x1, starting transfers between devices: 4.13 us -> 1.95 us  [shards(): top_in = lax.ppermute(g_top + corner_in, cols, to_right)]
    add x1, other arithmetic: 2.21 us -> 0.07 us  [shards(): top_in = lax.ppermute(g_top + corner_in, cols, to_right)]
    ppermute x1, starting transfers between devices: 1.92 us -> 3.62 us  [shards(): above_in = lax.ppermute(g_below, rows, down)]
  transfers between devices with their start and end apart: 14 -> 14, of which waited for: 6 -> 5; matrix products, arithmetic and copies ran while one was open for 5% -> 3% of each run, Pallas kernels for 8% -> 9%
where the time goes in v7:
time: 126 us; the launch traced here: 125 us
  Pallas kernels  39.7 us (32%)
  starting transfers between devices  36.4 us (29%)
  blocking collectives  21.1 us (17%)
  waiting for transfers between devices  20.4 us (16%)
  local copies, waits for them, and re-layouts  3.31 us (3%)
  other arithmetic  2.67 us (2%)
  between operations  1.51 us (1%)
    pallas_call x1, Pallas kernels, main_call(): pl.pallas_call(main_kernel, out_shape=(S(2, 512, 512), S(2, 256, 256), S(...  26.4 us
    all_to_all x1, blocking collectives, shards(): lax.all_to_all(jnp.broadcast_to(piece[None], half.shape), plane, 0, 0)  21.1 us
    all_to_all x1, waiting for transfers between devices, shards(): piece = lax.all_to_all(half, plane, 0, 0).sum(0)  9.73 us
    all_to_all x1, starting transfers between devices, shards(): piece = lax.all_to_all(half, plane, 0, 0).sum(0)  7.72 us
    pallas_call x1, Pallas kernels, prep_call(): pl.pallas_call(prep_kernel, grid=(8,), out_shape=jax.ShapeDtypeStruct((8,...  6.96 us
    ppermute x1, waiting for transfers between devices, shards(): right_bot = lax.ppermute(object_planes[:, W:, :W], cols, to_left)  5.35 us
    pallas_call x1, Pallas kernels, finish_call(): pl.pallas_call(finish_kernel, grid=(2, 3), out_shape=jax.ShapeDtypeStruct...  4.72 us
    ppermute x1, starting transfers between devices, shards(): bot_in = lax.ppermute(g_bot, cols, to_right)  4.69 us
  transfers between devices with their start and end apart: 14, of which 5 were waited for; matrix products, arithmetic and copies ran while one was open for 3% of the time, Pallas kernels for 9%

profile of v7, /device:TPU:1, one launch (start us, length us, event | category | flops | bytes accessed | tf_op | source)
XLA Modules:
  0.0 125.2 jit_solution(13771516166732919530)
XLA Ops:
  0.6 0.0 copy-start.2
  0.6 2.4 %fusion = (f32[2,256,256]{2,1,0:T(8,128)}, f32[2,256,256]{2,1,0:T(8,128)}) fusion(f32[2,512,512]{2,1,0:T(8,128)} %obj.1), kind=kLoop, calls=%fused_computation.2 | loop fusion | bytes 2097152 | tf_op jit(solution)/shard_map/slice | solution.py:376
  3.1 1.3 %collective-permute-start = (f32[2,256,256]{2,1,0:T(8,128)}, f32[2,256,256]{2,1,0:T(8,128)S(1)}, u32[]{:S(2)}, u32[]{:S(2)}) collective-permute-start(f32[2,256,256]{2,1,0:T(8,128)} %get-tuple-element.29), channel_id=1, source_target_pairs={{1,0},{2,1},{3,2},{4,3},{5,4},{6,5},{7,6},{8,7},{9,8},{10,9},{11,1... | collective-permute-start | bytes 1572872 | tf_op jit(solution)/shard_map/ppermute | solution.py:374
  4.4 0.1 slice.11
  4.4 3.3 %collective-permute-start.2 = (f32[2,256,512]{2,1,0:T(8,128)S(1)}, f32[2,256,512]{2,1,0:T(8,128)S(1)}, u32[]{:S(2)}, u32[]{:S(2)}) collective-permute-start(f32[2,256,512]{2,1,0:T(8,128)S(1)} %slice.11), channel_id=1, source_target_pairs={{16,0},{32,16},{48,32},{64,48},{80,64},{96,80},{112,96},{17,1},{33... | collective-permute-start | bytes 3145736 | tf_op jit(solution)/shard_map/ppermute | solution.py:375
  7.8 0.0 copy-start.6
  7.8 1.3 %collective-permute-start.1 = (f32[2,256,256]{2,1,0:T(8,128)}, f32[2,256,256]{2,1,0:T(8,128)}, u32[]{:S(2)}, u32[]{:S(2)}) collective-permute-start(f32[2,256,256]{2,1,0:T(8,128)} %get-tuple-element.28), channel_id=1, source_target_pairs={{1,0},{2,1},{3,2},{4,3},{5,4},{6,5},{7,6},{8,7},{9,8},{10,9},{11,1... | collective-permute-start | bytes 1572872 | tf_op jit(solution)/shard_map/ppermute | solution.py:376
  9.1 7.0 %roots.1.sq = f32[8,256,256]{2,1,0:T(8,128)} custom-call(s32[8,256,256]{2,1,0:T(8,128)} %counts.1, bf16[256,256]{1,0:T(8,128)(2,1)} %constant.31.clone.pm, bf16[256,256]{1,0:T(8,128)(2,1)} %constant.32.clone.pmt), custom_call_target="tpu_custom_call" | custom-call | tf_op jit(solution)/shard_map/roots/pallas_call | solution.py:305
  16.0 3.2 %collective-permute-done.right_top = f32[2,256,256]{2,1,0:T(8,128)S(1)} collective-permute-done((f32[2,256,256]{2,1,0:T(8,128)}, f32[2,256,256]{2,1,0:T(8,128)S(1)}, u32[]{:S(2)}, u32[]{:S(2)}) %collective-permute-start) | collective-permute-done | bytes 524320 | tf_op jit(solution)/shard_map/ppermute | solution.py:374
  19.3 4.0 %collective-permute-start.3 = (f32[2,256,256]{2,1,0:T(8,128)S(1)}, f32[2,256,256]{2,1,0:T(8,128)}, u32[]{:S(2)}, u32[]{:S(2)}) collective-permute-start(f32[2,256,256]{2,1,0:T(8,128)S(1)} %collective-permute-done.right_top), channel_id=1, source_target_pairs={{16,0},{32,16},{48,32},{64,48},{80,64},{96,80},{112,96},{17,1},{33... | collective-permute-start | bytes 1572872 | tf_op jit(solution)/shard_map/ppermute | solution.py:379
  23.9 0.7 copy.11.offs
  24.6 0.7 pad_add_fusion.anchor.place
  25.2 5.4 %collective-permute-done.1.right_bot = f32[2,256,256]{2,1,0:T(8,128)} collective-permute-done((f32[2,256,256]{2,1,0:T(8,128)}, f32[2,256,256]{2,1,0:T(8,128)}, u32[]{:S(2)}, u32[]{:S(2)}) %collective-permute-start.1) | collective-permute-done | bytes 524320 | tf_op jit(solution)/shard_map/ppermute | solution.py:376
  30.6 0.9 collective-permute-done.3.corner
  31.5 0.1 copy-done.3
  31.6 26.4 %slots.1 = (f32[2,512,512]{2,1,0:T(8,128)}, f32[2,256,256]{2,1,0:T(8,128)}, f32[2,256,256]{2,1,0:T(8,128)}, f32[2,256,256]{2,1,0:T(8,128)}, f32[2,256,512]{2,1,0...) custom-call(s32[8,2]{1,0:T(8,128)} %copy.11.offs, s32[1]{0:T(128)} %bitcast.8.live, ...), custom_call_target="tpu_custom_call" | custom-call | tf_op jit(solution)/shard_map/slots/pallas_call | solution.py:268
  58.0 0.1 collective-permute-start.5
  58.1 2.1 %collective-permute-start.10 = (f32[2,256,256]{2,1,0:T(8,128)}, f32[2,256,256]{2,1,0:T(8,128)S(1)}, u32[]{:S(2)}, u32[]{:S(2)}) collective-permute-start(f32[2,256,256]{2,1,0:T(8,128)} %get-tuple-element.24), channel_id=1, source_target_pairs={{0,16},{16,32},{32,48},{48,64},{64,80},{80,96},{96,112},{1,17},{17... | collective-permute-start | bytes 1572872 | tf_op jit(solution)/shard_map/ppermute | solution.py:386
  60.2 4.7 %collective-permute-start.6 = (f32[2,256,256]{2,1,0:T(8,128)}, f32[2,256,256]{2,1,0:T(8,128)S(1)}, u32[]{:S(2)}, u32[]{:S(2)}) collective-permute-start(f32[2,256,256]{2,1,0:T(8,128)} %get-tuple-element.21), channel_id=1, source_target_pairs={{0,1},{1,2},{2,3},{3,4},{4,5},{5,6},{6,7},{7,8},{8,9},{9,10},{10,1... | collective-permute-start | bytes 1572872 | tf_op jit(solution)/shard_map/ppermute | solution.py:387
  64.9 1.9 %add.23 = f32[2,256,256]{2,1,0:T(8,128)} add(f32[2,256,256]{2,1,0:T(8,128)} %get-tuple-element.19, f32[2,256,256]{2,1,0:T(8,128)S(1)} %collective-permute-done.5) | non-fusion elementwise | flops 131072 | bytes 1572864 | tf_op jit(solution)/shard_map/add | solution.py:389
  66.8 7.7 %all-to-all-start = ((f32[16,32,256]{2,1,0:T(8,128)}), f32[16,32,256]{2,1,0:T(8,128)S(1)}, u32[]{:S(2)}, u32[]{:S(2)}) async-start(f32[16,32,256]{2,1,0:T(8,128)} %bitcast.4), calls=%async_computation | async-start | bytes 1048576 | tf_op jit(solution)/shard_map/all_to_all | solution.py:392
  74.5 0.1 add.27
  74.6 1.9 %collective-permute-start.11 = (f32[2,256,256]{2,1,0:T(8,128)S(1)}, f32[2,256,256]{2,1,0:T(8,128)S(1)}, u32[]{:S(2)}, u32[]{:S(2)}) collective-permute-start(f32[2,256,256]{2,1,0:T(8,128)S(1)} %add.27), channel_id=1, source_target_pairs={{0,1},{1,2},{2,3},{3,4},{4,5},{5,6},{6,7},{7,8},{8,9},{9,10},{10,1... | collective-permute-start | bytes 1572872 | tf_op jit(solution)/shard_map/ppermute | solution.py:390
  76.6 9.7 %all-to-all-done = f32[16,32,256]{2,1,0:T(8,128)S(1)} async-done(((f32[16,32,256]{2,1,0:T(8,128)}), f32[16,32,256]{2,1,0:T(8,128)S(1)}, u32[]{:S(2)}, u32[]{:S(2)}) %all-to-all-start) | async-done | bytes 524320 | tf_op jit(solution)/shard_map/all_to_all | solution.py:392
  86.3 2.0 %collective-permute-start.9 = (f32[32,256]{1,0:T(8,128)S(1)}, f32[32,256]{1,0:T(8,128)S(1)}, u32[]{:S(2)}, u32[]{:S(2)}) collective-permute-start(f32[32,256]{1,0:T(8,128)S(1)} %reduce_sum.9), channel_id=1, source_target_pairs={{0,3},{1,0},{2,1},{3,2},{4,7},{5,4},{6,5},{7,6},{8,11},{9,8},{10,9... | collective-permute-start | bytes 98312 | tf_op jit(solution)/shard_map/ppermute | solution.py:355
  88.3 2.5 %collective-permute-start.7 = (f32[32,256]{1,0:T(8,128)S(1)}, f32[32,256]{1,0:T(8,128)S(1)}, u32[]{:S(2)}, u32[]{:S(2)}) collective-permute-start(f32[32,256]{1,0:T(8,128)S(1)} %reduce_sum.9), channel_id=1, source_target_pairs={{0,2},{1,3},{2,0},{3,1},{4,6},{5,7},{6,4},{7,5},{8,10},{9,11},{10,... | collective-permute-start | bytes 98312 | tf_op jit(solution)/shard_map/ppermute | solution.py:355
  90.8 3.6 %collective-permute-start.4 = (f32[2,256,512]{2,1,0:T(8,128)}, f32[2,256,512]{2,1,0:T(8,128)S(1)}, u32[]{:S(2)}, u32[]{:S(2)}) collective-permute-start(f32[2,256,512]{2,1,0:T(8,128)} %get-tuple-element.18), channel_id=1, source_target_pairs={{0,16},{16,32},{32,48},{48,64},{64,80},{80,96},{96,112},{1,17},{17... | collective-permute-start | bytes 3145736 | tf_op jit(solution)/shard_map/ppermute | solution.py:388
  94.5 1.2 collective-permute-done.7
  95.8 21.1 %all_to_all.10 = f32[16,32,256]{2,1,0:T(8,128)S(1)} all-to-all(f32[16,32,256]{2,1,0:T(8,128)S(1)} %broadcast_in_dim.2), channel_id=1, replica_groups=mesh['y'=4,'core'=2,'x'=4,'z'=4] {'y','x'}, dimensions={0} | all-to-all | bytes 1048576 | tf_op jit(solution)/shard_map/all_to_all | solution.py:397
  116.9 1.9 %collective-permute-start.12 = (f32[512,256]{1,0:T(8,128)S(1)}, f32[512,256]{1,0:T(8,128)S(1)}, u32[]{:S(2)}, u32[]{:S(2)}) collective-permute-start(f32[512,256]{1,0:T(8,128)S(1)} %bitcast.10), channel_id=1, source_target_pairs={{0,16},{16,0},{1,17},{17,1},{2,18},{18,2},{3,19},{19,3},{4,20},{20... | collective-permute-start | bytes 1572872 | tf_op jit(solution)/shard_map/ppermute | solution.py:351
  118.8 4.7 %finish.1 = f32[2,512,512]{2,1,0:T(8,128)} custom-call(f32[2,512,512]{2,1,0:T(8,128)} %get-tuple-element.17.part, f32[2,256,512]{2,1,0:T(8,128)S(1)} %collective-permute-done.4.above, f32[2,256,256]{2,1,0:T(8,128)S(1)} %collective-permute-done.11.top, f32[2,256,256]{2,1,0:T(8,128)S(1)} %collective-permute-done.6.bot), custom_call_target="tpu_custom_call", output_to_operand_aliasing={{}: (0, {})} | custom-call | tf_op jit(solution)/shard_map/finish/pallas_call | solution.py:338
  123.6 1.6 %probe.3 = f32[1024,256]{1,0:T(8,128)} custom-call(s32[3]{0:T(128)S(1)} %copy-done.1, f32[1024,256]{1,0:T(8,128)S(1)} %bitcast.9, f32[512,256]{1,0:T(8,128)S(1)} %bitcast.11, f32[512,256]{1,0:T(8,128)S(1)} %collective-permute-done.12.rest), custom_call_target="tpu_custom_call" | custom-call | tf_op jit(solution)/shard_map/probe/pallas_call | solution.py:401
  (24 shorter events, 0.1 us)
Async XLA Ops:
  0.6 3.7 %copy-start.2 = (f32[2,512,512]{2,1,0:T(8,128)S(1)}, f32[2,512,512]{2,1,0:T(8,128)}, u32[]{:S(2)}) copy-start(f32[2,512,512]{2,1,0:T(8,128)} %obj.1) | copy-start | bytes 6291460
  3.1 16.2 %collective-permute-start = (f32[2,256,256]{2,1,0:T(8,128)}, f32[2,256,256]{2,1,0:T(8,128)S(1)}, u32[]{:S(2)}, u32[]{:S(2)}) collective-permute-start(f32[2,256,256]{2,1,0:T(8,128)} %get-tuple-element.29), channel_id=1, source_target_pairs={{1,0},{2,1},{3,2},{4,3},{5,4},{6,5},{7,6},{8,7},{9,8},{10,9},{11,1... | collective-permute-start | bytes 1572872 | tf_op jit(solution)/shard_map/ppermute | solution.py:374
  4.4 26.2 %collective-permute-start.2 = (f32[2,256,512]{2,1,0:T(8,128)S(1)}, f32[2,256,512]{2,1,0:T(8,128)S(1)}, u32[]{:S(2)}, u32[]{:S(2)}) collective-permute-start(f32[2,256,512]{2,1,0:T(8,128)S(1)} %slice.11), channel_id=1, source_target_pairs={{16,0},{32,16},{48,32},{64,48},{80,64},{96,80},{112,96},{17,1},{33... | collective-permute-start | bytes 3145736 | tf_op jit(solution)/shard_map/ppermute | solution.py:375
  7.8 16.1 %copy-start.6 = (s32[8,2]{0,1:T(2,128)S(1)}, s32[8,2]{0,1:T(2,128)}, u32[]{:S(2)}) copy-start(s32[8,2]{0,1:T(2,128)} %param.10) | copy-start | bytes 196
  7.8 22.8 %collective-permute-start.1 = (f32[2,256,256]{2,1,0:T(8,128)}, f32[2,256,256]{2,1,0:T(8,128)}, u32[]{:S(2)}, u32[]{:S(2)}) collective-permute-start(f32[2,256,256]{2,1,0:T(8,128)} %get-tuple-element.28), channel_id=1, source_target_pairs={{1,0},{2,1},{3,2},{4,3},{5,4},{6,5},{7,6},{8,7},{9,8},{10,9},{11,1... | collective-permute-start | bytes 1572872 | tf_op jit(solution)/shard_map/ppermute | solution.py:376
  19.3 12.2 %copy-start.4 = (f32[2,256,256]{2,1,0:T(8,128)}, f32[2,256,256]{2,1,0:T(8,128)S(1)}, u32[]{:S(2)}) copy-start(f32[2,256,256]{2,1,0:T(8,128)S(1)} %collective-permute-done.right_top) | copy-start | bytes 1572868
  19.3 12.2 %collective-permute-start.3 = (f32[2,256,256]{2,1,0:T(8,128)S(1)}, f32[2,256,256]{2,1,0:T(8,128)}, u32[]{:S(2)}, u32[]{:S(2)}) collective-permute-start(f32[2,256,256]{2,1,0:T(8,128)S(1)} %collective-permute-done.right_top), channel_id=1, source_target_pairs={{16,0},{32,16},{48,32},{64,48},{80,64},{96,80},{112,96},{17,1},{33... | collective-permute-start | bytes 1572872 | tf_op jit(solution)/shard_map/ppermute | solution.py:379
  30.6 1.0 copy-start.3
  58.0 16.5 %copy-start.5 = (f32[2,256,256]{2,1,0:T(8,128)S(1)}, f32[2,256,256]{2,1,0:T(8,128)}, u32[]{:S(2)}) copy-start(f32[2,256,256]{2,1,0:T(8,128)} %get-tuple-element.23) | copy-start | bytes 1572868
  58.0 6.9 %collective-permute-start.5 = (f32[2,256,256]{2,1,0:T(8,128)}, f32[2,256,256]{2,1,0:T(8,128)S(1)}, u32[]{:S(2)}, u32[]{:S(2)}) collective-permute-start(f32[2,256,256]{2,1,0:T(8,128)} %get-tuple-element.20), channel_id=1, source_target_pairs={{0,16},{16,0},{1,17},{17,1},{2,18},{18,2},{3,19},{19,3},{4,20},{20... | collective-permute-start | bytes 1572872 | tf_op jit(solution)/shard_map/ppermute | solution.py:351
  58.1 16.4 %collective-permute-start.10 = (f32[2,256,256]{2,1,0:T(8,128)}, f32[2,256,256]{2,1,0:T(8,128)S(1)}, u32[]{:S(2)}, u32[]{:S(2)}) collective-permute-start(f32[2,256,256]{2,1,0:T(8,128)} %get-tuple-element.24), channel_id=1, source_target_pairs={{0,16},{16,32},{32,48},{48,64},{64,80},{80,96},{96,112},{1,17},{17... | collective-permute-start | bytes 1572872 | tf_op jit(solution)/shard_map/ppermute | solution.py:386
  60.2 26.2 %collective-permute-start.6 = (f32[2,256,256]{2,1,0:T(8,128)}, f32[2,256,256]{2,1,0:T(8,128)S(1)}, u32[]{:S(2)}, u32[]{:S(2)}) collective-permute-start(f32[2,256,256]{2,1,0:T(8,128)} %get-tuple-element.21), channel_id=1, source_target_pairs={{0,1},{1,2},{2,3},{3,4},{4,5},{5,6},{6,7},{7,8},{8,9},{9,10},{10,1... | collective-permute-start | bytes 1572872 | tf_op jit(solution)/shard_map/ppermute | solution.py:387
  66.8 19.5 %all-to-all-start = ((f32[16,32,256]{2,1,0:T(8,128)}), f32[16,32,256]{2,1,0:T(8,128)S(1)}, u32[]{:S(2)}, u32[]{:S(2)}) async-start(f32[16,32,256]{2,1,0:T(8,128)} %bitcast.4), calls=%async_computation | async-start | bytes 1048576 | tf_op jit(solution)/shard_map/all_to_all | solution.py:392
  74.6 21.1 %collective-permute-start.11 = (f32[2,256,256]{2,1,0:T(8,128)S(1)}, f32[2,256,256]{2,1,0:T(8,128)S(1)}, u32[]{:S(2)}, u32[]{:S(2)}) collective-permute-start(f32[2,256,256]{2,1,0:T(8,128)S(1)} %add.27), channel_id=1, source_target_pairs={{0,1},{1,2},{2,3},{3,4},{4,5},{5,6},{6,7},{7,8},{8,9},{9,10},{10,1... | collective-permute-start | bytes 1572872 | tf_op jit(solution)/shard_map/ppermute | solution.py:390
  86.3 8.1 %collective-permute-start.9 = (f32[32,256]{1,0:T(8,128)S(1)}, f32[32,256]{1,0:T(8,128)S(1)}, u32[]{:S(2)}, u32[]{:S(2)}) collective-permute-start(f32[32,256]{1,0:T(8,128)S(1)} %reduce_sum.9), channel_id=1, source_target_pairs={{0,3},{1,0},{2,1},{3,2},{4,7},{5,4},{6,5},{7,6},{8,11},{9,8},{10,9... | collective-permute-start | bytes 98312 | tf_op jit(solution)/shard_map/ppermute | solution.py:355
  88.3 6.1 %collective-permute-start.8 = (f32[32,256]{1,0:T(8,128)S(1)}, f32[32,256]{1,0:T(8,128)S(1)}, u32[]{:S(2)}, u32[]{:S(2)}) collective-permute-start(f32[32,256]{1,0:T(8,128)S(1)} %reduce_sum.9), channel_id=1, source_target_pairs={{0,1},{1,2},{2,3},{3,0},{4,5},{5,6},{6,7},{7,4},{8,9},{9,10},{10,1... | collective-permute-start | bytes 98312 | tf_op jit(solution)/shard_map/ppermute | solution.py:355
  88.3 7.4 %collective-permute-start.7 = (f32[32,256]{1,0:T(8,128)S(1)}, f32[32,256]{1,0:T(8,128)S(1)}, u32[]{:S(2)}, u32[]{:S(2)}) collective-permute-start(f32[32,256]{1,0:T(8,128)S(1)} %reduce_sum.9), channel_id=1, source_target_pairs={{0,2},{1,3},{2,0},{3,1},{4,6},{5,7},{6,4},{7,5},{8,10},{9,11},{10,... | collective-permute-start | bytes 98312 | tf_op jit(solution)/shard_map/ppermute | solution.py:355
  90.8 28.0 %collective-permute-start.4 = (f32[2,256,512]{2,1,0:T(8,128)}, f32[2,256,512]{2,1,0:T(8,128)S(1)}, u32[]{:S(2)}, u32[]{:S(2)}) collective-permute-start(f32[2,256,512]{2,1,0:T(8,128)} %get-tuple-element.18), channel_id=1, source_target_pairs={{0,16},{16,32},{32,48},{48,64},{64,80},{80,96},{96,112},{1,17},{17... | collective-permute-start | bytes 3145736 | tf_op jit(solution)/shard_map/ppermute | solution.py:388
  116.9 6.6 %collective-permute-start.12 = (f32[512,256]{1,0:T(8,128)S(1)}, f32[512,256]{1,0:T(8,128)S(1)}, u32[]{:S(2)}, u32[]{:S(2)}) collective-permute-start(f32[512,256]{1,0:T(8,128)S(1)} %bitcast.10), channel_id=1, source_target_pairs={{0,16},{16,0},{1,17},{17,1},{2,18},{18,2},{3,19},{19,3},{4,20},{20... | collective-permute-start | bytes 1572872 | tf_op jit(solution)/shard_map/ppermute | solution.py:351
  118.8 4.7 %copy-start = (f32[2,2,256,256]{3,2,1,0:T(8,128)S(1)}, f32[2,2,256,256]{3,2,1,0:T(8,128)}, u32[]{:S(2)}) copy-start(f32[2,2,256,256]{3,2,1,0:T(8,128)} %probe.2) | copy-start | bytes 3145732
  118.8 4.7 %copy-start.1 = (s32[3]{0:T(128)S(1)}, s32[3]{0:T(128)}, u32[]{:S(2)}) copy-start(s32[3]{0:T(128)} %pad_add_fusion.anchor.place) | copy-start | bytes 40

commit v8 on v7

--- a/solution.py
+++ b/solution.py
@@ -316,31 +316,48 @@
     return lax.ppermute(value, axes, pairs)
 
 
-def finish_kernel(part, above, top, bot, out):
-    q = pl.program_id(1)
-
-    @pl.when(q == 0)
-    def _():
-        out[...] = part[...] - 0.5 * (above[...] + top[...])
-
-    @pl.when(q == 1)
-    def _():
-        out[...] = part[...] - 0.5 * above[...]
-
-    @pl.when(q == 2)
-    def _():
-        out[...] = part[...] - 0.5 * bot[...]
+def finish_kernel(part, above, top, bot, out, upper, lower, ab, tp, bt, sems):
+    ins, outs = [], []
+    for c in range(2):
+        moves = [
+            (part.at[c, 0:W], upper.at[c]),
+            (above.at[c], ab.at[c]),
+            (top.at[c], tp.at[c]),
+            (part.at[c, W:, 0:W], lower.at[c]),
+            (bot.at[c], bt.at[c]),
+        ]
+        ins.append([pltpu.make_async_copy(s, d, sems.at[c, i]) for i, (s, d) in enumerate(moves)])
+        moves = [(upper.at[c], out.at[c, 0:W]), (lower.at[c], out.at[c, W:, 0:W])]
+        outs.append([pltpu.make_async_copy(s, d, sems.at[c, 5 + i]) for i, (s, d) in enumerate(moves)])
+    for copy in ins[0] + ins[1]:
+        copy.start()
+    for c in range(2):
+        for copy in ins[c]:
+            copy.wait()
+        upper[c, :, :W] = upper[c, :, :W] - 0.5 * (ab[c, :, :W] + tp[c])
+        upper[c, :, W:] = upper[c, :, W:] - 0.5 * ab[c, :, W:]
+        lower[c] = lower[c] - 0.5 * bt[c]
+        for copy in outs[c]:
+            copy.start()
+    for copy in outs[0] + outs[1]:
+        copy.wait()
 
 
 def finish_call(part, above, top, bot):
-    quarter = pl.BlockSpec((1, W, W), lambda c, q: (c, q // 2, q % 2))
-    plane = pl.BlockSpec((1, W, W), lambda c, q: (c, 0, 0))
+    any_ = pl.BlockSpec(memory_space=pl.ANY)
     return pl.pallas_call(
         finish_kernel,
-        grid=(2, 3),
         out_shape=jax.ShapeDtypeStruct((2, 512, 512), f32),
-        in_specs=[quarter, pl.BlockSpec((1, W, W), lambda c, q: (c, 0, q % 2)), plane, plane],
-        out_specs=quarter,
+        in_specs=[any_] * 4,
+        out_specs=any_,
+        scratch_shapes=[
+            pltpu.VMEM((2, W, 512), f32),
+            pltpu.VMEM((2, W, W), f32),
+            pltpu.VMEM((2, W, 512), f32),
+            pltpu.VMEM((2, W, W), f32),
+            pltpu.VMEM((2, W, W), f32),
+            pltpu.SemaphoreType.DMA((2, 7)),
+        ],
         input_output_aliases={0: 0},
         compiler_params=pltpu.CompilerParams(vmem_limit_bytes=8 * 2**20),
         name="finish",

time: 126 us -> 122 us (0.968)
  starting transfers between devices: 36.4 us -> 55.1 us
  Pallas kernels: 39.7 us -> 22.9 us
  waiting for transfers between devices: 20.4 us -> 16.6 us
  blocking collectives: 21.1 us -> 18.9 us
    pallas_call x1, Pallas kernels: 26.4 us -> 11.8 us  [main_call(): pl.pallas_call(main_kernel, out_shape=(S(2, 512, 512), S(2, 256, 256), S(...]
    ppermute x1, starting transfers between devices: 2.05 us -> 12 us  [shards(): corner_in = lax.ppermute(g_corner, rows, down)]
    ppermute x2, starting transfers between devices: 1.98 us -> 8.07 us  [swap_cores(): return lax.ppermute(value, 'core', [(0, 1), (1, 0)])]
    ppermute x3, starting transfers between devices: 4.5 us -> 7.55 us  [sum_everywhere(): lax.ppermute(value, axis, [(i, (i + k) % 4) for i in range(4)])]
    ppermute x1, starting transfers between devices: 4.69 us -> 2.03 us  [shards(): bot_in = lax.ppermute(g_bot, cols, to_right)]
    ppermute x1, starting transfers between devices: 1.95 us -> 4.6 us  [shards(): top_in = lax.ppermute(g_top + corner_in, cols, to_right)]
    all_to_all x1, waiting for transfers between devices: 9.73 us -> 7.09 us  [shards(): piece = lax.all_to_all(half, plane, 0, 0).sum(0)]
    all_to_all x1, blocking collectives: 21.1 us -> 18.9 us  [shards(): lax.all_to_all(jnp.broadcast_to(piece[None], half.shape), plane, 0, 0)]
  transfers between devices with their start and end apart: 14 -> 14, of which waited for: 5 -> 4; matrix products, arithmetic and copies ran while one was open for 3% -> 3% of each run, Pallas kernels for 9% -> 8%
where the time goes in v8:
time: 122 us; the launch traced here: 121 us
  starting transfers between devices  55.1 us (45%)
  Pallas kernels  22.9 us (19%)
  blocking collectives  18.9 us (15%)
  waiting for transfers between devices  16.6 us (14%)
  local copies, waits for them, and re-layouts  3.31 us (3%)
  other arithmetic  2.67 us (2%)
  between operations  1.54 us (1%)
    all_to_all x1, blocking collectives, shards(): lax.all_to_all(jnp.broadcast_to(piece[None], half.shape), plane, 0, 0)  18.9 us
    ppermute x1, starting transfers between devices, shards(): corner_in = lax.ppermute(g_corner, rows, down)  12 us
    pallas_call x1, Pallas kernels, main_call(): pl.pallas_call(main_kernel, out_shape=(S(2, 512, 512), S(2, 256, 256), S(...  11.8 us
    ppermute x2, starting transfers between devices, swap_cores(): return lax.ppermute(value, 'core', [(0, 1), (1, 0)])  8.07 us
    ppermute x3, starting transfers between devices, sum_everywhere(): lax.ppermute(value, axis, [(i, (i + k) % 4) for i in range(4)])  7.55 us
    all_to_all x1, starting transfers between devices, shards(): piece = lax.all_to_all(half, plane, 0, 0).sum(0)  7.45 us
    all_to_all x1, waiting for transfers between devices, shards(): piece = lax.all_to_all(half, plane, 0, 0).sum(0)  7.09 us
    pallas_call x1, Pallas kernels, prep_call(): pl.pallas_call(prep_kernel, grid=(8,), out_shape=jax.ShapeDtypeStruct((8,...  6.96 us
  transfers between devices with their start and end apart: 14, of which 4 were waited for; matrix products, arithmetic and copies ran while one was open for 3% of the time, Pallas kernels for 8%

profile of v8, /device:TPU:1, one launch (start us, length us, event | category | flops | bytes accessed | tf_op | source)
XLA Modules:
  0.0 121.0 jit_solution(17944931909307818347)
XLA Ops:
  0.6 0.0 copy-start.2
  0.6 2.4 %fusion = (f32[2,256,256]{2,1,0:T(8,128)}, f32[2,256,256]{2,1,0:T(8,128)}) fusion(f32[2,512,512]{2,1,0:T(8,128)} %obj.1), kind=kLoop, calls=%fused_computation.2 | loop fusion | bytes 2097152 | tf_op jit(solution)/shard_map/slice | solution.py:393
  3.1 1.3 %collective-permute-start = (f32[2,256,256]{2,1,0:T(8,128)}, f32[2,256,256]{2,1,0:T(8,128)S(1)}, u32[]{:S(2)}, u32[]{:S(2)}) collective-permute-start(f32[2,256,256]{2,1,0:T(8,128)} %get-tuple-element.29), channel_id=1, source_target_pairs={{1,0},{2,1},{3,2},{4,3},{5,4},{6,5},{7,6},{8,7},{9,8},{10,9},{11,1... | collective-permute-start | bytes 1572872 | tf_op jit(solution)/shard_map/ppermute | solution.py:391
  4.4 0.1 slice.11
  4.4 3.3 %collective-permute-start.2 = (f32[2,256,512]{2,1,0:T(8,128)S(1)}, f32[2,256,512]{2,1,0:T(8,128)S(1)}, u32[]{:S(2)}, u32[]{:S(2)}) collective-permute-start(f32[2,256,512]{2,1,0:T(8,128)S(1)} %slice.11), channel_id=1, source_target_pairs={{16,0},{32,16},{48,32},{64,48},{80,64},{96,80},{112,96},{17,1},{33... | collective-permute-start | bytes 3145736 | tf_op jit(solution)/shard_map/ppermute | solution.py:392
  7.8 0.0 copy-start.6
  7.8 1.3 %collective-permute-start.1 = (f32[2,256,256]{2,1,0:T(8,128)}, f32[2,256,256]{2,1,0:T(8,128)}, u32[]{:S(2)}, u32[]{:S(2)}) collective-permute-start(f32[2,256,256]{2,1,0:T(8,128)} %get-tuple-element.28), channel_id=1, source_target_pairs={{1,0},{2,1},{3,2},{4,3},{5,4},{6,5},{7,6},{8,7},{9,8},{10,9},{11,1... | collective-permute-start | bytes 1572872 | tf_op jit(solution)/shard_map/ppermute | solution.py:393
  9.1 7.0 %roots.1.sq = f32[8,256,256]{2,1,0:T(8,128)} custom-call(s32[8,256,256]{2,1,0:T(8,128)} %counts.1, bf16[256,256]{1,0:T(8,128)(2,1)} %constant.31.clone.pm, bf16[256,256]{1,0:T(8,128)(2,1)} %constant.32.clone.pmt), custom_call_target="tpu_custom_call" | custom-call | tf_op jit(solution)/shard_map/roots/pallas_call | solution.py:305
  16.0 3.2 %collective-permute-done.right_top = f32[2,256,256]{2,1,0:T(8,128)S(1)} collective-permute-done((f32[2,256,256]{2,1,0:T(8,128)}, f32[2,256,256]{2,1,0:T(8,128)S(1)}, u32[]{:S(2)}, u32[]{:S(2)}) %collective-permute-start) | collective-permute-done | bytes 524320 | tf_op jit(solution)/shard_map/ppermute | solution.py:391
  19.3 4.0 %collective-permute-start.3 = (f32[2,256,256]{2,1,0:T(8,128)S(1)}, f32[2,256,256]{2,1,0:T(8,128)}, u32[]{:S(2)}, u32[]{:S(2)}) collective-permute-start(f32[2,256,256]{2,1,0:T(8,128)S(1)} %collective-permute-done.right_top), channel_id=1, source_target_pairs={{16,0},{32,16},{48,32},{64,48},{80,64},{96,80},{112,96},{17,1},{33... | collective-permute-start | bytes 1572872 | tf_op jit(solution)/shard_map/ppermute | solution.py:396
  23.9 0.7 copy.11.offs
  24.6 0.7 pad_add_fusion.anchor.place
  25.2 5.4 %collective-permute-done.1.right_bot = f32[2,256,256]{2,1,0:T(8,128)} collective-permute-done((f32[2,256,256]{2,1,0:T(8,128)}, f32[2,256,256]{2,1,0:T(8,128)}, u32[]{:S(2)}, u32[]{:S(2)}) %collective-permute-start.1) | collective-permute-done | bytes 524320 | tf_op jit(solution)/shard_map/ppermute | solution.py:393
  30.6 0.9 collective-permute-done.3.corner
  31.5 0.1 copy-done.3
  31.6 11.8 %slots.1 = (f32[2,512,512]{2,1,0:T(8,128)}, f32[2,256,256]{2,1,0:T(8,128)}, f32[2,256,256]{2,1,0:T(8,128)}, f32[2,256,256]{2,1,0:T(8,128)}, f32[2,256,512]{2,1,0...) custom-call(s32[8,2]{1,0:T(8,128)} %copy.11.offs, s32[1]{0:T(128)} %bitcast.8.live, ...), custom_call_target="tpu_custom_call" | custom-call | tf_op jit(solution)/shard_map/slots/pallas_call | solution.py:268
  43.4 6.2 %collective-permute-start.5 = (f32[2,256,256]{2,1,0:T(8,128)}, f32[2,256,256]{2,1,0:T(8,128)S(1)}, u32[]{:S(2)}, u32[]{:S(2)}) collective-permute-start(f32[2,256,256]{2,1,0:T(8,128)} %get-tuple-element.20), channel_id=1, source_target_pairs={{0,16},{16,0},{1,17},{17,1},{2,18},{18,2},{3,19},{19,3},{4,20},{20... | collective-permute-start | bytes 1572872 | tf_op jit(solution)/shard_map/ppermute | solution.py:368
  49.6 12.0 %collective-permute-start.10 = (f32[2,256,256]{2,1,0:T(8,128)}, f32[2,256,256]{2,1,0:T(8,128)S(1)}, u32[]{:S(2)}, u32[]{:S(2)}) collective-permute-start(f32[2,256,256]{2,1,0:T(8,128)} %get-tuple-element.24), channel_id=1, source_target_pairs={{0,16},{16,32},{32,48},{48,64},{64,80},{80,96},{96,112},{1,17},{17... | collective-permute-start | bytes 1572872 | tf_op jit(solution)/shard_map/ppermute | solution.py:403
  61.6 2.0 %collective-permute-start.6 = (f32[2,256,256]{2,1,0:T(8,128)}, f32[2,256,256]{2,1,0:T(8,128)S(1)}, u32[]{:S(2)}, u32[]{:S(2)}) collective-permute-start(f32[2,256,256]{2,1,0:T(8,128)} %get-tuple-element.21), channel_id=1, source_target_pairs={{0,1},{1,2},{2,3},{3,4},{4,5},{5,6},{6,7},{7,8},{8,9},{9,10},{10,1... | collective-permute-start | bytes 1572872 | tf_op jit(solution)/shard_map/ppermute | solution.py:404
  63.7 0.0 collective-permute-done.5
  63.7 1.9 %add.23 = f32[2,256,256]{2,1,0:T(8,128)} add(f32[2,256,256]{2,1,0:T(8,128)} %get-tuple-element.19, f32[2,256,256]{2,1,0:T(8,128)S(1)} %collective-permute-done.5) | non-fusion elementwise | flops 131072 | bytes 1572864 | tf_op jit(solution)/shard_map/add | solution.py:406
  65.6 7.4 %all-to-all-start = ((f32[16,32,256]{2,1,0:T(8,128)}), f32[16,32,256]{2,1,0:T(8,128)S(1)}, u32[]{:S(2)}, u32[]{:S(2)}) async-start(f32[16,32,256]{2,1,0:T(8,128)} %bitcast.4), calls=%async_computation | async-start | bytes 1048576 | tf_op jit(solution)/shard_map/all_to_all | solution.py:409
  73.1 0.1 add.27
  73.1 4.6 %collective-permute-start.11 = (f32[2,256,256]{2,1,0:T(8,128)S(1)}, f32[2,256,256]{2,1,0:T(8,128)S(1)}, u32[]{:S(2)}, u32[]{:S(2)}) collective-permute-start(f32[2,256,256]{2,1,0:T(8,128)S(1)} %add.27), channel_id=1, source_target_pairs={{0,1},{1,2},{2,3},{3,4},{4,5},{5,6},{6,7},{7,8},{8,9},{9,10},{10,1... | collective-permute-start | bytes 1572872 | tf_op jit(solution)/shard_map/ppermute | solution.py:407
  77.7 7.1 %all-to-all-done = f32[16,32,256]{2,1,0:T(8,128)S(1)} async-done(((f32[16,32,256]{2,1,0:T(8,128)}), f32[16,32,256]{2,1,0:T(8,128)S(1)}, u32[]{:S(2)}, u32[]{:S(2)}) %all-to-all-start) | async-done | bytes 524320 | tf_op jit(solution)/shard_map/all_to_all | solution.py:409
  84.9 4.5 %collective-permute-start.9 = (f32[32,256]{1,0:T(8,128)S(1)}, f32[32,256]{1,0:T(8,128)S(1)}, u32[]{:S(2)}, u32[]{:S(2)}) collective-permute-start(f32[32,256]{1,0:T(8,128)S(1)} %reduce_sum.9), channel_id=1, source_target_pairs={{0,3},{1,0},{2,1},{3,2},{4,7},{5,4},{6,5},{7,6},{8,11},{9,8},{10,9... | collective-permute-start | bytes 98312 | tf_op jit(solution)/shard_map/ppermute | solution.py:372
  89.3 3.1 %collective-permute-start.7 = (f32[32,256]{1,0:T(8,128)S(1)}, f32[32,256]{1,0:T(8,128)S(1)}, u32[]{:S(2)}, u32[]{:S(2)}) collective-permute-start(f32[32,256]{1,0:T(8,128)S(1)} %reduce_sum.9), channel_id=1, source_target_pairs={{0,2},{1,3},{2,0},{3,1},{4,6},{5,7},{6,4},{7,5},{8,10},{9,11},{10,... | collective-permute-start | bytes 98312 | tf_op jit(solution)/shard_map/ppermute | solution.py:372
  92.4 3.5 %collective-permute-start.4 = (f32[2,256,512]{2,1,0:T(8,128)}, f32[2,256,512]{2,1,0:T(8,128)S(1)}, u32[]{:S(2)}, u32[]{:S(2)}) collective-permute-start(f32[2,256,512]{2,1,0:T(8,128)} %get-tuple-element.18), channel_id=1, source_target_pairs={{0,16},{16,32},{32,48},{48,64},{64,80},{80,96},{96,112},{1,17},{17... | collective-permute-start | bytes 3145736 | tf_op jit(solution)/shard_map/ppermute | solution.py:405
  96.0 18.9 %all_to_all.10 = f32[16,32,256]{2,1,0:T(8,128)S(1)} all-to-all(f32[16,32,256]{2,1,0:T(8,128)S(1)} %broadcast_in_dim.2), channel_id=1, replica_groups=mesh['y'=4,'core'=2,'x'=4,'z'=4] {'y','x'}, dimensions={0} | all-to-all | bytes 1048576 | tf_op jit(solution)/shard_map/all_to_all | solution.py:414
  115.0 1.9 %collective-permute-start.12 = (f32[512,256]{1,0:T(8,128)S(1)}, f32[512,256]{1,0:T(8,128)S(1)}, u32[]{:S(2)}, u32[]{:S(2)}) collective-permute-start(f32[512,256]{1,0:T(8,128)S(1)} %bitcast.10), channel_id=1, source_target_pairs={{0,16},{16,0},{1,17},{17,1},{2,18},{18,2},{3,19},{19,3},{4,20},{20... | collective-permute-start | bytes 1572872 | tf_op jit(solution)/shard_map/ppermute | solution.py:368
  116.8 2.5 %finish.1 = f32[2,512,512]{2,1,0:T(8,128)} custom-call(f32[2,512,512]{2,1,0:T(8,128)} %get-tuple-element.17.part, f32[2,256,512]{2,1,0:T(8,128)S(1)} %collective-permute-done.4.above, f32[2,256,256]{2,1,0:T(8,128)S(1)} %collective-permute-done.11.top, f32[2,256,256]{2,1,0:T(8,128)S(1)} %collective-permute-done.6.bot), custom_call_target="tpu_custom_call", output_to_operand_aliasing={{}: (0, {})} | custom-call | tf_op jit(solution)/shard_map/finish/pallas_call | solution.py:348
  119.4 1.6 %probe.3 = f32[1024,256]{1,0:T(8,128)} custom-call(s32[3]{0:T(128)S(1)} %copy-done.1, f32[1024,256]{1,0:T(8,128)S(1)} %bitcast.9, f32[512,256]{1,0:T(8,128)S(1)} %bitcast.11, f32[512,256]{1,0:T(8,128)S(1)} %collective-permute-done.12.rest), custom_call_target="tpu_custom_call" | custom-call | tf_op jit(solution)/shard_map/probe/pallas_call | solution.py:418
  (24 shorter events, 0.1 us)
Async XLA Ops:
  0.6 3.7 %copy-start.2 = (f32[2,512,512]{2,1,0:T(8,128)S(1)}, f32[2,512,512]{2,1,0:T(8,128)}, u32[]{:S(2)}) copy-start(f32[2,512,512]{2,1,0:T(8,128)} %obj.1) | copy-start | bytes 6291460
  3.1 16.2 %collective-permute-start = (f32[2,256,256]{2,1,0:T(8,128)}, f32[2,256,256]{2,1,0:T(8,128)S(1)}, u32[]{:S(2)}, u32[]{:S(2)}) collective-permute-start(f32[2,256,256]{2,1,0:T(8,128)} %get-tuple-element.29), channel_id=1, source_target_pairs={{1,0},{2,1},{3,2},{4,3},{5,4},{6,5},{7,6},{8,7},{9,8},{10,9},{11,1... | collective-permute-start | bytes 1572872 | tf_op jit(solution)/shard_map/ppermute | solution.py:391
  4.4 26.2 %collective-permute-start.2 = (f32[2,256,512]{2,1,0:T(8,128)S(1)}, f32[2,256,512]{2,1,0:T(8,128)S(1)}, u32[]{:S(2)}, u32[]{:S(2)}) collective-permute-start(f32[2,256,512]{2,1,0:T(8,128)S(1)} %slice.11), channel_id=1, source_target_pairs={{16,0},{32,16},{48,32},{64,48},{80,64},{96,80},{112,96},{17,1},{33... | collective-permute-start | bytes 3145736 | tf_op jit(solution)/shard_map/ppermute | solution.py:392
  7.8 16.1 %copy-start.6 = (s32[8,2]{0,1:T(2,128)S(1)}, s32[8,2]{0,1:T(2,128)}, u32[]{:S(2)}) copy-start(s32[8,2]{0,1:T(2,128)} %param.10) | copy-start | bytes 196
  7.8 22.8 %collective-permute-start.1 = (f32[2,256,256]{2,1,0:T(8,128)}, f32[2,256,256]{2,1,0:T(8,128)}, u32[]{:S(2)}, u32[]{:S(2)}) collective-permute-start(f32[2,256,256]{2,1,0:T(8,128)} %get-tuple-element.28), channel_id=1, source_target_pairs={{1,0},{2,1},{3,2},{4,3},{5,4},{6,5},{7,6},{8,7},{9,8},{10,9},{11,1... | collective-permute-start | bytes 1572872 | tf_op jit(solution)/shard_map/ppermute | solution.py:393
  19.3 12.2 %copy-start.4 = (f32[2,256,256]{2,1,0:T(8,128)}, f32[2,256,256]{2,1,0:T(8,128)S(1)}, u32[]{:S(2)}) copy-start(f32[2,256,256]{2,1,0:T(8,128)S(1)} %collective-permute-done.right_top) | copy-start | bytes 1572868
  19.3 12.2 %collective-permute-start.3 = (f32[2,256,256]{2,1,0:T(8,128)S(1)}, f32[2,256,256]{2,1,0:T(8,128)}, u32[]{:S(2)}, u32[]{:S(2)}) collective-permute-start(f32[2,256,256]{2,1,0:T(8,128)S(1)} %collective-permute-done.right_top), channel_id=1, source_target_pairs={{16,0},{32,16},{48,32},{64,48},{80,64},{96,80},{112,96},{17,1},{33... | collective-permute-start | bytes 1572872 | tf_op jit(solution)/shard_map/ppermute | solution.py:396
  30.6 1.0 copy-start.3
  43.4 29.7 %copy-start.5 = (f32[2,256,256]{2,1,0:T(8,128)S(1)}, f32[2,256,256]{2,1,0:T(8,128)}, u32[]{:S(2)}) copy-start(f32[2,256,256]{2,1,0:T(8,128)} %get-tuple-element.23) | copy-start | bytes 1572868
  43.4 20.3 %collective-permute-start.5 = (f32[2,256,256]{2,1,0:T(8,128)}, f32[2,256,256]{2,1,0:T(8,128)S(1)}, u32[]{:S(2)}, u32[]{:S(2)}) collective-permute-start(f32[2,256,256]{2,1,0:T(8,128)} %get-tuple-element.20), channel_id=1, source_target_pairs={{0,16},{16,0},{1,17},{17,1},{2,18},{18,2},{3,19},{19,3},{4,20},{20... | collective-permute-start | bytes 1572872 | tf_op jit(solution)/shard_map/ppermute | solution.py:368
  49.6 23.4 %collective-permute-start.10 = (f32[2,256,256]{2,1,0:T(8,128)}, f32[2,256,256]{2,1,0:T(8,128)S(1)}, u32[]{:S(2)}, u32[]{:S(2)}) collective-permute-start(f32[2,256,256]{2,1,0:T(8,128)} %get-tuple-element.24), channel_id=1, source_target_pairs={{0,16},{16,32},{32,48},{48,64},{64,80},{80,96},{96,112},{1,17},{17... | collective-permute-start | bytes 1572872 | tf_op jit(solution)/shard_map/ppermute | solution.py:403
  61.6 23.2 %collective-permute-start.6 = (f32[2,256,256]{2,1,0:T(8,128)}, f32[2,256,256]{2,1,0:T(8,128)S(1)}, u32[]{:S(2)}, u32[]{:S(2)}) collective-permute-start(f32[2,256,256]{2,1,0:T(8,128)} %get-tuple-element.21), channel_id=1, source_target_pairs={{0,1},{1,2},{2,3},{3,4},{4,5},{5,6},{6,7},{7,8},{8,9},{9,10},{10,1... | collective-permute-start | bytes 1572872 | tf_op jit(solution)/shard_map/ppermute | solution.py:404
  65.6 19.2 %all-to-all-start = ((f32[16,32,256]{2,1,0:T(8,128)}), f32[16,32,256]{2,1,0:T(8,128)S(1)}, u32[]{:S(2)}, u32[]{:S(2)}) async-start(f32[16,32,256]{2,1,0:T(8,128)} %bitcast.4), calls=%async_computation | async-start | bytes 1048576 | tf_op jit(solution)/shard_map/all_to_all | solution.py:409
  73.1 22.8 %collective-permute-start.11 = (f32[2,256,256]{2,1,0:T(8,128)S(1)}, f32[2,256,256]{2,1,0:T(8,128)S(1)}, u32[]{:S(2)}, u32[]{:S(2)}) collective-permute-start(f32[2,256,256]{2,1,0:T(8,128)S(1)} %add.27), channel_id=1, source_target_pairs={{0,1},{1,2},{2,3},{3,4},{4,5},{5,6},{6,7},{7,8},{8,9},{9,10},{10,1... | collective-permute-start | bytes 1572872 | tf_op jit(solution)/shard_map/ppermute | solution.py:407
  84.9 11.0 %collective-permute-start.9 = (f32[32,256]{1,0:T(8,128)S(1)}, f32[32,256]{1,0:T(8,128)S(1)}, u32[]{:S(2)}, u32[]{:S(2)}) collective-permute-start(f32[32,256]{1,0:T(8,128)S(1)} %reduce_sum.9), channel_id=1, source_target_pairs={{0,3},{1,0},{2,1},{3,2},{4,7},{5,4},{6,5},{7,6},{8,11},{9,8},{10,9... | collective-permute-start | bytes 98312 | tf_op jit(solution)/shard_map/ppermute | solution.py:372
  89.3 6.6 %collective-permute-start.8 = (f32[32,256]{1,0:T(8,128)S(1)}, f32[32,256]{1,0:T(8,128)S(1)}, u32[]{:S(2)}, u32[]{:S(2)}) collective-permute-start(f32[32,256]{1,0:T(8,128)S(1)} %reduce_sum.9), channel_id=1, source_target_pairs={{0,1},{1,2},{2,3},{3,0},{4,5},{5,6},{6,7},{7,4},{8,9},{9,10},{10,1... | collective-permute-start | bytes 98312 | tf_op jit(solution)/shard_map/ppermute | solution.py:372
  89.3 6.6 %collective-permute-start.7 = (f32[32,256]{1,0:T(8,128)S(1)}, f32[32,256]{1,0:T(8,128)S(1)}, u32[]{:S(2)}, u32[]{:S(2)}) collective-permute-start(f32[32,256]{1,0:T(8,128)S(1)} %reduce_sum.9), channel_id=1, source_target_pairs={{0,2},{1,3},{2,0},{3,1},{4,6},{5,7},{6,4},{7,5},{8,10},{9,11},{10,... | collective-permute-start | bytes 98312 | tf_op jit(solution)/shard_map/ppermute | solution.py:372
  92.4 24.4 %collective-permute-start.4 = (f32[2,256,512]{2,1,0:T(8,128)}, f32[2,256,512]{2,1,0:T(8,128)S(1)}, u32[]{:S(2)}, u32[]{:S(2)}) collective-permute-start(f32[2,256,512]{2,1,0:T(8,128)} %get-tuple-element.18), channel_id=1, source_target_pairs={{0,16},{16,32},{32,48},{48,64},{64,80},{80,96},{96,112},{1,17},{17... | collective-permute-start | bytes 3145736 | tf_op jit(solution)/shard_map/ppermute | solution.py:405
  115.0 4.4 %collective-permute-start.12 = (f32[512,256]{1,0:T(8,128)S(1)}, f32[512,256]{1,0:T(8,128)S(1)}, u32[]{:S(2)}, u32[]{:S(2)}) collective-permute-start(f32[512,256]{1,0:T(8,128)S(1)} %bitcast.10), channel_id=1, source_target_pairs={{0,16},{16,0},{1,17},{17,1},{2,18},{18,2},{3,19},{19,3},{4,20},{20... | collective-permute-start | bytes 1572872 | tf_op jit(solution)/shard_map/ppermute | solution.py:368
  116.8 2.6 %copy-start = (f32[2,2,256,256]{3,2,1,0:T(8,128)S(1)}, f32[2,2,256,256]{3,2,1,0:T(8,128)}, u32[]{:S(2)}) copy-start(f32[2,2,256,256]{3,2,1,0:T(8,128)} %probe.2) | copy-start | bytes 3145732
  116.8 2.6 %copy-start.1 = (s32[3]{0:T(128)S(1)}, s32[3]{0:T(128)}, u32[]{:S(2)}) copy-start(s32[3]{0:T(128)} %pad_add_fusion.anchor.place) | copy-start | bytes 40

commit v9 on v8

--- a/solution.py
+++ b/solution.py
@@ -364,6 +364,29 @@
     )(part, above, top, bot)
 
 
+def edges_kernel(obj, o_top, o_bot, o_below, sems):
+    moves = [(obj.at[:, 0:W, 0:W], o_top), (obj.at[:, W:, 0:W], o_bot), (obj.at[:, 0:W], o_below)]
+    copies = [pltpu.make_async_copy(s, d, sems.at[i]) for i, (s, d) in enumerate(moves)]
+    for copy in copies:
+        copy.start()
+    for copy in copies:
+        copy.wait()
+
+
+def edges_call(obj):
+    any_ = pl.BlockSpec(memory_space=pl.ANY)
+    S = lambda *s: jax.ShapeDtypeStruct(s, f32)
+    return pl.pallas_call(
+        edges_kernel,
+        out_shape=(S(2, W, W), S(2, W, W), S(2, W, 512)),
+        in_specs=[any_],
+        out_specs=[any_] * 3,
+        scratch_shapes=[pltpu.SemaphoreType.DMA((3,))],
+        compiler_params=pltpu.CompilerParams(vmem_limit_bytes=62 * 2**20),
+        name="edges",
+    )(obj)
+
+
 def swap_cores(value):
     return lax.ppermute(value, "core", [(0, 1), (1, 0)])
 
@@ -388,9 +411,10 @@
     to_left = [(i, i - 1) for i in range(1, n_col)]
     to_right = [(i - 1, i) for i in range(1, n_col)]
 
-    right_top = lax.ppermute(object_planes[:, :W, :W], cols, to_left)
-    below = lax.ppermute(object_planes[:, :W, :], rows, up)
-    right_bot = lax.ppermute(object_planes[:, W:, :W], cols, to_left)
+    edge_top, edge_bot, edge_below = edges_call(object_planes)
+    right_top = lax.ppermute(edge_top, cols, to_left)
+    below = lax.ppermute(edge_below, rows, up)
+    right_bot = lax.ppermute(edge_bot, cols, to_left)
     roots = prep_call(photon_counts)
     right_top, roots = lax.optimization_barrier((right_top, roots))
     corner = lax.ppermute(right_top, rows, up)
@@ -409,10 +433,10 @@
     piece = lax.all_to_all(half, plane, 0, 0).sum(0)
     piece, bot_in = lax.optimization_barrier((piece, bot_in))
     piece = sum_everywhere(piece, "z")
-    piece, top_in = lax.optimization_barrier((piece, top_in))
+    half = lax.all_to_all(jnp.broadcast_to(piece[None], half.shape), plane, 0, 0).reshape(512, W)
+    half, top_in = lax.optimization_barrier((half, top_in))
+    rest = swap_cores(half)
     new_object = finish_call(part, above_in, top_in, bot_in)
-    half = lax.all_to_all(jnp.broadcast_to(piece[None], half.shape), plane, 0, 0).reshape(512, W)
-    rest = swap_cores(half)
     smem, vmem = pl.BlockSpec(memory_space=pltpu.SMEM), pl.BlockSpec(memory_space=pltpu.VMEM)
     step = 1.0 / math.sqrt(offsets.shape[0] * n_row * n_col)
     new_probe = pl.pallas_call(

time: 122 us -> 183 us (1.50)
  Pallas kernels: 22.9 us -> 102 us
  blocking collectives: 18.9 us -> 0 us
  waiting for transfers between devices: 16.6 us -> 27.4 us
  starting transfers between devices: 55.1 us -> 45 us
    pallas_call x0 -> x1, Pallas kernels: none -> 64.7 us  [edges_call(): pl.pallas_call(edges_kernel, out_shape=(S(2, W, W), S(2, W, W), S(2, W, 5...]
    all_to_all x1 -> x0, blocking collectives: 18.9 us -> none  [shards(): lax.all_to_all(jnp.broadcast_to(piece[None], half.shape), plane, 0, 0)]
    pallas_call x1, Pallas kernels: 11.8 us -> 26.4 us  [main_call(): pl.pallas_call(main_kernel, out_shape=(S(2, 512, 512), S(2, 256, 256), S(...]
    ppermute x1, starting transfers between devices: 12 us -> 4.31 us  [shards(): corner_in = lax.ppermute(g_corner, rows, down)]
    ppermute x2, starting transfers between devices: 8.07 us -> 1.73 us  [swap_cores(): return lax.ppermute(value, 'core', [(0, 1), (1, 0)])]
    ppermute x1, waiting for transfers between devices: 0.01 us -> 6.33 us  [shards(): top_in = lax.ppermute(g_top + corner_in, cols, to_right)]
    all_to_all x0 -> x1, waiting for transfers between devices: none -> 5.04 us  [shards(): lax.all_to_all(jnp.broadcast_to(piece[None], half.shape), plane, 0, 0)]
    all_to_all x0 -> x1, starting transfers between devices: none -> 3.63 us  [shards(): lax.all_to_all(jnp.broadcast_to(piece[None], half.shape), plane, 0, 0)]
  transfers between devices with their start and end apart: 14 -> 15, of which waited for: 4 -> 7; matrix products, arithmetic and copies ran while one was open for 3% -> 2% of each run, Pallas kernels for 8% -> 5%
where the time goes in v9:
time: 183 us; the launch traced here: 182 us
  Pallas kernels  102 us (56%)
  starting transfers between devices  45 us (25%)
  waiting for transfers between devices  27.4 us (15%)
  local copies, waits for them, and re-layouts  3.31 us (2%)
  other arithmetic  2.67 us (1%)
    pallas_call x1, Pallas kernels, edges_call(): pl.pallas_call(edges_kernel, out_shape=(S(2, W, W), S(2, W, W), S(2, W, 5...  64.7 us
    pallas_call x1, Pallas kernels, main_call(): pl.pallas_call(main_kernel, out_shape=(S(2, 512, 512), S(2, 256, 256), S(...  26.4 us
    all_to_all x1, starting transfers between devices, shards(): piece = lax.all_to_all(half, plane, 0, 0).sum(0)  8.56 us
    pallas_call x1, Pallas kernels, prep_call(): pl.pallas_call(prep_kernel, grid=(8,), out_shape=jax.ShapeDtypeStruct((8,...  6.96 us
    ppermute x3, starting transfers between devices, sum_everywhere(): lax.ppermute(value, axis, [(i, (i + k) % 4) for i in range(4)])  6.64 us
    ppermute x1, waiting for transfers between devices, shards(): top_in = lax.ppermute(g_top + corner_in, cols, to_right)  6.33 us
    all_to_all x1, waiting for transfers between devices, shards(): piece = lax.all_to_all(half, plane, 0, 0).sum(0)  6.13 us
    ppermute x1, waiting for transfers between devices, shards(): right_bot = lax.ppermute(edge_bot, cols, to_left)  5.24 us
  transfers between devices with their start and end apart: 15, of which 7 were waited for; matrix products, arithmetic and copies ran while one was open for 2% of the time, Pallas kernels for 5%

profile of v9, /device:TPU:1, one launch (start us, length us, event | category | flops | bytes accessed | tf_op | source)
XLA Modules:
  0.0 182.0 jit_solution(2556109172612658935)
XLA Ops:
  0.6 64.7 %edges.1 = (f32[2,256,256]{2,1,0:T(8,128)}, f32[2,256,256]{2,1,0:T(8,128)}, f32[2,256,512]{2,1,0:T(8,128)}) custom-call(f32[2,512,512]{2,1,0:T(8,128)} %obj.3), custom_call_target="tpu_custom_call" | custom-call | tf_op jit(solution)/shard_map/edges/pallas_call | solution.py:379
  65.3 1.3 collective-permute-start
  66.6 3.3 %collective-permute-start.2 = (f32[2,256,512]{2,1,0:T(8,128)}, f32[2,256,512]{2,1,0:T(8,128)S(1)}, u32[]{:S(2)}, u32[]{:S(2)}) collective-permute-start(f32[2,256,512]{2,1,0:T(8,128)} %get-tuple-element.21), channel_id=1, source_target_pairs={{16,0},{32,16},{48,32},{64,48},{80,64},{96,80},{112,96},{17,1},{33... | collective-permute-start | bytes 3145736 | tf_op jit(solution)/shard_map/ppermute | solution.py:416
  69.9 1.3 collective-permute-start.1
  71.2 7.0 %roots.1.sq = f32[8,256,256]{2,1,0:T(8,128)} custom-call(s32[8,256,256]{2,1,0:T(8,128)} %counts.1, bf16[256,256]{1,0:T(8,128)(2,1)} %constant.31.clone.pm, bf16[256,256]{1,0:T(8,128)(2,1)} %constant.32.clone.pmt), custom_call_target="tpu_custom_call" | custom-call | tf_op jit(solution)/shard_map/roots/pallas_call | solution.py:305
  78.2 3.3 %collective-permute-done.right_top = f32[2,256,256]{2,1,0:T(8,128)S(1)} collective-permute-done((f32[2,256,256]{2,1,0:T(8,128)}, f32[2,256,256]{2,1,0:T(8,128)S(1)}, u32[]{:S(2)}, u32[]{:S(2)}) %collective-permute-start) | collective-permute-done | bytes 524320 | tf_op jit(solution)/shard_map/ppermute | solution.py:415
  81.5 4.0 %collective-permute-start.3 = (f32[2,256,256]{2,1,0:T(8,128)S(1)}, f32[2,256,256]{2,1,0:T(8,128)S(1)}, u32[]{:S(2)}, u32[]{:S(2)}) collective-permute-start(f32[2,256,256]{2,1,0:T(8,128)S(1)} %collective-permute-done.right_top), channel_id=1, source_target_pairs={{16,0},{32,16},{48,32},{64,48},{80,64},{96,80},{112,96},{17,1},{33... | collective-permute-start | bytes 1572872 | tf_op jit(solution)/shard_map/ppermute | solution.py:420
  86.2 0.7 copy.11.offs
  86.8 0.7 pad_add_fusion.anchor.place
  87.5 5.2 %collective-permute-done.1.right_bot = f32[2,256,256]{2,1,0:T(8,128)S(1)} collective-permute-done((f32[2,256,256]{2,1,0:T(8,128)}, f32[2,256,256]{2,1,0:T(8,128)S(1)}, u32[]{:S(2)}, u32[]{:S(2)}) %collective-permute-start.1) | collective-permute-done | bytes 524320 | tf_op jit(solution)/shard_map/ppermute | solution.py:417
  92.7 0.9 collective-permute-done.3.corner
  93.6 0.8 copy-done.5
  94.4 1.0 copy-done.2
  95.4 26.4 %slots.1 = (f32[2,512,512]{2,1,0:T(8,128)}, f32[2,256,256]{2,1,0:T(8,128)}, f32[2,256,256]{2,1,0:T(8,128)}, f32[2,256,256]{2,1,0:T(8,128)}, f32[2,256,512]{2,1,0...) custom-call(s32[8,2]{1,0:T(8,128)} %copy.11.offs, s32[1]{0:T(128)} %bitcast.8.live, ...), custom_call_target="tpu_custom_call" | custom-call | tf_op jit(solution)/shard_map/slots/pallas_call | solution.py:268
  121.8 0.6 collective-permute-start.5
  122.5 1.3 collective-permute-start.6
  123.8 0.4 collective-permute-done.5
  124.2 1.9 %add.23 = f32[2,256,256]{2,1,0:T(8,128)} add(f32[2,256,256]{2,1,0:T(8,128)} %get-tuple-element.25, f32[2,256,256]{2,1,0:T(8,128)S(1)} %collective-permute-done.5) | non-fusion elementwise | flops 131072 | bytes 1572864 | tf_op jit(solution)/shard_map/add | solution.py:430
  126.1 8.6 %all-to-all-start = ((f32[16,32,256]{2,1,0:T(8,128)}), f32[16,32,256]{2,1,0:T(8,128)S(1)}, u32[]{:S(2)}, u32[]{:S(2)}) async-start(f32[16,32,256]{2,1,0:T(8,128)} %bitcast.4), calls=%async_computation | async-start | bytes 1048576 | tf_op jit(solution)/shard_map/all_to_all | solution.py:433
  134.7 4.3 %collective-permute-start.10 = (f32[2,256,256]{2,1,0:T(8,128)S(1)}, f32[2,256,256]{2,1,0:T(8,128)S(1)}, u32[]{:S(2)}, u32[]{:S(2)}) collective-permute-start(f32[2,256,256]{2,1,0:T(8,128)S(1)} %copy-done.8), channel_id=1, source_target_pairs={{0,16},{16,32},{32,48},{48,64},{64,80},{80,96},{96,112},{1,17},{17... | collective-permute-start | bytes 1572872 | tf_op jit(solution)/shard_map/ppermute | solution.py:427
  139.0 6.1 %all-to-all-done = f32[16,32,256]{2,1,0:T(8,128)S(1)} async-done(((f32[16,32,256]{2,1,0:T(8,128)}), f32[16,32,256]{2,1,0:T(8,128)S(1)}, u32[]{:S(2)}, u32[]{:S(2)}) %all-to-all-start) | async-done | bytes 524320 | tf_op jit(solution)/shard_map/all_to_all | solution.py:433
  145.2 5.4 %collective-permute-start.9 = (f32[32,256]{1,0:T(8,128)S(1)}, f32[32,256]{1,0:T(8,128)S(1)}, u32[]{:S(2)}, u32[]{:S(2)}) collective-permute-start(f32[32,256]{1,0:T(8,128)S(1)} %reduce_sum.9), channel_id=1, source_target_pairs={{0,3},{1,0},{2,1},{3,2},{4,7},{5,4},{6,5},{7,6},{8,11},{9,8},{10,9... | collective-permute-start | bytes 98312 | tf_op jit(solution)/shard_map/ppermute | solution.py:395
  150.6 1.3 collective-permute-start.7
  151.8 4.7 %collective-permute-start.4 = (f32[2,256,512]{2,1,0:T(8,128)}, f32[2,256,512]{2,1,0:T(8,128)S(1)}, u32[]{:S(2)}, u32[]{:S(2)}) collective-permute-start(f32[2,256,512]{2,1,0:T(8,128)} %get-tuple-element.24), channel_id=1, source_target_pairs={{0,16},{16,32},{32,48},{48,64},{64,80},{80,96},{96,112},{1,17},{17... | collective-permute-start | bytes 3145736 | tf_op jit(solution)/shard_map/ppermute | solution.py:429
  156.6 4.2 %collective-permute-start.11 = (f32[2,256,256]{2,1,0:T(8,128)S(1)}, f32[2,256,256]{2,1,0:T(8,128)S(1)}, u32[]{:S(2)}, u32[]{:S(2)}) collective-permute-start(f32[2,256,256]{2,1,0:T(8,128)S(1)} %add.27), channel_id=1, source_target_pairs={{0,1},{1,2},{2,3},{3,4},{4,5},{5,6},{6,7},{7,8},{8,9},{9,10},{10,1... | collective-permute-start | bytes 1572872 | tf_op jit(solution)/shard_map/ppermute | solution.py:431
  160.9 0.8 broadcast_in_dim.2
  161.7 3.6 %all-to-all-start.1 = ((f32[16,32,256]{2,1,0:T(8,128)}), f32[16,32,256]{2,1,0:T(8,128)S(1)}, u32[]{:S(2)}, u32[]{:S(2)}) async-start(f32[16,32,256]{2,1,0:T(8,128)} %broadcast_in_dim.2), calls=%async_computation.1 | async-start | bytes 1048576 | tf_op jit(solution)/shard_map/all_to_all | solution.py:436
  165.3 6.3 %collective-permute-done.11.top = f32[2,256,256]{2,1,0:T(8,128)S(1)} collective-permute-done((f32[2,256,256]{2,1,0:T(8,128)S(1)}, f32[2,256,256]{2,1,0:T(8,128)S(1)}, u32[]{:S(2)}, u32[]{:S(2)}) %collective-permute-start.11) | collective-permute-done | bytes 524320 | tf_op jit(solution)/shard_map/ppermute | solution.py:431
  171.7 5.0 %all-to-all-done.1 = f32[16,32,256]{2,1,0:T(8,128)S(1)} async-done(((f32[16,32,256]{2,1,0:T(8,128)}), f32[16,32,256]{2,1,0:T(8,128)S(1)}, u32[]{:S(2)}, u32[]{:S(2)}) %all-to-all-start.1) | async-done | bytes 524320 | tf_op jit(solution)/shard_map/all_to_all | solution.py:436
  176.7 1.1 collective-permute-start.12
  177.8 2.5 %finish.1 = f32[2,512,512]{2,1,0:T(8,128)} custom-call(f32[2,512,512]{2,1,0:T(8,128)} %get-tuple-element.23.part, f32[2,256,512]{2,1,0:T(8,128)S(1)} %collective-permute-done.4.above, f32[2,256,256]{2,1,0:T(8,128)S(1)} %collective-permute-done.11.top, f32[2,256,256]{2,1,0:T(8,128)S(1)} %collective-permute-done.6.bot), custom_call_target="tpu_custom_call", output_to_operand_aliasing={{}: (0, {})} | custom-call | tf_op jit(solution)/shard_map/finish/pallas_call | solution.py:348
  180.4 1.6 probe.3
  (28 shorter events, 0.2 us)
Async XLA Ops:
  65.3 16.2 %collective-permute-start = (f32[2,256,256]{2,1,0:T(8,128)}, f32[2,256,256]{2,1,0:T(8,128)S(1)}, u32[]{:S(2)}, u32[]{:S(2)}) collective-permute-start(f32[2,256,256]{2,1,0:T(8,128)} %get-tuple-element.18), channel_id=1, source_target_pairs={{1,0},{2,1},{3,2},{4,3},{5,4},{6,5},{7,6},{8,7},{9,8},{10,9},{11,1... | collective-permute-start | bytes 1572872 | tf_op jit(solution)/shard_map/ppermute | solution.py:415
  66.6 27.0 %collective-permute-start.2 = (f32[2,256,512]{2,1,0:T(8,128)}, f32[2,256,512]{2,1,0:T(8,128)S(1)}, u32[]{:S(2)}, u32[]{:S(2)}) collective-permute-start(f32[2,256,512]{2,1,0:T(8,128)} %get-tuple-element.21), channel_id=1, source_target_pairs={{16,0},{32,16},{48,32},{64,48},{80,64},{96,80},{112,96},{17,1},{33... | collective-permute-start | bytes 3145736 | tf_op jit(solution)/shard_map/ppermute | solution.py:416
  69.9 16.2 %copy-start.7 = (s32[8,2]{0,1:T(2,128)S(1)}, s32[8,2]{0,1:T(2,128)}, u32[]{:S(2)}) copy-start(s32[8,2]{0,1:T(2,128)} %param.10) | copy-start | bytes 196
  69.9 22.8 %collective-permute-start.1 = (f32[2,256,256]{2,1,0:T(8,128)}, f32[2,256,256]{2,1,0:T(8,128)S(1)}, u32[]{:S(2)}, u32[]{:S(2)}) collective-permute-start(f32[2,256,256]{2,1,0:T(8,128)} %get-tuple-element.20), channel_id=1, source_target_pairs={{1,0},{2,1},{3,2},{4,3},{5,4},{6,5},{7,6},{8,7},{9,8},{10,9},{11,1... | collective-permute-start | bytes 1572872 | tf_op jit(solution)/shard_map/ppermute | solution.py:417
  81.5 12.9 %copy-start.3 = (f32[2,256,256]{2,1,0:T(8,128)}, f32[2,256,256]{2,1,0:T(8,128)S(1)}, u32[]{:S(2)}) copy-start(f32[2,256,256]{2,1,0:T(8,128)S(1)} %collective-permute-done.right_top) | copy-start | bytes 1572868
  81.5 12.1 %collective-permute-start.3 = (f32[2,256,256]{2,1,0:T(8,128)S(1)}, f32[2,256,256]{2,1,0:T(8,128)S(1)}, u32[]{:S(2)}, u32[]{:S(2)}) collective-permute-start(f32[2,256,256]{2,1,0:T(8,128)S(1)} %collective-permute-done.right_top), channel_id=1, source_target_pairs={{16,0},{32,16},{48,32},{64,48},{80,64},{96,80},{112,96},{17,1},{33... | collective-permute-start | bytes 1572872 | tf_op jit(solution)/shard_map/ppermute | solution.py:420
  92.7 0.9 copy-start.4
  93.6 0.8 copy-start.5
  94.4 1.0 copy-start.2
  121.8 12.9 %copy-start.8 = (f32[2,256,256]{2,1,0:T(8,128)S(1)}, f32[2,256,256]{2,1,0:T(8,128)}, u32[]{:S(2)}) copy-start(f32[2,256,256]{2,1,0:T(8,128)} %get-tuple-element.30) | copy-start | bytes 1572868
  121.8 34.7 %copy-start.6 = (f32[2,256,256]{2,1,0:T(8,128)S(1)}, f32[2,256,256]{2,1,0:T(8,128)}, u32[]{:S(2)}) copy-start(f32[2,256,256]{2,1,0:T(8,128)} %get-tuple-element.29) | copy-start | bytes 1572868
  121.8 2.4 %collective-permute-start.5 = (f32[2,256,256]{2,1,0:T(8,128)}, f32[2,256,256]{2,1,0:T(8,128)S(1)}, u32[]{:S(2)}, u32[]{:S(2)}) collective-permute-start(f32[2,256,256]{2,1,0:T(8,128)} %get-tuple-element.26), channel_id=1, source_target_pairs={{0,16},{16,0},{1,17},{17,1},{2,18},{18,2},{3,19},{19,3},{4,20},{20... | collective-permute-start | bytes 1572872 | tf_op jit(solution)/shard_map/ppermute | solution.py:391
  122.5 22.7 %collective-permute-start.6 = (f32[2,256,256]{2,1,0:T(8,128)}, f32[2,256,256]{2,1,0:T(8,128)S(1)}, u32[]{:S(2)}, u32[]{:S(2)}) collective-permute-start(f32[2,256,256]{2,1,0:T(8,128)} %get-tuple-element.27), channel_id=1, source_target_pairs={{0,1},{1,2},{2,3},{3,4},{4,5},{5,6},{6,7},{7,8},{8,9},{9,10},{10,1... | collective-permute-start | bytes 1572872 | tf_op jit(solution)/shard_map/ppermute | solution.py:428
  126.1 19.0 %all-to-all-start = ((f32[16,32,256]{2,1,0:T(8,128)}), f32[16,32,256]{2,1,0:T(8,128)S(1)}, u32[]{:S(2)}, u32[]{:S(2)}) async-start(f32[16,32,256]{2,1,0:T(8,128)} %bitcast.4), calls=%async_computation | async-start | bytes 1048576 | tf_op jit(solution)/shard_map/all_to_all | solution.py:433
  134.7 21.8 %collective-permute-start.10 = (f32[2,256,256]{2,1,0:T(8,128)S(1)}, f32[2,256,256]{2,1,0:T(8,128)S(1)}, u32[]{:S(2)}, u32[]{:S(2)}) collective-permute-start(f32[2,256,256]{2,1,0:T(8,128)S(1)} %copy-done.8), channel_id=1, source_target_pairs={{0,16},{16,32},{32,48},{48,64},{64,80},{80,96},{96,112},{1,17},{17... | collective-permute-start | bytes 1572872 | tf_op jit(solution)/shard_map/ppermute | solution.py:427
  145.2 15.6 %collective-permute-start.9 = (f32[32,256]{1,0:T(8,128)S(1)}, f32[32,256]{1,0:T(8,128)S(1)}, u32[]{:S(2)}, u32[]{:S(2)}) collective-permute-start(f32[32,256]{1,0:T(8,128)S(1)} %reduce_sum.9), channel_id=1, source_target_pairs={{0,3},{1,0},{2,1},{3,2},{4,7},{5,4},{6,5},{7,6},{8,11},{9,8},{10,9... | collective-permute-start | bytes 98312 | tf_op jit(solution)/shard_map/ppermute | solution.py:395
  150.6 10.3 %collective-permute-start.8 = (f32[32,256]{1,0:T(8,128)S(1)}, f32[32,256]{1,0:T(8,128)S(1)}, u32[]{:S(2)}, u32[]{:S(2)}) collective-permute-start(f32[32,256]{1,0:T(8,128)S(1)} %reduce_sum.9), channel_id=1, source_target_pairs={{0,1},{1,2},{2,3},{3,0},{4,5},{5,6},{6,7},{7,4},{8,9},{9,10},{10,1... | collective-permute-start | bytes 98312 | tf_op jit(solution)/shard_map/ppermute | solution.py:395
  150.6 10.3 %collective-permute-start.7 = (f32[32,256]{1,0:T(8,128)S(1)}, f32[32,256]{1,0:T(8,128)S(1)}, u32[]{:S(2)}, u32[]{:S(2)}) collective-permute-start(f32[32,256]{1,0:T(8,128)S(1)} %reduce_sum.9), channel_id=1, source_target_pairs={{0,2},{1,3},{2,0},{3,1},{4,6},{5,7},{6,4},{7,5},{8,10},{9,11},{10,... | collective-permute-start | bytes 98312 | tf_op jit(solution)/shard_map/ppermute | solution.py:395
  151.8 26.0 %collective-permute-start.4 = (f32[2,256,512]{2,1,0:T(8,128)}, f32[2,256,512]{2,1,0:T(8,128)S(1)}, u32[]{:S(2)}, u32[]{:S(2)}) collective-permute-start(f32[2,256,512]{2,1,0:T(8,128)} %get-tuple-element.24), channel_id=1, source_target_pairs={{0,16},{16,32},{32,48},{48,64},{64,80},{80,96},{96,112},{1,17},{17... | collective-permute-start | bytes 3145736 | tf_op jit(solution)/shard_map/ppermute | solution.py:429
  156.6 15.1 %collective-permute-start.11 = (f32[2,256,256]{2,1,0:T(8,128)S(1)}, f32[2,256,256]{2,1,0:T(8,128)S(1)}, u32[]{:S(2)}, u32[]{:S(2)}) collective-permute-start(f32[2,256,256]{2,1,0:T(8,128)S(1)} %add.27), channel_id=1, source_target_pairs={{0,1},{1,2},{2,3},{3,4},{4,5},{5,6},{6,7},{7,8},{8,9},{9,10},{10,1... | collective-permute-start | bytes 1572872 | tf_op jit(solution)/shard_map/ppermute | solution.py:431
  161.7 15.0 %all-to-all-start.1 = ((f32[16,32,256]{2,1,0:T(8,128)}), f32[16,32,256]{2,1,0:T(8,128)S(1)}, u32[]{:S(2)}, u32[]{:S(2)}) async-start(f32[16,32,256]{2,1,0:T(8,128)} %broadcast_in_dim.2), calls=%async_computation.1 | async-start | bytes 1048576 | tf_op jit(solution)/shard_map/all_to_all | solution.py:436
  176.7 3.7 %collective-permute-start.12 = (f32[512,256]{1,0:T(8,128)S(1)}, f32[512,256]{1,0:T(8,128)S(1)}, u32[]{:S(2)}, u32[]{:S(2)}) collective-permute-start(f32[512,256]{1,0:T(8,128)S(1)} %bitcast.10), channel_id=1, source_target_pairs={{0,16},{16,0},{1,17},{17,1},{2,18},{18,2},{3,19},{19,3},{4,20},{20... | collective-permute-start | bytes 1572872 | tf_op jit(solution)/shard_map/ppermute | solution.py:391
  177.8 2.6 %copy-start = (f32[2,2,256,256]{3,2,1,0:T(8,128)S(1)}, f32[2,2,256,256]{3,2,1,0:T(8,128)}, u32[]{:S(2)}) copy-start(f32[2,2,256,256]{3,2,1,0:T(8,128)} %probe.2) | copy-start | bytes 3145732
  177.8 2.6 %copy-start.1 = (s32[3]{0:T(128)S(1)}, s32[3]{0:T(128)}, u32[]{:S(2)}) copy-start(s32[3]{0:T(128)} %pad_add_fusion.anchor.place) | copy-start | bytes 40

commit v10 on v8

--- a/solution.py
+++ b/solution.py
@@ -308,6 +308,7 @@
         out_shape=jax.ShapeDtypeStruct((8, W, W), f32),
         in_specs=[blk, full, full],
         out_specs=blk,
+        compiler_params=pltpu.CompilerParams(vmem_limit_bytes=4 * 2**20),
         name="roots",
     )(counts, jnp.asarray(pm.astype(ml_dtypes.bfloat16)), jnp.asarray(pm.T.astype(ml_dtypes.bfloat16)))
 

time: 122 us -> 123 us (level)
  starting transfers between devices: 55.1 us -> 39 us
  Pallas kernels: 22.9 us -> 33.4 us
  local copies, waits for them, and re-layouts: 3.31 us -> 5.72 us
  waiting for transfers between devices: 16.6 us -> 19 us
  blocking collectives: 18.9 us -> 20.6 us
    pallas_call x1, Pallas kernels: 11.8 us -> 26.4 us  [main_call(): pl.pallas_call(main_kernel, out_shape=(S(2, 512, 512), S(2, 256, 256), S(...]
    ppermute x1, starting transfers between devices: 12 us -> 2.05 us  [shards(): corner_in = lax.ppermute(g_corner, rows, down)]
    ppermute x2, starting transfers between devices: 8.07 us -> 2 us  [swap_cores(): return lax.ppermute(value, 'core', [(0, 1), (1, 0)])]
    pallas_call x1, Pallas kernels: 6.96 us -> 2.83 us  [prep_call(): pl.pallas_call(prep_kernel, grid=(8,), out_shape=jax.ShapeDtypeStruct((8,...]
    ppermute x1, starting transfers between devices: 2.03 us -> 6 us  [shards(): bot_in = lax.ppermute(g_bot, cols, to_right)]
    all_to_all x1, blocking collectives: 18.9 us -> 20.6 us  [shards(): lax.all_to_all(jnp.broadcast_to(piece[None], half.shape), plane, 0, 0)]
    ppermute x1, starting transfers between devices: 4.6 us -> 3.11 us  [shards(): top_in = lax.ppermute(g_top + corner_in, cols, to_right)]
    unnamed x15 -> x21, local copies, waits for them, and re-layouts: 0.78 us -> 2.13 us
  transfers between devices with their start and end apart: 14 -> 14, of which waited for: 4 -> 4; matrix products, arithmetic and copies ran while one was open for 3% -> 4% of each run, Pallas kernels for 8% -> 4%
where the time goes in v10:
time: 123 us; the launch traced here: 122 us
  starting transfers between devices  39 us (32%)
  Pallas kernels  33.4 us (27%)
  blocking collectives  20.6 us (17%)
  waiting for transfers between devices  19 us (15%)
  local copies, waits for them, and re-layouts  5.72 us (5%)
  other arithmetic  2.63 us (2%)
  between operations  1.59 us (1%)
    pallas_call x1, Pallas kernels, main_call(): pl.pallas_call(main_kernel, out_shape=(S(2, 512, 512), S(2, 256, 256), S(...  26.4 us
    all_to_all x1, blocking collectives, shards(): lax.all_to_all(jnp.broadcast_to(piece[None], half.shape), plane, 0, 0)  20.6 us
    all_to_all x1, waiting for transfers between devices, shards(): piece = lax.all_to_all(half, plane, 0, 0).sum(0)  8.17 us
    ppermute x3, starting transfers between devices, sum_everywhere(): lax.ppermute(value, axis, [(i, (i + k) % 4) for i in range(4)])  6.45 us
    all_to_all x1, starting transfers between devices, shards(): piece = lax.all_to_all(half, plane, 0, 0).sum(0)  6.43 us
    ppermute x1, starting transfers between devices, shards(): bot_in = lax.ppermute(g_bot, cols, to_right)  6 us
    ppermute x1, waiting for transfers between devices, shards(): right_bot = lax.ppermute(object_planes[:, W:, :W], cols, to_left)  5.39 us
    ppermute x1, waiting for transfers between devices, shards(): right_top = lax.ppermute(object_planes[:, :W, :W], cols, to_left)  4.54 us
  transfers between devices with their start and end apart: 14, of which 4 were waited for; matrix products, arithmetic and copies ran while one was open for 4% of the time, Pallas kernels for 4%

profile of v10, /device:TPU:1, one launch (start us, length us, event | category | flops | bytes accessed | tf_op | source)
XLA Modules:
  0.0 121.9 jit_solution(8884955713968821584)
XLA Ops:
  0.6 0.0 copy-start.3
  0.6 0.0 copy-start.4
  0.7 2.3 %fusion = (f32[2,256,256]{2,1,0:T(8,128)}, f32[2,256,256]{2,1,0:T(8,128)S(1)}) fusion(f32[2,512,512]{2,1,0:T(8,128)} %obj.1), kind=kLoop, calls=%fused_computation.2 | loop fusion | bytes 2097152 | tf_op jit(solution)/shard_map/slice | solution.py:394
  2.9 1.3 %collective-permute-start = (f32[2,256,256]{2,1,0:T(8,128)S(1)}, f32[2,256,256]{2,1,0:T(8,128)S(1)}, u32[]{:S(2)}, u32[]{:S(2)}) collective-permute-start(f32[2,256,256]{2,1,0:T(8,128)S(1)} %get-tuple-element.29), channel_id=1, source_target_pairs={{1,0},{2,1},{3,2},{4,3},{5,4},{6,5},{7,6},{8,7},{9,8},{10,9},{11,1... | collective-permute-start | bytes 1572872 | tf_op jit(solution)/shard_map/ppermute | solution.py:392
  4.2 1.3 %slice.11 = f32[2,256,512]{2,1,0:T(8,128)S(1)} slice(f32[2,512,512]{2,1,0:T(8,128)} %obj.1), slice={[0:2], [0:256], [0:512]} | slice | bytes 2097152 | tf_op jit(solution)/shard_map/slice | solution.py:393
  5.5 3.3 %collective-permute-start.2 = (f32[2,256,512]{2,1,0:T(8,128)S(1)}, f32[2,256,512]{2,1,0:T(8,128)S(1)}, u32[]{:S(2)}, u32[]{:S(2)}) collective-permute-start(f32[2,256,512]{2,1,0:T(8,128)S(1)} %slice.11), channel_id=1, source_target_pairs={{16,0},{32,16},{48,32},{64,48},{80,64},{96,80},{112,96},{17,1},{33... | collective-permute-start | bytes 3145736 | tf_op jit(solution)/shard_map/ppermute | solution.py:393
  8.9 1.3 %collective-permute-start.1 = (f32[2,256,256]{2,1,0:T(8,128)}, f32[2,256,256]{2,1,0:T(8,128)}, u32[]{:S(2)}, u32[]{:S(2)}) collective-permute-start(f32[2,256,256]{2,1,0:T(8,128)} %get-tuple-element.28), channel_id=1, source_target_pairs={{1,0},{2,1},{3,2},{4,3},{5,4},{6,5},{7,6},{8,7},{9,8},{10,9},{11,1... | collective-permute-start | bytes 1572872 | tf_op jit(solution)/shard_map/ppermute | solution.py:394
  10.2 2.8 %roots.1.sq = f32[8,256,256]{2,1,0:T(8,128)S(1)} custom-call(s32[8,256,256]{2,1,0:T(8,128)S(1)} %copy-done.2, bf16[256,256]{1,0:T(8,128)(2,1)S(1)} %copy-done.4, bf16[256,256]{1,0:T(8,128)(2,1)S(1)} %copy-done.3), custom_call_target="tpu_custom_call" | custom-call | tf_op jit(solution)/shard_map/roots/pallas_call | solution.py:305
  13.0 1.3 %copy-done = f32[8,256,256]{2,1,0:T(8,128)} copy-done((f32[8,256,256]{2,1,0:T(8,128)}, f32[8,256,256]{2,1,0:T(8,128)S(1)}, u32[]{:S(2)}) %copy-start) | copy-done | bytes 2097176
  14.4 4.5 %collective-permute-done.right_top = f32[2,256,256]{2,1,0:T(8,128)S(1)} collective-permute-done((f32[2,256,256]{2,1,0:T(8,128)S(1)}, f32[2,256,256]{2,1,0:T(8,128)S(1)}, u32[]{:S(2)}, u32[]{:S(2)}) %collective-permute-start) | collective-permute-done | bytes 524320 | tf_op jit(solution)/shard_map/ppermute | solution.py:392
  18.9 4.0 %collective-permute-start.3 = (f32[2,256,256]{2,1,0:T(8,128)S(1)}, f32[2,256,256]{2,1,0:T(8,128)}, u32[]{:S(2)}, u32[]{:S(2)}) collective-permute-start(f32[2,256,256]{2,1,0:T(8,128)S(1)} %collective-permute-done.right_top), channel_id=1, source_target_pairs={{16,0},{32,16},{48,32},{64,48},{80,64},{96,80},{112,96},{17,1},{33... | collective-permute-start | bytes 1572872 | tf_op jit(solution)/shard_map/ppermute | solution.py:397
  23.6 0.7 copy.11.offs
  24.2 0.6 pad_add_fusion.anchor.place
  24.9 5.4 %collective-permute-done.1.right_bot = f32[2,256,256]{2,1,0:T(8,128)} collective-permute-done((f32[2,256,256]{2,1,0:T(8,128)}, f32[2,256,256]{2,1,0:T(8,128)}, u32[]{:S(2)}, u32[]{:S(2)}) %collective-permute-start.1) | collective-permute-done | bytes 524320 | tf_op jit(solution)/shard_map/ppermute | solution.py:394
  30.3 0.9 collective-permute-done.3.corner
  31.1 0.1 copy-done.6
  31.2 26.4 %slots.1 = (f32[2,512,512]{2,1,0:T(8,128)}, f32[2,256,256]{2,1,0:T(8,128)}, f32[2,256,256]{2,1,0:T(8,128)}, f32[2,256,256]{2,1,0:T(8,128)}, f32[2,256,512]{2,1,0...) custom-call(s32[8,2]{1,0:T(8,128)} %copy.11.offs, s32[1]{0:T(128)} %bitcast.8.live, ...), custom_call_target="tpu_custom_call" | custom-call | tf_op jit(solution)/shard_map/slots/pallas_call | solution.py:268
  57.6 0.1 collective-permute-start.5
  57.7 2.1 %collective-permute-start.10 = (f32[2,256,256]{2,1,0:T(8,128)}, f32[2,256,256]{2,1,0:T(8,128)S(1)}, u32[]{:S(2)}, u32[]{:S(2)}) collective-permute-start(f32[2,256,256]{2,1,0:T(8,128)} %get-tuple-element.24), channel_id=1, source_target_pairs={{0,16},{16,32},{32,48},{48,64},{64,80},{80,96},{96,112},{1,17},{17... | collective-permute-start | bytes 1572872 | tf_op jit(solution)/shard_map/ppermute | solution.py:404
  59.8 6.0 %collective-permute-start.6 = (f32[2,256,256]{2,1,0:T(8,128)}, f32[2,256,256]{2,1,0:T(8,128)S(1)}, u32[]{:S(2)}, u32[]{:S(2)}) collective-permute-start(f32[2,256,256]{2,1,0:T(8,128)} %get-tuple-element.21), channel_id=1, source_target_pairs={{0,1},{1,2},{2,3},{3,4},{4,5},{5,6},{6,7},{7,8},{8,9},{9,10},{10,1... | collective-permute-start | bytes 1572872 | tf_op jit(solution)/shard_map/ppermute | solution.py:405
  65.8 1.9 %add.23 = f32[2,256,256]{2,1,0:T(8,128)} add(f32[2,256,256]{2,1,0:T(8,128)} %get-tuple-element.19, f32[2,256,256]{2,1,0:T(8,128)S(1)} %collective-permute-done.5) | non-fusion elementwise | flops 131072 | bytes 1572864 | tf_op jit(solution)/shard_map/add | solution.py:407
  67.7 6.4 %all-to-all-start = ((f32[16,32,256]{2,1,0:T(8,128)}), f32[16,32,256]{2,1,0:T(8,128)S(1)}, u32[]{:S(2)}, u32[]{:S(2)}) async-start(f32[16,32,256]{2,1,0:T(8,128)} %bitcast.4), calls=%async_computation | async-start | bytes 1048576 | tf_op jit(solution)/shard_map/all_to_all | solution.py:410
  74.2 0.1 add.27
  74.2 3.1 %collective-permute-start.11 = (f32[2,256,256]{2,1,0:T(8,128)S(1)}, f32[2,256,256]{2,1,0:T(8,128)S(1)}, u32[]{:S(2)}, u32[]{:S(2)}) collective-permute-start(f32[2,256,256]{2,1,0:T(8,128)S(1)} %add.27), channel_id=1, source_target_pairs={{0,1},{1,2},{2,3},{3,4},{4,5},{5,6},{6,7},{7,8},{8,9},{9,10},{10,1... | collective-permute-start | bytes 1572872 | tf_op jit(solution)/shard_map/ppermute | solution.py:408
  77.4 8.2 %all-to-all-done = f32[16,32,256]{2,1,0:T(8,128)S(1)} async-done(((f32[16,32,256]{2,1,0:T(8,128)}), f32[16,32,256]{2,1,0:T(8,128)S(1)}, u32[]{:S(2)}, u32[]{:S(2)}) %all-to-all-start) | async-done | bytes 524320 | tf_op jit(solution)/shard_map/all_to_all | solution.py:410
  85.6 3.4 %collective-permute-start.9 = (f32[32,256]{1,0:T(8,128)S(1)}, f32[32,256]{1,0:T(8,128)S(1)}, u32[]{:S(2)}, u32[]{:S(2)}) collective-permute-start(f32[32,256]{1,0:T(8,128)S(1)} %reduce_sum.9), channel_id=1, source_target_pairs={{0,3},{1,0},{2,1},{3,2},{4,7},{5,4},{6,5},{7,6},{8,11},{9,8},{10,9... | collective-permute-start | bytes 98312 | tf_op jit(solution)/shard_map/ppermute | solution.py:373
  88.9 3.1 %collective-permute-start.7 = (f32[32,256]{1,0:T(8,128)S(1)}, f32[32,256]{1,0:T(8,128)S(1)}, u32[]{:S(2)}, u32[]{:S(2)}) collective-permute-start(f32[32,256]{1,0:T(8,128)S(1)} %reduce_sum.9), channel_id=1, source_target_pairs={{0,2},{1,3},{2,0},{3,1},{4,6},{5,7},{6,4},{7,5},{8,10},{9,11},{10,... | collective-permute-start | bytes 98312 | tf_op jit(solution)/shard_map/ppermute | solution.py:373
  92.0 3.0 %collective-permute-start.4 = (f32[2,256,512]{2,1,0:T(8,128)}, f32[2,256,512]{2,1,0:T(8,128)S(1)}, u32[]{:S(2)}, u32[]{:S(2)}) collective-permute-start(f32[2,256,512]{2,1,0:T(8,128)} %get-tuple-element.18), channel_id=1, source_target_pairs={{0,16},{16,32},{32,48},{48,64},{64,80},{80,96},{96,112},{1,17},{17... | collective-permute-start | bytes 3145736 | tf_op jit(solution)/shard_map/ppermute | solution.py:406
  95.2 20.6 %all_to_all.10 = f32[16,32,256]{2,1,0:T(8,128)S(1)} all-to-all(f32[16,32,256]{2,1,0:T(8,128)S(1)} %broadcast_in_dim.2), channel_id=1, replica_groups=mesh['y'=4,'core'=2,'x'=4,'z'=4] {'y','x'}, dimensions={0} | all-to-all | bytes 1048576 | tf_op jit(solution)/shard_map/all_to_all | solution.py:415
  115.8 1.9 %collective-permute-start.12 = (f32[512,256]{1,0:T(8,128)S(1)}, f32[512,256]{1,0:T(8,128)S(1)}, u32[]{:S(2)}, u32[]{:S(2)}) collective-permute-start(f32[512,256]{1,0:T(8,128)S(1)} %bitcast.10), channel_id=1, source_target_pairs={{0,16},{16,0},{1,17},{17,1},{2,18},{18,2},{3,19},{19,3},{4,20},{20... | collective-permute-start | bytes 1572872 | tf_op jit(solution)/shard_map/ppermute | solution.py:369
  117.7 2.5 %finish.1 = f32[2,512,512]{2,1,0:T(8,128)} custom-call(f32[2,512,512]{2,1,0:T(8,128)} %get-tuple-element.17.part, f32[2,256,512]{2,1,0:T(8,128)S(1)} %collective-permute-done.4.above, f32[2,256,256]{2,1,0:T(8,128)S(1)} %collective-permute-done.11.top, f32[2,256,256]{2,1,0:T(8,128)S(1)} %collective-permute-done.6.bot), custom_call_target="tpu_custom_call", output_to_operand_aliasing={{}: (0, {})} | custom-call | tf_op jit(solution)/shard_map/finish/pallas_call | solution.py:349
  120.3 1.6 %probe.3 = f32[1024,256]{1,0:T(8,128)} custom-call(s32[3]{0:T(128)S(1)} %copy-done.5, f32[1024,256]{1,0:T(8,128)S(1)} %bitcast.9, f32[512,256]{1,0:T(8,128)S(1)} %bitcast.11, f32[512,256]{1,0:T(8,128)S(1)} %collective-permute-done.12.rest), custom_call_target="tpu_custom_call" | custom-call | tf_op jit(solution)/shard_map/probe/pallas_call | solution.py:419
  (30 shorter events, 0.2 us)
Async XLA Ops:
  0.6 9.5 %copy-start.3 = (bf16[256,256]{1,0:T(8,128)(2,1)S(1)}, bf16[256,256]{1,0:T(8,128)(2,1)}, u32[]{:S(2)}) copy-start(bf16[256,256]{1,0:T(8,128)(2,1)} %constant.32.clone.pmt) | copy-start | bytes 393220
  0.6 9.5 %copy-start.4 = (bf16[256,256]{1,0:T(8,128)(2,1)S(1)}, bf16[256,256]{1,0:T(8,128)(2,1)}, u32[]{:S(2)}) copy-start(bf16[256,256]{1,0:T(8,128)(2,1)} %constant.31.clone.pm) | copy-start | bytes 393220
  0.7 9.5 %copy-start.2 = (s32[8,256,256]{2,1,0:T(8,128)S(1)}, s32[8,256,256]{2,1,0:T(8,128)}, u32[]{:S(2)}) copy-start(s32[8,256,256]{2,1,0:T(8,128)} %counts.1) | copy-start | bytes 6291460
  2.9 16.0 %collective-permute-start = (f32[2,256,256]{2,1,0:T(8,128)S(1)}, f32[2,256,256]{2,1,0:T(8,128)S(1)}, u32[]{:S(2)}, u32[]{:S(2)}) collective-permute-start(f32[2,256,256]{2,1,0:T(8,128)S(1)} %get-tuple-element.29), channel_id=1, source_target_pairs={{1,0},{2,1},{3,2},{4,3},{5,4},{6,5},{7,6},{8,7},{9,8},{10,9},{11,1... | collective-permute-start | bytes 1572872 | tf_op jit(solution)/shard_map/ppermute | solution.py:392
  5.5 24.7 %collective-permute-start.2 = (f32[2,256,512]{2,1,0:T(8,128)S(1)}, f32[2,256,512]{2,1,0:T(8,128)S(1)}, u32[]{:S(2)}, u32[]{:S(2)}) collective-permute-start(f32[2,256,512]{2,1,0:T(8,128)S(1)} %slice.11), channel_id=1, source_target_pairs={{16,0},{32,16},{48,32},{64,48},{80,64},{96,80},{112,96},{17,1},{33... | collective-permute-start | bytes 3145736 | tf_op jit(solution)/shard_map/ppermute | solution.py:393
  8.8 14.7 %copy-start.9 = (s32[8,2]{0,1:T(2,128)S(1)}, s32[8,2]{0,1:T(2,128)}, u32[]{:S(2)}) copy-start(s32[8,2]{0,1:T(2,128)} %param.10) | copy-start | bytes 196
  8.9 21.4 %collective-permute-start.1 = (f32[2,256,256]{2,1,0:T(8,128)}, f32[2,256,256]{2,1,0:T(8,128)}, u32[]{:S(2)}, u32[]{:S(2)}) collective-permute-start(f32[2,256,256]{2,1,0:T(8,128)} %get-tuple-element.28), channel_id=1, source_target_pairs={{1,0},{2,1},{3,2},{4,3},{5,4},{6,5},{7,6},{8,7},{9,8},{10,9},{11,1... | collective-permute-start | bytes 1572872 | tf_op jit(solution)/shard_map/ppermute | solution.py:394
  13.0 1.3 %copy-start = (f32[8,256,256]{2,1,0:T(8,128)}, f32[8,256,256]{2,1,0:T(8,128)S(1)}, u32[]{:S(2)}) copy-start(f32[8,256,256]{2,1,0:T(8,128)S(1)} %roots.1.sq) | copy-start | bytes 6291460
  18.9 12.2 %copy-start.7 = (f32[2,256,256]{2,1,0:T(8,128)}, f32[2,256,256]{2,1,0:T(8,128)S(1)}, u32[]{:S(2)}) copy-start(f32[2,256,256]{2,1,0:T(8,128)S(1)} %collective-permute-done.right_top) | copy-start | bytes 1572868
  18.9 12.2 %collective-permute-start.3 = (f32[2,256,256]{2,1,0:T(8,128)S(1)}, f32[2,256,256]{2,1,0:T(8,128)}, u32[]{:S(2)}, u32[]{:S(2)}) collective-permute-start(f32[2,256,256]{2,1,0:T(8,128)S(1)} %collective-permute-done.right_top), channel_id=1, source_target_pairs={{16,0},{32,16},{48,32},{64,48},{80,64},{96,80},{112,96},{17,1},{33... | collective-permute-start | bytes 1572872 | tf_op jit(solution)/shard_map/ppermute | solution.py:397
  30.3 1.0 copy-start.6
  57.6 16.5 %copy-start.8 = (f32[2,256,256]{2,1,0:T(8,128)S(1)}, f32[2,256,256]{2,1,0:T(8,128)}, u32[]{:S(2)}) copy-start(f32[2,256,256]{2,1,0:T(8,128)} %get-tuple-element.23) | copy-start | bytes 1572868
  57.6 8.2 %collective-permute-start.5 = (f32[2,256,256]{2,1,0:T(8,128)}, f32[2,256,256]{2,1,0:T(8,128)S(1)}, u32[]{:S(2)}, u32[]{:S(2)}) collective-permute-start(f32[2,256,256]{2,1,0:T(8,128)} %get-tuple-element.20), channel_id=1, source_target_pairs={{0,16},{16,0},{1,17},{17,1},{2,18},{18,2},{3,19},{19,3},{4,20},{20... | collective-permute-start | bytes 1572872 | tf_op jit(solution)/shard_map/ppermute | solution.py:369
  57.7 16.4 %collective-permute-start.10 = (f32[2,256,256]{2,1,0:T(8,128)}, f32[2,256,256]{2,1,0:T(8,128)S(1)}, u32[]{:S(2)}, u32[]{:S(2)}) collective-permute-start(f32[2,256,256]{2,1,0:T(8,128)} %get-tuple-element.24), channel_id=1, source_target_pairs={{0,16},{16,32},{32,48},{48,64},{64,80},{80,96},{96,112},{1,17},{17... | collective-permute-start | bytes 1572872 | tf_op jit(solution)/shard_map/ppermute | solution.py:404
  59.8 25.8 %collective-permute-start.6 = (f32[2,256,256]{2,1,0:T(8,128)}, f32[2,256,256]{2,1,0:T(8,128)S(1)}, u32[]{:S(2)}, u32[]{:S(2)}) collective-permute-start(f32[2,256,256]{2,1,0:T(8,128)} %get-tuple-element.21), channel_id=1, source_target_pairs={{0,1},{1,2},{2,3},{3,4},{4,5},{5,6},{6,7},{7,8},{8,9},{9,10},{10,1... | collective-permute-start | bytes 1572872 | tf_op jit(solution)/shard_map/ppermute | solution.py:405
  67.7 17.8 %all-to-all-start = ((f32[16,32,256]{2,1,0:T(8,128)}), f32[16,32,256]{2,1,0:T(8,128)S(1)}, u32[]{:S(2)}, u32[]{:S(2)}) async-start(f32[16,32,256]{2,1,0:T(8,128)} %bitcast.4), calls=%async_computation | async-start | bytes 1048576 | tf_op jit(solution)/shard_map/all_to_all | solution.py:410
  74.2 20.9 %collective-permute-start.11 = (f32[2,256,256]{2,1,0:T(8,128)S(1)}, f32[2,256,256]{2,1,0:T(8,128)S(1)}, u32[]{:S(2)}, u32[]{:S(2)}) collective-permute-start(f32[2,256,256]{2,1,0:T(8,128)S(1)} %add.27), channel_id=1, source_target_pairs={{0,1},{1,2},{2,3},{3,4},{4,5},{5,6},{6,7},{7,8},{8,9},{9,10},{10,1... | collective-permute-start | bytes 1572872 | tf_op jit(solution)/shard_map/ppermute | solution.py:408
  85.6 9.5 %collective-permute-start.9 = (f32[32,256]{1,0:T(8,128)S(1)}, f32[32,256]{1,0:T(8,128)S(1)}, u32[]{:S(2)}, u32[]{:S(2)}) collective-permute-start(f32[32,256]{1,0:T(8,128)S(1)} %reduce_sum.9), channel_id=1, source_target_pairs={{0,3},{1,0},{2,1},{3,2},{4,7},{5,4},{6,5},{7,6},{8,11},{9,8},{10,9... | collective-permute-start | bytes 98312 | tf_op jit(solution)/shard_map/ppermute | solution.py:373
  88.9 6.1 %collective-permute-start.8 = (f32[32,256]{1,0:T(8,128)S(1)}, f32[32,256]{1,0:T(8,128)S(1)}, u32[]{:S(2)}, u32[]{:S(2)}) collective-permute-start(f32[32,256]{1,0:T(8,128)S(1)} %reduce_sum.9), channel_id=1, source_target_pairs={{0,1},{1,2},{2,3},{3,0},{4,5},{5,6},{6,7},{7,4},{8,9},{9,10},{10,1... | collective-permute-start | bytes 98312 | tf_op jit(solution)/shard_map/ppermute | solution.py:373
  88.9 6.2 %collective-permute-start.7 = (f32[32,256]{1,0:T(8,128)S(1)}, f32[32,256]{1,0:T(8,128)S(1)}, u32[]{:S(2)}, u32[]{:S(2)}) collective-permute-start(f32[32,256]{1,0:T(8,128)S(1)} %reduce_sum.9), channel_id=1, source_target_pairs={{0,2},{1,3},{2,0},{3,1},{4,6},{5,7},{6,4},{7,5},{8,10},{9,11},{10,... | collective-permute-start | bytes 98312 | tf_op jit(solution)/shard_map/ppermute | solution.py:373
  92.0 25.7 %collective-permute-start.4 = (f32[2,256,512]{2,1,0:T(8,128)}, f32[2,256,512]{2,1,0:T(8,128)S(1)}, u32[]{:S(2)}, u32[]{:S(2)}) collective-permute-start(f32[2,256,512]{2,1,0:T(8,128)} %get-tuple-element.18), channel_id=1, source_target_pairs={{0,16},{16,32},{32,48},{48,64},{64,80},{80,96},{96,112},{1,17},{17... | collective-permute-start | bytes 3145736 | tf_op jit(solution)/shard_map/ppermute | solution.py:406
  115.8 4.5 %collective-permute-start.12 = (f32[512,256]{1,0:T(8,128)S(1)}, f32[512,256]{1,0:T(8,128)S(1)}, u32[]{:S(2)}, u32[]{:S(2)}) collective-permute-start(f32[512,256]{1,0:T(8,128)S(1)} %bitcast.10), channel_id=1, source_target_pairs={{0,16},{16,0},{1,17},{17,1},{2,18},{18,2},{3,19},{19,3},{4,20},{20... | collective-permute-start | bytes 1572872 | tf_op jit(solution)/shard_map/ppermute | solution.py:369
  117.7 2.6 %copy-start.1 = (f32[2,2,256,256]{3,2,1,0:T(8,128)S(1)}, f32[2,2,256,256]{3,2,1,0:T(8,128)}, u32[]{:S(2)}) copy-start(f32[2,2,256,256]{3,2,1,0:T(8,128)} %probe.2) | copy-start | bytes 3145732
  117.7 2.6 %copy-start.5 = (s32[3]{0:T(128)S(1)}, s32[3]{0:T(128)}, u32[]{:S(2)}) copy-start(s32[3]{0:T(128)} %pad_add_fusion.anchor.place) | copy-start | bytes 40

commit v11 on v10

--- a/solution.py
+++ b/solution.py
@@ -401,10 +401,11 @@
     part, g_top, g_bot, g_corner, g_below, mine, other = main_call(
         offsets, live_counts.reshape(1), place, object_planes, right_top, right_bot, below, corner, probe_planes, roots
     )
-    corner_in = lax.ppermute(g_corner, rows, down)
     bot_in = lax.ppermute(g_bot, cols, to_right)
     above_in = lax.ppermute(g_below, rows, down)
     half = (mine + swap_cores(other)).reshape(16, 32, W)
+    half, g_corner = lax.optimization_barrier((half, g_corner))
+    corner_in = lax.ppermute(g_corner, rows, down)
     top_in = lax.ppermute(g_top + corner_in, cols, to_right)
     plane = ("y", "x")
     piece = lax.all_to_all(half, plane, 0, 0).sum(0)

time: 123 us -> 127 us (1.033)
  waiting for transfers between devices: 19 us -> 23.6 us
    all_to_all x1, waiting for transfers between devices: 8.17 us -> 11 us  [shards(): piece = lax.all_to_all(half, plane, 0, 0).sum(0)]
    ppermute x1, starting transfers between devices: 6 us -> 3.57 us  [shards(): bot_in = lax.ppermute(g_bot, cols, to_right)]
    ppermute x1, starting transfers between devices: 3.11 us -> 1.32 us  [shards(): top_in = lax.ppermute(g_top + corner_in, cols, to_right)]
    ppermute x2, waiting for transfers between devices: 0.01 us -> 1.75 us  [swap_cores(): return lax.ppermute(value, 'core', [(0, 1), (1, 0)])]
    all_to_all x1, starting transfers between devices: 6.43 us -> 7.79 us  [shards(): piece = lax.all_to_all(half, plane, 0, 0).sum(0)]
    ppermute x2, starting transfers between devices: 2 us -> 3.27 us  [swap_cores(): return lax.ppermute(value, 'core', [(0, 1), (1, 0)])]
  transfers between devices with their start and end apart: 14 -> 14, of which waited for: 4 -> 5; matrix products, arithmetic and copies ran while one was open for 4% -> 2% of each run, Pallas kernels for 4% -> 4%
where the time goes in v11:
time: 127 us
  starting transfers between devices  38 us (30%)
  Pallas kernels  33.4 us (26%)
  waiting for transfers between devices  23.6 us (19%)
  blocking collectives  21.6 us (17%)
  local copies, waits for them, and re-layouts  5.72 us (5%)
  other arithmetic  2.63 us (2%)
  between operations  1.58 us (1%)
    pallas_call x1, Pallas kernels, main_call(): pl.pallas_call(main_kernel, out_shape=(S(2, 512, 512), S(2, 256, 256), S(...  26.4 us
    all_to_all x1, blocking collectives, shards(): lax.all_to_all(jnp.broadcast_to(piece[None], half.shape), plane, 0, 0)  21.6 us
    all_to_all x1, waiting for transfers between devices, shards(): piece = lax.all_to_all(half, plane, 0, 0).sum(0)  11 us
    all_to_all x1, starting transfers between devices, shards(): piece = lax.all_to_all(half, plane, 0, 0).sum(0)  7.79 us
    ppermute x3, starting transfers between devices, sum_everywhere(): lax.ppermute(value, axis, [(i, (i + k) % 4) for i in range(4)])  6.85 us
    ppermute x1, waiting for transfers between devices, shards(): right_bot = lax.ppermute(object_planes[:, W:, :W], cols, to_left)  5.39 us
    ppermute x1, waiting for transfers between devices, shards(): right_top = lax.ppermute(object_planes[:, :W, :W], cols, to_left)  4.54 us
    ppermute x1, starting transfers between devices, shards(): corner = lax.ppermute(right_top, rows, up)  3.99 us
  transfers between devices with their start and end apart: 14, of which 5 were waited for; matrix products, arithmetic and copies ran while one was open for 2% of the time, Pallas kernels for 4%

profile of v11, /device:TPU:1, one launch (start us, length us, event | category | flops | bytes accessed | tf_op | source)
XLA Modules:
  0.0 126.6 jit_solution(6951109092340684606)
XLA Ops:
  0.6 0.0 copy-start.3
  0.7 2.3 %fusion = (f32[2,256,256]{2,1,0:T(8,128)}, f32[2,256,256]{2,1,0:T(8,128)S(1)}) fusion(f32[2,512,512]{2,1,0:T(8,128)} %obj.1), kind=kLoop, calls=%fused_computation.2 | loop fusion | bytes 2097152 | tf_op jit(solution)/shard_map/slice | solution.py:394
  2.9 1.3 %collective-permute-start = (f32[2,256,256]{2,1,0:T(8,128)S(1)}, f32[2,256,256]{2,1,0:T(8,128)S(1)}, u32[]{:S(2)}, u32[]{:S(2)}) collective-permute-start(f32[2,256,256]{2,1,0:T(8,128)S(1)} %get-tuple-element.33), channel_id=1, source_target_pairs={{1,0},{2,1},{3,2},{4,3},{5,4},{6,5},{7,6},{8,7},{9,8},{10,9},{11,1... | collective-permute-start | bytes 1572872 | tf_op jit(solution)/shard_map/ppermute | solution.py:392
  4.2 1.3 %slice.11 = f32[2,256,512]{2,1,0:T(8,128)S(1)} slice(f32[2,512,512]{2,1,0:T(8,128)} %obj.1), slice={[0:2], [0:256], [0:512]} | slice | bytes 2097152 | tf_op jit(solution)/shard_map/slice | solution.py:393
  5.5 3.3 %collective-permute-start.2 = (f32[2,256,512]{2,1,0:T(8,128)S(1)}, f32[2,256,512]{2,1,0:T(8,128)S(1)}, u32[]{:S(2)}, u32[]{:S(2)}) collective-permute-start(f32[2,256,512]{2,1,0:T(8,128)S(1)} %slice.11), channel_id=1, source_target_pairs={{16,0},{32,16},{48,32},{64,48},{80,64},{96,80},{112,96},{17,1},{33... | collective-permute-start | bytes 3145736 | tf_op jit(solution)/shard_map/ppermute | solution.py:393
  8.9 1.3 %collective-permute-start.1 = (f32[2,256,256]{2,1,0:T(8,128)}, f32[2,256,256]{2,1,0:T(8,128)}, u32[]{:S(2)}, u32[]{:S(2)}) collective-permute-start(f32[2,256,256]{2,1,0:T(8,128)} %get-tuple-element.32), channel_id=1, source_target_pairs={{1,0},{2,1},{3,2},{4,3},{5,4},{6,5},{7,6},{8,7},{9,8},{10,9},{11,1... | collective-permute-start | bytes 1572872 | tf_op jit(solution)/shard_map/ppermute | solution.py:394
  10.2 2.8 %roots.1.sq = f32[8,256,256]{2,1,0:T(8,128)S(1)} custom-call(s32[8,256,256]{2,1,0:T(8,128)S(1)} %copy-done.2, bf16[256,256]{1,0:T(8,128)(2,1)S(1)} %copy-done.4, bf16[256,256]{1,0:T(8,128)(2,1)S(1)} %copy-done.3), custom_call_target="tpu_custom_call" | custom-call | tf_op jit(solution)/shard_map/roots/pallas_call | solution.py:305
  13.0 1.3 %copy-done = f32[8,256,256]{2,1,0:T(8,128)} copy-done((f32[8,256,256]{2,1,0:T(8,128)}, f32[8,256,256]{2,1,0:T(8,128)S(1)}, u32[]{:S(2)}) %copy-start) | copy-done | bytes 2097176
  14.4 4.5 %collective-permute-done.right_top = f32[2,256,256]{2,1,0:T(8,128)S(1)} collective-permute-done((f32[2,256,256]{2,1,0:T(8,128)S(1)}, f32[2,256,256]{2,1,0:T(8,128)S(1)}, u32[]{:S(2)}, u32[]{:S(2)}) %collective-permute-start) | collective-permute-done | bytes 524320 | tf_op jit(solution)/shard_map/ppermute | solution.py:392
  18.9 4.0 %collective-permute-start.3 = (f32[2,256,256]{2,1,0:T(8,128)S(1)}, f32[2,256,256]{2,1,0:T(8,128)}, u32[]{:S(2)}, u32[]{:S(2)}) collective-permute-start(f32[2,256,256]{2,1,0:T(8,128)S(1)} %collective-permute-done.right_top), channel_id=1, source_target_pairs={{16,0},{32,16},{48,32},{64,48},{80,64},{96,80},{112,96},{17,1},{33... | collective-permute-start | bytes 1572872 | tf_op jit(solution)/shard_map/ppermute | solution.py:397
  23.6 0.7 copy.11.offs
  24.2 0.6 pad_add_fusion.anchor.place
  24.9 5.4 %collective-permute-done.1.right_bot = f32[2,256,256]{2,1,0:T(8,128)} collective-permute-done((f32[2,256,256]{2,1,0:T(8,128)}, f32[2,256,256]{2,1,0:T(8,128)}, u32[]{:S(2)}, u32[]{:S(2)}) %collective-permute-start.1) | collective-permute-done | bytes 524320 | tf_op jit(solution)/shard_map/ppermute | solution.py:394
  30.3 0.9 collective-permute-done.3.corner
  31.1 0.1 copy-done.6
  31.2 26.4 %slots.1 = (f32[2,512,512]{2,1,0:T(8,128)}, f32[2,256,256]{2,1,0:T(8,128)}, f32[2,256,256]{2,1,0:T(8,128)}, f32[2,256,256]{2,1,0:T(8,128)}, f32[2,256,512]{2,1,0...) custom-call(s32[8,2]{1,0:T(8,128)} %copy.11.offs, s32[1]{0:T(128)} %bitcast.8.live, ...), custom_call_target="tpu_custom_call" | custom-call | tf_op jit(solution)/shard_map/slots/pallas_call | solution.py:268
  57.6 1.4 %collective-permute-start.5 = (f32[2,256,256]{2,1,0:T(8,128)}, f32[2,256,256]{2,1,0:T(8,128)S(1)}, u32[]{:S(2)}, u32[]{:S(2)}) collective-permute-start(f32[2,256,256]{2,1,0:T(8,128)} %get-tuple-element.22), channel_id=1, source_target_pairs={{0,16},{16,0},{1,17},{17,1},{2,18},{18,2},{3,19},{19,3},{4,20},{20... | collective-permute-start | bytes 1572872 | tf_op jit(solution)/shard_map/ppermute | solution.py:369
  59.0 1.7 %collective-permute-done.5 = f32[2,256,256]{2,1,0:T(8,128)S(1)} collective-permute-done((f32[2,256,256]{2,1,0:T(8,128)}, f32[2,256,256]{2,1,0:T(8,128)S(1)}, u32[]{:S(2)}, u32[]{:S(2)}) %collective-permute-start.5) | collective-permute-done | bytes 524320 | tf_op jit(solution)/shard_map/ppermute | solution.py:369
  60.7 1.9 %add.23 = f32[2,256,256]{2,1,0:T(8,128)} add(f32[2,256,256]{2,1,0:T(8,128)} %get-tuple-element.21, f32[2,256,256]{2,1,0:T(8,128)S(1)} %collective-permute-done.5) | non-fusion elementwise | flops 131072 | bytes 1572864 | tf_op jit(solution)/shard_map/add | solution.py:406
  62.6 1.9 %collective-permute-start.10 = (f32[2,256,256]{2,1,0:T(8,128)}, f32[2,256,256]{2,1,0:T(8,128)S(1)}, u32[]{:S(2)}, u32[]{:S(2)}) collective-permute-start(f32[2,256,256]{2,1,0:T(8,128)} %get-tuple-element.28), channel_id=1, source_target_pairs={{0,16},{16,32},{32,48},{48,64},{64,80},{80,96},{96,112},{1,17},{17... | collective-permute-start | bytes 1572872 | tf_op jit(solution)/shard_map/ppermute | solution.py:408
  64.6 3.6 %collective-permute-start.6 = (f32[2,256,256]{2,1,0:T(8,128)}, f32[2,256,256]{2,1,0:T(8,128)S(1)}, u32[]{:S(2)}, u32[]{:S(2)}) collective-permute-start(f32[2,256,256]{2,1,0:T(8,128)} %get-tuple-element.25), channel_id=1, source_target_pairs={{0,1},{1,2},{2,3},{3,4},{4,5},{5,6},{6,7},{7,8},{8,9},{9,10},{10,1... | collective-permute-start | bytes 1572872 | tf_op jit(solution)/shard_map/ppermute | solution.py:404
  68.1 7.8 %all-to-all-start = ((f32[16,32,256]{2,1,0:T(8,128)}), f32[16,32,256]{2,1,0:T(8,128)S(1)}, u32[]{:S(2)}, u32[]{:S(2)}) async-start(f32[16,32,256]{2,1,0:T(8,128)} %bitcast.4), calls=%async_computation | async-start | bytes 1048576 | tf_op jit(solution)/shard_map/all_to_all | solution.py:411
  75.9 0.1 add.27
  76.0 1.3 %collective-permute-start.11 = (f32[2,256,256]{2,1,0:T(8,128)S(1)}, f32[2,256,256]{2,1,0:T(8,128)S(1)}, u32[]{:S(2)}, u32[]{:S(2)}) collective-permute-start(f32[2,256,256]{2,1,0:T(8,128)S(1)} %add.27), channel_id=1, source_target_pairs={{0,1},{1,2},{2,3},{3,4},{4,5},{5,6},{6,7},{7,8},{8,9},{9,10},{10,1... | collective-permute-start | bytes 1572872 | tf_op jit(solution)/shard_map/ppermute | solution.py:409
  77.3 11.0 %all-to-all-done = f32[16,32,256]{2,1,0:T(8,128)S(1)} async-done(((f32[16,32,256]{2,1,0:T(8,128)}), f32[16,32,256]{2,1,0:T(8,128)S(1)}, u32[]{:S(2)}, u32[]{:S(2)}) %all-to-all-start) | async-done | bytes 524320 | tf_op jit(solution)/shard_map/all_to_all | solution.py:411
  88.4 5.1 %collective-permute-start.9 = (f32[32,256]{1,0:T(8,128)S(1)}, f32[32,256]{1,0:T(8,128)S(1)}, u32[]{:S(2)}, u32[]{:S(2)}) collective-permute-start(f32[32,256]{1,0:T(8,128)S(1)} %reduce_sum.9), channel_id=1, source_target_pairs={{0,3},{1,0},{2,1},{3,2},{4,7},{5,4},{6,5},{7,6},{8,11},{9,8},{10,9... | collective-permute-start | bytes 98312 | tf_op jit(solution)/shard_map/ppermute | solution.py:373
  93.5 1.8 %collective-permute-start.7 = (f32[32,256]{1,0:T(8,128)S(1)}, f32[32,256]{1,0:T(8,128)S(1)}, u32[]{:S(2)}, u32[]{:S(2)}) collective-permute-start(f32[32,256]{1,0:T(8,128)S(1)} %reduce_sum.9), channel_id=1, source_target_pairs={{0,2},{1,3},{2,0},{3,1},{4,6},{5,7},{6,4},{7,5},{8,10},{9,11},{10,... | collective-permute-start | bytes 98312 | tf_op jit(solution)/shard_map/ppermute | solution.py:373
  95.3 3.4 %collective-permute-start.4 = (f32[2,256,512]{2,1,0:T(8,128)}, f32[2,256,512]{2,1,0:T(8,128)S(1)}, u32[]{:S(2)}, u32[]{:S(2)}) collective-permute-start(f32[2,256,512]{2,1,0:T(8,128)} %get-tuple-element.20), channel_id=1, source_target_pairs={{0,16},{16,32},{32,48},{48,64},{64,80},{80,96},{96,112},{1,17},{17... | collective-permute-start | bytes 3145736 | tf_op jit(solution)/shard_map/ppermute | solution.py:405
  98.8 21.6 %all_to_all.10 = f32[16,32,256]{2,1,0:T(8,128)S(1)} all-to-all(f32[16,32,256]{2,1,0:T(8,128)S(1)} %broadcast_in_dim.2), channel_id=1, replica_groups=mesh['y'=4,'core'=2,'x'=4,'z'=4] {'y','x'}, dimensions={0} | all-to-all | bytes 1048576 | tf_op jit(solution)/shard_map/all_to_all | solution.py:416
  120.5 1.9 %collective-permute-start.12 = (f32[512,256]{1,0:T(8,128)S(1)}, f32[512,256]{1,0:T(8,128)S(1)}, u32[]{:S(2)}, u32[]{:S(2)}) collective-permute-start(f32[512,256]{1,0:T(8,128)S(1)} %bitcast.10), channel_id=1, source_target_pairs={{0,16},{16,0},{1,17},{17,1},{2,18},{18,2},{3,19},{19,3},{4,20},{20... | collective-permute-start | bytes 1572872 | tf_op jit(solution)/shard_map/ppermute | solution.py:369
  122.4 2.5 %finish.1 = f32[2,512,512]{2,1,0:T(8,128)} custom-call(f32[2,512,512]{2,1,0:T(8,128)} %get-tuple-element.19.part, f32[2,256,512]{2,1,0:T(8,128)S(1)} %collective-permute-done.4.above, f32[2,256,256]{2,1,0:T(8,128)S(1)} %collective-permute-done.11.top, f32[2,256,256]{2,1,0:T(8,128)S(1)} %collective-permute-done.6.bot), custom_call_target="tpu_custom_call", output_to_operand_aliasing={{}: (0, {})} | custom-call | tf_op jit(solution)/shard_map/finish/pallas_call | solution.py:349
  124.9 1.6 %probe.3 = f32[1024,256]{1,0:T(8,128)} custom-call(s32[3]{0:T(128)S(1)} %copy-done.5, f32[1024,256]{1,0:T(8,128)S(1)} %bitcast.9, f32[512,256]{1,0:T(8,128)S(1)} %bitcast.11, f32[512,256]{1,0:T(8,128)S(1)} %collective-permute-done.12.rest), custom_call_target="tpu_custom_call" | custom-call | tf_op jit(solution)/shard_map/probe/pallas_call | solution.py:420
  (30 shorter events, 0.2 us)
Async XLA Ops:
  0.6 9.5 %copy-start.3 = (bf16[256,256]{1,0:T(8,128)(2,1)S(1)}, bf16[256,256]{1,0:T(8,128)(2,1)}, u32[]{:S(2)}) copy-start(bf16[256,256]{1,0:T(8,128)(2,1)} %constant.32.clone.pmt) | copy-start | bytes 393220
  0.6 9.5 %copy-start.4 = (bf16[256,256]{1,0:T(8,128)(2,1)S(1)}, bf16[256,256]{1,0:T(8,128)(2,1)}, u32[]{:S(2)}) copy-start(bf16[256,256]{1,0:T(8,128)(2,1)} %constant.31.clone.pm) | copy-start | bytes 393220
  0.7 9.5 %copy-start.2 = (s32[8,256,256]{2,1,0:T(8,128)S(1)}, s32[8,256,256]{2,1,0:T(8,128)}, u32[]{:S(2)}) copy-start(s32[8,256,256]{2,1,0:T(8,128)} %counts.1) | copy-start | bytes 6291460
  2.9 16.0 %collective-permute-start = (f32[2,256,256]{2,1,0:T(8,128)S(1)}, f32[2,256,256]{2,1,0:T(8,128)S(1)}, u32[]{:S(2)}, u32[]{:S(2)}) collective-permute-start(f32[2,256,256]{2,1,0:T(8,128)S(1)} %get-tuple-element.33), channel_id=1, source_target_pairs={{1,0},{2,1},{3,2},{4,3},{5,4},{6,5},{7,6},{8,7},{9,8},{10,9},{11,1... | collective-permute-start | bytes 1572872 | tf_op jit(solution)/shard_map/ppermute | solution.py:392
  5.5 24.7 %collective-permute-start.2 = (f32[2,256,512]{2,1,0:T(8,128)S(1)}, f32[2,256,512]{2,1,0:T(8,128)S(1)}, u32[]{:S(2)}, u32[]{:S(2)}) collective-permute-start(f32[2,256,512]{2,1,0:T(8,128)S(1)} %slice.11), channel_id=1, source_target_pairs={{16,0},{32,16},{48,32},{64,48},{80,64},{96,80},{112,96},{17,1},{33... | collective-permute-start | bytes 3145736 | tf_op jit(solution)/shard_map/ppermute | solution.py:393
  8.8 14.7 %copy-start.9 = (s32[8,2]{0,1:T(2,128)S(1)}, s32[8,2]{0,1:T(2,128)}, u32[]{:S(2)}) copy-start(s32[8,2]{0,1:T(2,128)} %param.10) | copy-start | bytes 196
  8.9 21.4 %collective-permute-start.1 = (f32[2,256,256]{2,1,0:T(8,128)}, f32[2,256,256]{2,1,0:T(8,128)}, u32[]{:S(2)}, u32[]{:S(2)}) collective-permute-start(f32[2,256,256]{2,1,0:T(8,128)} %get-tuple-element.32), channel_id=1, source_target_pairs={{1,0},{2,1},{3,2},{4,3},{5,4},{6,5},{7,6},{8,7},{9,8},{10,9},{11,1... | collective-permute-start | bytes 1572872 | tf_op jit(solution)/shard_map/ppermute | solution.py:394
  13.0 1.3 %copy-start = (f32[8,256,256]{2,1,0:T(8,128)}, f32[8,256,256]{2,1,0:T(8,128)S(1)}, u32[]{:S(2)}) copy-start(f32[8,256,256]{2,1,0:T(8,128)S(1)} %roots.1.sq) | copy-start | bytes 6291460
  18.9 12.2 %copy-start.7 = (f32[2,256,256]{2,1,0:T(8,128)}, f32[2,256,256]{2,1,0:T(8,128)S(1)}, u32[]{:S(2)}) copy-start(f32[2,256,256]{2,1,0:T(8,128)S(1)} %collective-permute-done.right_top) | copy-start | bytes 1572868
  18.9 12.2 %collective-permute-start.3 = (f32[2,256,256]{2,1,0:T(8,128)S(1)}, f32[2,256,256]{2,1,0:T(8,128)}, u32[]{:S(2)}, u32[]{:S(2)}) collective-permute-start(f32[2,256,256]{2,1,0:T(8,128)S(1)} %collective-permute-done.right_top), channel_id=1, source_target_pairs={{16,0},{32,16},{48,32},{64,48},{80,64},{96,80},{112,96},{17,1},{33... | collective-permute-start | bytes 1572872 | tf_op jit(solution)/shard_map/ppermute | solution.py:397
  30.3 1.0 copy-start.6
  57.6 18.3 %copy-start.8 = (f32[2,256,256]{2,1,0:T(8,128)S(1)}, f32[2,256,256]{2,1,0:T(8,128)}, u32[]{:S(2)}) copy-start(f32[2,256,256]{2,1,0:T(8,128)} %get-tuple-element.27) | copy-start | bytes 1572868
  57.6 3.1 %collective-permute-start.5 = (f32[2,256,256]{2,1,0:T(8,128)}, f32[2,256,256]{2,1,0:T(8,128)S(1)}, u32[]{:S(2)}, u32[]{:S(2)}) collective-permute-start(f32[2,256,256]{2,1,0:T(8,128)} %get-tuple-element.22), channel_id=1, source_target_pairs={{0,16},{16,0},{1,17},{17,1},{2,18},{18,2},{3,19},{19,3},{4,20},{20... | collective-permute-start | bytes 1572872 | tf_op jit(solution)/shard_map/ppermute | solution.py:369
  62.6 13.3 %collective-permute-start.10 = (f32[2,256,256]{2,1,0:T(8,128)}, f32[2,256,256]{2,1,0:T(8,128)S(1)}, u32[]{:S(2)}, u32[]{:S(2)}) collective-permute-start(f32[2,256,256]{2,1,0:T(8,128)} %get-tuple-element.28), channel_id=1, source_target_pairs={{0,16},{16,32},{32,48},{48,64},{64,80},{80,96},{96,112},{1,17},{17... | collective-permute-start | bytes 1572872 | tf_op jit(solution)/shard_map/ppermute | solution.py:408
  64.6 23.9 %collective-permute-start.6 = (f32[2,256,256]{2,1,0:T(8,128)}, f32[2,256,256]{2,1,0:T(8,128)S(1)}, u32[]{:S(2)}, u32[]{:S(2)}) collective-permute-start(f32[2,256,256]{2,1,0:T(8,128)} %get-tuple-element.25), channel_id=1, source_target_pairs={{0,1},{1,2},{2,3},{3,4},{4,5},{5,6},{6,7},{7,8},{8,9},{9,10},{10,1... | collective-permute-start | bytes 1572872 | tf_op jit(solution)/shard_map/ppermute | solution.py:404
  68.1 20.2 %all-to-all-start = ((f32[16,32,256]{2,1,0:T(8,128)}), f32[16,32,256]{2,1,0:T(8,128)S(1)}, u32[]{:S(2)}, u32[]{:S(2)}) async-start(f32[16,32,256]{2,1,0:T(8,128)} %bitcast.4), calls=%async_computation | async-start | bytes 1048576 | tf_op jit(solution)/shard_map/all_to_all | solution.py:411
  76.0 22.8 %collective-permute-start.11 = (f32[2,256,256]{2,1,0:T(8,128)S(1)}, f32[2,256,256]{2,1,0:T(8,128)S(1)}, u32[]{:S(2)}, u32[]{:S(2)}) collective-permute-start(f32[2,256,256]{2,1,0:T(8,128)S(1)} %add.27), channel_id=1, source_target_pairs={{0,1},{1,2},{2,3},{3,4},{4,5},{5,6},{6,7},{7,8},{8,9},{9,10},{10,1... | collective-permute-start | bytes 1572872 | tf_op jit(solution)/shard_map/ppermute | solution.py:409
  88.4 10.3 %collective-permute-start.9 = (f32[32,256]{1,0:T(8,128)S(1)}, f32[32,256]{1,0:T(8,128)S(1)}, u32[]{:S(2)}, u32[]{:S(2)}) collective-permute-start(f32[32,256]{1,0:T(8,128)S(1)} %reduce_sum.9), channel_id=1, source_target_pairs={{0,3},{1,0},{2,1},{3,2},{4,7},{5,4},{6,5},{7,6},{8,11},{9,8},{10,9... | collective-permute-start | bytes 98312 | tf_op jit(solution)/shard_map/ppermute | solution.py:373
  93.5 5.2 %collective-permute-start.8 = (f32[32,256]{1,0:T(8,128)S(1)}, f32[32,256]{1,0:T(8,128)S(1)}, u32[]{:S(2)}, u32[]{:S(2)}) collective-permute-start(f32[32,256]{1,0:T(8,128)S(1)} %reduce_sum.9), channel_id=1, source_target_pairs={{0,1},{1,2},{2,3},{3,0},{4,5},{5,6},{6,7},{7,4},{8,9},{9,10},{10,1... | collective-permute-start | bytes 98312 | tf_op jit(solution)/shard_map/ppermute | solution.py:373
  93.5 5.2 %collective-permute-start.7 = (f32[32,256]{1,0:T(8,128)S(1)}, f32[32,256]{1,0:T(8,128)S(1)}, u32[]{:S(2)}, u32[]{:S(2)}) collective-permute-start(f32[32,256]{1,0:T(8,128)S(1)} %reduce_sum.9), channel_id=1, source_target_pairs={{0,2},{1,3},{2,0},{3,1},{4,6},{5,7},{6,4},{7,5},{8,10},{9,11},{10,... | collective-permute-start | bytes 98312 | tf_op jit(solution)/shard_map/ppermute | solution.py:373
  95.3 27.1 %collective-permute-start.4 = (f32[2,256,512]{2,1,0:T(8,128)}, f32[2,256,512]{2,1,0:T(8,128)S(1)}, u32[]{:S(2)}, u32[]{:S(2)}) collective-permute-start(f32[2,256,512]{2,1,0:T(8,128)} %get-tuple-element.20), channel_id=1, source_target_pairs={{0,16},{16,32},{32,48},{48,64},{64,80},{80,96},{96,112},{1,17},{17... | collective-permute-start | bytes 3145736 | tf_op jit(solution)/shard_map/ppermute | solution.py:405
  120.5 4.5 %collective-permute-start.12 = (f32[512,256]{1,0:T(8,128)S(1)}, f32[512,256]{1,0:T(8,128)S(1)}, u32[]{:S(2)}, u32[]{:S(2)}) collective-permute-start(f32[512,256]{1,0:T(8,128)S(1)} %bitcast.10), channel_id=1, source_target_pairs={{0,16},{16,0},{1,17},{17,1},{2,18},{18,2},{3,19},{19,3},{4,20},{20... | collective-permute-start | bytes 1572872 | tf_op jit(solution)/shard_map/ppermute | solution.py:369
  122.4 2.6 %copy-start.1 = (f32[2,2,256,256]{3,2,1,0:T(8,128)S(1)}, f32[2,2,256,256]{3,2,1,0:T(8,128)}, u32[]{:S(2)}) copy-start(f32[2,2,256,256]{3,2,1,0:T(8,128)} %probe.2) | copy-start | bytes 3145732
  122.4 2.6 %copy-start.5 = (s32[3]{0:T(128)S(1)}, s32[3]{0:T(128)}, u32[]{:S(2)}) copy-start(s32[3]{0:T(128)} %pad_add_fusion.anchor.place) | copy-start | bytes 40
